TPU v7x, 32 devices: a whole 2x2x4 slice. The times are simulated.
32 devices in a mesh: lon: 4 (over y, core), lat: 8 (over z, x).
Axes of the slice: x: 2, y: 2, z: 4, core: 2. Of those that a mesh axis runs over, the one named last changes fastest.
Arguments:
- state_pert: bfloat16 [32, 16, 6, 128, 256], P('lon', 'lat'), may hold values from -6 to 6
- state_mean: float32 [32, 16, 6, 256], P('lon', 'lat'), may hold values from -6 to 6
- obs_anom: bfloat16 [6144, 128, 128], P(('lon', 'lat')), may hold values from -6 to 6
- innov: float32 [6144, 128], P(('lon', 'lat')), may hold values from -12 to 12
- obs_rinv: float32 [6144, 128], P(('lon', 'lat')), may hold values from 0.25 to 4
- obs_lon: int32 [6144, 128], P(('lon', 'lat')), may hold values from 0 to 511, as said below
- obs_lat: int32 [6144, 128], P(('lon', 'lat')), may hold values from 40 to 215, as said below
- block_list: int32 [32, 16, 48], P('lon', 'lat'), may hold values from 0 to 6143, as said below
- block_count: int32 [32, 16], P('lon', 'lat'), may hold values from 24 to 48
Outputs:
- analysis: float32 [32, 16, 6, 128, 256], P('lon', 'lat')
Inputs may be any that keep to these rules, and one draw needn't show every extreme that they name: `block_list`: block b is held by the device of flat index b // 192 over lon+lat. The first 48 entries of a patch's list name distinct blocks. Over all list entries of the patches of one device, each holder holds exactly 24 of the named blocks (counting repeats over patches). Only the first block_count entries of a patch's list are used. `obs_lon`: the longitude indices of one block's observations lie within 32 consecutive columns, counted around the periodic grid. `obs_lat`: the latitude indices of one block's observations lie within 32 consecutive columns.
All inputs are finite; a program needn't handle non-finite values.
Results may differ from a plain program's by a relative error of at most 0.0023.
Values may be sent and summed in bfloat16 or wider, within the bound.
No kernel may reach another device: no remote copies, remote signals or barrier semaphores. Data moves between devices by JAX's collectives and lax.ppermute only.
A program may use at most 192 MiB of HBM per device.

v0:
```python
import jax
import jax.numpy as jnp
from jax import lax
from jax.sharding import PartitionSpec as P

PSIDE = 16
NS_ITERS = 5


loc_scale = 48.0


def product(left, right):
    return jnp.dot(left, right, precision=lax.Precision.HIGHEST)


def analyse(
    deviations,
    centre_state,
    anomalies,
    obs_fields,
    used_count,
    centre_lon,
    centre_lat,
    inflation,
    grid_lon,
):
    members = anomalies.shape[1]
    in_list = (jnp.arange(anomalies.shape[0]) < used_count).astype(jnp.float32)
    lon_gap = jnp.abs(obs_fields[:, 2] - centre_lon)
    lon_gap = jnp.minimum(lon_gap, grid_lon - lon_gap)
    lat_gap = obs_fields[:, 3] - centre_lat
    weight = (
        obs_fields[:, 1]
        * jnp.exp(-(lon_gap * lon_gap + lat_gap * lat_gap) / (2.0 * loc_scale * loc_scale))
        * in_list[:, None]
    )
    scaled = (anomalies * weight[:, None, :]).astype(jnp.bfloat16)
    gram_matrix = jnp.einsum("lko,lmo->km", scaled, anomalies, preferred_element_type=jnp.float32)
    projected = jnp.einsum(
        "lko,lo->k", scaled.astype(jnp.float32), obs_fields[:, 0], precision=lax.Precision.HIGHEST
    )
    identity = jnp.eye(members, dtype=jnp.float32)
    system = (members - 1) / inflation * identity + gram_matrix
    scaling = jnp.sqrt(jnp.sum(system * system))
    root = system / scaling
    inverse_root = identity
    for _ in range(NS_ITERS):
        factor = 1.5 * identity - 0.5 * product(inverse_root, root)
        root = product(root, factor)
        inverse_root = product(factor, inverse_root)
    inverse_sqrt = inverse_root / jnp.sqrt(scaling)
    mean_weights = product(inverse_sqrt, product(inverse_sqrt, projected[:, None]))
    weights = (jnp.sqrt(jnp.float32(members - 1)) * inverse_sqrt + mean_weights).astype(
        jnp.bfloat16
    )
    change = jnp.einsum("fjc,jk->fkc", deviations, weights, preferred_element_type=jnp.float32)
    return centre_state[:, None, :] + change


def on_device(
    state_pert, state_mean, obs_anom, innov, obs_rinv, obs_lon, obs_lat, block_list, block_count
):
    holders = lax.axis_size(("lon", "lat"))
    lon_devices = lax.axis_size("lon")
    lon_patches, lat_patches, fields, members, columns = state_pert.shape
    list_length = block_list.shape[2]
    held_blocks, _, block_obs = obs_anom.shape
    slot_total = lon_patches * lat_patches * list_length
    per_owner = slot_total // holders
    spread = jnp.einsum("bko,bko->bo", obs_anom, obs_anom, preferred_element_type=jnp.float32) / (
        members - 1
    )
    totals = lax.psum(
        (jnp.sum(obs_rinv * innov * innov), jnp.sum(obs_rinv * spread)), ("lon", "lat")
    )
    total_obs = holders * held_blocks * block_obs
    inflation = totals[0] / (totals[1] + total_obs)
    wanted = block_list.reshape(slot_total)
    holder = wanted // held_blocks
    held_index = wanted % held_blocks
    slot_order = jnp.arange(slot_total)
    earlier_same = (holder[:, None] == holder[None, :]) & (
        slot_order[None, :] < slot_order[:, None]
    )
    slot_rank = jnp.sum(earlier_same.astype(jnp.int32), axis=1)
    bucket = holder * per_owner + slot_rank
    requests = jnp.zeros((holders * per_owner,), jnp.int32).at[bucket].set(held_index)
    obs_fields = jnp.stack(
        [innov, obs_rinv, obs_lon.astype(jnp.float32), obs_lat.astype(jnp.float32)], axis=1
    )
    asked_for = lax.all_to_all(
        requests.reshape(holders, per_owner),
        ("lon", "lat"),
        split_axis=0,
        concat_axis=0,
        tiled=True,
    )
    got_anomalies = lax.all_to_all(
        obs_anom[asked_for], ("lon", "lat"), split_axis=0, concat_axis=0, tiled=True
    )
    got_fields = lax.all_to_all(
        obs_fields[asked_for], ("lon", "lat"), split_axis=0, concat_axis=0, tiled=True
    )
    patch_total = lon_patches * lat_patches
    slot_anomalies = got_anomalies.reshape(holders * per_owner, members, block_obs)[bucket]
    slot_anomalies = slot_anomalies.reshape(patch_total, list_length, members, block_obs)
    slot_fields = got_fields.reshape(holders * per_owner, 4, block_obs)[bucket]
    slot_fields = slot_fields.reshape(patch_total, list_length, 4, block_obs)
    patch_index = jnp.arange(patch_total)
    lon_first = lax.axis_index("lon") * lon_patches
    lat_first = lax.axis_index("lat") * lat_patches
    centre_lon = ((lon_first + patch_index // lat_patches) * PSIDE).astype(jnp.float32) + (
        PSIDE - 1
    ) / 2.0
    centre_lat = ((lat_first + patch_index % lat_patches) * PSIDE).astype(jnp.float32) + (
        PSIDE - 1
    ) / 2.0
    grid_lon = jnp.float32(lon_devices * lon_patches * PSIDE)

    def patch_update(inputs):
        deviations, centre_state, anomalies, fields_here, used_count, lon_centre, lat_centre = (
            inputs
        )
        return analyse(
            deviations,
            centre_state,
            anomalies,
            fields_here,
            used_count,
            lon_centre,
            lat_centre,
            inflation,
            grid_lon,
        )

    inputs = (
        state_pert.reshape(patch_total, fields, members, columns),
        state_mean.reshape(patch_total, fields, columns),
        slot_anomalies,
        slot_fields,
        block_count.reshape(patch_total),
        centre_lon,
        centre_lat,
    )
    updated = lax.map(patch_update, inputs)
    return updated.reshape(lon_patches, lat_patches, fields, members, columns)


def solution(mesh):
    in_specs = (
        P("lon", "lat", None, None, None),
        P("lon", "lat", None, None),
        P(("lon", "lat"), None, None),
        P(("lon", "lat"), None),
        P(("lon", "lat"), None),
        P(("lon", "lat"), None),
        P(("lon", "lat"), None),
        P("lon", "lat", None),
        P("lon", "lat"),
    )
    out_specs = P("lon", "lat", None, None, None)
    return jax.shard_map(
        on_device, mesh=mesh, in_specs=in_specs, out_specs=out_specs, check_vma=False
    )
```

profile of v0, /device:TPU:0, one launch (start us, length us, event | category | flops | bytes accessed | tf_op | source)
XLA Modules:
  0.0 955.9 jit_solution(11030705795602043068)
XLA Ops:
  2.3 3.4 scatter_custom_fusion
  6.4 7.3 all-to-all-start
  16.8 3.9 all-to-all-done
  20.8 3.4 gather_fusion.2
  26.9 22.0 %gather_fusion = bf16[768,128,128]{2,1,0:T(8,128)(2,1)} fusion(bf16[192,128,128]{2,1,0:T(8,128)(2,1)} %param.13, s32[1024]{0:T(1024)S(1)} %pad_clamp_fusion.1), kind=kCustom, calls=%fused_computation | custom fusion | bytes 50334720 | tf_op jit(solution)/shard_map/gather | solution.py:100
  48.9 16.8 %all-to-all-done.2 = f32[32,24,4,128]{3,2,1,0:T(4,128)S(1)} async-done(((f32[32,24,4,128]{3,2,1,0:T(4,128)}), f32[32,24,4,128]{3,2,1,0:T(4,128)S(1)}, u32[]{:S(2)}, u32[]{:S(2)}) %all-to-all-start.2) | async-done | bytes 1572896 | tf_op jit(solution)/shard_map/all_to_all | solution.py:102
  65.8 4.1 all-to-all-start.1
  69.9 5.3 fusion.50
  75.9 594.0 %all-reduce = (f32[]{:T(128)}, f32[]{:T(128)}) all-reduce(f32[]{:T(128)} %get-tuple-element.153, f32[]{:T(128)} %get-tuple-element.152), channel_id=1, replica_groups=mesh['lon'=4,'lat'=8] {'lon','lat'}, use_global_device_ids=true, to_apply=%region_3.0 | all-reduce | flops 2 | bytes 16 | tf_op jit(solution)/shard_map/psum | solution.py:74
  674.4 27.4 %gather_fusion.1 = bf16[768,128,128]{2,1,0:T(8,128)(2,1)} fusion(bf16[768,128,128]{2,1,0:T(8,128)(2,1)} %bitcast.27, s32[1024]{0:T(1024)S(1)} %pad_clamp_fusion), kind=kCustom, calls=%fused_computation.1 | custom fusion | bytes 50334720 | tf_op jit(solution)/shard_map/gather | solution.py:106
  701.8 254.2 %while.12 = (s32[]{:T(128)}, f32[16,6,128,256]{3,2,1,0:T(8,128)}, f32[16,6,256]{2,1,0:T(8,128)S(1)}, f32[]{:T(128)}, bf16[16,48,128,128]{3,2,1,0:T(8,128)(2,1)},...) while((s32[]{:T(128)}, f32[16,6,128,256]{3,2,1,0:T(8,128)}, ...), condition=%wide.region_8.9_spmd, body=%wide.region_6.8_spmd.sunk | while | flops 619339904 | bytes 9421381 | solution.py:146
  705.5 3.1 multiply_reduce_fusion.3
  721.3 3.1 multiply_reduce_fusion.3
  737.2 3.1 multiply_reduce_fusion.3
  753.1 3.2 multiply_reduce_fusion.3
  769.0 3.2 multiply_reduce_fusion.3
  784.9 3.2 multiply_reduce_fusion.3
  816.7 3.1 multiply_reduce_fusion.3
  832.6 3.1 multiply_reduce_fusion.3
  864.3 3.1 multiply_reduce_fusion.3
  880.1 3.1 multiply_reduce_fusion.3
  896.0 3.2 multiply_reduce_fusion.3
  911.9 3.2 multiply_reduce_fusion.3
  927.9 3.1 multiply_reduce_fusion.3
  (454 shorter events, 212.4 us)
Async XLA Ops:
  6.4 14.3 %all-to-all-start = ((s32[32,1,24]{2,1,0:T(1,128)}), s32[32,1,24]{2,1,0:T(1,128)S(1)}, u32[]{:S(2)}, u32[]{:S(2)}) async-start(s32[32,1,24]{2,1,0:T(1,128)} %bitcast.24), calls=%async_computation | async-start | bytes 32768 | tf_op jit(solution)/shard_map/all_to_all | solution.py:92
  24.2 41.5 %all-to-all-start.2 = ((f32[32,24,4,128]{3,2,1,0:T(4,128)}), f32[32,24,4,128]{3,2,1,0:T(4,128)S(1)}, u32[]{:S(2)}, u32[]{:S(2)}) async-start(f32[32,24,4,128]{3,2,1,0:T(4,128)} %bitcast.33), calls=%async_computation.2 | async-start | bytes 3145728 | tf_op jit(solution)/shard_map/all_to_all | solution.py:102
  65.8 608.6 %all-to-all-start.1 = ((bf16[32,24,128,128]{3,2,1,0:T(8,128)(2,1)}), bf16[32,24,128,128]{3,2,1,0:T(8,128)(2,1)}, u32[]{:S(2)}, u32[]{:S(2)}) async-start(bf16[32,24,128,128]{3,2,1,0:T(8,128)(2,1)} %bitcast.197), calls=%async_computation.1 | async-start | bytes 50331648 | tf_op jit(solution)/shard_map/all_to_all | solution.py:99
  69.9 5.3 copy-start
  69.9 5.3 copy-start.1
  69.9 600.1 %copy-start.2 = (f32[8,2,6,256]{3,1,2,0:T(2,128)S(1)}, f32[8,2,6,256]{3,1,2,0:T(2,128)}, u32[]{:S(2)}) copy-start(f32[8,2,6,256]{3,1,2,0:T(2,128)} %param.12) | copy-start | bytes 294916
  69.9 600.1 %copy-start.3 = (s32[8,2]{0,1:T(2,128)S(1)}, s32[8,2]{0,1:T(2,128)}, u32[]{:S(2)}) copy-start(s32[8,2]{0,1:T(2,128)} %param.19) | copy-start | bytes 196
where the time goes:
time: 958 us; the launch traced here: 956 us
  blocking collectives  594 us (62%)
  matrix products  182 us (19%)
  local copies, waits for them, and re-layouts  89 us (9%)
  other arithmetic  41 us (4%)
  waiting for transfers between devices  20.7 us (2%)
  starting transfers between devices  14.1 us (1%)
  loops' own time  13.6 us (1%)
    psum x1, blocking collectives, on_device(): lax.psum((jnp.sum(obs_rinv * innov * innov), jnp.sum(obs_rinv * spread)),...  594 us
    dot_general x256, matrix products, product(): return jnp.dot(left, right, precision=lax.Precision.HIGHEST)  51.7 us
    dot_general x16, matrix products, analyse(): jnp.einsum('lko,lmo->km', scaled, anomalies, preferred_element_type=jnp.f...  49.9 us
    dot_general x16, matrix products, analyse(): jnp.einsum('lko,lo->k', scaled.astype(jnp.float32), obs_fields[:, 0], pre...  43.7 us
    dot_general x16, matrix products, analyse(): jnp.einsum('fjc,jk->fkc', deviations, weights, preferred_element_type=jnp...  36.5 us
    dynamic_slice x80, local copies, waits for them, and re-layouts, on_device(): updated = lax.map(patch_update, inputs)  28.6 us
    gather x1, local copies, waits for them, and re-layouts, on_device(): got_anomalies.reshape(holders * per_owner, members, block_obs)[bucket]  27.4 us
    gather x1, local copies, waits for them, and re-layouts, on_device(): obs_anom[asked_for]  22 us
  transfers between devices with their start and end apart: 3, of which 2 were waited for; matrix products, arithmetic and copies ran while one was open for 4% of the time, Pallas kernels for 0%

commit v1 on v0

v1 whole, which is shorter than its diff:
```python
import functools

import jax
import jax.numpy as jnp
from jax import lax
from jax.experimental import pallas as pl
from jax.experimental.pallas import tpu as pltpu
from jax.sharding import PartitionSpec as P

PSIDE = 16
NS_ITERS = 5
LOC_SCALE = 48.0
GROUP = 4
EXT = 16
F32 = jnp.float32
BF16 = jnp.bfloat16
NT = (((1,), (1,)), ((), ()))


def halves(value):
    high = value.astype(BF16)
    return high, (value - high.astype(F32)).astype(BF16)


def request_table(block_list, block_count, holders, held_blocks):
    patches, length = block_list.shape
    slots = patches * length
    per_owner = slots // holders
    wanted = block_list.reshape(slots)
    used = (lax.broadcasted_iota(jnp.int32, (patches, length), 1) < block_count[:, None]).reshape(
        slots
    )
    holder = jnp.where(used, wanted // held_blocks, holders)
    order = jnp.arange(slots)
    before = (holder[:, None] == holder[None, :]) & (order[None, :] < order[:, None])
    rank = jnp.sum(before.astype(jnp.int32), axis=1)
    code = (order // length) * held_blocks + wanted % held_blocks
    place = holder * per_owner + rank
    hit = (place[None, :] == jnp.arange(holders * per_owner)[:, None]) & used[None, :]
    table = jnp.sum(jnp.where(hit, code[None, :], 0), axis=1).reshape(holders, per_owner)
    number = jnp.sum((holder[None, :] == jnp.arange(holders)[:, None]).astype(jnp.int32), axis=1)
    return jnp.concatenate([table, number[:, None]], axis=1)


def gram_kernel(
    sizes,
    targets_ref,
    requests_ref,
    anom_ref,
    ext_ref,
    lon_ref,
    lat_ref,
    rinv_ref,
    totals_ref,
    send_ref,
    keep_ref,
    acc_ref,
):
    patches, lat_patches, lon_patches, lat_devices, held, per_owner, grid_lon, sent = sizes
    step = pl.program_id(0)
    target = targets_ref[step]
    lon_first = (target // lat_devices) * lon_patches
    lat_first = (target % lat_devices) * lat_patches
    members = anom_ref.shape[1]
    acc_ref[...] = jnp.zeros_like(acc_ref)
    number = requests_ref[target, per_owner]

    def group(start, _):
        products = []
        for i in range(GROUP):
            entry = start * GROUP + i
            code = requests_ref[target, jnp.minimum(entry, per_owner - 1)]
            patch = code // held
            block = code % held
            centre_lon = (lon_first + patch // lat_patches) * (2 * PSIDE) + (PSIDE - 1)
            centre_lat = (lat_first + patch % lat_patches) * (2 * PSIDE) + (PSIDE - 1)
            lon_gap = jnp.abs(2 * lon_ref[pl.ds(block, 1), :] - centre_lon)
            lon_gap = jnp.minimum(lon_gap, 2 * grid_lon - lon_gap)
            lat_gap = 2 * lat_ref[pl.ds(block, 1), :] - centre_lat
            square = (lon_gap * lon_gap + lat_gap * lat_gap).astype(F32)
            rinv = jnp.where(entry < number, rinv_ref[pl.ds(block, 1), :], 0.0)
            weight = rinv * jnp.exp(square * (-1.0 / (8.0 * LOC_SCALE * LOC_SCALE)))
            anom = anom_ref[block]
            scaled = (anom.astype(F32) * weight).astype(BF16)
            left = jnp.concatenate([anom, ext_ref[block]], axis=0)
            product = lax.dot_general(left, scaled, NT, preferred_element_type=F32)
            products.append((patch, product[: members + 8]))
        for patch, product in products:
            acc_ref[patch] += product
        return 0

    lax.fori_loop(0, (number + GROUP - 1) // GROUP, group, 0)

    row = lax.broadcasted_iota(jnp.int32, (members, members), 0)
    column = lax.broadcasted_iota(jnp.int32, (members, members), 1)
    line = lax.broadcasted_iota(jnp.int32, (8, members), 0)

    def emit(out_ref):
        for pair in range(patches // 2):
            first = acc_ref[2 * pair]
            second = acc_ref[2 * pair + 1]
            packed = jnp.where(row < column, first[:members], second[:members])
            out_ref[0, pair, :members, :] = packed.astype(BF16)
            rows = totals_ref[...]
            for place, values in ((0, first), (2, second)):
                diagonal = jnp.sum(
                    jnp.where(row == column, values[:members], 0.0), axis=0, keepdims=True
                )
                projected = values[members : members + 1] + values[members + 1 : members + 2]
                rows = jnp.where(line == place, diagonal, rows)
                rows = jnp.where(line == place + 1, projected, rows)
            high = rows.astype(BF16).astype(F32)
            out_ref[0, pair, members:, :] = jnp.concatenate([high, rows - high], axis=0).astype(
                BF16
            )

    @pl.when(step < sent)
    def _():
        emit(send_ref)

    @pl.when(step >= sent)
    def _():
        emit(keep_ref)


def partial_grams(sizes, targets, requests, anom, ext, lon, lat, rinv, totals):
    patches, per_owner = sizes[0], sizes[5]
    sent = targets.shape[0] // 2
    members = anom.shape[1]
    rows = members + EXT
    block = (1, patches // 2, rows, members)
    whole = pl.BlockSpec(memory_space=pltpu.VMEM)
    half = jax.ShapeDtypeStruct((sent, patches // 2, rows, members), BF16)
    entries = 2 * sent * per_owner
    return pl.pallas_call(
        functools.partial(gram_kernel, (*sizes, sent)),
        out_shape=[half, half],
        grid_spec=pltpu.PrefetchScalarGridSpec(
            num_scalar_prefetch=2,
            grid=(2 * sent,),
            in_specs=[whole] * 6,
            out_specs=[
                pl.BlockSpec(block, lambda i, *_: (jnp.minimum(i, sent - 1), 0, 0, 0)),
                pl.BlockSpec(block, lambda i, *_: (jnp.maximum(i - sent, 0), 0, 0, 0)),
            ],
            scratch_shapes=[pltpu.VMEM((patches, members + 8, members), F32)],
        ),
        compiler_params=pltpu.CompilerParams(vmem_limit_bytes=32 * 2**20),
        cost_estimate=pl.CostEstimate(
            flops=entries * 8 * members**3, bytes_accessed=anom.size * 2, transcendentals=0
        ),
        name="partial_grams",
    )(targets, requests, anom, ext, lon, lat, rinv, totals)


def added(left, right):
    members = left.shape[-1]
    total = left.astype(F32) + right.astype(F32)
    rows = total[:, members : members + 8] + total[:, members + 8 :]
    high = rows.astype(BF16).astype(F32)
    rows = jnp.concatenate([high, rows - high], axis=1)
    return total[:, :members].astype(BF16), rows.astype(BF16)


def add_kernel(count, *refs):
    keep, got, outs = refs[:count], refs[count : 2 * count], refs[2 * count :]
    for i in range(count):
        members = keep[i].shape[-1]
        body, rows = added(keep[i][0], got[i][0])
        outs[i][0, :, :members, :] = body
        outs[i][0, :, members:, :] = rows


def add_all(keep, got):
    count = len(keep)
    shape = keep[0].shape
    spec = pl.BlockSpec((1, *shape[1:]), lambda i: (i, 0, 0, 0))
    size = keep[0].size * count
    return pl.pallas_call(
        functools.partial(add_kernel, count),
        out_shape=[jax.ShapeDtypeStruct(shape, BF16)] * count,
        grid=(shape[0],),
        in_specs=[spec] * (2 * count),
        out_specs=[spec] * count,
        compiler_params=pltpu.CompilerParams(vmem_limit_bytes=16 * 2**20),
        cost_estimate=pl.CostEstimate(flops=size * 4, bytes_accessed=size * 6, transcendentals=0),
        name="add_partials",
    )(*keep, *got)


def product(left, right):
    left_high, left_low = left
    right_high, right_low = right
    return jnp.dot(
        jnp.concatenate([left_high, left_low, left_high], axis=1),
        jnp.concatenate([right_high, right_high, right_low], axis=0),
        preferred_element_type=F32,
    )


def solve_kernel(count, total_obs, *refs):
    parts, (out_ref,) = refs[:count], refs[count:]
    pairs, rows, members = parts[0].shape
    row = lax.broadcasted_iota(jnp.int32, (members, members), 0)
    column = lax.broadcasted_iota(jnp.int32, (members, members), 1)
    identity = (row == column).astype(F32)

    def gathered(pair):
        total = parts[0][pair].astype(F32)
        for part in parts[1:]:
            total = total + part[pair].astype(F32)
        return total[:members], total[members : members + 8] + total[members + 8 :]

    def some(step, _):
        systems, projected = [], []
        for pair in (2 * step, 2 * step + 1):
            packed, values = gathered(pair)
            flipped = packed.T
            innovation = jnp.sum(values[4:5], axis=1, keepdims=True)
            spread = jnp.sum(values[5:6], axis=1, keepdims=True)
            ridge = (members - 1) * (spread + total_obs) / innovation
            for place, full in (
                (0, jnp.where(row < column, packed, flipped)),
                (2, jnp.where(row > column, packed, flipped)),
            ):
                full = jnp.where(row == column, values[place : place + 1], full)
                systems.append(full + ridge * identity)
                projected.append(values[place + 1 : place + 2])
        scalings, roots, inverses = [], [], []
        for system in systems:
            squares = jnp.sum(system * system, axis=0, keepdims=True)
            scaling = jnp.sqrt(jnp.sum(squares, axis=1, keepdims=True))
            scalings.append(scaling)
            roots.append(system / scaling)
        factors = [1.5 * identity - 0.5 * root for root in roots]
        roots = [product(halves(f), halves(r)) for f, r in zip(factors, roots)]
        inverses = factors
        for iteration in range(1, NS_ITERS):
            split_roots = [halves(r) for r in roots]
            split_inverses = [halves(z) for z in inverses]
            factors = [
                halves(1.5 * identity - 0.5 * product(z, r))
                for z, r in zip(split_inverses, split_roots)
            ]
            if iteration < NS_ITERS - 1:
                both = [
                    product(f, [jnp.concatenate([a, b], axis=1) for a, b in zip(r, z)])
                    for f, r, z in zip(factors, split_roots, split_inverses)
                ]
                roots = [b[:, :members] for b in both]
                inverses = [b[:, members:] for b in both]
            else:
                inverses = [product(f, z) for f, z in zip(factors, split_inverses)]
        for i in range(4):
            inverse_sqrt = inverses[i] * lax.rsqrt(scalings[i])
            inner = jnp.sum(inverse_sqrt * projected[i], axis=1, keepdims=True)
            mean = jnp.sum(inverse_sqrt * inner, axis=0, keepdims=True)
            out_ref[4 * step + i] = (
                jnp.sqrt(F32(members - 1)) * inverse_sqrt + mean
            ).astype(BF16)
        return 0

    lax.fori_loop(0, pairs // 2, some, 0)


def solve(parts, total_obs):
    pairs, rows, members = parts[0].shape
    whole = pl.BlockSpec(memory_space=pltpu.VMEM)
    return pl.pallas_call(
        functools.partial(solve_kernel, len(parts), total_obs),
        out_shape=jax.ShapeDtypeStruct((2 * pairs, members, members), BF16),
        in_specs=[whole] * len(parts),
        out_specs=whole,
        compiler_params=pltpu.CompilerParams(vmem_limit_bytes=32 * 2**20),
        name="solve",
    )(*parts)


def analysis_kernel(weights_ref, pert_ref, mean_ref, out_ref):
    for field in range(pert_ref.shape[1]):
        change = jnp.dot(weights_ref[0], pert_ref[0, field], preferred_element_type=F32)
        out_ref[0, field] = change + mean_ref[0, field : field + 1]


def analysis(weights, pert, mean):
    patches, fields, members, columns = pert.shape
    return pl.pallas_call(
        analysis_kernel,
        out_shape=jax.ShapeDtypeStruct(pert.shape, F32),
        grid=(patches,),
        in_specs=[
            pl.BlockSpec((1, members, members), lambda i: (i, 0, 0)),
            pl.BlockSpec((1, fields, members, columns), lambda i: (i, 0, 0, 0)),
            pl.BlockSpec((1, fields, columns), lambda i: (i, 0, 0)),
        ],
        out_specs=pl.BlockSpec((1, fields, members, columns), lambda i: (i, 0, 0, 0)),
        compiler_params=pltpu.CompilerParams(vmem_limit_bytes=16 * 2**20),
        name="analysis",
    )(weights, pert, mean)


def swap(value, axis, flip):
    size = lax.axis_size(axis)
    return lax.ppermute(value, axis, [(i, i ^ flip) for i in range(size)])


def on_device(
    state_pert, state_mean, obs_anom, innov, obs_rinv, obs_lon, obs_lat, block_list, block_count
):
    lon_devices, lat_devices = lax.axis_size("lon"), lax.axis_size("lat")
    holders = lon_devices * lat_devices
    lon_patches, lat_patches, fields, members, columns = state_pert.shape
    patches = lon_patches * lat_patches
    length = block_list.shape[2]
    held, _, block_obs = obs_anom.shape
    per_owner = patches * length // holders
    table = request_table(
        block_list.reshape(patches, length), block_count.reshape(patches), holders, held
    )
    requests = lax.all_to_all(table, ("lon", "lat"), split_axis=0, concat_axis=0, tiled=True)

    squares = jnp.sum(jnp.square(obs_anom.astype(F32)), axis=1) / (members - 1)
    zero = jnp.zeros((block_obs,), F32)
    totals = jnp.stack(
        [zero] * 4
        + [jnp.sum(obs_rinv * innov * innov, axis=0), jnp.sum(obs_rinv * squares, axis=0)]
        + [zero] * 2
    )
    innov_high = innov.astype(BF16).astype(F32)
    line = lax.broadcasted_iota(jnp.int32, (held, EXT, block_obs), 1)
    ext = jnp.where(
        line == 0,
        innov_high[:, None, :],
        jnp.where(line == 1, (innov - innov_high)[:, None, :], 0.0),
    ).astype(BF16)

    me_lon, me_lat = lax.axis_index("lon"), lax.axis_index("lat")
    sizes = (
        patches,
        lat_patches,
        lon_patches,
        lat_devices,
        held,
        per_owner,
        lon_devices * lon_patches * PSIDE,
    )

    def chunk(far):
        others = [(lon, near) for lon in range(0, lon_devices, 2) for near in range(2)]
        order = [(lon + core, near) for core in (1, 0) for lon, near in others]
        targets = jnp.stack(
            [(me_lon ^ lon) * lat_devices + (me_lat ^ (2 * far + near)) for lon, near in order]
        ).astype(jnp.int32)
        send, keep = partial_grams(
            sizes, targets, requests, obs_anom, ext, obs_lon, obs_lat, obs_rinv, totals
        )
        got = swap(send, "lon", 1)
        [total] = add_all([keep], [got])
        total = total.reshape(lon_devices // 2, 2, *total.shape[1:])
        cut = patches // 4
        first, second = total[:, :, :cut], total[:, :, cut:]
        shape = (-1, *first.shape[2:])
        far_lon = lon_devices // 4
        keeps = [first[:, 0], second[:far_lon].reshape(shape)]
        gots = [swap(first[:, 1], "lat", 1), swap(second[far_lon:].reshape(shape), "lon", lon_devices // 2)]
        first, second = add_all(keeps, gots)
        second = second.reshape(far_lon, 2, *second.shape[1:])
        keeps = [first[:far_lon], second[:, 0]]
        gots = [swap(first[far_lon:], "lon", lon_devices // 2), swap(second[:, 1], "lat", 1)]
        left = far_lon
        first, second = add_all(keeps, gots)
        while left > 1:
            left //= 2
            keeps = [first[:left], second[:left]]
            gots = [swap(v[left:], "lon", 2 * left) for v in (first, second)]
            first, second = add_all(keeps, gots)
        return jnp.concatenate([first[0], second[0]], axis=0)

    parts = []
    for far in reversed(range(lat_devices // 2)):
        total = chunk(far)
        parts.append(swap(total, "lat", 2 * far) if far else total)
    weights = solve(parts, holders * held * block_obs)
    updated = analysis(
        weights,
        state_pert.reshape(patches, fields, members, columns),
        state_mean.reshape(patches, fields, columns),
    )
    return updated.reshape(lon_patches, lat_patches, fields, members, columns)


def solution(mesh):
    in_specs = (
        P("lon", "lat", None, None, None),
        P("lon", "lat", None, None),
        P(("lon", "lat"), None, None),
        P(("lon", "lat"), None),
        P(("lon", "lat"), None),
        P(("lon", "lat"), None),
        P(("lon", "lat"), None),
        P("lon", "lat", None),
        P("lon", "lat"),
    )
    out_specs = P("lon", "lat", None, None, None)
    return jax.shard_map(
        on_device, mesh=mesh, in_specs=in_specs, out_specs=out_specs, check_vma=False
    )
```

time: 958 us -> 185 us (0.19)
  blocking collectives: 594 us -> 0 us
  matrix products: 182 us -> 0 us
  Pallas kernels: 0 us -> 82.9 us
  local copies, waits for them, and re-layouts: 89 us -> 25.6 us
  other arithmetic: 41 us -> 10.1 us
  starting transfers between devices: 14.1 us -> 31.3 us
  loops' own time: 13.6 us -> 0 us
  waiting for transfers between devices: 20.7 us -> 31.2 us
    psum x1 -> x0, blocking collectives: 594 us -> none  [on_device(): lax.psum((jnp.sum(obs_rinv * innov * innov), jnp.sum(obs_rinv * spread)),...]
    dot_general x304 -> x0, matrix products: 182 us -> none  [the longest x256 51.7 us: product(): return jnp.dot(left, right, precision=lax.Precision.HIGHEST)]
    pallas_call x0 -> x18, Pallas kernels: none -> 82.9 us  [the longest x4 60.9 us: partial_grams(): pl.pallas_call(functools.partial(gram_kernel, (*sizes, sent)), out_shape=...]
    gather x4 -> x0, local copies, waits for them, and re-layouts: 55.6 us -> none  [the longest x1 27.4 us: on_device(): got_anomalies.reshape(holders * per_owner, members, block_obs)[bucket]]
    ppermute x0 -> x23, waiting for transfers between devices: none -> 31.2 us  [swap(): return lax.ppermute(value, axis, [(i, i ^ flip) for i in range(size)])]
    dynamic_slice x80 -> x0, local copies, waits for them, and re-layouts: 28.6 us -> none  [on_device(): updated = lax.map(patch_update, inputs)]
    ppermute x0 -> x23, starting transfers between devices: none -> 24 us  [swap(): return lax.ppermute(value, axis, [(i, i ^ flip) for i in range(size)])]
    unnamed x10 -> x58, local copies, waits for them, and re-layouts: 0.12 us -> 22.4 us
  transfers between devices with their start and end apart: 3 -> 24, of which waited for: 2 -> 10; matrix products, arithmetic and copies ran while one was open for 4% -> 5% of each run, Pallas kernels for 0% -> 27%
where the time goes in v1:
time: 185 us; the launch traced here: 182 us
  Pallas kernels  82.9 us (45%)
  starting transfers between devices  31.3 us (17%)
  waiting for transfers between devices  31.2 us (17%)
  local copies, waits for them, and re-layouts  25.6 us (14%)
  other arithmetic  10.1 us (5%)
    pallas_call x4, Pallas kernels, partial_grams(): pl.pallas_call(functools.partial(gram_kernel, (*sizes, sent)), out_shape=...  60.9 us
    ppermute x23, waiting for transfers between devices, swap(): return lax.ppermute(value, axis, [(i, i ^ flip) for i in range(size)])  31.2 us
    ppermute x23, starting transfers between devices, swap(): return lax.ppermute(value, axis, [(i, i ^ flip) for i in range(size)])  24 us
    unnamed x58, local copies, waits for them, and re-layouts  22.4 us
    pallas_call x1, Pallas kernels, analysis(): pl.pallas_call(analysis_kernel, out_shape=jax.ShapeDtypeStruct(pert.shape...  9.35 us
    pallas_call x1, Pallas kernels, solve(): pl.pallas_call(functools.partial(solve_kernel, len(parts), total_obs), ou...  8.31 us
    all_to_all x1, starting transfers between devices, on_device(): lax.all_to_all(table, ('lon', 'lat'), split_axis=0, concat_axis=0, tiled=...  7.3 us
    reduce_sum x1, other arithmetic, on_device(): squares = jnp.sum(jnp.square(obs_anom.astype(F32)), axis=1) / (members - 1)  5.25 us
  transfers between devices with their start and end apart: 24, of which 10 were waited for; matrix products, arithmetic and copies ran while one was open for 5% of the time, Pallas kernels for 27%

profile of v1, /device:TPU:0, one launch (start us, length us, event | category | flops | bytes accessed | tf_op | source)
XLA Modules:
  0.0 181.7 jit_solution(890450962470594144)
XLA Ops:
  4.6 7.3 %all-to-all-start = ((s32[32,1,25]{2,1,0:T(1,128)}), s32[32,1,25]{2,1,0:T(1,128)S(1)}, u32[]{:S(2)}, u32[]{:S(2)}) async-start(s32[32,1,25]{2,1,0:T(1,128)} %bitcast.10), calls=%async_computation | async-start | bytes 32768 | tf_op jit(solution)/shard_map/all_to_all | solution.py:320
  13.0 5.3 %multiply_reduce_fusion = f32[192,128]{1,0:T(8,128)S(1)} fusion(bf16[192,128,128]{2,1,0:T(8,128)(2,1)} %anom_ref.7), kind=kLoop, calls=%fused_computation | loop fusion | flops 9412608 | bytes 6389760 | tf_op jit(solution)/shard_map/reduce_sum | solution.py:322
  19.3 2.8 %copy-done = bf16[192,128,128]{2,1,0:T(8,128)(2,1)S(1)} copy-done((bf16[192,128,128]{2,1,0:T(8,128)(2,1)S(1)}, bf16[192,128,128]{2,1,0:T(8,128)(2,1)}, u32[]{:S(2)}) %copy-start) | copy-done | bytes 6291480
  22.1 15.5 %partial_grams.7 = (bf16[4,8,144,128]{3,2,1,0:T(8,128)(2,1)}, bf16[4,8,144,128]{3,2,1,0:T(8,128)(2,1)S(1)}) custom-call(s32[8]{0:T(128)S(1)} %stack.163.targets_ref, s32[32,25]{1,0:T(8,128)S(1)} %bitcast.130, bf16[192,128,128]{2,1,0:T(8,128)(2,1)S(1)} %copy-done, bf16[192,16,128]{2,1,0:T(8,128)(2,1)S(1)} %select_convert_fusion.ext_ref, ...), custom_call_target="tpu_custom_call" | custom-call | flops 3221225472 | bytes 6291456 | tf_op jit(solution)/shard_map/partial_grams/pallas_call | solution.py:135
  38.2 2.8 %copy-done.1 = bf16[192,128,128]{2,1,0:T(8,128)(2,1)S(1)} copy-done((bf16[192,128,128]{2,1,0:T(8,128)(2,1)S(1)}, bf16[192,128,128]{2,1,0:T(8,128)(2,1)}, u32[]{:S(2)}) %copy-start.1) | copy-done | bytes 6291480
  46.1 16.1 %partial_grams.6 = (bf16[4,8,144,128]{3,2,1,0:T(8,128)(2,1)}, bf16[4,8,144,128]{3,2,1,0:T(8,128)(2,1)S(1)}) custom-call(s32[8]{0:T(128)S(1)} %copy-done.16, s32[32,25]{1,0:T(8,128)S(1)} %bitcast.131, bf16[192,128,128]{2,1,0:T(8,128)(2,1)S(1)} %copy-done.1, bf16[192,16,128]{2,1,0:T(8,128)(2,1)S(1)} %copy-done.5, s32[192,128]{1,0:T(8,128)S(1)} %copy-done.19, ...), custom_call_target="tpu_custom_call" | custom-call | flops 3221225472 | bytes 6291456 | tf_op jit(solution)/shard_map/partial_grams/pallas_call | solution.py:135
  63.4 2.8 %copy-done.2 = bf16[192,128,128]{2,1,0:T(8,128)(2,1)S(1)} copy-done((bf16[192,128,128]{2,1,0:T(8,128)(2,1)S(1)}, bf16[192,128,128]{2,1,0:T(8,128)(2,1)}, u32[]{:S(2)}) %copy-start.2) | copy-done | bytes 6291480
  71.3 14.7 %partial_grams.5 = (bf16[4,8,144,128]{3,2,1,0:T(8,128)(2,1)S(1)}, bf16[4,8,144,128]{3,2,1,0:T(8,128)(2,1)S(1)}) custom-call(s32[8]{0:T(128)S(1)} %copy-done.17, s32[32,25]{1,0:T(8,128)S(1)} %bitcast.132, bf16[192,128,128]{2,1,0:T(8,128)(2,1)S(1)} %copy-done.2, bf16[192,16,128]{2,1,0:T(8,128)(2,1)S(1)} %copy-done.6, s32[192,128]{1,0:T(8,128)S(1)} %copy-done.20, ...), custom_call_target="tpu_custom_call" | custom-call | flops 3221225472 | bytes 6291456 | tf_op jit(solution)/shard_map/partial_grams/pallas_call | solution.py:135
  86.1 2.8 %copy-done.3 = bf16[192,128,128]{2,1,0:T(8,128)(2,1)S(1)} copy-done((bf16[192,128,128]{2,1,0:T(8,128)(2,1)S(1)}, bf16[192,128,128]{2,1,0:T(8,128)(2,1)}, u32[]{:S(2)}) %copy-start.3) | copy-done | bytes 6291480
  88.9 14.7 %partial_grams.4 = (bf16[4,8,144,128]{3,2,1,0:T(8,128)(2,1)S(1)}, bf16[4,8,144,128]{3,2,1,0:T(8,128)(2,1)S(1)}) custom-call(s32[8]{0:T(128)S(1)} %copy-done.15, s32[32,25]{1,0:T(8,128)S(1)} %bitcast.133, bf16[192,128,128]{2,1,0:T(8,128)(2,1)S(1)} %copy-done.3, bf16[192,16,128]{2,1,0:T(8,128)(2,1)S(1)} %copy-done.7, s32[192,128]{1,0:T(8,128)S(1)} %copy-done.20, ...), custom_call_target="tpu_custom_call" | custom-call | flops 3221225472 | bytes 6291456 | tf_op jit(solution)/shard_map/partial_grams/pallas_call | solution.py:135
  104.5 2.2 %add_partials.18 = bf16[4,8,144,128]{3,2,1,0:T(8,128)(2,1)S(1)} custom-call(bf16[4,8,144,128]{3,2,1,0:T(8,128)(2,1)S(1)} %get-tuple-element.41.refs_0_, bf16[4,8,144,128]{3,2,1,0:T(8,128)(2,1)} %collective-permute-done.12.refs_1_), custom_call_target="tpu_custom_call" | custom-call | flops 2359296 | bytes 3538944 | tf_op jit(solution)/shard_map/add_partials/pallas_call | solution.py:179
  106.8 2.1 %collective-permute-start.14 = (bf16[2,4,144,128]{3,2,1,0:T(8,128)(2,1)S(1)}, bf16[2,4,144,128]{3,2,1,0:T(8,128)(2,1)S(1)}, u32[]{:S(2)}, u32[]{:S(2)}) collective-permute-start(bf16[2,4,144,128]{3,2,1,0:T(8,128)(2,1)S(1)} %get-tuple-element.59), channel_id=1, source_target_pairs={{0,16},{8,24},{16,0},{24,8},{1,17},{9,25},{17,1},{25,9},{2,18},{10... | collective-permute-start | bytes 884744 | tf_op jit(solution)/shard_map/ppermute | solution.py:304
  111.8 2.1 %collective-permute-done.20.refs_3_ = bf16[2,4,144,128]{3,2,1,0:T(8,128)(2,1)S(1)} collective-permute-done((bf16[2,4,144,128]{3,2,1,0:T(8,128)(2,1)S(1)}, bf16[2,4,144,128]{3,2,1,0:T(8,128)(2,1)S(1)}, u32[]{:S(2)}, u32[]{:S(2)}) %collective-permute-start.20) | collective-permute-done | bytes 294944 | tf_op jit(solution)/shard_map/ppermute | solution.py:304
  116.3 3.9 %collective-permute-done.14.refs_3_ = bf16[2,4,144,128]{3,2,1,0:T(8,128)(2,1)S(1)} collective-permute-done((bf16[2,4,144,128]{3,2,1,0:T(8,128)(2,1)S(1)}, bf16[2,4,144,128]{3,2,1,0:T(8,128)(2,1)S(1)}, u32[]{:S(2)}, u32[]{:S(2)}) %collective-permute-start.14) | collective-permute-done | bytes 294944 | tf_op jit(solution)/shard_map/ppermute | solution.py:304
  120.7 2.0 %collective-permute-start.15 = (bf16[1,4,144,128]{3,2,1,0:T(8,128)(2,1)S(1)}, bf16[1,4,144,128]{3,2,1,0:T(8,128)(2,1)S(1)}, u32[]{:S(2)}, u32[]{:S(2)}) collective-permute-start(bf16[1,4,144,128]{3,2,1,0:T(8,128)(2,1)S(1)} %get-tuple-element.77), channel_id=1, source_target_pairs={{0,16},{8,24},{16,0},{24,8},{1,17},{9,25},{17,1},{25,9},{2,18},{10... | collective-permute-start | bytes 442376 | tf_op jit(solution)/shard_map/ppermute | solution.py:304
  122.7 3.8 %collective-permute-done.8.refs_3_ = bf16[2,4,144,128]{3,2,1,0:T(8,128)(2,1)S(1)} collective-permute-done((bf16[2,4,144,128]{3,2,1,0:T(8,128)(2,1)S(1)}, bf16[2,4,144,128]{3,2,1,0:T(8,128)(2,1)S(1)}, u32[]{:S(2)}, u32[]{:S(2)}) %collective-permute-start.8) | collective-permute-done | bytes 294944 | tf_op jit(solution)/shard_map/ppermute | solution.py:304
  127.0 2.0 %collective-permute-start.9 = (bf16[1,4,144,128]{3,2,1,0:T(8,128)(2,1)S(1)}, bf16[1,4,144,128]{3,2,1,0:T(8,128)(2,1)S(1)}, u32[]{:S(2)}, u32[]{:S(2)}) collective-permute-start(bf16[1,4,144,128]{3,2,1,0:T(8,128)(2,1)S(1)} %get-tuple-element.81), channel_id=1, source_target_pairs={{0,16},{8,24},{16,0},{24,8},{1,17},{9,25},{17,1},{25,9},{2,18},{10... | collective-permute-start | bytes 442376 | tf_op jit(solution)/shard_map/ppermute | solution.py:304
  129.1 3.8 %collective-permute-done.2.refs_3_ = bf16[2,4,144,128]{3,2,1,0:T(8,128)(2,1)S(1)} collective-permute-done((bf16[2,4,144,128]{3,2,1,0:T(8,128)(2,1)S(1)}, bf16[2,4,144,128]{3,2,1,0:T(8,128)(2,1)S(1)}, u32[]{:S(2)}, u32[]{:S(2)}) %collective-permute-start.2) | collective-permute-done | bytes 294944 | tf_op jit(solution)/shard_map/ppermute | solution.py:304
  136.4 2.7 %collective-permute-start.17 = (bf16[8,144,128]{2,1,0:T(8,128)(2,1)S(1)}, bf16[8,144,128]{2,1,0:T(8,128)(2,1)S(1)}, u32[]{:S(2)}, u32[]{:S(2)}) collective-permute-start(bf16[8,144,128]{2,1,0:T(8,128)(2,1)S(1)} %pad_maximum_fusion.2), channel_id=1, source_target_pairs={{0,2},{1,3},{2,0},{3,1},{4,6},{5,7},{6,4},{7,5},{8,10},{9,11},{10,... | collective-permute-start | bytes 884744 | tf_op jit(solution)/shard_map/ppermute | solution.py:304
  139.8 3.8 %collective-permute-start.11 = (bf16[8,144,128]{2,1,0:T(8,128)(2,1)S(1)}, bf16[8,144,128]{2,1,0:T(8,128)(2,1)S(1)}, u32[]{:S(2)}, u32[]{:S(2)}) collective-permute-start(bf16[8,144,128]{2,1,0:T(8,128)(2,1)S(1)} %pad_maximum_fusion.1), channel_id=1, source_target_pairs={{0,4},{1,5},{2,6},{3,7},{4,0},{5,1},{6,2},{7,3},{8,12},{9,13},{10,... | collective-permute-start | bytes 884744 | tf_op jit(solution)/shard_map/ppermute | solution.py:304
  147.7 2.5 %collective-permute-done.21.refs_2_ = bf16[1,4,144,128]{3,2,1,0:T(8,128)(2,1)S(1)} collective-permute-done((bf16[1,4,144,128]{3,2,1,0:T(8,128)(2,1)S(1)}, bf16[1,4,144,128]{3,2,1,0:T(8,128)(2,1)S(1)}, u32[]{:S(2)}, u32[]{:S(2)}) %collective-permute-start.21) | collective-permute-done | bytes 147488 | tf_op jit(solution)/shard_map/ppermute | solution.py:304
  151.7 12.3 %collective-permute-done.11.refs_1_ = bf16[8,144,128]{2,1,0:T(8,128)(2,1)S(1)} collective-permute-done((bf16[8,144,128]{2,1,0:T(8,128)(2,1)S(1)}, bf16[8,144,128]{2,1,0:T(8,128)(2,1)S(1)}, u32[]{:S(2)}, u32[]{:S(2)}) %collective-permute-start.11) | collective-permute-done | bytes 294944 | tf_op jit(solution)/shard_map/ppermute | solution.py:304
  164.0 8.3 %solve.1.weights_ref = bf16[16,128,128]{2,1,0:T(8,128)(2,1)S(1)} custom-call(bf16[8,144,128]{2,1,0:T(8,128)(2,1)S(1)} %collective-permute-done.5.refs_0_, bf16[8,144,128]{2,1,0:T(8,128)(2,1)S(1)} %collective-permute-done.11.refs_1_, bf16[8,144,128]{2,1,0:T(8,128)(2,1)S(1)} %collective-permute-done.17.refs_2_, bf16[8,144,128]{2,1,0:T(8,128)(2,1)S(1)} %pad_maximum_fusion.3.refs_3_), custom_call_target="tpu_custom_call" | custom-call | tf_op jit(solution)/shard_map/solve/pallas_call | solution.py:269
  172.3 9.3 %analysis.1 = f32[16,6,128,256]{3,2,1,0:T(8,128)} custom-call(bf16[16,128,128]{2,1,0:T(8,128)(2,1)S(1)} %solve.1.weights_ref, bf16[16,6,128,256]{3,2,1,0:T(8,128)(2,1)S(1)} %bitcast.108, f32[16,6,256]{2,1,0:T(8,128)S(1)} %bitcast.117), custom_call_target="tpu_custom_call" | custom-call | tf_op jit(solution)/shard_map/analysis/pallas_call | solution.py:287
  (151 shorter events, 35.5 us)
Async XLA Ops:
  4.6 14.4 %all-to-all-start = ((s32[32,1,25]{2,1,0:T(1,128)}), s32[32,1,25]{2,1,0:T(1,128)S(1)}, u32[]{:S(2)}, u32[]{:S(2)}) async-start(s32[32,1,25]{2,1,0:T(1,128)} %bitcast.10), calls=%async_computation | async-start | bytes 32768 | tf_op jit(solution)/shard_map/all_to_all | solution.py:320
  37.6 66.1 %collective-permute-start.18 = (bf16[4,8,144,128]{3,2,1,0:T(8,128)(2,1)}, bf16[4,8,144,128]{3,2,1,0:T(8,128)(2,1)S(1)}, u32[]{:S(2)}, u32[]{:S(2)}) collective-permute-start(bf16[4,8,144,128]{3,2,1,0:T(8,128)(2,1)} %get-tuple-element.48), channel_id=1, source_target_pairs={{0,8},{8,0},{16,24},{24,16},{1,9},{9,1},{17,25},{25,17},{2,10},{10... | collective-permute-start | bytes 3538952 | tf_op jit(solution)/shard_map/ppermute | solution.py:304
  62.1 42.4 %collective-permute-start.12 = (bf16[4,8,144,128]{3,2,1,0:T(8,128)(2,1)}, bf16[4,8,144,128]{3,2,1,0:T(8,128)(2,1)}, u32[]{:S(2)}, u32[]{:S(2)}) collective-permute-start(bf16[4,8,144,128]{3,2,1,0:T(8,128)(2,1)} %get-tuple-element.42), channel_id=1, source_target_pairs={{0,8},{8,0},{16,24},{24,16},{1,9},{9,1},{17,25},{25,17},{2,10},{10... | collective-permute-start | bytes 3538952 | tf_op jit(solution)/shard_map/ppermute | solution.py:304
  86.0 22.9 %collective-permute-start.6 = (bf16[4,8,144,128]{3,2,1,0:T(8,128)(2,1)S(1)}, bf16[4,8,144,128]{3,2,1,0:T(8,128)(2,1)S(1)}, u32[]{:S(2)}, u32[]{:S(2)}) collective-permute-start(bf16[4,8,144,128]{3,2,1,0:T(8,128)(2,1)S(1)} %get-tuple-element.36), channel_id=1, source_target_pairs={{0,8},{8,0},{16,24},{24,16},{1,9},{9,1},{17,25},{25,17},{2,10},{10... | collective-permute-start | bytes 3538952 | tf_op jit(solution)/shard_map/ppermute | solution.py:304
  103.6 7.7 %collective-permute-start = (bf16[4,8,144,128]{3,2,1,0:T(8,128)(2,1)S(1)}, bf16[4,8,144,128]{3,2,1,0:T(8,128)(2,1)S(1)}, u32[]{:S(2)}, u32[]{:S(2)}) collective-permute-start(bf16[4,8,144,128]{3,2,1,0:T(8,128)(2,1)S(1)} %get-tuple-element.30), channel_id=1, source_target_pairs={{0,8},{8,0},{16,24},{24,16},{1,9},{9,1},{17,25},{25,17},{2,10},{10... | collective-permute-start | bytes 3538952 | tf_op jit(solution)/shard_map/ppermute | solution.py:304
  104.1 9.9 %collective-permute-start.20 = (bf16[2,4,144,128]{3,2,1,0:T(8,128)(2,1)S(1)}, bf16[2,4,144,128]{3,2,1,0:T(8,128)(2,1)S(1)}, u32[]{:S(2)}, u32[]{:S(2)}) collective-permute-start(bf16[2,4,144,128]{3,2,1,0:T(8,128)(2,1)S(1)} %get-tuple-element.55), channel_id=1, source_target_pairs={{0,16},{8,24},{16,0},{24,8},{1,17},{9,25},{17,1},{25,9},{2,18},{10... | collective-permute-start | bytes 884744 | tf_op jit(solution)/shard_map/ppermute | solution.py:304
  104.2 10.0 %collective-permute-start.19 = (bf16[2,4,144,128]{3,2,1,0:T(8,128)(2,1)S(1)}, bf16[2,4,144,128]{3,2,1,0:T(8,128)(2,1)S(1)}, u32[]{:S(2)}, u32[]{:S(2)}) collective-permute-start(bf16[2,4,144,128]{3,2,1,0:T(8,128)(2,1)S(1)} %get-tuple-element.57), channel_id=1, source_target_pairs={{0,1},{1,0},{2,3},{3,2},{4,5},{5,4},{6,7},{7,6},{8,9},{9,8},{10,11... | collective-permute-start | bytes 884744 | tf_op jit(solution)/shard_map/ppermute | solution.py:304
  106.8 13.5 %collective-permute-start.14 = (bf16[2,4,144,128]{3,2,1,0:T(8,128)(2,1)S(1)}, bf16[2,4,144,128]{3,2,1,0:T(8,128)(2,1)S(1)}, u32[]{:S(2)}, u32[]{:S(2)}) collective-permute-start(bf16[2,4,144,128]{3,2,1,0:T(8,128)(2,1)S(1)} %get-tuple-element.59), channel_id=1, source_target_pairs={{0,16},{8,24},{16,0},{24,8},{1,17},{9,25},{17,1},{25,9},{2,18},{10... | collective-permute-start | bytes 884744 | tf_op jit(solution)/shard_map/ppermute | solution.py:304
  108.9 11.6 %collective-permute-start.13 = (bf16[2,4,144,128]{3,2,1,0:T(8,128)(2,1)S(1)}, bf16[2,4,144,128]{3,2,1,0:T(8,128)(2,1)S(1)}, u32[]{:S(2)}, u32[]{:S(2)}) collective-permute-start(bf16[2,4,144,128]{3,2,1,0:T(8,128)(2,1)S(1)} %get-tuple-element.61), channel_id=1, source_target_pairs={{0,1},{1,0},{2,3},{3,2},{4,5},{5,4},{6,7},{7,6},{8,9},{9,8},{10,11... | collective-permute-start | bytes 884744 | tf_op jit(solution)/shard_map/ppermute | solution.py:304
  111.7 14.9 %collective-permute-start.8 = (bf16[2,4,144,128]{3,2,1,0:T(8,128)(2,1)S(1)}, bf16[2,4,144,128]{3,2,1,0:T(8,128)(2,1)S(1)}, u32[]{:S(2)}, u32[]{:S(2)}) collective-permute-start(bf16[2,4,144,128]{3,2,1,0:T(8,128)(2,1)S(1)} %get-tuple-element.63), channel_id=1, source_target_pairs={{0,16},{8,24},{16,0},{24,8},{1,17},{9,25},{17,1},{25,9},{2,18},{10... | collective-permute-start | bytes 884744 | tf_op jit(solution)/shard_map/ppermute | solution.py:304
  114.0 12.9 %collective-permute-start.7 = (bf16[2,4,144,128]{3,2,1,0:T(8,128)(2,1)S(1)}, bf16[2,4,144,128]{3,2,1,0:T(8,128)(2,1)S(1)}, u32[]{:S(2)}, u32[]{:S(2)}) collective-permute-start(bf16[2,4,144,128]{3,2,1,0:T(8,128)(2,1)S(1)} %get-tuple-element.65), channel_id=1, source_target_pairs={{0,1},{1,0},{2,3},{3,2},{4,5},{5,4},{6,7},{7,6},{8,9},{9,8},{10,11... | collective-permute-start | bytes 884744 | tf_op jit(solution)/shard_map/ppermute | solution.py:304
  114.2 18.7 %collective-permute-start.2 = (bf16[2,4,144,128]{3,2,1,0:T(8,128)(2,1)S(1)}, bf16[2,4,144,128]{3,2,1,0:T(8,128)(2,1)S(1)}, u32[]{:S(2)}, u32[]{:S(2)}) collective-permute-start(bf16[2,4,144,128]{3,2,1,0:T(8,128)(2,1)S(1)} %get-tuple-element.67), channel_id=1, source_target_pairs={{0,16},{8,24},{16,0},{24,8},{1,17},{9,25},{17,1},{25,9},{2,18},{10... | collective-permute-start | bytes 884744 | tf_op jit(solution)/shard_map/ppermute | solution.py:304
  120.3 12.9 %collective-permute-start.1 = (bf16[2,4,144,128]{3,2,1,0:T(8,128)(2,1)S(1)}, bf16[2,4,144,128]{3,2,1,0:T(8,128)(2,1)S(1)}, u32[]{:S(2)}, u32[]{:S(2)}) collective-permute-start(bf16[2,4,144,128]{3,2,1,0:T(8,128)(2,1)S(1)} %get-tuple-element.69), channel_id=1, source_target_pairs={{0,1},{1,0},{2,3},{3,2},{4,5},{5,4},{6,7},{7,6},{8,9},{9,8},{10,11... | collective-permute-start | bytes 884744 | tf_op jit(solution)/shard_map/ppermute | solution.py:304
  120.7 15.3 %collective-permute-start.15 = (bf16[1,4,144,128]{3,2,1,0:T(8,128)(2,1)S(1)}, bf16[1,4,144,128]{3,2,1,0:T(8,128)(2,1)S(1)}, u32[]{:S(2)}, u32[]{:S(2)}) collective-permute-start(bf16[1,4,144,128]{3,2,1,0:T(8,128)(2,1)S(1)} %get-tuple-element.77), channel_id=1, source_target_pairs={{0,16},{8,24},{16,0},{24,8},{1,17},{9,25},{17,1},{25,9},{2,18},{10... | collective-permute-start | bytes 442376 | tf_op jit(solution)/shard_map/ppermute | solution.py:304
  126.6 9.7 %collective-permute-start.16 = (bf16[1,4,144,128]{3,2,1,0:T(8,128)(2,1)S(1)}, bf16[1,4,144,128]{3,2,1,0:T(8,128)(2,1)S(1)}, u32[]{:S(2)}, u32[]{:S(2)}) collective-permute-start(bf16[1,4,144,128]{3,2,1,0:T(8,128)(2,1)S(1)} %get-tuple-element.75), channel_id=1, source_target_pairs={{0,1},{1,0},{2,3},{3,2},{4,5},{5,4},{6,7},{7,6},{8,9},{9,8},{10,11... | collective-permute-start | bytes 442376 | tf_op jit(solution)/shard_map/ppermute | solution.py:304
  127.0 12.2 %collective-permute-start.9 = (bf16[1,4,144,128]{3,2,1,0:T(8,128)(2,1)S(1)}, bf16[1,4,144,128]{3,2,1,0:T(8,128)(2,1)S(1)}, u32[]{:S(2)}, u32[]{:S(2)}) collective-permute-start(bf16[1,4,144,128]{3,2,1,0:T(8,128)(2,1)S(1)} %get-tuple-element.81), channel_id=1, source_target_pairs={{0,16},{8,24},{16,0},{24,8},{1,17},{9,25},{17,1},{25,9},{2,18},{10... | collective-permute-start | bytes 442376 | tf_op jit(solution)/shard_map/ppermute | solution.py:304
  132.9 6.8 %collective-permute-start.10 = (bf16[1,4,144,128]{3,2,1,0:T(8,128)(2,1)S(1)}, bf16[1,4,144,128]{3,2,1,0:T(8,128)(2,1)S(1)}, u32[]{:S(2)}, u32[]{:S(2)}) collective-permute-start(bf16[1,4,144,128]{3,2,1,0:T(8,128)(2,1)S(1)} %get-tuple-element.79), channel_id=1, source_target_pairs={{0,1},{1,0},{2,3},{3,2},{4,5},{5,4},{6,7},{7,6},{8,9},{9,8},{10,11... | collective-permute-start | bytes 442376 | tf_op jit(solution)/shard_map/ppermute | solution.py:304
  133.4 10.2 %collective-permute-start.3 = (bf16[1,4,144,128]{3,2,1,0:T(8,128)(2,1)S(1)}, bf16[1,4,144,128]{3,2,1,0:T(8,128)(2,1)S(1)}, u32[]{:S(2)}, u32[]{:S(2)}) collective-permute-start(bf16[1,4,144,128]{3,2,1,0:T(8,128)(2,1)S(1)} %get-tuple-element.85), channel_id=1, source_target_pairs={{0,16},{8,24},{16,0},{24,8},{1,17},{9,25},{17,1},{25,9},{2,18},{10... | collective-permute-start | bytes 442376 | tf_op jit(solution)/shard_map/ppermute | solution.py:304
  136.1 7.5 %collective-permute-start.4 = (bf16[1,4,144,128]{3,2,1,0:T(8,128)(2,1)S(1)}, bf16[1,4,144,128]{3,2,1,0:T(8,128)(2,1)S(1)}, u32[]{:S(2)}, u32[]{:S(2)}) collective-permute-start(bf16[1,4,144,128]{3,2,1,0:T(8,128)(2,1)S(1)} %get-tuple-element.83), channel_id=1, source_target_pairs={{0,1},{1,0},{2,3},{3,2},{4,5},{5,4},{6,7},{7,6},{8,9},{9,8},{10,11... | collective-permute-start | bytes 442376 | tf_op jit(solution)/shard_map/ppermute | solution.py:304
  136.4 15.3 %collective-permute-start.17 = (bf16[8,144,128]{2,1,0:T(8,128)(2,1)S(1)}, bf16[8,144,128]{2,1,0:T(8,128)(2,1)S(1)}, u32[]{:S(2)}, u32[]{:S(2)}) collective-permute-start(bf16[8,144,128]{2,1,0:T(8,128)(2,1)S(1)} %pad_maximum_fusion.2), channel_id=1, source_target_pairs={{0,2},{1,3},{2,0},{3,1},{4,6},{5,7},{6,4},{7,5},{8,10},{9,11},{10,... | collective-permute-start | bytes 884744 | tf_op jit(solution)/shard_map/ppermute | solution.py:304
  139.8 24.1 %collective-permute-start.11 = (bf16[8,144,128]{2,1,0:T(8,128)(2,1)S(1)}, bf16[8,144,128]{2,1,0:T(8,128)(2,1)S(1)}, u32[]{:S(2)}, u32[]{:S(2)}) collective-permute-start(bf16[8,144,128]{2,1,0:T(8,128)(2,1)S(1)} %pad_maximum_fusion.1), channel_id=1, source_target_pairs={{0,4},{1,5},{2,6},{3,7},{4,0},{5,1},{6,2},{7,3},{8,12},{9,13},{10,... | collective-permute-start | bytes 884744 | tf_op jit(solution)/shard_map/ppermute | solution.py:304
  143.7 20.2 %collective-permute-start.5 = (bf16[8,144,128]{2,1,0:T(8,128)(2,1)S(1)}, bf16[8,144,128]{2,1,0:T(8,128)(2,1)S(1)}, u32[]{:S(2)}, u32[]{:S(2)}) collective-permute-start(bf16[8,144,128]{2,1,0:T(8,128)(2,1)S(1)} %pad_maximum_fusion), channel_id=1, source_target_pairs={{0,6},{1,7},{2,4},{3,5},{4,2},{5,3},{6,0},{7,1},{8,14},{9,15},{10,... | collective-permute-start | bytes 884744 | tf_op jit(solution)/shard_map/ppermute | solution.py:304
  145.0 5.2 %collective-permute-start.21 = (bf16[1,4,144,128]{3,2,1,0:T(8,128)(2,1)S(1)}, bf16[1,4,144,128]{3,2,1,0:T(8,128)(2,1)S(1)}, u32[]{:S(2)}, u32[]{:S(2)}) collective-permute-start(bf16[1,4,144,128]{3,2,1,0:T(8,128)(2,1)S(1)} %get-tuple-element.73), channel_id=1, source_target_pairs={{0,16},{8,24},{16,0},{24,8},{1,17},{9,25},{17,1},{25,9},{2,18},{10... | collective-permute-start | bytes 442376 | tf_op jit(solution)/shard_map/ppermute | solution.py:304
  146.4 5.1 %collective-permute-start.22 = (bf16[1,4,144,128]{3,2,1,0:T(8,128)(2,1)S(1)}, bf16[1,4,144,128]{3,2,1,0:T(8,128)(2,1)S(1)}, u32[]{:S(2)}, u32[]{:S(2)}) collective-permute-start(bf16[1,4,144,128]{3,2,1,0:T(8,128)(2,1)S(1)} %get-tuple-element.71), channel_id=1, source_target_pairs={{0,1},{1,0},{2,3},{3,2},{4,5},{5,4},{6,7},{7,6},{8,9},{9,8},{10,11... | collective-permute-start | bytes 442376 | tf_op jit(solution)/shard_map/ppermute | solution.py:304
  (28 other events, 218.5 us)

commit v2 on v1

--- a/solution.py
+++ b/solution.py
@@ -42,26 +42,71 @@
     return jnp.concatenate([table, number[:, None]], axis=1)
 
 
+def stage_kernel(
+    chunk, anom_hbm, innov_ref, rinv_ref, lon_ref, lat_ref, left_ref, fields_ref, totals_ref, sems
+):
+    held, members, block_obs = anom_hbm.shape
+    copies = []
+    for i in range(held // chunk):
+        span = pl.ds(i * chunk, chunk)
+        copy = pltpu.make_async_copy(
+            anom_hbm.at[span], left_ref.at[span, pl.ds(0, members), :], sems.at[i]
+        )
+        copy.start()
+        copies.append(copy)
+    fields_ref[0] = (2 * lon_ref[...]).astype(F32)
+    fields_ref[1] = (2 * lat_ref[...]).astype(F32)
+    fields_ref[2] = rinv_ref[...]
+    line = lax.broadcasted_iota(jnp.int32, (EXT, block_obs), 0)
+    sums = jnp.zeros((8, block_obs), F32)
+    for i, copy in enumerate(copies):
+        copy.wait()
+
+        def block(j, total, first=i * chunk):
+            at = first + j
+            values = left_ref[at, :members, :].astype(F32)
+            squares = jnp.sum((values * values).reshape(members // 8, 8, block_obs), axis=0)
+            innov = innov_ref[pl.ds(at, 1), :]
+            high = innov.astype(BF16).astype(F32)
+            rows = jnp.where(line == 0, high, jnp.where(line == 1, innov - high, 0.0))
+            left_ref[at, members:, :] = rows.astype(BF16)
+            return total + squares * rinv_ref[pl.ds(at, 1), :]
+
+        sums = lax.fori_loop(0, chunk, block, sums, unroll=4)
+    innovation = jnp.sum(rinv_ref[...] * innov_ref[...] * innov_ref[...], axis=0, keepdims=True)
+    spread = jnp.sum(sums, axis=0, keepdims=True) / (members - 1)
+    line = lax.broadcasted_iota(jnp.int32, (8, block_obs), 0)
+    totals_ref[...] = jnp.where(line == 4, innovation, jnp.where(line == 5, spread, 0.0))
+
+
+def stage(anom, innov, rinv, lon, lat):
+    held, members, block_obs = anom.shape
+    chunk = 16 if held % 16 == 0 else held
+    whole = pl.BlockSpec(memory_space=pltpu.VMEM)
+    return pl.pallas_call(
+        functools.partial(stage_kernel, chunk),
+        out_shape=[
+            pltpu.VMEM((held, members + EXT, block_obs), BF16),
+            pltpu.VMEM((3, held, block_obs), F32),
+            pltpu.VMEM((8, block_obs), F32),
+        ],
+        in_specs=[pl.BlockSpec(memory_space=pltpu.HBM)] + [whole] * 4,
+        out_specs=[whole] * 3,
+        scratch_shapes=[pltpu.SemaphoreType.DMA((held // chunk,))],
+        compiler_params=pltpu.CompilerParams(vmem_limit_bytes=4 * 2**20),
+        cost_estimate=pl.CostEstimate(flops=0, bytes_accessed=anom.size * 4, transcendentals=0),
+        name="stage",
+    )(anom, innov, rinv, lon, lat)
+
+
 def gram_kernel(
-    sizes,
-    targets_ref,
-    requests_ref,
-    anom_ref,
-    ext_ref,
-    lon_ref,
-    lat_ref,
-    rinv_ref,
-    totals_ref,
-    send_ref,
-    keep_ref,
-    acc_ref,
+    sizes, targets_ref, requests_ref, left_ref, fields_ref, totals_ref, out_ref, acc_ref
 ):
-    patches, lat_patches, lon_patches, lat_devices, held, per_owner, grid_lon, sent = sizes
-    step = pl.program_id(0)
-    target = targets_ref[step]
+    patches, lat_patches, lon_patches, lat_devices, held, per_owner, grid_lon = sizes
+    target = targets_ref[pl.program_id(0)]
     lon_first = (target // lat_devices) * lon_patches
     lat_first = (target % lat_devices) * lat_patches
-    members = anom_ref.shape[1]
+    members = left_ref.shape[2]
     acc_ref[...] = jnp.zeros_like(acc_ref)
     number = requests_ref[target, per_owner]
 
@@ -74,15 +119,15 @@
             block = code % held
             centre_lon = (lon_first + patch // lat_patches) * (2 * PSIDE) + (PSIDE - 1)
             centre_lat = (lat_first + patch % lat_patches) * (2 * PSIDE) + (PSIDE - 1)
-            lon_gap = jnp.abs(2 * lon_ref[pl.ds(block, 1), :] - centre_lon)
-            lon_gap = jnp.minimum(lon_gap, 2 * grid_lon - lon_gap)
-            lat_gap = 2 * lat_ref[pl.ds(block, 1), :] - centre_lat
-            square = (lon_gap * lon_gap + lat_gap * lat_gap).astype(F32)
-            rinv = jnp.where(entry < number, rinv_ref[pl.ds(block, 1), :], 0.0)
+            row = pl.ds(block, 1)
+            lon_gap = jnp.abs(fields_ref[0, row, :] - centre_lon.astype(F32))
+            lon_gap = jnp.minimum(lon_gap, 2.0 * grid_lon - lon_gap)
+            lat_gap = fields_ref[1, row, :] - centre_lat.astype(F32)
+            square = lon_gap * lon_gap + lat_gap * lat_gap
+            rinv = jnp.where(entry < number, fields_ref[2, row, :], 0.0)
             weight = rinv * jnp.exp(square * (-1.0 / (8.0 * LOC_SCALE * LOC_SCALE)))
-            anom = anom_ref[block]
-            scaled = (anom.astype(F32) * weight).astype(BF16)
-            left = jnp.concatenate([anom, ext_ref[block]], axis=0)
+            left = left_ref[block]
+            scaled = (left[:members].astype(F32) * weight).astype(BF16)
             product = lax.dot_general(left, scaled, NT, preferred_element_type=F32)
             products.append((patch, product[: members + 8]))
         for patch, product in products:
@@ -94,63 +139,45 @@
     row = lax.broadcasted_iota(jnp.int32, (members, members), 0)
     column = lax.broadcasted_iota(jnp.int32, (members, members), 1)
     line = lax.broadcasted_iota(jnp.int32, (8, members), 0)
-
-    def emit(out_ref):
-        for pair in range(patches // 2):
-            first = acc_ref[2 * pair]
-            second = acc_ref[2 * pair + 1]
-            packed = jnp.where(row < column, first[:members], second[:members])
-            out_ref[0, pair, :members, :] = packed.astype(BF16)
-            rows = totals_ref[...]
-            for place, values in ((0, first), (2, second)):
-                diagonal = jnp.sum(
-                    jnp.where(row == column, values[:members], 0.0), axis=0, keepdims=True
-                )
-                projected = values[members : members + 1] + values[members + 1 : members + 2]
-                rows = jnp.where(line == place, diagonal, rows)
-                rows = jnp.where(line == place + 1, projected, rows)
-            high = rows.astype(BF16).astype(F32)
-            out_ref[0, pair, members:, :] = jnp.concatenate([high, rows - high], axis=0).astype(
-                BF16
+    for pair in range(patches // 2):
+        first = acc_ref[2 * pair]
+        second = acc_ref[2 * pair + 1]
+        packed = jnp.where(row < column, first[:members], second[:members])
+        out_ref[0, pair, :members, :] = packed.astype(BF16)
+        rows = totals_ref[...]
+        for place, values in ((0, first), (2, second)):
+            diagonal = jnp.sum(
+                jnp.where(row == column, values[:members], 0.0), axis=0, keepdims=True
             )
-
-    @pl.when(step < sent)
-    def _():
-        emit(send_ref)
-
-    @pl.when(step >= sent)
-    def _():
-        emit(keep_ref)
-
-
-def partial_grams(sizes, targets, requests, anom, ext, lon, lat, rinv, totals):
+            projected = values[members : members + 1] + values[members + 1 : members + 2]
+            rows = jnp.where(line == place, diagonal, rows)
+            rows = jnp.where(line == place + 1, projected, rows)
+        high = rows.astype(BF16).astype(F32)
+        out_ref[0, pair, members:, :] = jnp.concatenate([high, rows - high], axis=0).astype(BF16)
+
+
+def partial_grams(sizes, targets, requests, staged):
     patches, per_owner = sizes[0], sizes[5]
-    sent = targets.shape[0] // 2
-    members = anom.shape[1]
+    count = targets.shape[0]
+    members = staged[0].shape[2]
     rows = members + EXT
     block = (1, patches // 2, rows, members)
-    whole = pl.BlockSpec(memory_space=pltpu.VMEM)
-    half = jax.ShapeDtypeStruct((sent, patches // 2, rows, members), BF16)
-    entries = 2 * sent * per_owner
     return pl.pallas_call(
-        functools.partial(gram_kernel, (*sizes, sent)),
-        out_shape=[half, half],
+        functools.partial(gram_kernel, sizes),
+        out_shape=jax.ShapeDtypeStruct((count, *block[1:]), BF16),
         grid_spec=pltpu.PrefetchScalarGridSpec(
             num_scalar_prefetch=2,
-            grid=(2 * sent,),
-            in_specs=[whole] * 6,
-            out_specs=[
-                pl.BlockSpec(block, lambda i, *_: (jnp.minimum(i, sent - 1), 0, 0, 0)),
-                pl.BlockSpec(block, lambda i, *_: (jnp.maximum(i - sent, 0), 0, 0, 0)),
-            ],
+            grid=(count,),
+            in_specs=[pl.BlockSpec(memory_space=pltpu.VMEM)] * 3,
+            out_specs=pl.BlockSpec(block, lambda i, *_: (i, 0, 0, 0)),
             scratch_shapes=[pltpu.VMEM((patches, members + 8, members), F32)],
         ),
-        compiler_params=pltpu.CompilerParams(vmem_limit_bytes=32 * 2**20),
+        compiler_params=pltpu.CompilerParams(vmem_limit_bytes=6 * 2**20),
         cost_estimate=pl.CostEstimate(
-            flops=entries * 8 * members**3, bytes_accessed=anom.size * 2, transcendentals=0
+            flops=count * per_owner * 40 * members**3, bytes_accessed=0, transcendentals=0
         ),
         name="partial_grams",
-    )(targets, requests, anom, ext, lon, lat, rinv, totals)
+    )(targets, requests, *staged)
 
 
 def added(left, right):
@@ -319,20 +346,8 @@
     )
     requests = lax.all_to_all(table, ("lon", "lat"), split_axis=0, concat_axis=0, tiled=True)
 
-    squares = jnp.sum(jnp.square(obs_anom.astype(F32)), axis=1) / (members - 1)
-    zero = jnp.zeros((block_obs,), F32)
-    totals = jnp.stack(
-        [zero] * 4
-        + [jnp.sum(obs_rinv * innov * innov, axis=0), jnp.sum(obs_rinv * squares, axis=0)]
-        + [zero] * 2
-    )
-    innov_high = innov.astype(BF16).astype(F32)
-    line = lax.broadcasted_iota(jnp.int32, (held, EXT, block_obs), 1)
-    ext = jnp.where(
-        line == 0,
-        innov_high[:, None, :],
-        jnp.where(line == 1, (innov - innov_high)[:, None, :], 0.0),
-    ).astype(BF16)
+    staged = stage(obs_anom, innov, obs_rinv, obs_lon, obs_lat)
+    staged = [pltpu.with_memory_space_constraint(v, pltpu.VMEM) for v in staged]
 
     me_lon, me_lat = lax.axis_index("lon"), lax.axis_index("lat")
     sizes = (
@@ -345,41 +360,80 @@
         lon_devices * lon_patches * PSIDE,
     )
 
-    def chunk(far):
-        others = [(lon, near) for lon in range(0, lon_devices, 2) for near in range(2)]
-        order = [(lon + core, near) for core in (1, 0) for lon, near in others]
+    y_count = lon_devices // 2
+
+    def grams(far, core, after):
+        order = [(2 * y + core, 2 * far + near) for y in range(y_count) for near in range(2)]
         targets = jnp.stack(
-            [(me_lon ^ lon) * lat_devices + (me_lat ^ (2 * far + near)) for lon, near in order]
+            [(me_lon ^ lon) * lat_devices + (me_lat ^ lat) for lon, lat in order]
         ).astype(jnp.int32)
-        send, keep = partial_grams(
-            sizes, targets, requests, obs_anom, ext, obs_lon, obs_lat, obs_rinv, totals
-        )
+        targets, _ = lax.optimization_barrier((targets, after))
+        return partial_grams(sizes, targets, requests, staged)
+
+    def steps(far):
+        send = yield far, 1
         got = swap(send, "lon", 1)
+        keep = yield far, 0
         [total] = add_all([keep], [got])
-        total = total.reshape(lon_devices // 2, 2, *total.shape[1:])
+        total = total.reshape(y_count, 2, *total.shape[1:])
         cut = patches // 4
         first, second = total[:, :, :cut], total[:, :, cut:]
         shape = (-1, *first.shape[2:])
-        far_lon = lon_devices // 4
-        keeps = [first[:, 0], second[:far_lon].reshape(shape)]
-        gots = [swap(first[:, 1], "lat", 1), swap(second[far_lon:].reshape(shape), "lon", lon_devices // 2)]
+        left = y_count // 2
+        keeps = [first[:, 0], second[:left].reshape(shape)]
+        gots = [
+            swap(first[:, 1], "lat", 1),
+            swap(second[left:].reshape(shape), "lon", lon_devices // 2),
+        ]
+        gots = yield gots, [total]
         first, second = add_all(keeps, gots)
-        second = second.reshape(far_lon, 2, *second.shape[1:])
-        keeps = [first[:far_lon], second[:, 0]]
-        gots = [swap(first[far_lon:], "lon", lon_devices // 2), swap(second[:, 1], "lat", 1)]
-        left = far_lon
+        sums = [first, second]
+        second = second.reshape(left, 2, *second.shape[1:])
+        keeps = [first[:left], second[:, 0]]
+        gots = [
+            swap(first[left:], "lon", lon_devices // 2),
+            swap(second[:, 1], "lat", 1),
+        ]
+        gots = yield gots, sums
         first, second = add_all(keeps, gots)
         while left > 1:
             left //= 2
             keeps = [first[:left], second[:left]]
             gots = [swap(v[left:], "lon", 2 * left) for v in (first, second)]
             first, second = add_all(keeps, gots)
-        return jnp.concatenate([first[0], second[0]], axis=0)
-
-    parts = []
+        total = jnp.concatenate([first[0], second[0]], axis=0)
+        yield (swap(total, "lat", 2 * far) if far else total), total
+
+    parts, open_chunks, after = [], [], []
+
+    def advance(latest):
+        nonlocal open_chunks, after
+        still, after = [], []
+        for chunk, waits in open_chunks:
+            if latest is not None:
+                waits, _ = lax.optimization_barrier((waits, latest))
+            waits, sums = chunk.send(waits)
+            if isinstance(sums, list):
+                still.append((chunk, waits))
+                after += sums
+            else:
+                parts.append(waits)
+                after.append(sums)
+        open_chunks = still
+
+    latest = None
     for far in reversed(range(lat_devices // 2)):
-        total = chunk(far)
-        parts.append(swap(total, "lat", 2 * far) if far else total)
+        chunk = steps(far)
+        send = grams(*next(chunk), after)
+        request = chunk.send(send)
+        advance(send)
+        keep = grams(*request, after)
+        waits, sums = chunk.send(keep)
+        advance(keep)
+        open_chunks.append((chunk, waits))
+        after += sums
+    while open_chunks:
+        advance(None)
     weights = solve(parts, holders * held * block_obs)
     updated = analysis(
         weights,

time: 185 us -> 164 us (0.89); the launches traced: 182 us -> 164 us
  waiting for transfers between devices: 31.2 us -> 18.7 us
  other arithmetic: 10.1 us -> 5.39 us
  local copies, waits for them, and re-layouts: 25.6 us -> 20.9 us
  starting transfers between devices: 31.3 us -> 36 us
    ppermute x23, waiting for transfers between devices: 31.2 us -> 18.7 us  [swap(): return lax.ppermute(value, axis, [(i, i ^ flip) for i in range(size)])]
    reduce_sum x2 -> x0, other arithmetic: 5.3 us -> none  [the longest x1 5.25 us: on_device(): squares = jnp.sum(jnp.square(obs_anom.astype(F32)), axis=1) / (members - 1)]
    ppermute x23, starting transfers between devices: 24 us -> 28.7 us  [swap(): return lax.ppermute(value, axis, [(i, i ^ flip) for i in range(size)])]
    unnamed x58 -> x38, local copies, waits for them, and re-layouts: 22.4 us -> 18.2 us
    another operation x8 -> x0, local copies, waits for them, and re-layouts: 2.05 us -> none  [the longest x4 1.97 us: chunk(): jnp.stack([(me_lon ^ lon) * lat_devices + (me_lat ^ 2 * far + near) for l...]
    pallas_call x4 -> x9, Pallas kernels: 60.9 us -> 61.2 us  [the longest x8 58.8 us: partial_grams(): pl.pallas_call(functools.partial(gram_kernel, sizes), out_shape=jax.Shape...]
  transfers between devices with their start and end apart: 24 -> 24, of which waited for: 10 -> 5; matrix products, arithmetic and copies ran while one was open for 5% -> 1% of each run, Pallas kernels for 27% -> 34%
where the time goes in v2:
time: 164 us
  Pallas kernels  82.5 us (50%)
  starting transfers between devices  36 us (22%)
  local copies, waits for them, and re-layouts  20.9 us (13%)
  waiting for transfers between devices  18.7 us (11%)
  other arithmetic  5.39 us (3%)
    pallas_call x8, Pallas kernels, partial_grams(): pl.pallas_call(functools.partial(gram_kernel, sizes), out_shape=jax.Shape...  58.8 us
    ppermute x23, starting transfers between devices, swap(): return lax.ppermute(value, axis, [(i, i ^ flip) for i in range(size)])  28.7 us
    ppermute x23, waiting for transfers between devices, swap(): return lax.ppermute(value, axis, [(i, i ^ flip) for i in range(size)])  18.7 us
    unnamed x38, local copies, waits for them, and re-layouts  18.2 us
    pallas_call x1, Pallas kernels, analysis(): pl.pallas_call(analysis_kernel, out_shape=jax.ShapeDtypeStruct(pert.shape...  9.35 us
    pallas_call x1, Pallas kernels, solve(): pl.pallas_call(functools.partial(solve_kernel, len(parts), total_obs), ou...  8.31 us
    all_to_all x1, starting transfers between devices, on_device(): lax.all_to_all(table, ('lon', 'lat'), split_axis=0, concat_axis=0, tiled=...  7.3 us
    pallas_call x12, Pallas kernels, add_all(): pl.pallas_call(functools.partial(add_kernel, count), out_shape=[jax.Shape...  3.59 us
  transfers between devices with their start and end apart: 24, of which 5 were waited for; matrix products, arithmetic and copies ran while one was open for 1% of the time, Pallas kernels for 34%

profile of v2, /device:TPU:0, one launch (start us, length us, event | category | flops | bytes accessed | tf_op | source)
XLA Modules:
  0.0 164.0 jit_solution(5034856327319772499)
XLA Ops:
  4.6 7.3 %all-to-all-start = ((s32[32,1,25]{2,1,0:T(1,128)}), s32[32,1,25]{2,1,0:T(1,128)S(1)}, u32[]{:S(2)}, u32[]{:S(2)}) async-start(s32[32,1,25]{2,1,0:T(1,128)} %bitcast.6), calls=%async_computation | async-start | bytes 32768 | tf_op jit(solution)/shard_map/all_to_all | solution.py:347
  12.2 2.8 %copy-done = bf16[192,128,128]{2,1,0:T(8,128)(2,1)S(1)} copy-done((bf16[192,128,128]{2,1,0:T(8,128)(2,1)S(1)}, bf16[192,128,128]{2,1,0:T(8,128)(2,1)}, u32[]{:S(2)}) %copy-start) | copy-done | bytes 6291480
  18.5 2.5 %stage.1 = (bf16[192,144,128]{2,1,0:T(8,128)(2,1)S(1)}, f32[3,192,128]{2,1,0:T(8,128)S(1)}, f32[8,128]{1,0:T(8,128)S(1)}) custom-call(bf16[192,128,128]{2,1,0:T(8,128)(2,1)S(1)} %copy-done, f32[192,128]{1,0:T(8,128)S(1)} %copy-done.3, f32[192,128]{1,0:T(8,128)S(1)} %copy-done.4, s32[192,128]{1,0:T(8,128)S(1)} %copy-done.5, s32[192,128]{1,0:T(8,128)S(1)} %copy-done.6), custom_call_target="tpu_custom_call" | custom-call | bytes 12582912 | tf_op jit(solution)/shard_map/stage/pallas_call | solution.py:86
  21.0 3.0 %copy-done.7 = bf16[192,144,128]{2,1,0:T(8,128)(2,1)} copy-done((bf16[192,144,128]{2,1,0:T(8,128)(2,1)}, bf16[192,144,128]{2,1,0:T(8,128)(2,1)S(1)}, u32[]{:S(2)}) %copy-start.7) | copy-done | bytes 7077912
  24.0 3.1 %copy-done.8 = bf16[192,144,128]{2,1,0:T(8,128)(2,1)S(1)} copy-done((bf16[192,144,128]{2,1,0:T(8,128)(2,1)S(1)}, bf16[192,144,128]{2,1,0:T(8,128)(2,1)}, u32[]{:S(2)}) %copy-start.8) | copy-done | bytes 7077912
  27.1 7.9 %partial_grams.9 = bf16[4,8,144,128]{3,2,1,0:T(8,128)(2,1)S(1)} custom-call(s32[4]{0:T(128)S(1)} %pad_add_fusion.2.targets_ref, s32[32,25]{1,0:T(8,128)S(1)} %bitcast.128, bf16[192,144,128]{2,1,0:T(8,128)(2,1)S(1)} %copy-done.8, f32[3,192,128]{2,1,0:T(8,128)S(1)} %get-tuple-element.43.fields_ref, f32[8,128]{1,0:T(8,128)S(1)} %get-tuple-element.44.totals_ref), custom_call_target="tpu_custom_call" | custom-call | flops 8053063680 | tf_op jit(solution)/shard_map/partial_grams/pallas_call | solution.py:165
  35.4 6.5 %partial_grams.8.refs_0_ = bf16[4,8,144,128]{3,2,1,0:T(8,128)(2,1)S(1)} custom-call(s32[4]{0:T(128)S(1)} %pad_add_fusion.1.targets_ref, s32[32,25]{1,0:T(8,128)S(1)} %bitcast.129, bf16[192,144,128]{2,1,0:T(8,128)(2,1)S(1)} %copy-done.9, f32[3,192,128]{2,1,0:T(8,128)S(1)} %get-tuple-element.43.fields_ref, f32[8,128]{1,0:T(8,128)S(1)} %get-tuple-element.44.totals_ref), custom_call_target="tpu_custom_call" | custom-call | flops 8053063680 | tf_op jit(solution)/shard_map/partial_grams/pallas_call | solution.py:165
  42.4 3.9 %collective-permute-start.1 = (bf16[2,4,144,128]{3,2,1,0:T(8,128)(2,1)S(1)}, bf16[2,4,144,128]{3,2,1,0:T(8,128)(2,1)S(1)}, u32[]{:S(2)}, u32[]{:S(2)}) collective-permute-start(bf16[2,4,144,128]{3,2,1,0:T(8,128)(2,1)S(1)} %get-tuple-element.93), channel_id=1, source_target_pairs={{0,1},{1,0},{2,3},{3,2},{4,5},{5,4},{6,7},{7,6},{8,9},{9,8},{10,11... | collective-permute-start | bytes 884744 | tf_op jit(solution)/shard_map/ppermute | solution.py:331
  47.8 7.3 %partial_grams.10 = bf16[4,8,144,128]{3,2,1,0:T(8,128)(2,1)S(1)} custom-call(s32[4]{0:T(128)S(1)} %pad_add_fusion.3.targets_ref, s32[32,25]{1,0:T(8,128)S(1)} %bitcast.130, bf16[192,144,128]{2,1,0:T(8,128)(2,1)S(1)} %copy-done.9, f32[3,192,128]{2,1,0:T(8,128)S(1)} %get-tuple-element.43.fields_ref, f32[8,128]{1,0:T(8,128)S(1)} %get-tuple-element.44.totals_ref), custom_call_target="tpu_custom_call" | custom-call | flops 8053063680 | tf_op jit(solution)/shard_map/partial_grams/pallas_call | solution.py:165
  57.5 6.7 %partial_grams.11.refs_0_ = bf16[4,8,144,128]{3,2,1,0:T(8,128)(2,1)S(1)} custom-call(s32[4]{0:T(128)S(1)} %pad_add_fusion.4.targets_ref, s32[32,25]{1,0:T(8,128)S(1)} %bitcast.131, bf16[192,144,128]{2,1,0:T(8,128)(2,1)S(1)} %copy-done.9, f32[3,192,128]{2,1,0:T(8,128)S(1)} %get-tuple-element.43.fields_ref, f32[8,128]{1,0:T(8,128)S(1)} %get-tuple-element.44.totals_ref), custom_call_target="tpu_custom_call" | custom-call | flops 8053063680 | tf_op jit(solution)/shard_map/partial_grams/pallas_call | solution.py:165
  65.6 2.6 %collective-permute-start.7 = (bf16[2,4,144,128]{3,2,1,0:T(8,128)(2,1)S(1)}, bf16[2,4,144,128]{3,2,1,0:T(8,128)(2,1)S(1)}, u32[]{:S(2)}, u32[]{:S(2)}) collective-permute-start(bf16[2,4,144,128]{3,2,1,0:T(8,128)(2,1)S(1)} %get-tuple-element.89), channel_id=1, source_target_pairs={{0,1},{1,0},{2,3},{3,2},{4,5},{5,4},{6,7},{7,6},{8,9},{9,8},{10,11... | collective-permute-start | bytes 884744 | tf_op jit(solution)/shard_map/ppermute | solution.py:331
  69.1 7.6 %partial_grams.12 = bf16[4,8,144,128]{3,2,1,0:T(8,128)(2,1)S(1)} custom-call(s32[4]{0:T(128)S(1)} %pad_add_fusion.5.targets_ref, s32[32,25]{1,0:T(8,128)S(1)} %bitcast.132, bf16[192,144,128]{2,1,0:T(8,128)(2,1)S(1)} %copy-done.9, f32[3,192,128]{2,1,0:T(8,128)S(1)} %get-tuple-element.43.fields_ref, f32[8,128]{1,0:T(8,128)S(1)} %get-tuple-element.44.totals_ref), custom_call_target="tpu_custom_call" | custom-call | flops 8053063680 | tf_op jit(solution)/shard_map/partial_grams/pallas_call | solution.py:165
  78.7 7.0 %partial_grams.13.refs_0_ = bf16[4,8,144,128]{3,2,1,0:T(8,128)(2,1)S(1)} custom-call(s32[4]{0:T(128)S(1)} %pad_add_fusion.6.targets_ref, s32[32,25]{1,0:T(8,128)S(1)} %bitcast.133, bf16[192,144,128]{2,1,0:T(8,128)(2,1)S(1)} %copy-done.9, f32[3,192,128]{2,1,0:T(8,128)S(1)} %get-tuple-element.43.fields_ref, f32[8,128]{1,0:T(8,128)S(1)} %get-tuple-element.44.totals_ref), custom_call_target="tpu_custom_call" | custom-call | flops 8053063680 | tf_op jit(solution)/shard_map/partial_grams/pallas_call | solution.py:165
  91.3 8.3 %partial_grams.14 = bf16[4,8,144,128]{3,2,1,0:T(8,128)(2,1)} custom-call(s32[4]{0:T(128)S(1)} %pad_add_fusion.7.targets_ref, s32[32,25]{1,0:T(8,128)S(1)} %bitcast.134, bf16[192,144,128]{2,1,0:T(8,128)(2,1)S(1)} %copy-done.9, f32[3,192,128]{2,1,0:T(8,128)S(1)} %get-tuple-element.43.fields_ref, f32[8,128]{1,0:T(8,128)S(1)} %get-tuple-element.44.totals_ref), custom_call_target="tpu_custom_call" | custom-call | flops 8053063680 | tf_op jit(solution)/shard_map/partial_grams/pallas_call | solution.py:165
  103.0 3.0 %copy-done.10 = bf16[192,144,128]{2,1,0:T(8,128)(2,1)S(1)} copy-done((bf16[192,144,128]{2,1,0:T(8,128)(2,1)S(1)}, bf16[192,144,128]{2,1,0:T(8,128)(2,1)}, u32[]{:S(2)}) %copy-start.10) | copy-done | bytes 7077912
  106.0 7.3 %partial_grams.15.refs_0_ = bf16[4,8,144,128]{3,2,1,0:T(8,128)(2,1)S(1)} custom-call(s32[4]{0:T(128)S(1)} %pad_add_fusion.8.targets_ref, s32[32,25]{1,0:T(8,128)S(1)} %bitcast.135, bf16[192,144,128]{2,1,0:T(8,128)(2,1)S(1)} %copy-done.10, f32[3,192,128]{2,1,0:T(8,128)S(1)} %copy-done.12, f32[8,128]{1,0:T(8,128)S(1)} %get-tuple-element.44.totals_ref), custom_call_target="tpu_custom_call" | custom-call | flops 8053063680 | tf_op jit(solution)/shard_map/partial_grams/pallas_call | solution.py:165
  115.8 2.1 %collective-permute-start.16 = (bf16[1,4,144,128]{3,2,1,0:T(8,128)(2,1)S(1)}, bf16[1,4,144,128]{3,2,1,0:T(8,128)(2,1)S(1)}, u32[]{:S(2)}, u32[]{:S(2)}) collective-permute-start(bf16[1,4,144,128]{3,2,1,0:T(8,128)(2,1)S(1)} %get-tuple-element.99), channel_id=1, source_target_pairs={{0,1},{1,0},{2,3},{3,2},{4,5},{5,4},{6,7},{7,6},{8,9},{9,8},{10,11... | collective-permute-start | bytes 442376 | tf_op jit(solution)/shard_map/ppermute | solution.py:331
  118.0 3.0 %collective-permute-start.5 = (bf16[8,144,128]{2,1,0:T(8,128)(2,1)S(1)}, bf16[8,144,128]{2,1,0:T(8,128)(2,1)S(1)}, u32[]{:S(2)}, u32[]{:S(2)}) collective-permute-start(bf16[8,144,128]{2,1,0:T(8,128)(2,1)S(1)} %copy-done.13), channel_id=1, source_target_pairs={{0,6},{1,7},{2,4},{3,5},{4,2},{5,3},{6,0},{7,1},{8,14},{9,15},{10,... | collective-permute-start | bytes 884744 | tf_op jit(solution)/shard_map/ppermute | solution.py:331
  121.0 5.5 %collective-permute-done.16.refs_3_ = bf16[1,4,144,128]{3,2,1,0:T(8,128)(2,1)S(1)} collective-permute-done((bf16[1,4,144,128]{3,2,1,0:T(8,128)(2,1)S(1)}, bf16[1,4,144,128]{3,2,1,0:T(8,128)(2,1)S(1)}, u32[]{:S(2)}, u32[]{:S(2)}) %collective-permute-start.16) | collective-permute-done | bytes 147488 | tf_op jit(solution)/shard_map/ppermute | solution.py:331
  126.5 3.2 %collective-permute-start.11 = (bf16[8,144,128]{2,1,0:T(8,128)(2,1)S(1)}, bf16[8,144,128]{2,1,0:T(8,128)(2,1)S(1)}, u32[]{:S(2)}, u32[]{:S(2)}) collective-permute-start(bf16[8,144,128]{2,1,0:T(8,128)(2,1)S(1)} %copy-done.14), channel_id=1, source_target_pairs={{0,4},{1,5},{2,6},{3,7},{4,0},{5,1},{6,2},{7,3},{8,12},{9,13},{10,... | collective-permute-start | bytes 884744 | tf_op jit(solution)/shard_map/ppermute | solution.py:331
  133.2 2.8 %collective-permute-done.21.refs_2_ = bf16[1,4,144,128]{3,2,1,0:T(8,128)(2,1)S(1)} collective-permute-done((bf16[1,4,144,128]{3,2,1,0:T(8,128)(2,1)S(1)}, bf16[1,4,144,128]{3,2,1,0:T(8,128)(2,1)S(1)}, u32[]{:S(2)}, u32[]{:S(2)}) %collective-permute-start.21) | collective-permute-done | bytes 147488 | tf_op jit(solution)/shard_map/ppermute | solution.py:331
  137.8 8.4 %collective-permute-done.11.refs_1_ = bf16[8,144,128]{2,1,0:T(8,128)(2,1)S(1)} collective-permute-done((bf16[8,144,128]{2,1,0:T(8,128)(2,1)S(1)}, bf16[8,144,128]{2,1,0:T(8,128)(2,1)S(1)}, u32[]{:S(2)}, u32[]{:S(2)}) %collective-permute-start.11) | collective-permute-done | bytes 294944 | tf_op jit(solution)/shard_map/ppermute | solution.py:331
  146.3 8.3 %solve.1.weights_ref = bf16[16,128,128]{2,1,0:T(8,128)(2,1)S(1)} custom-call(bf16[8,144,128]{2,1,0:T(8,128)(2,1)S(1)} %collective-permute-done.5.refs_0_, bf16[8,144,128]{2,1,0:T(8,128)(2,1)S(1)} %collective-permute-done.11.refs_1_, bf16[8,144,128]{2,1,0:T(8,128)(2,1)S(1)} %collective-permute-done.17.refs_2_, bf16[8,144,128]{2,1,0:T(8,128)(2,1)S(1)} %pad_maximum_fusion.3.refs_3_), custom_call_target="tpu_custom_call" | custom-call | tf_op jit(solution)/shard_map/solve/pallas_call | solution.py:296
  154.6 9.3 %analysis.1 = f32[16,6,128,256]{3,2,1,0:T(8,128)} custom-call(bf16[16,128,128]{2,1,0:T(8,128)(2,1)S(1)} %solve.1.weights_ref, bf16[16,6,128,256]{3,2,1,0:T(8,128)(2,1)S(1)} %bitcast.106, f32[16,6,256]{2,1,0:T(8,128)S(1)} %bitcast.115), custom_call_target="tpu_custom_call" | custom-call | tf_op jit(solution)/shard_map/analysis/pallas_call | solution.py:314
  (130 shorter events, 33.8 us)
Async XLA Ops:
  4.6 19.4 %all-to-all-start = ((s32[32,1,25]{2,1,0:T(1,128)}), s32[32,1,25]{2,1,0:T(1,128)S(1)}, u32[]{:S(2)}, u32[]{:S(2)}) async-start(s32[32,1,25]{2,1,0:T(1,128)} %bitcast.6), calls=%async_computation | async-start | bytes 32768 | tf_op jit(solution)/shard_map/all_to_all | solution.py:347
  35.0 6.9 %collective-permute-start = (bf16[4,8,144,128]{3,2,1,0:T(8,128)(2,1)S(1)}, bf16[4,8,144,128]{3,2,1,0:T(8,128)(2,1)S(1)}, u32[]{:S(2)}, u32[]{:S(2)}) collective-permute-start(bf16[4,8,144,128]{3,2,1,0:T(8,128)(2,1)S(1)} %partial_grams.9), channel_id=1, source_target_pairs={{0,8},{8,0},{16,24},{24,16},{1,9},{9,1},{17,25},{25,17},{2,10},{10... | collective-permute-start | bytes 3538952 | tf_op jit(solution)/shard_map/ppermute | solution.py:331
  42.4 12.9 %collective-permute-start.1 = (bf16[2,4,144,128]{3,2,1,0:T(8,128)(2,1)S(1)}, bf16[2,4,144,128]{3,2,1,0:T(8,128)(2,1)S(1)}, u32[]{:S(2)}, u32[]{:S(2)}) collective-permute-start(bf16[2,4,144,128]{3,2,1,0:T(8,128)(2,1)S(1)} %get-tuple-element.93), channel_id=1, source_target_pairs={{0,1},{1,0},{2,3},{3,2},{4,5},{5,4},{6,7},{7,6},{8,9},{9,8},{10,11... | collective-permute-start | bytes 884744 | tf_op jit(solution)/shard_map/ppermute | solution.py:331
  46.3 9.1 %collective-permute-start.2 = (bf16[2,4,144,128]{3,2,1,0:T(8,128)(2,1)S(1)}, bf16[2,4,144,128]{3,2,1,0:T(8,128)(2,1)S(1)}, u32[]{:S(2)}, u32[]{:S(2)}) collective-permute-start(bf16[2,4,144,128]{3,2,1,0:T(8,128)(2,1)S(1)} %get-tuple-element.91), channel_id=1, source_target_pairs={{0,16},{8,24},{16,0},{24,8},{1,17},{9,25},{17,1},{25,9},{2,18},{10... | collective-permute-start | bytes 884744 | tf_op jit(solution)/shard_map/ppermute | solution.py:331
  55.2 10.0 %collective-permute-start.6 = (bf16[4,8,144,128]{3,2,1,0:T(8,128)(2,1)S(1)}, bf16[4,8,144,128]{3,2,1,0:T(8,128)(2,1)S(1)}, u32[]{:S(2)}, u32[]{:S(2)}) collective-permute-start(bf16[4,8,144,128]{3,2,1,0:T(8,128)(2,1)S(1)} %partial_grams.10), channel_id=1, source_target_pairs={{0,8},{8,0},{16,24},{24,16},{1,9},{9,1},{17,25},{25,17},{2,10},{10... | collective-permute-start | bytes 3538952 | tf_op jit(solution)/shard_map/ppermute | solution.py:331
  55.6 8.7 %collective-permute-start.4 = (bf16[1,4,144,128]{3,2,1,0:T(8,128)(2,1)S(1)}, bf16[1,4,144,128]{3,2,1,0:T(8,128)(2,1)S(1)}, u32[]{:S(2)}, u32[]{:S(2)}) collective-permute-start(bf16[1,4,144,128]{3,2,1,0:T(8,128)(2,1)S(1)} %get-tuple-element.107), channel_id=1, source_target_pairs={{0,1},{1,0},{2,3},{3,2},{4,5},{5,4},{6,7},{7,6},{8,9},{9,8},{10,11... | collective-permute-start | bytes 442376 | tf_op jit(solution)/shard_map/ppermute | solution.py:331
  56.0 8.3 %collective-permute-start.3 = (bf16[1,4,144,128]{3,2,1,0:T(8,128)(2,1)S(1)}, bf16[1,4,144,128]{3,2,1,0:T(8,128)(2,1)S(1)}, u32[]{:S(2)}, u32[]{:S(2)}) collective-permute-start(bf16[1,4,144,128]{3,2,1,0:T(8,128)(2,1)S(1)} %get-tuple-element.109), channel_id=1, source_target_pairs={{0,16},{8,24},{16,0},{24,8},{1,17},{9,25},{17,1},{25,9},{2,18},{10... | collective-permute-start | bytes 442376 | tf_op jit(solution)/shard_map/ppermute | solution.py:331
  65.6 11.2 %collective-permute-start.7 = (bf16[2,4,144,128]{3,2,1,0:T(8,128)(2,1)S(1)}, bf16[2,4,144,128]{3,2,1,0:T(8,128)(2,1)S(1)}, u32[]{:S(2)}, u32[]{:S(2)}) collective-permute-start(bf16[2,4,144,128]{3,2,1,0:T(8,128)(2,1)S(1)} %get-tuple-element.89), channel_id=1, source_target_pairs={{0,1},{1,0},{2,3},{3,2},{4,5},{5,4},{6,7},{7,6},{8,9},{9,8},{10,11... | collective-permute-start | bytes 884744 | tf_op jit(solution)/shard_map/ppermute | solution.py:331
  68.2 8.6 %collective-permute-start.8 = (bf16[2,4,144,128]{3,2,1,0:T(8,128)(2,1)S(1)}, bf16[2,4,144,128]{3,2,1,0:T(8,128)(2,1)S(1)}, u32[]{:S(2)}, u32[]{:S(2)}) collective-permute-start(bf16[2,4,144,128]{3,2,1,0:T(8,128)(2,1)S(1)} %get-tuple-element.87), channel_id=1, source_target_pairs={{0,16},{8,24},{16,0},{24,8},{1,17},{9,25},{17,1},{25,9},{2,18},{10... | collective-permute-start | bytes 884744 | tf_op jit(solution)/shard_map/ppermute | solution.py:331
  76.7 9.9 %collective-permute-start.12 = (bf16[4,8,144,128]{3,2,1,0:T(8,128)(2,1)S(1)}, bf16[4,8,144,128]{3,2,1,0:T(8,128)(2,1)S(1)}, u32[]{:S(2)}, u32[]{:S(2)}) collective-permute-start(bf16[4,8,144,128]{3,2,1,0:T(8,128)(2,1)S(1)} %partial_grams.12), channel_id=1, source_target_pairs={{0,8},{8,0},{16,24},{24,16},{1,9},{9,1},{17,25},{25,17},{2,10},{10... | collective-permute-start | bytes 3538952 | tf_op jit(solution)/shard_map/ppermute | solution.py:331
  77.1 8.7 %collective-permute-start.10 = (bf16[1,4,144,128]{3,2,1,0:T(8,128)(2,1)S(1)}, bf16[1,4,144,128]{3,2,1,0:T(8,128)(2,1)S(1)}, u32[]{:S(2)}, u32[]{:S(2)}) collective-permute-start(bf16[1,4,144,128]{3,2,1,0:T(8,128)(2,1)S(1)} %get-tuple-element.103), channel_id=1, source_target_pairs={{0,1},{1,0},{2,3},{3,2},{4,5},{5,4},{6,7},{7,6},{8,9},{9,8},{10,11... | collective-permute-start | bytes 442376 | tf_op jit(solution)/shard_map/ppermute | solution.py:331
  77.2 8.5 %collective-permute-start.9 = (bf16[1,4,144,128]{3,2,1,0:T(8,128)(2,1)S(1)}, bf16[1,4,144,128]{3,2,1,0:T(8,128)(2,1)S(1)}, u32[]{:S(2)}, u32[]{:S(2)}) collective-permute-start(bf16[1,4,144,128]{3,2,1,0:T(8,128)(2,1)S(1)} %get-tuple-element.105), channel_id=1, source_target_pairs={{0,16},{8,24},{16,0},{24,8},{1,17},{9,25},{17,1},{25,9},{2,18},{10... | collective-permute-start | bytes 442376 | tf_op jit(solution)/shard_map/ppermute | solution.py:331
  88.7 11.0 %collective-permute-start.13 = (bf16[2,4,144,128]{3,2,1,0:T(8,128)(2,1)}, bf16[2,4,144,128]{3,2,1,0:T(8,128)(2,1)}, u32[]{:S(2)}, u32[]{:S(2)}) collective-permute-start(bf16[2,4,144,128]{3,2,1,0:T(8,128)(2,1)} %get-tuple-element.85), channel_id=1, source_target_pairs={{0,1},{1,0},{2,3},{3,2},{4,5},{5,4},{6,7},{7,6},{8,9},{9,8},{10,11... | collective-permute-start | bytes 884744 | tf_op jit(solution)/shard_map/ppermute | solution.py:331
  89.9 9.8 %collective-permute-start.14 = (bf16[2,4,144,128]{3,2,1,0:T(8,128)(2,1)}, bf16[2,4,144,128]{3,2,1,0:T(8,128)(2,1)}, u32[]{:S(2)}, u32[]{:S(2)}) collective-permute-start(bf16[2,4,144,128]{3,2,1,0:T(8,128)(2,1)} %get-tuple-element.83), channel_id=1, source_target_pairs={{0,16},{8,24},{16,0},{24,8},{1,17},{9,25},{17,1},{25,9},{2,18},{10... | collective-permute-start | bytes 884744 | tf_op jit(solution)/shard_map/ppermute | solution.py:331
  99.6 13.7 %collective-permute-start.18 = (bf16[4,8,144,128]{3,2,1,0:T(8,128)(2,1)}, bf16[4,8,144,128]{3,2,1,0:T(8,128)(2,1)S(1)}, u32[]{:S(2)}, u32[]{:S(2)}) collective-permute-start(bf16[4,8,144,128]{3,2,1,0:T(8,128)(2,1)} %partial_grams.14), channel_id=1, source_target_pairs={{0,8},{8,0},{16,24},{24,16},{1,9},{9,1},{17,25},{25,17},{2,10},{10... | collective-permute-start | bytes 3538952 | tf_op jit(solution)/shard_map/ppermute | solution.py:331
  113.8 16.7 %collective-permute-start.20 = (bf16[2,4,144,128]{3,2,1,0:T(8,128)(2,1)S(1)}, bf16[2,4,144,128]{3,2,1,0:T(8,128)(2,1)S(1)}, u32[]{:S(2)}, u32[]{:S(2)}) collective-permute-start(bf16[2,4,144,128]{3,2,1,0:T(8,128)(2,1)S(1)} %get-tuple-element.79), channel_id=1, source_target_pairs={{0,16},{8,24},{16,0},{24,8},{1,17},{9,25},{17,1},{25,9},{2,18},{10... | collective-permute-start | bytes 884744 | tf_op jit(solution)/shard_map/ppermute | solution.py:331
  115.8 14.8 %collective-permute-start.19 = (bf16[2,4,144,128]{3,2,1,0:T(8,128)(2,1)S(1)}, bf16[2,4,144,128]{3,2,1,0:T(8,128)(2,1)S(1)}, u32[]{:S(2)}, u32[]{:S(2)}) collective-permute-start(bf16[2,4,144,128]{3,2,1,0:T(8,128)(2,1)S(1)} %get-tuple-element.81), channel_id=1, source_target_pairs={{0,1},{1,0},{2,3},{3,2},{4,5},{5,4},{6,7},{7,6},{8,9},{9,8},{10,11... | collective-permute-start | bytes 884744 | tf_op jit(solution)/shard_map/ppermute | solution.py:331
  115.8 10.8 %collective-permute-start.16 = (bf16[1,4,144,128]{3,2,1,0:T(8,128)(2,1)S(1)}, bf16[1,4,144,128]{3,2,1,0:T(8,128)(2,1)S(1)}, u32[]{:S(2)}, u32[]{:S(2)}) collective-permute-start(bf16[1,4,144,128]{3,2,1,0:T(8,128)(2,1)S(1)} %get-tuple-element.99), channel_id=1, source_target_pairs={{0,1},{1,0},{2,3},{3,2},{4,5},{5,4},{6,7},{7,6},{8,9},{9,8},{10,11... | collective-permute-start | bytes 442376 | tf_op jit(solution)/shard_map/ppermute | solution.py:331
  117.9 11.9 %collective-permute-start.15 = (bf16[1,4,144,128]{3,2,1,0:T(8,128)(2,1)S(1)}, bf16[1,4,144,128]{3,2,1,0:T(8,128)(2,1)S(1)}, u32[]{:S(2)}, u32[]{:S(2)}) collective-permute-start(bf16[1,4,144,128]{3,2,1,0:T(8,128)(2,1)S(1)} %get-tuple-element.101), channel_id=1, source_target_pairs={{0,16},{8,24},{16,0},{24,8},{1,17},{9,25},{17,1},{25,9},{2,18},{10... | collective-permute-start | bytes 442376 | tf_op jit(solution)/shard_map/ppermute | solution.py:331
  118.0 19.8 %collective-permute-start.5 = (bf16[8,144,128]{2,1,0:T(8,128)(2,1)S(1)}, bf16[8,144,128]{2,1,0:T(8,128)(2,1)S(1)}, u32[]{:S(2)}, u32[]{:S(2)}) collective-permute-start(bf16[8,144,128]{2,1,0:T(8,128)(2,1)S(1)} %copy-done.13), channel_id=1, source_target_pairs={{0,6},{1,7},{2,4},{3,5},{4,2},{5,3},{6,0},{7,1},{8,14},{9,15},{10,... | collective-permute-start | bytes 884744 | tf_op jit(solution)/shard_map/ppermute | solution.py:331
  126.5 19.7 %collective-permute-start.11 = (bf16[8,144,128]{2,1,0:T(8,128)(2,1)S(1)}, bf16[8,144,128]{2,1,0:T(8,128)(2,1)S(1)}, u32[]{:S(2)}, u32[]{:S(2)}) collective-permute-start(bf16[8,144,128]{2,1,0:T(8,128)(2,1)S(1)} %copy-done.14), channel_id=1, source_target_pairs={{0,4},{1,5},{2,6},{3,7},{4,0},{5,1},{6,2},{7,3},{8,12},{9,13},{10,... | collective-permute-start | bytes 884744 | tf_op jit(solution)/shard_map/ppermute | solution.py:331
  129.8 16.4 %collective-permute-start.17 = (bf16[8,144,128]{2,1,0:T(8,128)(2,1)S(1)}, bf16[8,144,128]{2,1,0:T(8,128)(2,1)S(1)}, u32[]{:S(2)}, u32[]{:S(2)}) collective-permute-start(bf16[8,144,128]{2,1,0:T(8,128)(2,1)S(1)} %pad_maximum_fusion.2), channel_id=1, source_target_pairs={{0,2},{1,3},{2,0},{3,1},{4,6},{5,7},{6,4},{7,5},{8,10},{9,11},{10,... | collective-permute-start | bytes 884744 | tf_op jit(solution)/shard_map/ppermute | solution.py:331
  130.8 5.2 %collective-permute-start.21 = (bf16[1,4,144,128]{3,2,1,0:T(8,128)(2,1)S(1)}, bf16[1,4,144,128]{3,2,1,0:T(8,128)(2,1)S(1)}, u32[]{:S(2)}, u32[]{:S(2)}) collective-permute-start(bf16[1,4,144,128]{3,2,1,0:T(8,128)(2,1)S(1)} %get-tuple-element.97), channel_id=1, source_target_pairs={{0,16},{8,24},{16,0},{24,8},{1,17},{9,25},{17,1},{25,9},{2,18},{10... | collective-permute-start | bytes 442376 | tf_op jit(solution)/shard_map/ppermute | solution.py:331
  132.6 5.1 %collective-permute-start.22 = (bf16[1,4,144,128]{3,2,1,0:T(8,128)(2,1)S(1)}, bf16[1,4,144,128]{3,2,1,0:T(8,128)(2,1)S(1)}, u32[]{:S(2)}, u32[]{:S(2)}) collective-permute-start(bf16[1,4,144,128]{3,2,1,0:T(8,128)(2,1)S(1)} %get-tuple-element.95), channel_id=1, source_target_pairs={{0,1},{1,0},{2,3},{3,2},{4,5},{5,4},{6,7},{7,6},{8,9},{9,8},{10,11... | collective-permute-start | bytes 442376 | tf_op jit(solution)/shard_map/ppermute | solution.py:331
  (18 other events, 225.9 us)

commit v3 on v2

--- a/solution.py
+++ b/solution.py
@@ -43,23 +43,34 @@
 
 
 def stage_kernel(
-    chunk, anom_hbm, innov_ref, rinv_ref, lon_ref, lat_ref, left_ref, fields_ref, totals_ref, sems
+    chunk,
+    anom_hbm,
+    innov_hbm,
+    rinv_hbm,
+    lon_hbm,
+    lat_hbm,
+    left_ref,
+    rinv_ref,
+    lon_ref,
+    lat_ref,
+    totals_ref,
+    innov_ref,
+    sems,
 ):
     held, members, block_obs = anom_hbm.shape
-    copies = []
+    pairs = [(rinv_hbm, rinv_ref), (innov_hbm, innov_ref)]
     for i in range(held // chunk):
         span = pl.ds(i * chunk, chunk)
-        copy = pltpu.make_async_copy(
-            anom_hbm.at[span], left_ref.at[span, pl.ds(0, members), :], sems.at[i]
-        )
+        pairs.append((anom_hbm.at[span], left_ref.at[span, pl.ds(0, members), :]))
+    pairs += [(lon_hbm, lon_ref), (lat_hbm, lat_ref)]
+    copies = [pltpu.make_async_copy(a, b, sems.at[i]) for i, (a, b) in enumerate(pairs)]
+    for copy in copies:
         copy.start()
-        copies.append(copy)
-    fields_ref[0] = (2 * lon_ref[...]).astype(F32)
-    fields_ref[1] = (2 * lat_ref[...]).astype(F32)
-    fields_ref[2] = rinv_ref[...]
+    copies[0].wait()
+    copies[1].wait()
     line = lax.broadcasted_iota(jnp.int32, (EXT, block_obs), 0)
     sums = jnp.zeros((8, block_obs), F32)
-    for i, copy in enumerate(copies):
+    for i, copy in enumerate(copies[2:-2]):
         copy.wait()
 
         def block(j, total, first=i * chunk):
@@ -77,33 +88,53 @@
     spread = jnp.sum(sums, axis=0, keepdims=True) / (members - 1)
     line = lax.broadcasted_iota(jnp.int32, (8, block_obs), 0)
     totals_ref[...] = jnp.where(line == 4, innovation, jnp.where(line == 5, spread, 0.0))
+    copies[-2].wait()
+    copies[-1].wait()
 
 
 def stage(anom, innov, rinv, lon, lat):
     held, members, block_obs = anom.shape
     chunk = 16 if held % 16 == 0 else held
-    whole = pl.BlockSpec(memory_space=pltpu.VMEM)
+    operands = [pltpu.with_memory_space_constraint(v, pltpu.HBM) for v in (anom, innov, rinv, lon, lat)]
     return pl.pallas_call(
         functools.partial(stage_kernel, chunk),
         out_shape=[
             pltpu.VMEM((held, members + EXT, block_obs), BF16),
-            pltpu.VMEM((3, held, block_obs), F32),
+            pltpu.VMEM((held, block_obs), F32),
+            pltpu.VMEM((held, block_obs), jnp.int32),
+            pltpu.VMEM((held, block_obs), jnp.int32),
             pltpu.VMEM((8, block_obs), F32),
         ],
-        in_specs=[pl.BlockSpec(memory_space=pltpu.HBM)] + [whole] * 4,
-        out_specs=[whole] * 3,
-        scratch_shapes=[pltpu.SemaphoreType.DMA((held // chunk,))],
+        in_specs=[pl.BlockSpec(memory_space=pltpu.HBM)] * 5,
+        out_specs=[pl.BlockSpec(memory_space=pltpu.VMEM)] * 5,
+        scratch_shapes=[
+            pltpu.VMEM((held, block_obs), F32),
+            pltpu.SemaphoreType.DMA((held // chunk + 4,)),
+        ],
         compiler_params=pltpu.CompilerParams(vmem_limit_bytes=4 * 2**20),
         cost_estimate=pl.CostEstimate(flops=0, bytes_accessed=anom.size * 4, transcendentals=0),
         name="stage",
-    )(anom, innov, rinv, lon, lat)
+    )(*operands)
 
 
 def gram_kernel(
-    sizes, targets_ref, requests_ref, left_ref, fields_ref, totals_ref, out_ref, acc_ref
+    sizes,
+    far,
+    core,
+    requests_ref,
+    left_ref,
+    rinv_ref,
+    obs_lon_ref,
+    obs_lat_ref,
+    totals_ref,
+    out_ref,
+    acc_ref,
 ):
     patches, lat_patches, lon_patches, lat_devices, held, per_owner, grid_lon = sizes
-    target = targets_ref[pl.program_id(0)]
+    step = pl.program_id(0)
+    me = requests_ref[0, per_owner + 1]
+    distance = (2 * (step // 2) + core) * lat_devices + (2 * far + step % 2)
+    target = me ^ distance
     lon_first = (target // lat_devices) * lon_patches
     lat_first = (target % lat_devices) * lat_patches
     members = left_ref.shape[2]
@@ -120,11 +151,11 @@
             centre_lon = (lon_first + patch // lat_patches) * (2 * PSIDE) + (PSIDE - 1)
             centre_lat = (lat_first + patch % lat_patches) * (2 * PSIDE) + (PSIDE - 1)
             row = pl.ds(block, 1)
-            lon_gap = jnp.abs(fields_ref[0, row, :] - centre_lon.astype(F32))
-            lon_gap = jnp.minimum(lon_gap, 2.0 * grid_lon - lon_gap)
-            lat_gap = fields_ref[1, row, :] - centre_lat.astype(F32)
-            square = lon_gap * lon_gap + lat_gap * lat_gap
-            rinv = jnp.where(entry < number, fields_ref[2, row, :], 0.0)
+            lon_gap = jnp.abs(2 * obs_lon_ref[row, :] - centre_lon)
+            lon_gap = jnp.minimum(lon_gap, 2 * grid_lon - lon_gap)
+            lat_gap = 2 * obs_lat_ref[row, :] - centre_lat
+            square = (lon_gap * lon_gap + lat_gap * lat_gap).astype(F32)
+            rinv = jnp.where(entry < number, rinv_ref[row, :], 0.0)
             weight = rinv * jnp.exp(square * (-1.0 / (8.0 * LOC_SCALE * LOC_SCALE)))
             left = left_ref[block]
             scaled = (left[:members].astype(F32) * weight).astype(BF16)
@@ -156,28 +187,27 @@
         out_ref[0, pair, members:, :] = jnp.concatenate([high, rows - high], axis=0).astype(BF16)
 
 
-def partial_grams(sizes, targets, requests, staged):
+def partial_grams(sizes, far, core, count, requests, staged):
     patches, per_owner = sizes[0], sizes[5]
-    count = targets.shape[0]
     members = staged[0].shape[2]
     rows = members + EXT
     block = (1, patches // 2, rows, members)
     return pl.pallas_call(
-        functools.partial(gram_kernel, sizes),
+        functools.partial(gram_kernel, sizes, far, core),
         out_shape=jax.ShapeDtypeStruct((count, *block[1:]), BF16),
         grid_spec=pltpu.PrefetchScalarGridSpec(
-            num_scalar_prefetch=2,
+            num_scalar_prefetch=1,
             grid=(count,),
-            in_specs=[pl.BlockSpec(memory_space=pltpu.VMEM)] * 3,
+            in_specs=[pl.BlockSpec(memory_space=pltpu.VMEM)] * 5,
             out_specs=pl.BlockSpec(block, lambda i, *_: (i, 0, 0, 0)),
             scratch_shapes=[pltpu.VMEM((patches, members + 8, members), F32)],
         ),
         compiler_params=pltpu.CompilerParams(vmem_limit_bytes=6 * 2**20),
         cost_estimate=pl.CostEstimate(
-            flops=count * per_owner * 40 * members**3, bytes_accessed=0, transcendentals=0
+            flops=count * per_owner * 100 * members**3, bytes_accessed=0, transcendentals=0
         ),
         name="partial_grams",
-    )(targets, requests, *staged)
+    )(requests, *staged)
 
 
 def added(left, right):
@@ -189,27 +219,27 @@
     return total[:, :members].astype(BF16), rows.astype(BF16)
 
 
-def add_kernel(count, *refs):
+def add_kernel(count, plan, *refs):
     keep, got, outs = refs[:count], refs[count : 2 * count], refs[2 * count :]
-    for i in range(count):
-        members = keep[i].shape[-1]
-        body, rows = added(keep[i][0], got[i][0])
-        outs[i][0, :, :members, :] = body
-        outs[i][0, :, members:, :] = rows
-
-
-def add_all(keep, got):
+    for part, index, low, high, out, place, at in plan:
+        members = keep[part].shape[-1]
+        body, rows = added(keep[part][index, low:high], got[part][index, low:high])
+        to = slice(at, at + high - low)
+        outs[out][place, to, :members, :] = body
+        outs[out][place, to, members:, :] = rows
+
+
+def add_all(keep, got, plan, shapes):
     count = len(keep)
-    shape = keep[0].shape
-    spec = pl.BlockSpec((1, *shape[1:]), lambda i: (i, 0, 0, 0))
-    size = keep[0].size * count
+    inner = keep[0].shape[2:]
+    whole = pl.BlockSpec(memory_space=pltpu.VMEM)
+    size = sum(v.size for v in keep)
     return pl.pallas_call(
-        functools.partial(add_kernel, count),
-        out_shape=[jax.ShapeDtypeStruct(shape, BF16)] * count,
-        grid=(shape[0],),
-        in_specs=[spec] * (2 * count),
-        out_specs=[spec] * count,
-        compiler_params=pltpu.CompilerParams(vmem_limit_bytes=16 * 2**20),
+        functools.partial(add_kernel, count, plan),
+        out_shape=[jax.ShapeDtypeStruct((*shape, *inner), BF16) for shape in shapes],
+        in_specs=[whole] * (2 * count),
+        out_specs=[whole] * len(shapes),
+        compiler_params=pltpu.CompilerParams(vmem_limit_bytes=8 * 2**20),
         cost_estimate=pl.CostEstimate(flops=size * 4, bytes_accessed=size * 6, transcendentals=0),
         name="add_partials",
     )(*keep, *got)
@@ -298,7 +328,7 @@
         out_shape=jax.ShapeDtypeStruct((2 * pairs, members, members), BF16),
         in_specs=[whole] * len(parts),
         out_specs=whole,
-        compiler_params=pltpu.CompilerParams(vmem_limit_bytes=32 * 2**20),
+        compiler_params=pltpu.CompilerParams(vmem_limit_bytes=8 * 2**20),
         name="solve",
     )(*parts)
 
@@ -321,7 +351,7 @@
             pl.BlockSpec((1, fields, columns), lambda i: (i, 0, 0)),
         ],
         out_specs=pl.BlockSpec((1, fields, members, columns), lambda i: (i, 0, 0, 0)),
-        compiler_params=pltpu.CompilerParams(vmem_limit_bytes=16 * 2**20),
+        compiler_params=pltpu.CompilerParams(vmem_limit_bytes=8 * 2**20),
         name="analysis",
     )(weights, pert, mean)
 
@@ -346,10 +376,12 @@
     )
     requests = lax.all_to_all(table, ("lon", "lat"), split_axis=0, concat_axis=0, tiled=True)
 
-    staged = stage(obs_anom, innov, obs_rinv, obs_lon, obs_lat)
-    staged = [pltpu.with_memory_space_constraint(v, pltpu.VMEM) for v in staged]
-
-    me_lon, me_lat = lax.axis_index("lon"), lax.axis_index("lat")
+    me = lax.axis_index(("lon", "lat")).astype(jnp.int32)
+    requests = jnp.concatenate([requests, jnp.full((holders, 1), me)], axis=1)
+    requests, observed = lax.optimization_barrier(
+        (requests, (obs_anom, innov, obs_rinv, obs_lon, obs_lat))
+    )
+    staged = stage(*observed)
     sizes = (
         patches,
         lat_patches,
@@ -359,82 +391,103 @@
         per_owner,
         lon_devices * lon_patches * PSIDE,
     )
-
     y_count = lon_devices // 2
+    pairs = patches // 2
+    cut = pairs // 2
 
     def grams(far, core, after):
-        order = [(2 * y + core, 2 * far + near) for y in range(y_count) for near in range(2)]
-        targets = jnp.stack(
-            [(me_lon ^ lon) * lat_devices + (me_lat ^ lat) for lon, lat in order]
-        ).astype(jnp.int32)
-        targets, _ = lax.optimization_barrier((targets, after))
-        return partial_grams(sizes, targets, requests, staged)
+        tied, _ = lax.optimization_barrier((requests, after))
+        return partial_grams(sizes, far, core, lon_devices, tied, staged)
 
     def steps(far):
         send = yield far, 1
         got = swap(send, "lon", 1)
-        keep = yield far, 0
-        [total] = add_all([keep], [got])
-        total = total.reshape(y_count, 2, *total.shape[1:])
-        cut = patches // 4
-        first, second = total[:, :, :cut], total[:, :, cut:]
-        shape = (-1, *first.shape[2:])
+        keep = yield [got], [send]
         left = y_count // 2
-        keeps = [first[:, 0], second[:left].reshape(shape)]
-        gots = [
-            swap(first[:, 1], "lat", 1),
-            swap(second[left:].reshape(shape), "lon", lon_devices // 2),
-        ]
-        gots = yield gots, [total]
-        first, second = add_all(keeps, gots)
-        sums = [first, second]
-        second = second.reshape(left, 2, *second.shape[1:])
-        keeps = [first[:left], second[:, 0]]
-        gots = [
-            swap(first[left:], "lon", lon_devices // 2),
-            swap(second[:, 1], "lat", 1),
-        ]
-        gots = yield gots, sums
-        first, second = add_all(keeps, gots)
+        plan = []
+        for y in range(y_count):
+            for near in range(2):
+                plan.append((0, 2 * y + near, 0, cut, near, y, 0))
+                far_y, place = divmod(y, left)
+                plan.append((0, 2 * y + near, cut, pairs, 2 + far_y, 2 * place + near, 0))
+        keep_a, send_a, keep_b, send_b = add_all(
+            [keep[0]],
+            [keep[1]],
+            plan,
+            [(y_count, cut)] * 2 + [(2 * left, pairs - cut)] * 2,
+        )
+        got_a, got_b = yield [swap(send_a, "lat", 1), swap(send_b, "lon", y_count)], [send_a, send_b]
+        plan = []
+        for y in range(y_count):
+            far_y, place = divmod(y, left)
+            plan.append((0, y, 0, cut, far_y, place, 0))
+        for y in range(left):
+            for near in range(2):
+                plan.append((1, 2 * y + near, 0, pairs - cut, 2 + near, y, 0))
+        keep_a, send_a, keep_b, send_b = add_all(
+            [keep_a, keep_b],
+            [got_a, got_b],
+            plan,
+            [(left, cut)] * 2 + [(left, pairs - cut)] * 2,
+        )
+        got_a, got_b = yield [swap(send_a, "lon", y_count), swap(send_b, "lat", 1)], [send_a, send_b]
         while left > 1:
             left //= 2
-            keeps = [first[:left], second[:left]]
-            gots = [swap(v[left:], "lon", 2 * left) for v in (first, second)]
-            first, second = add_all(keeps, gots)
-        total = jnp.concatenate([first[0], second[0]], axis=0)
-        yield (swap(total, "lat", 2 * far) if far else total), total
-
-    parts, open_chunks, after = [], [], []
+            plan = []
+            for part in range(2):
+                for y in range(2 * left):
+                    far_y, place = divmod(y, left)
+                    plan.append((part, y, 0, keep_a.shape[1] if part == 0 else pairs - cut, 2 * part + far_y, place, 0))
+            keep_a, send_a, keep_b, send_b = add_all(
+                [keep_a, keep_b],
+                [got_a, got_b],
+                plan,
+                [(left, cut)] * 2 + [(left, pairs - cut)] * 2,
+            )
+            got_a, got_b = yield (
+                [swap(send_a, "lon", 2 * left), swap(send_b, "lon", 2 * left)],
+                [send_a, send_b],
+            )
+        plan = [(0, 0, 0, cut, 0, 0, 0), (1, 0, 0, pairs - cut, 0, 0, cut)]
+        [total] = add_all([keep_a, keep_b], [got_a, got_b], plan, [(1, pairs)])
+        if far:
+            [total] = yield [swap(total, "lat", 2 * far)], [total]
+        parts.append(total)
+
+    parts, open_chunks, sent = [], [], []
 
     def advance(latest):
-        nonlocal open_chunks, after
-        still, after = [], []
+        nonlocal open_chunks, sent
+        flat = [w for _, waits in open_chunks for w in waits]
+        if latest is not None:
+            latest, flat = lax.optimization_barrier((latest, flat))
+        still, sent = [], []
         for chunk, waits in open_chunks:
-            if latest is not None:
-                waits, _ = lax.optimization_barrier((waits, latest))
-            waits, sums = chunk.send(waits)
-            if isinstance(sums, list):
+            now, flat = flat[: len(waits)], flat[len(waits) :]
+            if latest is not None and chunk is newest:
+                now = [latest, *now]
+            try:
+                waits, sums = chunk.send(now)
                 still.append((chunk, waits))
-                after += sums
-            else:
-                parts.append(waits)
-                after.append(sums)
+                sent += sums
+            except StopIteration:
+                pass
         open_chunks = still
 
-    latest = None
+    newest = None
     for far in reversed(range(lat_devices // 2)):
         chunk = steps(far)
-        send = grams(*next(chunk), after)
-        request = chunk.send(send)
+        send = grams(*next(chunk), sent)
         advance(send)
-        keep = grams(*request, after)
-        waits, sums = chunk.send(keep)
+        waits, sums = chunk.send(send)
+        newest = chunk
+        open_chunks.append((chunk, waits))
+        keep = grams(far, 0, sent + sums)
         advance(keep)
-        open_chunks.append((chunk, waits))
-        after += sums
+        newest = None
     while open_chunks:
         advance(None)
-    weights = solve(parts, holders * held * block_obs)
+    weights = solve([v[0] for v in parts], holders * held * block_obs)
     updated = analysis(
         weights,
         state_pert.reshape(patches, fields, members, columns),

time: 164 us -> 140 us (0.85)
  local copies, waits for them, and re-layouts: 20.9 us -> 1.39 us
  starting transfers between devices: 36 us -> 30.2 us
  waiting for transfers between devices: 18.7 us -> 21.8 us
  other arithmetic: 5.39 us -> 3.23 us
    unnamed x38 -> x8, local copies, waits for them, and re-layouts: 18.2 us -> 0.79 us
    all_to_all x1, waiting for transfers between devices: 0.01 us -> 7.03 us  [on_device(): lax.all_to_all(table, ('lon', 'lat'), split_axis=0, concat_axis=0, tiled=...]
    ppermute x23, starting transfers between devices: 28.7 us -> 22.9 us  [swap(): return lax.ppermute(value, axis, [(i, i ^ flip) for i in range(size)])]
    ppermute x23, waiting for transfers between devices: 18.7 us -> 14.8 us  [swap(): return lax.ppermute(value, axis, [(i, i ^ flip) for i in range(size)])]
  transfers between devices with their start and end apart: 24 -> 24, of which waited for: 5 -> 8; matrix products, arithmetic and copies ran while one was open for 1% -> 0% of each run, Pallas kernels for 34% -> 39%
where the time goes in v3:
time: 140 us
  Pallas kernels  83 us (59%)
  starting transfers between devices  30.2 us (22%)
  waiting for transfers between devices  21.8 us (16%)
  other arithmetic  3.23 us (2%)
    pallas_call x8, Pallas kernels, partial_grams(): pl.pallas_call(functools.partial(gram_kernel, sizes, far, core), out_shap...  60 us
    ppermute x23, starting transfers between devices, swap(): return lax.ppermute(value, axis, [(i, i ^ flip) for i in range(size)])  22.9 us
    ppermute x23, waiting for transfers between devices, swap(): return lax.ppermute(value, axis, [(i, i ^ flip) for i in range(size)])  14.8 us
    pallas_call x1, Pallas kernels, analysis(): pl.pallas_call(analysis_kernel, out_shape=jax.ShapeDtypeStruct(pert.shape...  9.35 us
    pallas_call x1, Pallas kernels, solve(): pl.pallas_call(functools.partial(solve_kernel, len(parts), total_obs), ou...  8.31 us
    all_to_all x1, starting transfers between devices, on_device(): lax.all_to_all(table, ('lon', 'lat'), split_axis=0, concat_axis=0, tiled=...  7.3 us
    all_to_all x1, waiting for transfers between devices, on_device(): lax.all_to_all(table, ('lon', 'lat'), split_axis=0, concat_axis=0, tiled=...  7.03 us
    pallas_call x1, Pallas kernels, stage(): pl.pallas_call(functools.partial(stage_kernel, chunk), out_shape=[pltpu.V...  3.21 us
  transfers between devices with their start and end apart: 24, of which 8 were waited for; matrix products, arithmetic and copies ran while one was open for 0% of the time, Pallas kernels for 39%

profile of v3, /device:TPU:0, one launch (start us, length us, event | category | flops | bytes accessed | tf_op | source)
XLA Modules:
  0.0 140.0 jit_solution(8095165840216649383)
XLA Ops:
  4.6 7.3 %all-to-all-start = ((s32[32,1,25]{2,1,0:T(1,128)}), s32[32,1,25]{2,1,0:T(1,128)S(1)}, u32[]{:S(2)}, u32[]{:S(2)}) async-start(s32[32,1,25]{2,1,0:T(1,128)} %bitcast.2), calls=%async_computation | async-start | bytes 32768 | tf_op jit(solution)/shard_map/all_to_all | solution.py:377
  11.9 7.0 %all-to-all-done = s32[32,1,25]{2,1,0:T(1,128)S(1)} async-done(((s32[32,1,25]{2,1,0:T(1,128)}), s32[32,1,25]{2,1,0:T(1,128)S(1)}, u32[]{:S(2)}, u32[]{:S(2)}) %all-to-all-start) | async-done | bytes 3232 | tf_op jit(solution)/shard_map/all_to_all | solution.py:377
  19.0 3.2 %stage.1 = (bf16[192,144,128]{2,1,0:T(8,128)(2,1)S(1)}, f32[192,128]{1,0:T(8,128)S(1)}, s32[192,128]{1,0:T(8,128)S(1)}, s32[192,128]{1,0:T(8,128)S(1)}, f32[8,128]{1,0:T(8,128)S(1)}) custom-call(bf16[192,128,128]{2,1,0:T(8,128)(2,1)} %anom_hbm, f32[192,128]{1,0:T(8,128)} %innov_hbm, f32[192,128]{1,0:T(8,128)} %rinv_hbm, s32[192,128]{1,0:T(8,128)} %lon_hbm, ...), custom_call_target="tpu_custom_call" | custom-call | bytes 12582912 | tf_op jit(solution)/shard_map/stage/pallas_call | solution.py:99
  22.2 7.3 %partial_grams.8 = bf16[4,8,144,128]{3,2,1,0:T(8,128)(2,1)S(1)} custom-call(s32[32,26]{1,0:T(8,128)S(1)} %concatenate.7.requests_ref, bf16[192,144,128]{2,1,0:T(8,128)(2,1)S(1)} %get-tuple-element.83.left_ref, f32[192,128]{1,0:T(8,128)S(1)} %get-tuple-element.84.rinv_ref, s32[192,128]{1,0:T(8,128)S(1)} %get-tuple-element.85.obs_lon_ref, ...), custom_call_target="tpu_custom_call" | custom-call | flops 20132659200 | tf_op jit(solution)/shard_map/partial_grams/pallas_call | solution.py:195
  29.6 7.3 %partial_grams.9.refs_0_ = bf16[4,8,144,128]{3,2,1,0:T(8,128)(2,1)S(1)} custom-call(s32[32,26]{1,0:T(8,128)S(1)} %concatenate.7.requests_ref, bf16[192,144,128]{2,1,0:T(8,128)(2,1)S(1)} %get-tuple-element.83.left_ref, f32[192,128]{1,0:T(8,128)S(1)} %get-tuple-element.84.rinv_ref, s32[192,128]{1,0:T(8,128)S(1)} %get-tuple-element.85.obs_lon_ref, ...), custom_call_target="tpu_custom_call" | custom-call | flops 20132659200 | tf_op jit(solution)/shard_map/partial_grams/pallas_call | solution.py:195
  38.8 7.9 %partial_grams.10 = bf16[4,8,144,128]{3,2,1,0:T(8,128)(2,1)S(1)} custom-call(s32[32,26]{1,0:T(8,128)S(1)} %concatenate.7.requests_ref, bf16[192,144,128]{2,1,0:T(8,128)(2,1)S(1)} %get-tuple-element.83.left_ref, f32[192,128]{1,0:T(8,128)S(1)} %get-tuple-element.84.rinv_ref, s32[192,128]{1,0:T(8,128)S(1)} %get-tuple-element.85.obs_lon_ref, ...), custom_call_target="tpu_custom_call" | custom-call | flops 20132659200 | tf_op jit(solution)/shard_map/partial_grams/pallas_call | solution.py:195
  49.6 7.6 %partial_grams.11.refs_0_ = bf16[4,8,144,128]{3,2,1,0:T(8,128)(2,1)S(1)} custom-call(s32[32,26]{1,0:T(8,128)S(1)} %concatenate.7.requests_ref, bf16[192,144,128]{2,1,0:T(8,128)(2,1)S(1)} %get-tuple-element.83.left_ref, f32[192,128]{1,0:T(8,128)S(1)} %get-tuple-element.84.rinv_ref, s32[192,128]{1,0:T(8,128)S(1)} %get-tuple-element.85.obs_lon_ref, ...), custom_call_target="tpu_custom_call" | custom-call | flops 20132659200 | tf_op jit(solution)/shard_map/partial_grams/pallas_call | solution.py:195
  57.3 1.4 %collective-permute-start.6 = (bf16[1,8,144,128]{3,2,1,0:T(8,128)(2,1)S(1)}, bf16[1,8,144,128]{3,2,1,0:T(8,128)(2,1)S(1)}, u32[]{:S(2)}, u32[]{:S(2)}) collective-permute-start(bf16[1,8,144,128]{3,2,1,0:T(8,128)(2,1)S(1)} %add_partials.14), channel_id=1, source_target_pairs={{0,6},{1,7},{2,4},{3,5},{4,2},{5,3},{6,0},{7,1},{8,14},{9,15},{10,... | collective-permute-start | bytes 884744 | tf_op jit(solution)/shard_map/ppermute | solution.py:361
  60.6 7.6 %partial_grams.12 = bf16[4,8,144,128]{3,2,1,0:T(8,128)(2,1)S(1)} custom-call(s32[32,26]{1,0:T(8,128)S(1)} %concatenate.7.requests_ref, bf16[192,144,128]{2,1,0:T(8,128)(2,1)S(1)} %get-tuple-element.83.left_ref, f32[192,128]{1,0:T(8,128)S(1)} %get-tuple-element.84.rinv_ref, s32[192,128]{1,0:T(8,128)S(1)} %get-tuple-element.85.obs_lon_ref, ...), custom_call_target="tpu_custom_call" | custom-call | flops 20132659200 | tf_op jit(solution)/shard_map/partial_grams/pallas_call | solution.py:195
  69.4 1.7 %collective-permute-start.10 = (bf16[1,4,144,128]{3,2,1,0:T(8,128)(2,1)S(1)}, bf16[1,4,144,128]{3,2,1,0:T(8,128)(2,1)S(1)}, u32[]{:S(2)}, u32[]{:S(2)}) collective-permute-start(bf16[1,4,144,128]{3,2,1,0:T(8,128)(2,1)S(1)} %get-tuple-element.118), channel_id=1, source_target_pairs={{0,1},{1,0},{2,3},{3,2},{4,5},{5,4},{6,7},{7,6},{8,9},{9,8},{10,11... | collective-permute-start | bytes 442376 | tf_op jit(solution)/shard_map/ppermute | solution.py:361
  71.1 7.3 %partial_grams.13.refs_0_ = bf16[4,8,144,128]{3,2,1,0:T(8,128)(2,1)S(1)} custom-call(s32[32,26]{1,0:T(8,128)S(1)} %concatenate.7.requests_ref, bf16[192,144,128]{2,1,0:T(8,128)(2,1)S(1)} %get-tuple-element.83.left_ref, f32[192,128]{1,0:T(8,128)S(1)} %get-tuple-element.84.rinv_ref, s32[192,128]{1,0:T(8,128)S(1)} %get-tuple-element.85.obs_lon_ref, ...), custom_call_target="tpu_custom_call" | custom-call | flops 20132659200 | tf_op jit(solution)/shard_map/partial_grams/pallas_call | solution.py:195
  78.6 5.2 %collective-permute-start.12 = (bf16[1,8,144,128]{3,2,1,0:T(8,128)(2,1)S(1)}, bf16[1,8,144,128]{3,2,1,0:T(8,128)(2,1)S(1)}, u32[]{:S(2)}, u32[]{:S(2)}) collective-permute-start(bf16[1,8,144,128]{3,2,1,0:T(8,128)(2,1)S(1)} %add_partials.17), channel_id=1, source_target_pairs={{0,4},{1,5},{2,6},{3,7},{4,0},{5,1},{6,2},{7,3},{8,12},{9,13},{10,... | collective-permute-start | bytes 884744 | tf_op jit(solution)/shard_map/ppermute | solution.py:361
  84.2 1.3 collective-permute-start.14
  85.5 7.6 %partial_grams.14 = bf16[4,8,144,128]{3,2,1,0:T(8,128)(2,1)S(1)} custom-call(s32[32,26]{1,0:T(8,128)S(1)} %concatenate.7.requests_ref, bf16[192,144,128]{2,1,0:T(8,128)(2,1)S(1)} %get-tuple-element.83.left_ref, f32[192,128]{1,0:T(8,128)S(1)} %get-tuple-element.84.rinv_ref, s32[192,128]{1,0:T(8,128)S(1)} %get-tuple-element.85.obs_lon_ref, ...), custom_call_target="tpu_custom_call" | custom-call | flops 20132659200 | tf_op jit(solution)/shard_map/partial_grams/pallas_call | solution.py:195
  93.2 3.8 %collective-permute-done.12 = bf16[1,8,144,128]{3,2,1,0:T(8,128)(2,1)S(1)} collective-permute-done((bf16[1,8,144,128]{3,2,1,0:T(8,128)(2,1)S(1)}, bf16[1,8,144,128]{3,2,1,0:T(8,128)(2,1)S(1)}, u32[]{:S(2)}, u32[]{:S(2)}) %collective-permute-start.12) | collective-permute-done | bytes 294944 | tf_op jit(solution)/shard_map/ppermute | solution.py:361
  98.0 7.3 %partial_grams.15.refs_0_ = bf16[4,8,144,128]{3,2,1,0:T(8,128)(2,1)S(1)} custom-call(s32[32,26]{1,0:T(8,128)S(1)} %concatenate.7.requests_ref, bf16[192,144,128]{2,1,0:T(8,128)(2,1)S(1)} %get-tuple-element.83.left_ref, f32[192,128]{1,0:T(8,128)S(1)} %get-tuple-element.84.rinv_ref, s32[192,128]{1,0:T(8,128)S(1)} %get-tuple-element.85.obs_lon_ref, ...), custom_call_target="tpu_custom_call" | custom-call | flops 20132659200 | tf_op jit(solution)/shard_map/partial_grams/pallas_call | solution.py:195
  106.8 2.2 %collective-permute-start.20 = (bf16[2,4,144,128]{3,2,1,0:T(8,128)(2,1)S(1)}, bf16[2,4,144,128]{3,2,1,0:T(8,128)(2,1)S(1)}, u32[]{:S(2)}, u32[]{:S(2)}) collective-permute-start(bf16[2,4,144,128]{3,2,1,0:T(8,128)(2,1)S(1)} %get-tuple-element.144), channel_id=1, source_target_pairs={{0,16},{8,24},{16,0},{24,8},{1,17},{9,25},{17,1},{25,9},{2,18},{10... | collective-permute-start | bytes 884744 | tf_op jit(solution)/shard_map/ppermute | solution.py:361
  109.2 4.5 %collective-permute-done.19.refs_2_ = bf16[2,4,144,128]{3,2,1,0:T(8,128)(2,1)S(1)} collective-permute-done((bf16[2,4,144,128]{3,2,1,0:T(8,128)(2,1)S(1)}, bf16[2,4,144,128]{3,2,1,0:T(8,128)(2,1)S(1)}, u32[]{:S(2)}, u32[]{:S(2)}) %collective-permute-start.19) | collective-permute-done | bytes 294944 | tf_op jit(solution)/shard_map/ppermute | solution.py:361
  113.7 1.3 collective-permute-done.20.refs_3_
  115.2 1.8 %collective-permute-start.21 = (bf16[1,4,144,128]{3,2,1,0:T(8,128)(2,1)S(1)}, bf16[1,4,144,128]{3,2,1,0:T(8,128)(2,1)S(1)}, u32[]{:S(2)}, u32[]{:S(2)}) collective-permute-start(bf16[1,4,144,128]{3,2,1,0:T(8,128)(2,1)S(1)} %get-tuple-element.147), channel_id=1, source_target_pairs={{0,16},{8,24},{16,0},{24,8},{1,17},{9,25},{17,1},{25,9},{2,18},{10... | collective-permute-start | bytes 442376 | tf_op jit(solution)/shard_map/ppermute | solution.py:361
  117.4 3.0 %collective-permute-done.21.refs_2_ = bf16[1,4,144,128]{3,2,1,0:T(8,128)(2,1)S(1)} collective-permute-done((bf16[1,4,144,128]{3,2,1,0:T(8,128)(2,1)S(1)}, bf16[1,4,144,128]{3,2,1,0:T(8,128)(2,1)S(1)}, u32[]{:S(2)}, u32[]{:S(2)}) %collective-permute-start.21) | collective-permute-done | bytes 147488 | tf_op jit(solution)/shard_map/ppermute | solution.py:361
  120.4 1.7 %collective-permute-done.22.refs_3_ = bf16[1,4,144,128]{3,2,1,0:T(8,128)(2,1)S(1)} collective-permute-done((bf16[1,4,144,128]{3,2,1,0:T(8,128)(2,1)S(1)}, bf16[1,4,144,128]{3,2,1,0:T(8,128)(2,1)S(1)}, u32[]{:S(2)}, u32[]{:S(2)}) %collective-permute-start.22) | collective-permute-done | bytes 147488 | tf_op jit(solution)/shard_map/ppermute | solution.py:361
  122.3 8.3 %solve.1.weights_ref = bf16[16,128,128]{2,1,0:T(8,128)(2,1)S(1)} custom-call(bf16[8,144,128]{2,1,0:T(8,128)(2,1)S(1)} %bitcast.17, bf16[8,144,128]{2,1,0:T(8,128)(2,1)S(1)} %bitcast.18, bf16[8,144,128]{2,1,0:T(8,128)(2,1)S(1)} %bitcast.19, bf16[8,144,128]{2,1,0:T(8,128)(2,1)S(1)} %bitcast.15), custom_call_target="tpu_custom_call" | custom-call | tf_op jit(solution)/shard_map/solve/pallas_call | solution.py:326
  130.6 9.3 %analysis.1 = f32[16,6,128,256]{3,2,1,0:T(8,128)} custom-call(bf16[16,128,128]{2,1,0:T(8,128)(2,1)S(1)} %solve.1.weights_ref, bf16[16,6,128,256]{3,2,1,0:T(8,128)(2,1)S(1)} %bitcast.14, f32[16,6,256]{2,1,0:T(8,128)S(1)} %bitcast.16), custom_call_target="tpu_custom_call" | custom-call | tf_op jit(solution)/shard_map/analysis/pallas_call | solution.py:344
  (73 shorter events, 16.2 us)
Async XLA Ops:
  4.6 14.3 %all-to-all-start = ((s32[32,1,25]{2,1,0:T(1,128)}), s32[32,1,25]{2,1,0:T(1,128)S(1)}, u32[]{:S(2)}, u32[]{:S(2)}) async-start(s32[32,1,25]{2,1,0:T(1,128)} %bitcast.2), calls=%async_computation | async-start | bytes 32768 | tf_op jit(solution)/shard_map/all_to_all | solution.py:377
  29.5 7.4 %collective-permute-start = (bf16[4,8,144,128]{3,2,1,0:T(8,128)(2,1)S(1)}, bf16[4,8,144,128]{3,2,1,0:T(8,128)(2,1)S(1)}, u32[]{:S(2)}, u32[]{:S(2)}) collective-permute-start(bf16[4,8,144,128]{3,2,1,0:T(8,128)(2,1)S(1)} %partial_grams.8), channel_id=1, source_target_pairs={{0,8},{8,0},{16,24},{24,16},{1,9},{9,1},{17,25},{25,17},{2,10},{10... | collective-permute-start | bytes 3538952 | tf_op jit(solution)/shard_map/ppermute | solution.py:361
  37.3 9.8 %collective-permute-start.1 = (bf16[2,4,144,128]{3,2,1,0:T(8,128)(2,1)S(1)}, bf16[2,4,144,128]{3,2,1,0:T(8,128)(2,1)S(1)}, u32[]{:S(2)}, u32[]{:S(2)}) collective-permute-start(bf16[2,4,144,128]{3,2,1,0:T(8,128)(2,1)S(1)} %get-tuple-element.93), channel_id=1, source_target_pairs={{0,1},{1,0},{2,3},{3,2},{4,5},{5,4},{6,7},{7,6},{8,9},{9,8},{10,11... | collective-permute-start | bytes 884744 | tf_op jit(solution)/shard_map/ppermute | solution.py:361
  37.7 9.4 %collective-permute-start.2 = (bf16[2,4,144,128]{3,2,1,0:T(8,128)(2,1)S(1)}, bf16[2,4,144,128]{3,2,1,0:T(8,128)(2,1)S(1)}, u32[]{:S(2)}, u32[]{:S(2)}) collective-permute-start(bf16[2,4,144,128]{3,2,1,0:T(8,128)(2,1)S(1)} %get-tuple-element.94), channel_id=1, source_target_pairs={{0,16},{8,24},{16,0},{24,8},{1,17},{9,25},{17,1},{25,9},{2,18},{10... | collective-permute-start | bytes 884744 | tf_op jit(solution)/shard_map/ppermute | solution.py:361
  46.7 10.6 %collective-permute-start.5 = (bf16[4,8,144,128]{3,2,1,0:T(8,128)(2,1)S(1)}, bf16[4,8,144,128]{3,2,1,0:T(8,128)(2,1)S(1)}, u32[]{:S(2)}, u32[]{:S(2)}) collective-permute-start(bf16[4,8,144,128]{3,2,1,0:T(8,128)(2,1)S(1)} %partial_grams.10), channel_id=1, source_target_pairs={{0,8},{8,0},{16,24},{24,16},{1,9},{9,1},{17,25},{25,17},{2,10},{10... | collective-permute-start | bytes 3538952 | tf_op jit(solution)/shard_map/ppermute | solution.py:361
  47.2 10.0 %collective-permute-start.3 = (bf16[1,4,144,128]{3,2,1,0:T(8,128)(2,1)S(1)}, bf16[1,4,144,128]{3,2,1,0:T(8,128)(2,1)S(1)}, u32[]{:S(2)}, u32[]{:S(2)}) collective-permute-start(bf16[1,4,144,128]{3,2,1,0:T(8,128)(2,1)S(1)} %get-tuple-element.100), channel_id=1, source_target_pairs={{0,16},{8,24},{16,0},{24,8},{1,17},{9,25},{17,1},{25,9},{2,18},{10... | collective-permute-start | bytes 442376 | tf_op jit(solution)/shard_map/ppermute | solution.py:361
  48.4 8.8 %collective-permute-start.4 = (bf16[1,4,144,128]{3,2,1,0:T(8,128)(2,1)S(1)}, bf16[1,4,144,128]{3,2,1,0:T(8,128)(2,1)S(1)}, u32[]{:S(2)}, u32[]{:S(2)}) collective-permute-start(bf16[1,4,144,128]{3,2,1,0:T(8,128)(2,1)S(1)} %get-tuple-element.101), channel_id=1, source_target_pairs={{0,1},{1,0},{2,3},{3,2},{4,5},{5,4},{6,7},{7,6},{8,9},{9,8},{10,11... | collective-permute-start | bytes 442376 | tf_op jit(solution)/shard_map/ppermute | solution.py:361
  57.3 11.0 %collective-permute-start.6 = (bf16[1,8,144,128]{3,2,1,0:T(8,128)(2,1)S(1)}, bf16[1,8,144,128]{3,2,1,0:T(8,128)(2,1)S(1)}, u32[]{:S(2)}, u32[]{:S(2)}) collective-permute-start(bf16[1,8,144,128]{3,2,1,0:T(8,128)(2,1)S(1)} %add_partials.14), channel_id=1, source_target_pairs={{0,6},{1,7},{2,4},{3,5},{4,2},{5,3},{6,0},{7,1},{8,14},{9,15},{10,... | collective-permute-start | bytes 884744 | tf_op jit(solution)/shard_map/ppermute | solution.py:361
  59.0 9.3 %collective-permute-start.7 = (bf16[2,4,144,128]{3,2,1,0:T(8,128)(2,1)S(1)}, bf16[2,4,144,128]{3,2,1,0:T(8,128)(2,1)S(1)}, u32[]{:S(2)}, u32[]{:S(2)}) collective-permute-start(bf16[2,4,144,128]{3,2,1,0:T(8,128)(2,1)S(1)} %get-tuple-element.107), channel_id=1, source_target_pairs={{0,1},{1,0},{2,3},{3,2},{4,5},{5,4},{6,7},{7,6},{8,9},{9,8},{10,11... | collective-permute-start | bytes 884744 | tf_op jit(solution)/shard_map/ppermute | solution.py:361
  59.4 8.9 %collective-permute-start.8 = (bf16[2,4,144,128]{3,2,1,0:T(8,128)(2,1)S(1)}, bf16[2,4,144,128]{3,2,1,0:T(8,128)(2,1)S(1)}, u32[]{:S(2)}, u32[]{:S(2)}) collective-permute-start(bf16[2,4,144,128]{3,2,1,0:T(8,128)(2,1)S(1)} %get-tuple-element.108), channel_id=1, source_target_pairs={{0,16},{8,24},{16,0},{24,8},{1,17},{9,25},{17,1},{25,9},{2,18},{10... | collective-permute-start | bytes 884744 | tf_op jit(solution)/shard_map/ppermute | solution.py:361
  68.3 10.2 %collective-permute-start.11 = (bf16[4,8,144,128]{3,2,1,0:T(8,128)(2,1)S(1)}, bf16[4,8,144,128]{3,2,1,0:T(8,128)(2,1)S(1)}, u32[]{:S(2)}, u32[]{:S(2)}) collective-permute-start(bf16[4,8,144,128]{3,2,1,0:T(8,128)(2,1)S(1)} %partial_grams.12), channel_id=1, source_target_pairs={{0,8},{8,0},{16,24},{24,16},{1,9},{9,1},{17,25},{25,17},{2,10},{10... | collective-permute-start | bytes 3538952 | tf_op jit(solution)/shard_map/ppermute | solution.py:361
  68.5 9.9 %collective-permute-start.9 = (bf16[1,4,144,128]{3,2,1,0:T(8,128)(2,1)S(1)}, bf16[1,4,144,128]{3,2,1,0:T(8,128)(2,1)S(1)}, u32[]{:S(2)}, u32[]{:S(2)}) collective-permute-start(bf16[1,4,144,128]{3,2,1,0:T(8,128)(2,1)S(1)} %get-tuple-element.117), channel_id=1, source_target_pairs={{0,16},{8,24},{16,0},{24,8},{1,17},{9,25},{17,1},{25,9},{2,18},{10... | collective-permute-start | bytes 442376 | tf_op jit(solution)/shard_map/ppermute | solution.py:361
  69.4 9.0 %collective-permute-start.10 = (bf16[1,4,144,128]{3,2,1,0:T(8,128)(2,1)S(1)}, bf16[1,4,144,128]{3,2,1,0:T(8,128)(2,1)S(1)}, u32[]{:S(2)}, u32[]{:S(2)}) collective-permute-start(bf16[1,4,144,128]{3,2,1,0:T(8,128)(2,1)S(1)} %get-tuple-element.118), channel_id=1, source_target_pairs={{0,1},{1,0},{2,3},{3,2},{4,5},{5,4},{6,7},{7,6},{8,9},{9,8},{10,11... | collective-permute-start | bytes 442376 | tf_op jit(solution)/shard_map/ppermute | solution.py:361
  78.6 18.4 %collective-permute-start.12 = (bf16[1,8,144,128]{3,2,1,0:T(8,128)(2,1)S(1)}, bf16[1,8,144,128]{3,2,1,0:T(8,128)(2,1)S(1)}, u32[]{:S(2)}, u32[]{:S(2)}) collective-permute-start(bf16[1,8,144,128]{3,2,1,0:T(8,128)(2,1)S(1)} %add_partials.17), channel_id=1, source_target_pairs={{0,4},{1,5},{2,6},{3,7},{4,0},{5,1},{6,2},{7,3},{8,12},{9,13},{10,... | collective-permute-start | bytes 884744 | tf_op jit(solution)/shard_map/ppermute | solution.py:361
  84.1 12.9 %collective-permute-start.13 = (bf16[2,4,144,128]{3,2,1,0:T(8,128)(2,1)S(1)}, bf16[2,4,144,128]{3,2,1,0:T(8,128)(2,1)S(1)}, u32[]{:S(2)}, u32[]{:S(2)}) collective-permute-start(bf16[2,4,144,128]{3,2,1,0:T(8,128)(2,1)S(1)} %get-tuple-element.124), channel_id=1, source_target_pairs={{0,1},{1,0},{2,3},{3,2},{4,5},{5,4},{6,7},{7,6},{8,9},{9,8},{10,11... | collective-permute-start | bytes 884744 | tf_op jit(solution)/shard_map/ppermute | solution.py:361
  84.2 12.8 %collective-permute-start.14 = (bf16[2,4,144,128]{3,2,1,0:T(8,128)(2,1)S(1)}, bf16[2,4,144,128]{3,2,1,0:T(8,128)(2,1)S(1)}, u32[]{:S(2)}, u32[]{:S(2)}) collective-permute-start(bf16[2,4,144,128]{3,2,1,0:T(8,128)(2,1)S(1)} %get-tuple-element.125), channel_id=1, source_target_pairs={{0,16},{8,24},{16,0},{24,8},{1,17},{9,25},{17,1},{25,9},{2,18},{10... | collective-permute-start | bytes 884744 | tf_op jit(solution)/shard_map/ppermute | solution.py:361
  93.1 12.3 %collective-permute-start.17 = (bf16[4,8,144,128]{3,2,1,0:T(8,128)(2,1)S(1)}, bf16[4,8,144,128]{3,2,1,0:T(8,128)(2,1)S(1)}, u32[]{:S(2)}, u32[]{:S(2)}) collective-permute-start(bf16[4,8,144,128]{3,2,1,0:T(8,128)(2,1)S(1)} %partial_grams.14), channel_id=1, source_target_pairs={{0,8},{8,0},{16,24},{24,16},{1,9},{9,1},{17,25},{25,17},{2,10},{10... | collective-permute-start | bytes 3538952 | tf_op jit(solution)/shard_map/ppermute | solution.py:361
  97.2 8.2 %collective-permute-start.15 = (bf16[1,4,144,128]{3,2,1,0:T(8,128)(2,1)S(1)}, bf16[1,4,144,128]{3,2,1,0:T(8,128)(2,1)S(1)}, u32[]{:S(2)}, u32[]{:S(2)}) collective-permute-start(bf16[1,4,144,128]{3,2,1,0:T(8,128)(2,1)S(1)} %get-tuple-element.134), channel_id=1, source_target_pairs={{0,16},{8,24},{16,0},{24,8},{1,17},{9,25},{17,1},{25,9},{2,18},{10... | collective-permute-start | bytes 442376 | tf_op jit(solution)/shard_map/ppermute | solution.py:361
  97.3 8.1 %collective-permute-start.16 = (bf16[1,4,144,128]{3,2,1,0:T(8,128)(2,1)S(1)}, bf16[1,4,144,128]{3,2,1,0:T(8,128)(2,1)S(1)}, u32[]{:S(2)}, u32[]{:S(2)}) collective-permute-start(bf16[1,4,144,128]{3,2,1,0:T(8,128)(2,1)S(1)} %get-tuple-element.135), channel_id=1, source_target_pairs={{0,1},{1,0},{2,3},{3,2},{4,5},{5,4},{6,7},{7,6},{8,9},{9,8},{10,11... | collective-permute-start | bytes 442376 | tf_op jit(solution)/shard_map/ppermute | solution.py:361
  105.7 8.0 %collective-permute-start.19 = (bf16[2,4,144,128]{3,2,1,0:T(8,128)(2,1)S(1)}, bf16[2,4,144,128]{3,2,1,0:T(8,128)(2,1)S(1)}, u32[]{:S(2)}, u32[]{:S(2)}) collective-permute-start(bf16[2,4,144,128]{3,2,1,0:T(8,128)(2,1)S(1)} %get-tuple-element.143), channel_id=1, source_target_pairs={{0,1},{1,0},{2,3},{3,2},{4,5},{5,4},{6,7},{7,6},{8,9},{9,8},{10,11... | collective-permute-start | bytes 884744 | tf_op jit(solution)/shard_map/ppermute | solution.py:361
  106.8 8.3 %collective-permute-start.20 = (bf16[2,4,144,128]{3,2,1,0:T(8,128)(2,1)S(1)}, bf16[2,4,144,128]{3,2,1,0:T(8,128)(2,1)S(1)}, u32[]{:S(2)}, u32[]{:S(2)}) collective-permute-start(bf16[2,4,144,128]{3,2,1,0:T(8,128)(2,1)S(1)} %get-tuple-element.144), channel_id=1, source_target_pairs={{0,16},{8,24},{16,0},{24,8},{1,17},{9,25},{17,1},{25,9},{2,18},{10... | collective-permute-start | bytes 884744 | tf_op jit(solution)/shard_map/ppermute | solution.py:361
  109.1 13.2 %collective-permute-start.18 = (bf16[1,8,144,128]{3,2,1,0:T(8,128)(2,1)S(1)}, bf16[1,8,144,128]{3,2,1,0:T(8,128)(2,1)S(1)}, u32[]{:S(2)}, u32[]{:S(2)}) collective-permute-start(bf16[1,8,144,128]{3,2,1,0:T(8,128)(2,1)S(1)} %add_partials.20), channel_id=1, source_target_pairs={{0,2},{1,3},{2,0},{3,1},{4,6},{5,7},{6,4},{7,5},{8,10},{9,11},{10,... | collective-permute-start | bytes 884744 | tf_op jit(solution)/shard_map/ppermute | solution.py:361
  115.2 5.2 %collective-permute-start.21 = (bf16[1,4,144,128]{3,2,1,0:T(8,128)(2,1)S(1)}, bf16[1,4,144,128]{3,2,1,0:T(8,128)(2,1)S(1)}, u32[]{:S(2)}, u32[]{:S(2)}) collective-permute-start(bf16[1,4,144,128]{3,2,1,0:T(8,128)(2,1)S(1)} %get-tuple-element.147), channel_id=1, source_target_pairs={{0,16},{8,24},{16,0},{24,8},{1,17},{9,25},{17,1},{25,9},{2,18},{10... | collective-permute-start | bytes 442376 | tf_op jit(solution)/shard_map/ppermute | solution.py:361
  117.0 5.1 %collective-permute-start.22 = (bf16[1,4,144,128]{3,2,1,0:T(8,128)(2,1)S(1)}, bf16[1,4,144,128]{3,2,1,0:T(8,128)(2,1)S(1)}, u32[]{:S(2)}, u32[]{:S(2)}) collective-permute-start(bf16[1,4,144,128]{3,2,1,0:T(8,128)(2,1)S(1)} %get-tuple-element.148), channel_id=1, source_target_pairs={{0,1},{1,0},{2,3},{3,2},{4,5},{5,4},{6,7},{7,6},{8,9},{9,8},{10,11... | collective-permute-start | bytes 442376 | tf_op jit(solution)/shard_map/ppermute | solution.py:361
  (3 other events, 78.8 us)

commit v4 on v3

--- a/solution.py
+++ b/solution.py
@@ -10,7 +10,6 @@
 PSIDE = 16
 NS_ITERS = 5
 LOC_SCALE = 48.0
-GROUP = 4
 EXT = 16
 F32 = jnp.float32
 BF16 = jnp.bfloat16
@@ -141,31 +140,26 @@
     acc_ref[...] = jnp.zeros_like(acc_ref)
     number = requests_ref[target, per_owner]
 
-    def group(start, _):
-        products = []
-        for i in range(GROUP):
-            entry = start * GROUP + i
-            code = requests_ref[target, jnp.minimum(entry, per_owner - 1)]
-            patch = code // held
-            block = code % held
-            centre_lon = (lon_first + patch // lat_patches) * (2 * PSIDE) + (PSIDE - 1)
-            centre_lat = (lat_first + patch % lat_patches) * (2 * PSIDE) + (PSIDE - 1)
-            row = pl.ds(block, 1)
-            lon_gap = jnp.abs(2 * obs_lon_ref[row, :] - centre_lon)
-            lon_gap = jnp.minimum(lon_gap, 2 * grid_lon - lon_gap)
-            lat_gap = 2 * obs_lat_ref[row, :] - centre_lat
-            square = (lon_gap * lon_gap + lat_gap * lat_gap).astype(F32)
-            rinv = jnp.where(entry < number, rinv_ref[row, :], 0.0)
-            weight = rinv * jnp.exp(square * (-1.0 / (8.0 * LOC_SCALE * LOC_SCALE)))
-            left = left_ref[block]
-            scaled = (left[:members].astype(F32) * weight).astype(BF16)
-            product = lax.dot_general(left, scaled, NT, preferred_element_type=F32)
-            products.append((patch, product[: members + 8]))
-        for patch, product in products:
-            acc_ref[patch] += product
-        return 0
-
-    lax.fori_loop(0, (number + GROUP - 1) // GROUP, group, 0)
+    products = []
+    for entry in range(per_owner):
+        code = requests_ref[target, entry]
+        patch = code // held
+        block = code % held
+        centre_lon = (lon_first + patch // lat_patches) * (2 * PSIDE) + (PSIDE - 1)
+        centre_lat = (lat_first + patch % lat_patches) * (2 * PSIDE) + (PSIDE - 1)
+        row = pl.ds(block, 1)
+        lon_gap = jnp.abs(2 * obs_lon_ref[row, :] - centre_lon)
+        lon_gap = jnp.minimum(lon_gap, 2 * grid_lon - lon_gap)
+        lat_gap = 2 * obs_lat_ref[row, :] - centre_lat
+        square = (lon_gap * lon_gap + lat_gap * lat_gap).astype(F32)
+        rinv = jnp.where(entry < number, rinv_ref[row, :], 0.0)
+        weight = rinv * jnp.exp(square * (-1.0 / (8.0 * LOC_SCALE * LOC_SCALE)))
+        left = left_ref[block]
+        scaled = (left[:members].astype(F32) * weight).astype(BF16)
+        product = lax.dot_general(left, scaled, NT, preferred_element_type=F32)
+        products.append((patch, product[: members + 8]))
+    for patch, product in products:
+        acc_ref[patch] += product
 
     row = lax.broadcasted_iota(jnp.int32, (members, members), 0)
     column = lax.broadcasted_iota(jnp.int32, (members, members), 1)
@@ -187,6 +181,23 @@
         out_ref[0, pair, members:, :] = jnp.concatenate([high, rows - high], axis=0).astype(BF16)
 
 
+def hold_kernel(table_hbm, held_ref, sem):
+    copy = pltpu.make_async_copy(table_hbm, held_ref, sem)
+    copy.start()
+    copy.wait()
+
+
+def hold(table):
+    return pl.pallas_call(
+        hold_kernel,
+        out_shape=pltpu.SMEM(table.shape, table.dtype),
+        in_specs=[pl.BlockSpec(memory_space=pl.ANY)],
+        out_specs=pl.BlockSpec(memory_space=pltpu.SMEM),
+        scratch_shapes=[pltpu.SemaphoreType.DMA(())],
+        name="hold",
+    )(table)
+
+
 def partial_grams(sizes, far, core, count, requests, staged):
     patches, per_owner = sizes[0], sizes[5]
     members = staged[0].shape[2]
@@ -196,13 +207,13 @@
         functools.partial(gram_kernel, sizes, far, core),
         out_shape=jax.ShapeDtypeStruct((count, *block[1:]), BF16),
         grid_spec=pltpu.PrefetchScalarGridSpec(
-            num_scalar_prefetch=1,
+            num_scalar_prefetch=0,
             grid=(count,),
-            in_specs=[pl.BlockSpec(memory_space=pltpu.VMEM)] * 5,
+            in_specs=[pl.BlockSpec(memory_space=pltpu.SMEM)] + [pl.BlockSpec(memory_space=pltpu.VMEM)] * 5,
             out_specs=pl.BlockSpec(block, lambda i, *_: (i, 0, 0, 0)),
             scratch_shapes=[pltpu.VMEM((patches, members + 8, members), F32)],
         ),
-        compiler_params=pltpu.CompilerParams(vmem_limit_bytes=6 * 2**20),
+        compiler_params=pltpu.CompilerParams(vmem_limit_bytes=8 * 2**20),
         cost_estimate=pl.CostEstimate(
             flops=count * per_owner * 100 * members**3, bytes_accessed=0, transcendentals=0
         ),
@@ -381,6 +392,7 @@
     requests, observed = lax.optimization_barrier(
         (requests, (obs_anom, innov, obs_rinv, obs_lon, obs_lat))
     )
+    requests = hold(requests)
     staged = stage(*observed)
     sizes = (
         patches,
@@ -396,8 +408,8 @@
     cut = pairs // 2
 
     def grams(far, core, after):
-        tied, _ = lax.optimization_barrier((requests, after))
-        return partial_grams(sizes, far, core, lon_devices, tied, staged)
+        rows, _ = lax.optimization_barrier((staged[-1], after))
+        return partial_grams(sizes, far, core, lon_devices, requests, [*staged[:-1], rows])
 
     def steps(far):
         send = yield far, 1

time: 140 us -> 119 us (0.85)
  Pallas kernels: 83 us -> 52.2 us
  waiting for transfers between devices: 21.8 us -> 30.8 us
    pallas_call x8, Pallas kernels: 60 us -> 28.3 us  [partial_grams(): pl.pallas_call(functools.partial(gram_kernel, sizes, far, core), out_shap...]
    ppermute x23, waiting for transfers between devices: 14.8 us -> 23.8 us  [swap(): return lax.ppermute(value, axis, [(i, i ^ flip) for i in range(size)])]
  transfers between devices with their start and end apart: 24 -> 24, of which waited for: 8 -> 13; matrix products, arithmetic and copies ran while one was open for 0% -> 0% of each run, Pallas kernels for 39% -> 22%
where the time goes in v4:
time: 119 us
  Pallas kernels  52.2 us (44%)
  waiting for transfers between devices  30.8 us (26%)
  starting transfers between devices  30.6 us (26%)
  other arithmetic  3.23 us (3%)
  local copies, waits for them, and re-layouts  1.99 us (2%)
    pallas_call x8, Pallas kernels, partial_grams(): pl.pallas_call(functools.partial(gram_kernel, sizes, far, core), out_shap...  28.3 us
    ppermute x23, waiting for transfers between devices, swap(): return lax.ppermute(value, axis, [(i, i ^ flip) for i in range(size)])  23.8 us
    ppermute x23, starting transfers between devices, swap(): return lax.ppermute(value, axis, [(i, i ^ flip) for i in range(size)])  23.3 us
    pallas_call x1, Pallas kernels, analysis(): pl.pallas_call(analysis_kernel, out_shape=jax.ShapeDtypeStruct(pert.shape...  9.35 us
    pallas_call x1, Pallas kernels, solve(): pl.pallas_call(functools.partial(solve_kernel, len(parts), total_obs), ou...  8.32 us
    all_to_all x1, starting transfers between devices, on_device(): lax.all_to_all(table, ('lon', 'lat'), split_axis=0, concat_axis=0, tiled=...  7.3 us
    all_to_all x1, waiting for transfers between devices, on_device(): lax.all_to_all(table, ('lon', 'lat'), split_axis=0, concat_axis=0, tiled=...  7.03 us
    pallas_call x1, Pallas kernels, stage(): pl.pallas_call(functools.partial(stage_kernel, chunk), out_shape=[pltpu.V...  3.22 us
  transfers between devices with their start and end apart: 24, of which 13 were waited for; matrix products, arithmetic and copies ran while one was open for 0% of the time, Pallas kernels for 22%

profile of v4, /device:TPU:0, one launch (start us, length us, event | category | flops | bytes accessed | tf_op | source)
XLA Modules:
  0.0 119.1 jit_solution(7650153283704816028)
XLA Ops:
  4.6 7.3 %all-to-all-start = ((s32[32,1,25]{2,1,0:T(1,128)}), s32[32,1,25]{2,1,0:T(1,128)S(1)}, u32[]{:S(2)}, u32[]{:S(2)}) async-start(s32[32,1,25]{2,1,0:T(1,128)} %bitcast.2), calls=%async_computation | async-start | bytes 32768 | tf_op jit(solution)/shard_map/all_to_all | solution.py:388
  11.9 7.0 %all-to-all-done = s32[32,1,25]{2,1,0:T(1,128)S(1)} async-done(((s32[32,1,25]{2,1,0:T(1,128)}), s32[32,1,25]{2,1,0:T(1,128)S(1)}, u32[]{:S(2)}, u32[]{:S(2)}) %all-to-all-start) | async-done | bytes 3232 | tf_op jit(solution)/shard_map/all_to_all | solution.py:388
  20.5 3.2 %stage.1 = (bf16[192,144,128]{2,1,0:T(8,128)(2,1)S(1)}, f32[192,128]{1,0:T(8,128)S(1)}, s32[192,128]{1,0:T(8,128)S(1)}, s32[192,128]{1,0:T(8,128)S(1)}, f32[8,128]{1,0:T(8,128)S(1)}) custom-call(bf16[192,128,128]{2,1,0:T(8,128)(2,1)} %anom_hbm, f32[192,128]{1,0:T(8,128)} %innov_hbm, f32[192,128]{1,0:T(8,128)} %rinv_hbm, s32[192,128]{1,0:T(8,128)} %lon_hbm, ...), custom_call_target="tpu_custom_call" | custom-call | bytes 12582912 | tf_op jit(solution)/shard_map/stage/pallas_call | solution.py:98
  23.7 3.5 %partial_grams.8 = bf16[4,8,144,128]{3,2,1,0:T(8,128)(2,1)S(1)} custom-call(s32[32,26]{1,0:T(8,128)S(4)} %hold.1.requests_ref, bf16[192,144,128]{2,1,0:T(8,128)(2,1)S(1)} %get-tuple-element.83.left_ref, f32[192,128]{1,0:T(8,128)S(1)} %get-tuple-element.84.rinv_ref, s32[192,128]{1,0:T(8,128)S(1)} %get-tuple-element.85.obs_lon_ref, ...), custom_call_target="tpu_custom_call" | custom-call | flops 20132659200 | tf_op jit(solution)/shard_map/partial_grams/pallas_call | solution.py:206
  27.4 3.5 %partial_grams.9.refs_0_ = bf16[4,8,144,128]{3,2,1,0:T(8,128)(2,1)S(1)} custom-call(s32[32,26]{1,0:T(8,128)S(4)} %hold.1.requests_ref, bf16[192,144,128]{2,1,0:T(8,128)(2,1)S(1)} %get-tuple-element.83.left_ref, f32[192,128]{1,0:T(8,128)S(1)} %get-tuple-element.84.rinv_ref, s32[192,128]{1,0:T(8,128)S(1)} %get-tuple-element.85.obs_lon_ref, ...), custom_call_target="tpu_custom_call" | custom-call | flops 20132659200 | tf_op jit(solution)/shard_map/partial_grams/pallas_call | solution.py:206
  32.5 3.5 %partial_grams.10 = bf16[4,8,144,128]{3,2,1,0:T(8,128)(2,1)S(1)} custom-call(s32[32,26]{1,0:T(8,128)S(4)} %hold.1.requests_ref, bf16[192,144,128]{2,1,0:T(8,128)(2,1)S(1)} %get-tuple-element.83.left_ref, f32[192,128]{1,0:T(8,128)S(1)} %get-tuple-element.84.rinv_ref, s32[192,128]{1,0:T(8,128)S(1)} %get-tuple-element.85.obs_lon_ref, ...), custom_call_target="tpu_custom_call" | custom-call | flops 20132659200 | tf_op jit(solution)/shard_map/partial_grams/pallas_call | solution.py:206
  36.1 4.5 %collective-permute-done.1.refs_2_ = bf16[2,4,144,128]{3,2,1,0:T(8,128)(2,1)S(1)} collective-permute-done((bf16[2,4,144,128]{3,2,1,0:T(8,128)(2,1)S(1)}, bf16[2,4,144,128]{3,2,1,0:T(8,128)(2,1)S(1)}, u32[]{:S(2)}, u32[]{:S(2)}) %collective-permute-start.1) | collective-permute-done | bytes 294944 | tf_op jit(solution)/shard_map/ppermute | solution.py:372
  43.3 3.5 %partial_grams.11.refs_0_ = bf16[4,8,144,128]{3,2,1,0:T(8,128)(2,1)S(1)} custom-call(s32[32,26]{1,0:T(8,128)S(4)} %hold.1.requests_ref, bf16[192,144,128]{2,1,0:T(8,128)(2,1)S(1)} %get-tuple-element.83.left_ref, f32[192,128]{1,0:T(8,128)S(1)} %get-tuple-element.84.rinv_ref, s32[192,128]{1,0:T(8,128)S(1)} %get-tuple-element.85.obs_lon_ref, ...), custom_call_target="tpu_custom_call" | custom-call | flops 20132659200 | tf_op jit(solution)/shard_map/partial_grams/pallas_call | solution.py:206
  47.9 1.5 %collective-permute-start.7 = (bf16[2,4,144,128]{3,2,1,0:T(8,128)(2,1)S(1)}, bf16[2,4,144,128]{3,2,1,0:T(8,128)(2,1)S(1)}, u32[]{:S(2)}, u32[]{:S(2)}) collective-permute-start(bf16[2,4,144,128]{3,2,1,0:T(8,128)(2,1)S(1)} %get-tuple-element.107), channel_id=1, source_target_pairs={{0,1},{1,0},{2,3},{3,2},{4,5},{5,4},{6,7},{7,6},{8,9},{9,8},{10,11... | collective-permute-start | bytes 884744 | tf_op jit(solution)/shard_map/ppermute | solution.py:372
  50.9 3.5 %partial_grams.12 = bf16[4,8,144,128]{3,2,1,0:T(8,128)(2,1)S(1)} custom-call(s32[32,26]{1,0:T(8,128)S(4)} %hold.1.requests_ref, bf16[192,144,128]{2,1,0:T(8,128)(2,1)S(1)} %get-tuple-element.83.left_ref, f32[192,128]{1,0:T(8,128)S(1)} %get-tuple-element.84.rinv_ref, s32[192,128]{1,0:T(8,128)S(1)} %get-tuple-element.85.obs_lon_ref, ...), custom_call_target="tpu_custom_call" | custom-call | flops 20132659200 | tf_op jit(solution)/shard_map/partial_grams/pallas_call | solution.py:206
  54.5 2.1 %collective-permute-done.6 = bf16[1,8,144,128]{3,2,1,0:T(8,128)(2,1)S(1)} collective-permute-done((bf16[1,8,144,128]{3,2,1,0:T(8,128)(2,1)S(1)}, bf16[1,8,144,128]{3,2,1,0:T(8,128)(2,1)S(1)}, u32[]{:S(2)}, u32[]{:S(2)}) %collective-permute-start.6) | collective-permute-done | bytes 294944 | tf_op jit(solution)/shard_map/ppermute | solution.py:372
  59.2 3.5 %partial_grams.13.refs_0_ = bf16[4,8,144,128]{3,2,1,0:T(8,128)(2,1)S(1)} custom-call(s32[32,26]{1,0:T(8,128)S(4)} %hold.1.requests_ref, bf16[192,144,128]{2,1,0:T(8,128)(2,1)S(1)} %get-tuple-element.83.left_ref, f32[192,128]{1,0:T(8,128)S(1)} %get-tuple-element.84.rinv_ref, s32[192,128]{1,0:T(8,128)S(1)} %get-tuple-element.85.obs_lon_ref, ...), custom_call_target="tpu_custom_call" | custom-call | flops 20132659200 | tf_op jit(solution)/shard_map/partial_grams/pallas_call | solution.py:206
  63.5 5.1 %collective-permute-start.12 = (bf16[1,8,144,128]{3,2,1,0:T(8,128)(2,1)S(1)}, bf16[1,8,144,128]{3,2,1,0:T(8,128)(2,1)S(1)}, u32[]{:S(2)}, u32[]{:S(2)}) collective-permute-start(bf16[1,8,144,128]{3,2,1,0:T(8,128)(2,1)S(1)} %add_partials.17), channel_id=1, source_target_pairs={{0,4},{1,5},{2,6},{3,7},{4,0},{5,1},{6,2},{7,3},{8,12},{9,13},{10,... | collective-permute-start | bytes 884744 | tf_op jit(solution)/shard_map/ppermute | solution.py:372
  70.5 3.5 %partial_grams.14 = bf16[4,8,144,128]{3,2,1,0:T(8,128)(2,1)S(1)} custom-call(s32[32,26]{1,0:T(8,128)S(4)} %hold.1.requests_ref, bf16[192,144,128]{2,1,0:T(8,128)(2,1)S(1)} %get-tuple-element.83.left_ref, f32[192,128]{1,0:T(8,128)S(1)} %get-tuple-element.84.rinv_ref, s32[192,128]{1,0:T(8,128)S(1)} %get-tuple-element.85.obs_lon_ref, ...), custom_call_target="tpu_custom_call" | custom-call | flops 20132659200 | tf_op jit(solution)/shard_map/partial_grams/pallas_call | solution.py:206
  74.1 6.0 %collective-permute-done.12 = bf16[1,8,144,128]{3,2,1,0:T(8,128)(2,1)S(1)} collective-permute-done((bf16[1,8,144,128]{3,2,1,0:T(8,128)(2,1)S(1)}, bf16[1,8,144,128]{3,2,1,0:T(8,128)(2,1)S(1)}, u32[]{:S(2)}, u32[]{:S(2)}) %collective-permute-start.12) | collective-permute-done | bytes 294944 | tf_op jit(solution)/shard_map/ppermute | solution.py:372
  81.7 3.5 %partial_grams.15.refs_0_ = bf16[4,8,144,128]{3,2,1,0:T(8,128)(2,1)S(1)} custom-call(s32[32,26]{1,0:T(8,128)S(4)} %hold.1.requests_ref, bf16[192,144,128]{2,1,0:T(8,128)(2,1)S(1)} %get-tuple-element.83.left_ref, f32[192,128]{1,0:T(8,128)S(1)} %get-tuple-element.84.rinv_ref, s32[192,128]{1,0:T(8,128)S(1)} %get-tuple-element.85.obs_lon_ref, ...), custom_call_target="tpu_custom_call" | custom-call | flops 20132659200 | tf_op jit(solution)/shard_map/partial_grams/pallas_call | solution.py:206
  87.2 1.6 %collective-permute-start.20 = (bf16[2,4,144,128]{3,2,1,0:T(8,128)(2,1)S(1)}, bf16[2,4,144,128]{3,2,1,0:T(8,128)(2,1)S(1)}, u32[]{:S(2)}, u32[]{:S(2)}) collective-permute-start(bf16[2,4,144,128]{3,2,1,0:T(8,128)(2,1)S(1)} %get-tuple-element.144), channel_id=1, source_target_pairs={{0,16},{8,24},{16,0},{24,8},{1,17},{9,25},{17,1},{25,9},{2,18},{10... | collective-permute-start | bytes 884744 | tf_op jit(solution)/shard_map/ppermute | solution.py:372
  89.0 4.0 %collective-permute-done.19.refs_2_ = bf16[2,4,144,128]{3,2,1,0:T(8,128)(2,1)S(1)} collective-permute-done((bf16[2,4,144,128]{3,2,1,0:T(8,128)(2,1)S(1)}, bf16[2,4,144,128]{3,2,1,0:T(8,128)(2,1)S(1)}, u32[]{:S(2)}, u32[]{:S(2)}) %collective-permute-start.19) | collective-permute-done | bytes 294944 | tf_op jit(solution)/shard_map/ppermute | solution.py:372
  92.9 1.5 %collective-permute-done.20.refs_3_ = bf16[2,4,144,128]{3,2,1,0:T(8,128)(2,1)S(1)} collective-permute-done((bf16[2,4,144,128]{3,2,1,0:T(8,128)(2,1)S(1)}, bf16[2,4,144,128]{3,2,1,0:T(8,128)(2,1)S(1)}, u32[]{:S(2)}, u32[]{:S(2)}) %collective-permute-start.20) | collective-permute-done | bytes 294944 | tf_op jit(solution)/shard_map/ppermute | solution.py:372
  94.6 1.6 %collective-permute-start.21 = (bf16[1,4,144,128]{3,2,1,0:T(8,128)(2,1)S(1)}, bf16[1,4,144,128]{3,2,1,0:T(8,128)(2,1)S(1)}, u32[]{:S(2)}, u32[]{:S(2)}) collective-permute-start(bf16[1,4,144,128]{3,2,1,0:T(8,128)(2,1)S(1)} %get-tuple-element.147), channel_id=1, source_target_pairs={{0,16},{8,24},{16,0},{24,8},{1,17},{9,25},{17,1},{25,9},{2,18},{10... | collective-permute-start | bytes 442376 | tf_op jit(solution)/shard_map/ppermute | solution.py:372
  97.3 2.5 %collective-permute-done.21.refs_2_ = bf16[1,4,144,128]{3,2,1,0:T(8,128)(2,1)S(1)} collective-permute-done((bf16[1,4,144,128]{3,2,1,0:T(8,128)(2,1)S(1)}, bf16[1,4,144,128]{3,2,1,0:T(8,128)(2,1)S(1)}, u32[]{:S(2)}, u32[]{:S(2)}) %collective-permute-start.21) | collective-permute-done | bytes 147488 | tf_op jit(solution)/shard_map/ppermute | solution.py:372
  99.8 1.5 %collective-permute-done.22.refs_3_ = bf16[1,4,144,128]{3,2,1,0:T(8,128)(2,1)S(1)} collective-permute-done((bf16[1,4,144,128]{3,2,1,0:T(8,128)(2,1)S(1)}, bf16[1,4,144,128]{3,2,1,0:T(8,128)(2,1)S(1)}, u32[]{:S(2)}, u32[]{:S(2)}) %collective-permute-start.22) | collective-permute-done | bytes 147488 | tf_op jit(solution)/shard_map/ppermute | solution.py:372
  101.4 8.3 %solve.1.weights_ref = bf16[16,128,128]{2,1,0:T(8,128)(2,1)S(1)} custom-call(bf16[8,144,128]{2,1,0:T(8,128)(2,1)S(1)} %bitcast.17, bf16[8,144,128]{2,1,0:T(8,128)(2,1)S(1)} %bitcast.18, bf16[8,144,128]{2,1,0:T(8,128)(2,1)S(1)} %bitcast.19, bf16[8,144,128]{2,1,0:T(8,128)(2,1)S(1)} %bitcast.15), custom_call_target="tpu_custom_call" | custom-call | tf_op jit(solution)/shard_map/solve/pallas_call | solution.py:337
  109.7 9.4 %analysis.1 = f32[16,6,128,256]{3,2,1,0:T(8,128)} custom-call(bf16[16,128,128]{2,1,0:T(8,128)(2,1)S(1)} %solve.1.weights_ref, bf16[16,6,128,256]{3,2,1,0:T(8,128)(2,1)S(1)} %bitcast.14, f32[16,6,256]{2,1,0:T(8,128)S(1)} %bitcast.16), custom_call_target="tpu_custom_call" | custom-call | tf_op jit(solution)/shard_map/analysis/pallas_call | solution.py:355
  (74 shorter events, 23.4 us)
Async XLA Ops:
  4.6 14.3 %all-to-all-start = ((s32[32,1,25]{2,1,0:T(1,128)}), s32[32,1,25]{2,1,0:T(1,128)S(1)}, u32[]{:S(2)}, u32[]{:S(2)}) async-start(s32[32,1,25]{2,1,0:T(1,128)} %bitcast.2), calls=%async_computation | async-start | bytes 32768 | tf_op jit(solution)/shard_map/all_to_all | solution.py:388
  27.3 3.6 %collective-permute-start = (bf16[4,8,144,128]{3,2,1,0:T(8,128)(2,1)S(1)}, bf16[4,8,144,128]{3,2,1,0:T(8,128)(2,1)S(1)}, u32[]{:S(2)}, u32[]{:S(2)}) collective-permute-start(bf16[4,8,144,128]{3,2,1,0:T(8,128)(2,1)S(1)} %partial_grams.8), channel_id=1, source_target_pairs={{0,8},{8,0},{16,24},{24,16},{1,9},{9,1},{17,25},{25,17},{2,10},{10... | collective-permute-start | bytes 3538952 | tf_op jit(solution)/shard_map/ppermute | solution.py:372
  31.2 9.4 %collective-permute-start.1 = (bf16[2,4,144,128]{3,2,1,0:T(8,128)(2,1)S(1)}, bf16[2,4,144,128]{3,2,1,0:T(8,128)(2,1)S(1)}, u32[]{:S(2)}, u32[]{:S(2)}) collective-permute-start(bf16[2,4,144,128]{3,2,1,0:T(8,128)(2,1)S(1)} %get-tuple-element.93), channel_id=1, source_target_pairs={{0,1},{1,0},{2,3},{3,2},{4,5},{5,4},{6,7},{7,6},{8,9},{9,8},{10,11... | collective-permute-start | bytes 884744 | tf_op jit(solution)/shard_map/ppermute | solution.py:372
  31.9 9.1 %collective-permute-start.2 = (bf16[2,4,144,128]{3,2,1,0:T(8,128)(2,1)S(1)}, bf16[2,4,144,128]{3,2,1,0:T(8,128)(2,1)S(1)}, u32[]{:S(2)}, u32[]{:S(2)}) collective-permute-start(bf16[2,4,144,128]{3,2,1,0:T(8,128)(2,1)S(1)} %get-tuple-element.94), channel_id=1, source_target_pairs={{0,16},{8,24},{16,0},{24,8},{1,17},{9,25},{17,1},{25,9},{2,18},{10... | collective-permute-start | bytes 884744 | tf_op jit(solution)/shard_map/ppermute | solution.py:372
  36.1 10.9 %collective-permute-start.5 = (bf16[4,8,144,128]{3,2,1,0:T(8,128)(2,1)S(1)}, bf16[4,8,144,128]{3,2,1,0:T(8,128)(2,1)S(1)}, u32[]{:S(2)}, u32[]{:S(2)}) collective-permute-start(bf16[4,8,144,128]{3,2,1,0:T(8,128)(2,1)S(1)} %partial_grams.10), channel_id=1, source_target_pairs={{0,8},{8,0},{16,24},{24,16},{1,9},{9,1},{17,25},{25,17},{2,10},{10... | collective-permute-start | bytes 3538952 | tf_op jit(solution)/shard_map/ppermute | solution.py:372
  41.2 5.6 %collective-permute-start.3 = (bf16[1,4,144,128]{3,2,1,0:T(8,128)(2,1)S(1)}, bf16[1,4,144,128]{3,2,1,0:T(8,128)(2,1)S(1)}, u32[]{:S(2)}, u32[]{:S(2)}) collective-permute-start(bf16[1,4,144,128]{3,2,1,0:T(8,128)(2,1)S(1)} %get-tuple-element.100), channel_id=1, source_target_pairs={{0,16},{8,24},{16,0},{24,8},{1,17},{9,25},{17,1},{25,9},{2,18},{10... | collective-permute-start | bytes 442376 | tf_op jit(solution)/shard_map/ppermute | solution.py:372
  41.8 5.1 %collective-permute-start.4 = (bf16[1,4,144,128]{3,2,1,0:T(8,128)(2,1)S(1)}, bf16[1,4,144,128]{3,2,1,0:T(8,128)(2,1)S(1)}, u32[]{:S(2)}, u32[]{:S(2)}) collective-permute-start(bf16[1,4,144,128]{3,2,1,0:T(8,128)(2,1)S(1)} %get-tuple-element.101), channel_id=1, source_target_pairs={{0,1},{1,0},{2,3},{3,2},{4,5},{5,4},{6,7},{7,6},{8,9},{9,8},{10,11... | collective-permute-start | bytes 442376 | tf_op jit(solution)/shard_map/ppermute | solution.py:372
  47.1 9.5 %collective-permute-start.6 = (bf16[1,8,144,128]{3,2,1,0:T(8,128)(2,1)S(1)}, bf16[1,8,144,128]{3,2,1,0:T(8,128)(2,1)S(1)}, u32[]{:S(2)}, u32[]{:S(2)}) collective-permute-start(bf16[1,8,144,128]{3,2,1,0:T(8,128)(2,1)S(1)} %add_partials.14), channel_id=1, source_target_pairs={{0,6},{1,7},{2,4},{3,5},{4,2},{5,3},{6,0},{7,1},{8,14},{9,15},{10,... | collective-permute-start | bytes 884744 | tf_op jit(solution)/shard_map/ppermute | solution.py:372
  47.9 8.7 %collective-permute-start.7 = (bf16[2,4,144,128]{3,2,1,0:T(8,128)(2,1)S(1)}, bf16[2,4,144,128]{3,2,1,0:T(8,128)(2,1)S(1)}, u32[]{:S(2)}, u32[]{:S(2)}) collective-permute-start(bf16[2,4,144,128]{3,2,1,0:T(8,128)(2,1)S(1)} %get-tuple-element.107), channel_id=1, source_target_pairs={{0,1},{1,0},{2,3},{3,2},{4,5},{5,4},{6,7},{7,6},{8,9},{9,8},{10,11... | collective-permute-start | bytes 884744 | tf_op jit(solution)/shard_map/ppermute | solution.py:372
  49.5 7.1 %collective-permute-start.8 = (bf16[2,4,144,128]{3,2,1,0:T(8,128)(2,1)S(1)}, bf16[2,4,144,128]{3,2,1,0:T(8,128)(2,1)S(1)}, u32[]{:S(2)}, u32[]{:S(2)}) collective-permute-start(bf16[2,4,144,128]{3,2,1,0:T(8,128)(2,1)S(1)} %get-tuple-element.108), channel_id=1, source_target_pairs={{0,16},{8,24},{16,0},{24,8},{1,17},{9,25},{17,1},{25,9},{2,18},{10... | collective-permute-start | bytes 884744 | tf_op jit(solution)/shard_map/ppermute | solution.py:372
  54.4 8.9 %collective-permute-start.11 = (bf16[4,8,144,128]{3,2,1,0:T(8,128)(2,1)S(1)}, bf16[4,8,144,128]{3,2,1,0:T(8,128)(2,1)S(1)}, u32[]{:S(2)}, u32[]{:S(2)}) collective-permute-start(bf16[4,8,144,128]{3,2,1,0:T(8,128)(2,1)S(1)} %partial_grams.12), channel_id=1, source_target_pairs={{0,8},{8,0},{16,24},{24,16},{1,9},{9,1},{17,25},{25,17},{2,10},{10... | collective-permute-start | bytes 3538952 | tf_op jit(solution)/shard_map/ppermute | solution.py:372
  56.8 6.0 %collective-permute-start.9 = (bf16[1,4,144,128]{3,2,1,0:T(8,128)(2,1)S(1)}, bf16[1,4,144,128]{3,2,1,0:T(8,128)(2,1)S(1)}, u32[]{:S(2)}, u32[]{:S(2)}) collective-permute-start(bf16[1,4,144,128]{3,2,1,0:T(8,128)(2,1)S(1)} %get-tuple-element.117), channel_id=1, source_target_pairs={{0,16},{8,24},{16,0},{24,8},{1,17},{9,25},{17,1},{25,9},{2,18},{10... | collective-permute-start | bytes 442376 | tf_op jit(solution)/shard_map/ppermute | solution.py:372
  58.2 5.1 %collective-permute-start.10 = (bf16[1,4,144,128]{3,2,1,0:T(8,128)(2,1)S(1)}, bf16[1,4,144,128]{3,2,1,0:T(8,128)(2,1)S(1)}, u32[]{:S(2)}, u32[]{:S(2)}) collective-permute-start(bf16[1,4,144,128]{3,2,1,0:T(8,128)(2,1)S(1)} %get-tuple-element.118), channel_id=1, source_target_pairs={{0,1},{1,0},{2,3},{3,2},{4,5},{5,4},{6,7},{7,6},{8,9},{9,8},{10,11... | collective-permute-start | bytes 442376 | tf_op jit(solution)/shard_map/ppermute | solution.py:372
  63.5 16.6 %collective-permute-start.12 = (bf16[1,8,144,128]{3,2,1,0:T(8,128)(2,1)S(1)}, bf16[1,8,144,128]{3,2,1,0:T(8,128)(2,1)S(1)}, u32[]{:S(2)}, u32[]{:S(2)}) collective-permute-start(bf16[1,8,144,128]{3,2,1,0:T(8,128)(2,1)S(1)} %add_partials.17), channel_id=1, source_target_pairs={{0,4},{1,5},{2,6},{3,7},{4,0},{5,1},{6,2},{7,3},{8,12},{9,13},{10,... | collective-permute-start | bytes 884744 | tf_op jit(solution)/shard_map/ppermute | solution.py:372
  68.8 11.2 %collective-permute-start.13 = (bf16[2,4,144,128]{3,2,1,0:T(8,128)(2,1)S(1)}, bf16[2,4,144,128]{3,2,1,0:T(8,128)(2,1)S(1)}, u32[]{:S(2)}, u32[]{:S(2)}) collective-permute-start(bf16[2,4,144,128]{3,2,1,0:T(8,128)(2,1)S(1)} %get-tuple-element.124), channel_id=1, source_target_pairs={{0,1},{1,0},{2,3},{3,2},{4,5},{5,4},{6,7},{7,6},{8,9},{9,8},{10,11... | collective-permute-start | bytes 884744 | tf_op jit(solution)/shard_map/ppermute | solution.py:372
  69.9 10.1 %collective-permute-start.14 = (bf16[2,4,144,128]{3,2,1,0:T(8,128)(2,1)S(1)}, bf16[2,4,144,128]{3,2,1,0:T(8,128)(2,1)S(1)}, u32[]{:S(2)}, u32[]{:S(2)}) collective-permute-start(bf16[2,4,144,128]{3,2,1,0:T(8,128)(2,1)S(1)} %get-tuple-element.125), channel_id=1, source_target_pairs={{0,16},{8,24},{16,0},{24,8},{1,17},{9,25},{17,1},{25,9},{2,18},{10... | collective-permute-start | bytes 884744 | tf_op jit(solution)/shard_map/ppermute | solution.py:372
  74.0 11.8 %collective-permute-start.17 = (bf16[4,8,144,128]{3,2,1,0:T(8,128)(2,1)S(1)}, bf16[4,8,144,128]{3,2,1,0:T(8,128)(2,1)S(1)}, u32[]{:S(2)}, u32[]{:S(2)}) collective-permute-start(bf16[4,8,144,128]{3,2,1,0:T(8,128)(2,1)S(1)} %partial_grams.14), channel_id=1, source_target_pairs={{0,8},{8,0},{16,24},{24,16},{1,9},{9,1},{17,25},{25,17},{2,10},{10... | collective-permute-start | bytes 3538952 | tf_op jit(solution)/shard_map/ppermute | solution.py:372
  80.2 5.2 %collective-permute-start.15 = (bf16[1,4,144,128]{3,2,1,0:T(8,128)(2,1)S(1)}, bf16[1,4,144,128]{3,2,1,0:T(8,128)(2,1)S(1)}, u32[]{:S(2)}, u32[]{:S(2)}) collective-permute-start(bf16[1,4,144,128]{3,2,1,0:T(8,128)(2,1)S(1)} %get-tuple-element.134), channel_id=1, source_target_pairs={{0,16},{8,24},{16,0},{24,8},{1,17},{9,25},{17,1},{25,9},{2,18},{10... | collective-permute-start | bytes 442376 | tf_op jit(solution)/shard_map/ppermute | solution.py:372
  80.7 5.1 %collective-permute-start.16 = (bf16[1,4,144,128]{3,2,1,0:T(8,128)(2,1)S(1)}, bf16[1,4,144,128]{3,2,1,0:T(8,128)(2,1)S(1)}, u32[]{:S(2)}, u32[]{:S(2)}) collective-permute-start(bf16[1,4,144,128]{3,2,1,0:T(8,128)(2,1)S(1)} %get-tuple-element.135), channel_id=1, source_target_pairs={{0,1},{1,0},{2,3},{3,2},{4,5},{5,4},{6,7},{7,6},{8,9},{9,8},{10,11... | collective-permute-start | bytes 442376 | tf_op jit(solution)/shard_map/ppermute | solution.py:372
  86.1 6.8 %collective-permute-start.19 = (bf16[2,4,144,128]{3,2,1,0:T(8,128)(2,1)S(1)}, bf16[2,4,144,128]{3,2,1,0:T(8,128)(2,1)S(1)}, u32[]{:S(2)}, u32[]{:S(2)}) collective-permute-start(bf16[2,4,144,128]{3,2,1,0:T(8,128)(2,1)S(1)} %get-tuple-element.143), channel_id=1, source_target_pairs={{0,1},{1,0},{2,3},{3,2},{4,5},{5,4},{6,7},{7,6},{8,9},{9,8},{10,11... | collective-permute-start | bytes 884744 | tf_op jit(solution)/shard_map/ppermute | solution.py:372
  87.2 7.2 %collective-permute-start.20 = (bf16[2,4,144,128]{3,2,1,0:T(8,128)(2,1)S(1)}, bf16[2,4,144,128]{3,2,1,0:T(8,128)(2,1)S(1)}, u32[]{:S(2)}, u32[]{:S(2)}) collective-permute-start(bf16[2,4,144,128]{3,2,1,0:T(8,128)(2,1)S(1)} %get-tuple-element.144), channel_id=1, source_target_pairs={{0,16},{8,24},{16,0},{24,8},{1,17},{9,25},{17,1},{25,9},{2,18},{10... | collective-permute-start | bytes 884744 | tf_op jit(solution)/shard_map/ppermute | solution.py:372
  88.9 12.5 %collective-permute-start.18 = (bf16[1,8,144,128]{3,2,1,0:T(8,128)(2,1)S(1)}, bf16[1,8,144,128]{3,2,1,0:T(8,128)(2,1)S(1)}, u32[]{:S(2)}, u32[]{:S(2)}) collective-permute-start(bf16[1,8,144,128]{3,2,1,0:T(8,128)(2,1)S(1)} %add_partials.20), channel_id=1, source_target_pairs={{0,2},{1,3},{2,0},{3,1},{4,6},{5,7},{6,4},{7,5},{8,10},{9,11},{10,... | collective-permute-start | bytes 884744 | tf_op jit(solution)/shard_map/ppermute | solution.py:372
  94.6 5.2 %collective-permute-start.21 = (bf16[1,4,144,128]{3,2,1,0:T(8,128)(2,1)S(1)}, bf16[1,4,144,128]{3,2,1,0:T(8,128)(2,1)S(1)}, u32[]{:S(2)}, u32[]{:S(2)}) collective-permute-start(bf16[1,4,144,128]{3,2,1,0:T(8,128)(2,1)S(1)} %get-tuple-element.147), channel_id=1, source_target_pairs={{0,16},{8,24},{16,0},{24,8},{1,17},{9,25},{17,1},{25,9},{2,18},{10... | collective-permute-start | bytes 442376 | tf_op jit(solution)/shard_map/ppermute | solution.py:372
  96.1 5.1 %collective-permute-start.22 = (bf16[1,4,144,128]{3,2,1,0:T(8,128)(2,1)S(1)}, bf16[1,4,144,128]{3,2,1,0:T(8,128)(2,1)S(1)}, u32[]{:S(2)}, u32[]{:S(2)}) collective-permute-start(bf16[1,4,144,128]{3,2,1,0:T(8,128)(2,1)S(1)} %get-tuple-element.148), channel_id=1, source_target_pairs={{0,1},{1,0},{2,3},{3,2},{4,5},{5,4},{6,7},{7,6},{8,9},{9,8},{10,11... | collective-permute-start | bytes 442376 | tf_op jit(solution)/shard_map/ppermute | solution.py:372
  (3 other events, 70.0 us)

commit v5 on v4

--- a/solution.py
+++ b/solution.py
@@ -266,105 +266,100 @@
     )
 
 
-def solve_kernel(count, total_obs, *refs):
-    parts, (out_ref,) = refs[:count], refs[count:]
-    pairs, rows, members = parts[0].shape
+def solve_group(parts, total_obs, first, count):
+    members = parts[0].shape[-1]
     row = lax.broadcasted_iota(jnp.int32, (members, members), 0)
     column = lax.broadcasted_iota(jnp.int32, (members, members), 1)
     identity = (row == column).astype(F32)
-
-    def gathered(pair):
-        total = parts[0][pair].astype(F32)
+    systems, projected = [], []
+    for pair in range(count):
+        total = parts[0][0, first + pair].astype(F32)
         for part in parts[1:]:
-            total = total + part[pair].astype(F32)
-        return total[:members], total[members : members + 8] + total[members + 8 :]
-
-    def some(step, _):
-        systems, projected = [], []
-        for pair in (2 * step, 2 * step + 1):
-            packed, values = gathered(pair)
-            flipped = packed.T
-            innovation = jnp.sum(values[4:5], axis=1, keepdims=True)
-            spread = jnp.sum(values[5:6], axis=1, keepdims=True)
-            ridge = (members - 1) * (spread + total_obs) / innovation
-            for place, full in (
-                (0, jnp.where(row < column, packed, flipped)),
-                (2, jnp.where(row > column, packed, flipped)),
-            ):
-                full = jnp.where(row == column, values[place : place + 1], full)
-                systems.append(full + ridge * identity)
-                projected.append(values[place + 1 : place + 2])
-        scalings, roots, inverses = [], [], []
-        for system in systems:
-            squares = jnp.sum(system * system, axis=0, keepdims=True)
-            scaling = jnp.sqrt(jnp.sum(squares, axis=1, keepdims=True))
-            scalings.append(scaling)
-            roots.append(system / scaling)
-        factors = [1.5 * identity - 0.5 * root for root in roots]
-        roots = [product(halves(f), halves(r)) for f, r in zip(factors, roots)]
-        inverses = factors
-        for iteration in range(1, NS_ITERS):
-            split_roots = [halves(r) for r in roots]
-            split_inverses = [halves(z) for z in inverses]
-            factors = [
-                halves(1.5 * identity - 0.5 * product(z, r))
-                for z, r in zip(split_inverses, split_roots)
+            total = total + part[0, first + pair].astype(F32)
+        packed = total[:members]
+        values = total[members : members + 8] + total[members + 8 :]
+        flipped = packed.T
+        innovation = jnp.sum(values[4:5], axis=1, keepdims=True)
+        spread = jnp.sum(values[5:6], axis=1, keepdims=True)
+        ridge = (members - 1) * (spread + total_obs) / innovation
+        for place, full in (
+            (0, jnp.where(row < column, packed, flipped)),
+            (2, jnp.where(row > column, packed, flipped)),
+        ):
+            systems.append(jnp.where(row == column, values[place : place + 1] + ridge, full))
+            projected.append(values[place + 1 : place + 2])
+    scalings, roots = [], []
+    for system in systems:
+        squares = jnp.sum(system * system, axis=0, keepdims=True)
+        scaling = jnp.sqrt(jnp.sum(squares, axis=1, keepdims=True))
+        scalings.append(scaling)
+        roots.append(system * (1.0 / scaling))
+    factors = [1.5 * identity - 0.5 * root for root in roots]
+    roots = [product(halves(f), halves(r)) for f, r in zip(factors, roots)]
+    inverses = factors
+    for iteration in range(1, NS_ITERS):
+        split_roots = [halves(r) for r in roots]
+        split_inverses = [halves(z) for z in inverses]
+        factors = [
+            halves(1.5 * identity - 0.5 * product(z, r))
+            for z, r in zip(split_inverses, split_roots)
+        ]
+        if iteration < NS_ITERS - 1:
+            both = [
+                product(f, [jnp.concatenate([a, b], axis=1) for a, b in zip(r, z)])
+                for f, r, z in zip(factors, split_roots, split_inverses)
             ]
-            if iteration < NS_ITERS - 1:
-                both = [
-                    product(f, [jnp.concatenate([a, b], axis=1) for a, b in zip(r, z)])
-                    for f, r, z in zip(factors, split_roots, split_inverses)
-                ]
-                roots = [b[:, :members] for b in both]
-                inverses = [b[:, members:] for b in both]
-            else:
-                inverses = [product(f, z) for f, z in zip(factors, split_inverses)]
-        for i in range(4):
-            inverse_sqrt = inverses[i] * lax.rsqrt(scalings[i])
-            inner = jnp.sum(inverse_sqrt * projected[i], axis=1, keepdims=True)
-            mean = jnp.sum(inverse_sqrt * inner, axis=0, keepdims=True)
-            out_ref[4 * step + i] = (
-                jnp.sqrt(F32(members - 1)) * inverse_sqrt + mean
-            ).astype(BF16)
-        return 0
-
-    lax.fori_loop(0, pairs // 2, some, 0)
-
-
-def solve(parts, total_obs):
-    pairs, rows, members = parts[0].shape
+            roots = [b[:, :members] for b in both]
+            inverses = [b[:, members:] for b in both]
+        else:
+            inverses = [product(f, z) for f, z in zip(factors, split_inverses)]
+    weights = []
+    for scaling, inverse, values in zip(scalings, inverses, projected):
+        inverse_sqrt = inverse * lax.rsqrt(scaling)
+        inner = jnp.sum(inverse_sqrt * values, axis=1, keepdims=True)
+        mean = jnp.sum(inverse_sqrt * inner, axis=0, keepdims=True)
+        weights.append((jnp.sqrt(F32(members - 1)) * inverse_sqrt + mean).astype(BF16))
+    return weights
+
+
+def analysis_kernel(count, total_obs, group, *refs):
+    parts, (pert_ref, mean_ref, out_ref, weights_ref) = refs[:count], refs[count:]
+    step = pl.program_id(0)
+    size, fields = pert_ref.shape[:2]
+    now, before = lax.rem(step, 2), lax.rem(step + 1, 2)
+    for patch in range(size):
+        held = weights_ref[before, patch]
+        for field in range(fields):
+            change = jnp.dot(held, pert_ref[patch, field], preferred_element_type=F32)
+            out_ref[patch, field] = change + mean_ref[patch, field : field + 1]
+    groups = pl.num_programs(0) - 1
+    first = jnp.minimum(step, groups - 1) * (group // 2)
+    for patch, weights in enumerate(solve_group(parts, total_obs, first, group // 2)):
+        weights_ref[now, patch] = weights
+
+
+def analysis(parts, total_obs, pert, mean):
+    patches, fields, members, columns = pert.shape
+    group = patches // 2
     whole = pl.BlockSpec(memory_space=pltpu.VMEM)
     return pl.pallas_call(
-        functools.partial(solve_kernel, len(parts), total_obs),
-        out_shape=jax.ShapeDtypeStruct((2 * pairs, members, members), BF16),
-        in_specs=[whole] * len(parts),
-        out_specs=whole,
-        compiler_params=pltpu.CompilerParams(vmem_limit_bytes=8 * 2**20),
-        name="solve",
-    )(*parts)
-
-
-def analysis_kernel(weights_ref, pert_ref, mean_ref, out_ref):
-    for field in range(pert_ref.shape[1]):
-        change = jnp.dot(weights_ref[0], pert_ref[0, field], preferred_element_type=F32)
-        out_ref[0, field] = change + mean_ref[0, field : field + 1]
-
-
-def analysis(weights, pert, mean):
-    patches, fields, members, columns = pert.shape
-    return pl.pallas_call(
-        analysis_kernel,
+        functools.partial(analysis_kernel, len(parts), total_obs, group),
         out_shape=jax.ShapeDtypeStruct(pert.shape, F32),
-        grid=(patches,),
-        in_specs=[
-            pl.BlockSpec((1, members, members), lambda i: (i, 0, 0)),
-            pl.BlockSpec((1, fields, members, columns), lambda i: (i, 0, 0, 0)),
-            pl.BlockSpec((1, fields, columns), lambda i: (i, 0, 0)),
+        grid=(patches // group + 1,),
+        in_specs=[whole] * len(parts)
+        + [
+            pl.BlockSpec(
+                (group, fields, members, columns), lambda i: (jnp.maximum(i - 1, 0), 0, 0, 0)
+            ),
+            pl.BlockSpec((group, fields, columns), lambda i: (jnp.maximum(i - 1, 0), 0, 0)),
         ],
-        out_specs=pl.BlockSpec((1, fields, members, columns), lambda i: (i, 0, 0, 0)),
-        compiler_params=pltpu.CompilerParams(vmem_limit_bytes=8 * 2**20),
+        out_specs=pl.BlockSpec(
+            (group, fields, members, columns), lambda i: (jnp.maximum(i - 1, 0), 0, 0, 0)
+        ),
+        scratch_shapes=[pltpu.VMEM((2, group, members, members), BF16)],
+        compiler_params=pltpu.CompilerParams(vmem_limit_bytes=40 * 2**20),
         name="analysis",
-    )(weights, pert, mean)
+    )(*parts, pert, mean)
 
 
 def swap(value, axis, flip):
@@ -490,18 +485,17 @@
     for far in reversed(range(lat_devices // 2)):
         chunk = steps(far)
         send = grams(*next(chunk), sent)
-        advance(send)
         waits, sums = chunk.send(send)
         newest = chunk
         open_chunks.append((chunk, waits))
-        keep = grams(far, 0, sent + sums)
+        keep = grams(far, 0, sums)
         advance(keep)
         newest = None
     while open_chunks:
         advance(None)
-    weights = solve([v[0] for v in parts], holders * held * block_obs)
     updated = analysis(
-        weights,
+        parts,
+        holders * held * block_obs,
         state_pert.reshape(patches, fields, members, columns),
         state_mean.reshape(patches, fields, columns),
     )

time: 119 us -> 104 us (0.87)
  waiting for transfers between devices: 30.8 us -> 21.4 us
  Pallas kernels: 52.2 us -> 45 us
    ppermute x23, waiting for transfers between devices: 23.8 us -> 14.4 us  [swap(): return lax.ppermute(value, axis, [(i, i ^ flip) for i in range(size)])]
    pallas_call x2 -> x1, Pallas kernels: 17.7 us -> 10.4 us  [analysis(): pl.pallas_call(functools.partial(analysis_kernel, len(parts), total_obs,...]
  transfers between devices with their start and end apart: 24 -> 24, of which waited for: 13 -> 8; matrix products, arithmetic and copies ran while one was open for 0% -> 0% of each run, Pallas kernels for 22% -> 25%
where the time goes in v5:
time: 104 us; the launch traced here: 103 us
  Pallas kernels  45 us (43%)
  starting transfers between devices  31.5 us (30%)
  waiting for transfers between devices  21.4 us (21%)
  other arithmetic  3.23 us (3%)
  local copies, waits for them, and re-layouts  2 us (2%)
    pallas_call x8, Pallas kernels, partial_grams(): pl.pallas_call(functools.partial(gram_kernel, sizes, far, core), out_shap...  28.4 us
    ppermute x23, starting transfers between devices, swap(): return lax.ppermute(value, axis, [(i, i ^ flip) for i in range(size)])  24.2 us
    ppermute x23, waiting for transfers between devices, swap(): return lax.ppermute(value, axis, [(i, i ^ flip) for i in range(size)])  14.4 us
    pallas_call x1, Pallas kernels, analysis(): pl.pallas_call(functools.partial(analysis_kernel, len(parts), total_obs,...  10.4 us
    all_to_all x1, starting transfers between devices, on_device(): lax.all_to_all(table, ('lon', 'lat'), split_axis=0, concat_axis=0, tiled=...  7.3 us
    all_to_all x1, waiting for transfers between devices, on_device(): lax.all_to_all(table, ('lon', 'lat'), split_axis=0, concat_axis=0, tiled=...  7.03 us
    pallas_call x1, Pallas kernels, stage(): pl.pallas_call(functools.partial(stage_kernel, chunk), out_shape=[pltpu.V...  3.22 us
  transfers between devices with their start and end apart: 24, of which 8 were waited for; matrix products, arithmetic and copies ran while one was open for 0% of the time, Pallas kernels for 25%

profile of v5, /device:TPU:0, one launch (start us, length us, event | category | flops | bytes accessed | tf_op | source)
XLA Modules:
  0.0 103.5 jit_solution(7169045079475284345)
XLA Ops:
  4.6 7.3 %all-to-all-start = ((s32[32,1,25]{2,1,0:T(1,128)}), s32[32,1,25]{2,1,0:T(1,128)S(1)}, u32[]{:S(2)}, u32[]{:S(2)}) async-start(s32[32,1,25]{2,1,0:T(1,128)} %bitcast.2), calls=%async_computation | async-start | bytes 32768 | tf_op jit(solution)/shard_map/all_to_all | solution.py:383
  11.9 7.0 %all-to-all-done = s32[32,1,25]{2,1,0:T(1,128)S(1)} async-done(((s32[32,1,25]{2,1,0:T(1,128)}), s32[32,1,25]{2,1,0:T(1,128)S(1)}, u32[]{:S(2)}, u32[]{:S(2)}) %all-to-all-start) | async-done | bytes 3232 | tf_op jit(solution)/shard_map/all_to_all | solution.py:383
  20.5 3.2 %stage.1 = (bf16[192,144,128]{2,1,0:T(8,128)(2,1)S(1)}, f32[192,128]{1,0:T(8,128)S(1)}, s32[192,128]{1,0:T(8,128)S(1)}, s32[192,128]{1,0:T(8,128)S(1)}, f32[8,128]{1,0:T(8,128)S(1)}) custom-call(bf16[192,128,128]{2,1,0:T(8,128)(2,1)} %anom_hbm, f32[192,128]{1,0:T(8,128)} %innov_hbm, f32[192,128]{1,0:T(8,128)} %rinv_hbm, s32[192,128]{1,0:T(8,128)} %lon_hbm, ...), custom_call_target="tpu_custom_call" | custom-call | bytes 12582912 | tf_op jit(solution)/shard_map/stage/pallas_call | solution.py:98
  23.7 3.6 %partial_grams.8 = bf16[4,8,144,128]{3,2,1,0:T(8,128)(2,1)S(1)} custom-call(s32[32,26]{1,0:T(8,128)S(4)} %hold.1.requests_ref, bf16[192,144,128]{2,1,0:T(8,128)(2,1)S(1)} %get-tuple-element.80.left_ref, f32[192,128]{1,0:T(8,128)S(1)} %get-tuple-element.81.rinv_ref, s32[192,128]{1,0:T(8,128)S(1)} %get-tuple-element.82.obs_lon_ref, ...), custom_call_target="tpu_custom_call" | custom-call | flops 20132659200 | tf_op jit(solution)/shard_map/partial_grams/pallas_call | solution.py:206
  27.4 3.5 %partial_grams.9.refs_0_ = bf16[4,8,144,128]{3,2,1,0:T(8,128)(2,1)S(1)} custom-call(s32[32,26]{1,0:T(8,128)S(4)} %hold.1.requests_ref, bf16[192,144,128]{2,1,0:T(8,128)(2,1)S(1)} %get-tuple-element.80.left_ref, f32[192,128]{1,0:T(8,128)S(1)} %get-tuple-element.81.rinv_ref, s32[192,128]{1,0:T(8,128)S(1)} %get-tuple-element.82.obs_lon_ref, ...), custom_call_target="tpu_custom_call" | custom-call | flops 20132659200 | tf_op jit(solution)/shard_map/partial_grams/pallas_call | solution.py:206
  32.5 3.5 %partial_grams.10 = bf16[4,8,144,128]{3,2,1,0:T(8,128)(2,1)S(1)} custom-call(s32[32,26]{1,0:T(8,128)S(4)} %hold.1.requests_ref, bf16[192,144,128]{2,1,0:T(8,128)(2,1)S(1)} %get-tuple-element.80.left_ref, f32[192,128]{1,0:T(8,128)S(1)} %get-tuple-element.81.rinv_ref, s32[192,128]{1,0:T(8,128)S(1)} %get-tuple-element.82.obs_lon_ref, ...), custom_call_target="tpu_custom_call" | custom-call | flops 20132659200 | tf_op jit(solution)/shard_map/partial_grams/pallas_call | solution.py:206
  36.1 3.5 %partial_grams.11.refs_0_ = bf16[4,8,144,128]{3,2,1,0:T(8,128)(2,1)S(1)} custom-call(s32[32,26]{1,0:T(8,128)S(4)} %hold.1.requests_ref, bf16[192,144,128]{2,1,0:T(8,128)(2,1)S(1)} %get-tuple-element.80.left_ref, f32[192,128]{1,0:T(8,128)S(1)} %get-tuple-element.81.rinv_ref, s32[192,128]{1,0:T(8,128)S(1)} %get-tuple-element.82.obs_lon_ref, ...), custom_call_target="tpu_custom_call" | custom-call | flops 20132659200 | tf_op jit(solution)/shard_map/partial_grams/pallas_call | solution.py:206
  41.8 1.4 %collective-permute-start.5 = (bf16[1,4,144,128]{3,2,1,0:T(8,128)(2,1)S(1)}, bf16[1,4,144,128]{3,2,1,0:T(8,128)(2,1)S(1)}, u32[]{:S(2)}, u32[]{:S(2)}) collective-permute-start(bf16[1,4,144,128]{3,2,1,0:T(8,128)(2,1)S(1)} %get-tuple-element.99), channel_id=1, source_target_pairs={{0,1},{1,0},{2,3},{3,2},{4,5},{5,4},{6,7},{7,6},{8,9},{9,8},{10,11... | collective-permute-start | bytes 442376 | tf_op jit(solution)/shard_map/ppermute | solution.py:367
  44.2 1.4 %collective-permute-start.7 = (bf16[2,4,144,128]{3,2,1,0:T(8,128)(2,1)S(1)}, bf16[2,4,144,128]{3,2,1,0:T(8,128)(2,1)S(1)}, u32[]{:S(2)}, u32[]{:S(2)}) collective-permute-start(bf16[2,4,144,128]{3,2,1,0:T(8,128)(2,1)S(1)} %get-tuple-element.103), channel_id=1, source_target_pairs={{0,16},{8,24},{16,0},{24,8},{1,17},{9,25},{17,1},{25,9},{2,18},{10... | collective-permute-start | bytes 884744 | tf_op jit(solution)/shard_map/ppermute | solution.py:367
  45.7 3.5 %partial_grams.12 = bf16[4,8,144,128]{3,2,1,0:T(8,128)(2,1)S(1)} custom-call(s32[32,26]{1,0:T(8,128)S(4)} %hold.1.requests_ref, bf16[192,144,128]{2,1,0:T(8,128)(2,1)S(1)} %get-tuple-element.80.left_ref, f32[192,128]{1,0:T(8,128)S(1)} %get-tuple-element.81.rinv_ref, s32[192,128]{1,0:T(8,128)S(1)} %get-tuple-element.82.obs_lon_ref, ...), custom_call_target="tpu_custom_call" | custom-call | flops 20132659200 | tf_op jit(solution)/shard_map/partial_grams/pallas_call | solution.py:206
  49.3 3.6 %partial_grams.13.refs_0_ = bf16[4,8,144,128]{3,2,1,0:T(8,128)(2,1)S(1)} custom-call(s32[32,26]{1,0:T(8,128)S(4)} %hold.1.requests_ref, bf16[192,144,128]{2,1,0:T(8,128)(2,1)S(1)} %get-tuple-element.80.left_ref, f32[192,128]{1,0:T(8,128)S(1)} %get-tuple-element.81.rinv_ref, s32[192,128]{1,0:T(8,128)S(1)} %get-tuple-element.82.obs_lon_ref, ...), custom_call_target="tpu_custom_call" | custom-call | flops 20132659200 | tf_op jit(solution)/shard_map/partial_grams/pallas_call | solution.py:206
  54.7 1.4 %collective-permute-start.11 = (bf16[1,4,144,128]{3,2,1,0:T(8,128)(2,1)S(1)}, bf16[1,4,144,128]{3,2,1,0:T(8,128)(2,1)S(1)}, u32[]{:S(2)}, u32[]{:S(2)}) collective-permute-start(bf16[1,4,144,128]{3,2,1,0:T(8,128)(2,1)S(1)} %get-tuple-element.113), channel_id=1, source_target_pairs={{0,1},{1,0},{2,3},{3,2},{4,5},{5,4},{6,7},{7,6},{8,9},{9,8},{10,11... | collective-permute-start | bytes 442376 | tf_op jit(solution)/shard_map/ppermute | solution.py:367
  59.0 3.5 %partial_grams.14 = bf16[4,8,144,128]{3,2,1,0:T(8,128)(2,1)S(1)} custom-call(s32[32,26]{1,0:T(8,128)S(4)} %hold.1.requests_ref, bf16[192,144,128]{2,1,0:T(8,128)(2,1)S(1)} %get-tuple-element.80.left_ref, f32[192,128]{1,0:T(8,128)S(1)} %get-tuple-element.81.rinv_ref, s32[192,128]{1,0:T(8,128)S(1)} %get-tuple-element.82.obs_lon_ref, ...), custom_call_target="tpu_custom_call" | custom-call | flops 20132659200 | tf_op jit(solution)/shard_map/partial_grams/pallas_call | solution.py:206
  62.6 3.6 %partial_grams.15.refs_0_ = bf16[4,8,144,128]{3,2,1,0:T(8,128)(2,1)S(1)} custom-call(s32[32,26]{1,0:T(8,128)S(4)} %hold.1.requests_ref, bf16[192,144,128]{2,1,0:T(8,128)(2,1)S(1)} %get-tuple-element.80.left_ref, f32[192,128]{1,0:T(8,128)S(1)} %get-tuple-element.81.rinv_ref, s32[192,128]{1,0:T(8,128)S(1)} %get-tuple-element.82.obs_lon_ref, ...), custom_call_target="tpu_custom_call" | custom-call | flops 20132659200 | tf_op jit(solution)/shard_map/partial_grams/pallas_call | solution.py:206
  66.6 1.4 %collective-permute-start.19 = (bf16[2,4,144,128]{3,2,1,0:T(8,128)(2,1)S(1)}, bf16[2,4,144,128]{3,2,1,0:T(8,128)(2,1)S(1)}, u32[]{:S(2)}, u32[]{:S(2)}) collective-permute-start(bf16[2,4,144,128]{3,2,1,0:T(8,128)(2,1)S(1)} %get-tuple-element.137), channel_id=1, source_target_pairs={{0,1},{1,0},{2,3},{3,2},{4,5},{5,4},{6,7},{7,6},{8,9},{9,8},{10,11... | collective-permute-start | bytes 884744 | tf_op jit(solution)/shard_map/ppermute | solution.py:367
  71.0 4.8 %collective-permute-start.15 = (bf16[1,8,144,128]{3,2,1,0:T(8,128)(2,1)S(1)}, bf16[1,8,144,128]{3,2,1,0:T(8,128)(2,1)S(1)}, u32[]{:S(2)}, u32[]{:S(2)}) collective-permute-start(bf16[1,8,144,128]{3,2,1,0:T(8,128)(2,1)S(1)} %add_partials.18), channel_id=1, source_target_pairs={{0,4},{1,5},{2,6},{3,7},{4,0},{5,1},{6,2},{7,3},{8,12},{9,13},{10,... | collective-permute-start | bytes 884744 | tf_op jit(solution)/shard_map/ppermute | solution.py:367
  75.8 4.5 %collective-permute-done.16.refs_2_ = bf16[1,4,144,128]{3,2,1,0:T(8,128)(2,1)S(1)} collective-permute-done((bf16[1,4,144,128]{3,2,1,0:T(8,128)(2,1)S(1)}, bf16[1,4,144,128]{3,2,1,0:T(8,128)(2,1)S(1)}, u32[]{:S(2)}, u32[]{:S(2)}) %collective-permute-start.16) | collective-permute-done | bytes 147488 | tf_op jit(solution)/shard_map/ppermute | solution.py:367
  80.4 1.6 %collective-permute-start.18 = (bf16[1,8,144,128]{3,2,1,0:T(8,128)(2,1)S(1)}, bf16[1,8,144,128]{3,2,1,0:T(8,128)(2,1)S(1)}, u32[]{:S(2)}, u32[]{:S(2)}) collective-permute-start(bf16[1,8,144,128]{3,2,1,0:T(8,128)(2,1)S(1)} %add_partials.20), channel_id=1, source_target_pairs={{0,2},{1,3},{2,0},{3,1},{4,6},{5,7},{6,4},{7,5},{8,10},{9,11},{10,... | collective-permute-start | bytes 884744 | tf_op jit(solution)/shard_map/ppermute | solution.py:367
  82.2 1.7 %collective-permute-start.21 = (bf16[1,4,144,128]{3,2,1,0:T(8,128)(2,1)S(1)}, bf16[1,4,144,128]{3,2,1,0:T(8,128)(2,1)S(1)}, u32[]{:S(2)}, u32[]{:S(2)}) collective-permute-start(bf16[1,4,144,128]{3,2,1,0:T(8,128)(2,1)S(1)} %get-tuple-element.141), channel_id=1, source_target_pairs={{0,16},{8,24},{16,0},{24,8},{1,17},{9,25},{17,1},{25,9},{2,18},{10... | collective-permute-start | bytes 442376 | tf_op jit(solution)/shard_map/ppermute | solution.py:367
  83.8 1.4 %collective-permute-start.22 = (bf16[1,4,144,128]{3,2,1,0:T(8,128)(2,1)S(1)}, bf16[1,4,144,128]{3,2,1,0:T(8,128)(2,1)S(1)}, u32[]{:S(2)}, u32[]{:S(2)}) collective-permute-start(bf16[1,4,144,128]{3,2,1,0:T(8,128)(2,1)S(1)} %get-tuple-element.142), channel_id=1, source_target_pairs={{0,1},{1,0},{2,3},{3,2},{4,5},{5,4},{6,7},{7,6},{8,9},{9,8},{10,11... | collective-permute-start | bytes 442376 | tf_op jit(solution)/shard_map/ppermute | solution.py:367
  85.2 2.2 %collective-permute-done.21.refs_2_ = bf16[1,4,144,128]{3,2,1,0:T(8,128)(2,1)S(1)} collective-permute-done((bf16[1,4,144,128]{3,2,1,0:T(8,128)(2,1)S(1)}, bf16[1,4,144,128]{3,2,1,0:T(8,128)(2,1)S(1)}, u32[]{:S(2)}, u32[]{:S(2)}) %collective-permute-start.21) | collective-permute-done | bytes 147488 | tf_op jit(solution)/shard_map/ppermute | solution.py:367
  87.4 1.6 %collective-permute-done.22.refs_3_ = bf16[1,4,144,128]{3,2,1,0:T(8,128)(2,1)S(1)} collective-permute-done((bf16[1,4,144,128]{3,2,1,0:T(8,128)(2,1)S(1)}, bf16[1,4,144,128]{3,2,1,0:T(8,128)(2,1)S(1)}, u32[]{:S(2)}, u32[]{:S(2)}) %collective-permute-start.22) | collective-permute-done | bytes 147488 | tf_op jit(solution)/shard_map/ppermute | solution.py:367
  89.1 4.0 %collective-permute-done.18.refs_2_ = bf16[1,8,144,128]{3,2,1,0:T(8,128)(2,1)S(1)} collective-permute-done((bf16[1,8,144,128]{3,2,1,0:T(8,128)(2,1)S(1)}, bf16[1,8,144,128]{3,2,1,0:T(8,128)(2,1)S(1)}, u32[]{:S(2)}, u32[]{:S(2)}) %collective-permute-start.18) | collective-permute-done | bytes 294944 | tf_op jit(solution)/shard_map/ppermute | solution.py:367
  93.0 10.4 %analysis.1 = f32[16,6,128,256]{3,2,1,0:T(8,128)} custom-call(bf16[1,8,144,128]{3,2,1,0:T(8,128)(2,1)S(1)} %collective-permute-done.9.refs_0_, bf16[1,8,144,128]{3,2,1,0:T(8,128)(2,1)S(1)} %collective-permute-done.15.refs_1_, bf16[1,8,144,128]{3,2,1,0:T(8,128)(2,1)S(1)} %collective-permute-done.18.refs_2_, ...), custom_call_target="tpu_custom_call" | custom-call | tf_op jit(solution)/shard_map/analysis/pallas_call | solution.py:345
  (73 shorter events, 19.5 us)
Async XLA Ops:
  4.6 14.3 %all-to-all-start = ((s32[32,1,25]{2,1,0:T(1,128)}), s32[32,1,25]{2,1,0:T(1,128)S(1)}, u32[]{:S(2)}, u32[]{:S(2)}) async-start(s32[32,1,25]{2,1,0:T(1,128)} %bitcast.2), calls=%async_computation | async-start | bytes 32768 | tf_op jit(solution)/shard_map/all_to_all | solution.py:383
  27.3 3.6 %collective-permute-start = (bf16[4,8,144,128]{3,2,1,0:T(8,128)(2,1)S(1)}, bf16[4,8,144,128]{3,2,1,0:T(8,128)(2,1)S(1)}, u32[]{:S(2)}, u32[]{:S(2)}) collective-permute-start(bf16[4,8,144,128]{3,2,1,0:T(8,128)(2,1)S(1)} %partial_grams.8), channel_id=1, source_target_pairs={{0,8},{8,0},{16,24},{24,16},{1,9},{9,1},{17,25},{25,17},{2,10},{10... | collective-permute-start | bytes 3538952 | tf_op jit(solution)/shard_map/ppermute | solution.py:367
  31.2 9.4 %collective-permute-start.1 = (bf16[2,4,144,128]{3,2,1,0:T(8,128)(2,1)S(1)}, bf16[2,4,144,128]{3,2,1,0:T(8,128)(2,1)S(1)}, u32[]{:S(2)}, u32[]{:S(2)}) collective-permute-start(bf16[2,4,144,128]{3,2,1,0:T(8,128)(2,1)S(1)} %get-tuple-element.90), channel_id=1, source_target_pairs={{0,1},{1,0},{2,3},{3,2},{4,5},{5,4},{6,7},{7,6},{8,9},{9,8},{10,11... | collective-permute-start | bytes 884744 | tf_op jit(solution)/shard_map/ppermute | solution.py:367
  31.9 9.1 %collective-permute-start.2 = (bf16[2,4,144,128]{3,2,1,0:T(8,128)(2,1)S(1)}, bf16[2,4,144,128]{3,2,1,0:T(8,128)(2,1)S(1)}, u32[]{:S(2)}, u32[]{:S(2)}) collective-permute-start(bf16[2,4,144,128]{3,2,1,0:T(8,128)(2,1)S(1)} %get-tuple-element.91), channel_id=1, source_target_pairs={{0,16},{8,24},{16,0},{24,8},{1,17},{9,25},{17,1},{25,9},{2,18},{10... | collective-permute-start | bytes 884744 | tf_op jit(solution)/shard_map/ppermute | solution.py:367
  36.1 5.0 %collective-permute-start.3 = (bf16[4,8,144,128]{3,2,1,0:T(8,128)(2,1)S(1)}, bf16[4,8,144,128]{3,2,1,0:T(8,128)(2,1)S(1)}, u32[]{:S(2)}, u32[]{:S(2)}) collective-permute-start(bf16[4,8,144,128]{3,2,1,0:T(8,128)(2,1)S(1)} %partial_grams.10), channel_id=1, source_target_pairs={{0,8},{8,0},{16,24},{24,16},{1,9},{9,1},{17,25},{25,17},{2,10},{10... | collective-permute-start | bytes 3538952 | tf_op jit(solution)/shard_map/ppermute | solution.py:367
  41.2 11.7 %collective-permute-start.4 = (bf16[1,4,144,128]{3,2,1,0:T(8,128)(2,1)S(1)}, bf16[1,4,144,128]{3,2,1,0:T(8,128)(2,1)S(1)}, u32[]{:S(2)}, u32[]{:S(2)}) collective-permute-start(bf16[1,4,144,128]{3,2,1,0:T(8,128)(2,1)S(1)} %get-tuple-element.98), channel_id=1, source_target_pairs={{0,16},{8,24},{16,0},{24,8},{1,17},{9,25},{17,1},{25,9},{2,18},{10... | collective-permute-start | bytes 442376 | tf_op jit(solution)/shard_map/ppermute | solution.py:367
  41.8 11.0 %collective-permute-start.5 = (bf16[1,4,144,128]{3,2,1,0:T(8,128)(2,1)S(1)}, bf16[1,4,144,128]{3,2,1,0:T(8,128)(2,1)S(1)}, u32[]{:S(2)}, u32[]{:S(2)}) collective-permute-start(bf16[1,4,144,128]{3,2,1,0:T(8,128)(2,1)S(1)} %get-tuple-element.99), channel_id=1, source_target_pairs={{0,1},{1,0},{2,3},{3,2},{4,5},{5,4},{6,7},{7,6},{8,9},{9,8},{10,11... | collective-permute-start | bytes 442376 | tf_op jit(solution)/shard_map/ppermute | solution.py:367
  43.5 10.1 %collective-permute-start.6 = (bf16[2,4,144,128]{3,2,1,0:T(8,128)(2,1)S(1)}, bf16[2,4,144,128]{3,2,1,0:T(8,128)(2,1)S(1)}, u32[]{:S(2)}, u32[]{:S(2)}) collective-permute-start(bf16[2,4,144,128]{3,2,1,0:T(8,128)(2,1)S(1)} %get-tuple-element.102), channel_id=1, source_target_pairs={{0,1},{1,0},{2,3},{3,2},{4,5},{5,4},{6,7},{7,6},{8,9},{9,8},{10,11... | collective-permute-start | bytes 884744 | tf_op jit(solution)/shard_map/ppermute | solution.py:367
  44.2 9.4 %collective-permute-start.7 = (bf16[2,4,144,128]{3,2,1,0:T(8,128)(2,1)S(1)}, bf16[2,4,144,128]{3,2,1,0:T(8,128)(2,1)S(1)}, u32[]{:S(2)}, u32[]{:S(2)}) collective-permute-start(bf16[2,4,144,128]{3,2,1,0:T(8,128)(2,1)S(1)} %get-tuple-element.103), channel_id=1, source_target_pairs={{0,16},{8,24},{16,0},{24,8},{1,17},{9,25},{17,1},{25,9},{2,18},{10... | collective-permute-start | bytes 884744 | tf_op jit(solution)/shard_map/ppermute | solution.py:367
  49.2 4.5 %collective-permute-start.8 = (bf16[4,8,144,128]{3,2,1,0:T(8,128)(2,1)S(1)}, bf16[4,8,144,128]{3,2,1,0:T(8,128)(2,1)S(1)}, u32[]{:S(2)}, u32[]{:S(2)}) collective-permute-start(bf16[4,8,144,128]{3,2,1,0:T(8,128)(2,1)S(1)} %partial_grams.12), channel_id=1, source_target_pairs={{0,8},{8,0},{16,24},{24,16},{1,9},{9,1},{17,25},{25,17},{2,10},{10... | collective-permute-start | bytes 3538952 | tf_op jit(solution)/shard_map/ppermute | solution.py:367
  53.8 8.7 %collective-permute-start.10 = (bf16[1,4,144,128]{3,2,1,0:T(8,128)(2,1)S(1)}, bf16[1,4,144,128]{3,2,1,0:T(8,128)(2,1)S(1)}, u32[]{:S(2)}, u32[]{:S(2)}) collective-permute-start(bf16[1,4,144,128]{3,2,1,0:T(8,128)(2,1)S(1)} %get-tuple-element.112), channel_id=1, source_target_pairs={{0,16},{8,24},{16,0},{24,8},{1,17},{9,25},{17,1},{25,9},{2,18},{10... | collective-permute-start | bytes 442376 | tf_op jit(solution)/shard_map/ppermute | solution.py:367
  54.7 11.6 %collective-permute-start.11 = (bf16[1,4,144,128]{3,2,1,0:T(8,128)(2,1)S(1)}, bf16[1,4,144,128]{3,2,1,0:T(8,128)(2,1)S(1)}, u32[]{:S(2)}, u32[]{:S(2)}) collective-permute-start(bf16[1,4,144,128]{3,2,1,0:T(8,128)(2,1)S(1)} %get-tuple-element.113), channel_id=1, source_target_pairs={{0,1},{1,0},{2,3},{3,2},{4,5},{5,4},{6,7},{7,6},{8,9},{9,8},{10,11... | collective-permute-start | bytes 442376 | tf_op jit(solution)/shard_map/ppermute | solution.py:367
  56.1 10.1 %collective-permute-start.9 = (bf16[1,8,144,128]{3,2,1,0:T(8,128)(2,1)S(1)}, bf16[1,8,144,128]{3,2,1,0:T(8,128)(2,1)S(1)}, u32[]{:S(2)}, u32[]{:S(2)}) collective-permute-start(bf16[1,8,144,128]{3,2,1,0:T(8,128)(2,1)S(1)} %add_partials.15), channel_id=1, source_target_pairs={{0,6},{1,7},{2,4},{3,5},{4,2},{5,3},{6,0},{7,1},{8,14},{9,15},{10,... | collective-permute-start | bytes 884744 | tf_op jit(solution)/shard_map/ppermute | solution.py:367
  57.1 9.2 %collective-permute-start.12 = (bf16[2,4,144,128]{3,2,1,0:T(8,128)(2,1)S(1)}, bf16[2,4,144,128]{3,2,1,0:T(8,128)(2,1)S(1)}, u32[]{:S(2)}, u32[]{:S(2)}) collective-permute-start(bf16[2,4,144,128]{3,2,1,0:T(8,128)(2,1)S(1)} %get-tuple-element.116), channel_id=1, source_target_pairs={{0,1},{1,0},{2,3},{3,2},{4,5},{5,4},{6,7},{7,6},{8,9},{9,8},{10,11... | collective-permute-start | bytes 884744 | tf_op jit(solution)/shard_map/ppermute | solution.py:367
  57.8 8.5 %collective-permute-start.13 = (bf16[2,4,144,128]{3,2,1,0:T(8,128)(2,1)S(1)}, bf16[2,4,144,128]{3,2,1,0:T(8,128)(2,1)S(1)}, u32[]{:S(2)}, u32[]{:S(2)}) collective-permute-start(bf16[2,4,144,128]{3,2,1,0:T(8,128)(2,1)S(1)} %get-tuple-element.117), channel_id=1, source_target_pairs={{0,16},{8,24},{16,0},{24,8},{1,17},{9,25},{17,1},{25,9},{2,18},{10... | collective-permute-start | bytes 884744 | tf_op jit(solution)/shard_map/ppermute | solution.py:367
  62.6 3.7 %collective-permute-start.14 = (bf16[4,8,144,128]{3,2,1,0:T(8,128)(2,1)S(1)}, bf16[4,8,144,128]{3,2,1,0:T(8,128)(2,1)S(1)}, u32[]{:S(2)}, u32[]{:S(2)}) collective-permute-start(bf16[4,8,144,128]{3,2,1,0:T(8,128)(2,1)S(1)} %partial_grams.14), channel_id=1, source_target_pairs={{0,8},{8,0},{16,24},{24,16},{1,9},{9,1},{17,25},{25,17},{2,10},{10... | collective-permute-start | bytes 3538952 | tf_op jit(solution)/shard_map/ppermute | solution.py:367
  66.6 15.4 %collective-permute-start.19 = (bf16[2,4,144,128]{3,2,1,0:T(8,128)(2,1)S(1)}, bf16[2,4,144,128]{3,2,1,0:T(8,128)(2,1)S(1)}, u32[]{:S(2)}, u32[]{:S(2)}) collective-permute-start(bf16[2,4,144,128]{3,2,1,0:T(8,128)(2,1)S(1)} %get-tuple-element.137), channel_id=1, source_target_pairs={{0,1},{1,0},{2,3},{3,2},{4,5},{5,4},{6,7},{7,6},{8,9},{9,8},{10,11... | collective-permute-start | bytes 884744 | tf_op jit(solution)/shard_map/ppermute | solution.py:367
  68.0 14.0 %collective-permute-start.20 = (bf16[2,4,144,128]{3,2,1,0:T(8,128)(2,1)S(1)}, bf16[2,4,144,128]{3,2,1,0:T(8,128)(2,1)S(1)}, u32[]{:S(2)}, u32[]{:S(2)}) collective-permute-start(bf16[2,4,144,128]{3,2,1,0:T(8,128)(2,1)S(1)} %get-tuple-element.138), channel_id=1, source_target_pairs={{0,16},{8,24},{16,0},{24,8},{1,17},{9,25},{17,1},{25,9},{2,18},{10... | collective-permute-start | bytes 884744 | tf_op jit(solution)/shard_map/ppermute | solution.py:367
  69.3 11.0 %collective-permute-start.16 = (bf16[1,4,144,128]{3,2,1,0:T(8,128)(2,1)S(1)}, bf16[1,4,144,128]{3,2,1,0:T(8,128)(2,1)S(1)}, u32[]{:S(2)}, u32[]{:S(2)}) collective-permute-start(bf16[1,4,144,128]{3,2,1,0:T(8,128)(2,1)S(1)} %get-tuple-element.131), channel_id=1, source_target_pairs={{0,16},{8,24},{16,0},{24,8},{1,17},{9,25},{17,1},{25,9},{2,18},{10... | collective-permute-start | bytes 442376 | tf_op jit(solution)/shard_map/ppermute | solution.py:367
  70.3 10.0 %collective-permute-start.17 = (bf16[1,4,144,128]{3,2,1,0:T(8,128)(2,1)S(1)}, bf16[1,4,144,128]{3,2,1,0:T(8,128)(2,1)S(1)}, u32[]{:S(2)}, u32[]{:S(2)}) collective-permute-start(bf16[1,4,144,128]{3,2,1,0:T(8,128)(2,1)S(1)} %get-tuple-element.132), channel_id=1, source_target_pairs={{0,1},{1,0},{2,3},{3,2},{4,5},{5,4},{6,7},{7,6},{8,9},{9,8},{10,11... | collective-permute-start | bytes 442376 | tf_op jit(solution)/shard_map/ppermute | solution.py:367
  71.0 18.0 %collective-permute-start.15 = (bf16[1,8,144,128]{3,2,1,0:T(8,128)(2,1)S(1)}, bf16[1,8,144,128]{3,2,1,0:T(8,128)(2,1)S(1)}, u32[]{:S(2)}, u32[]{:S(2)}) collective-permute-start(bf16[1,8,144,128]{3,2,1,0:T(8,128)(2,1)S(1)} %add_partials.18), channel_id=1, source_target_pairs={{0,4},{1,5},{2,6},{3,7},{4,0},{5,1},{6,2},{7,3},{8,12},{9,13},{10,... | collective-permute-start | bytes 884744 | tf_op jit(solution)/shard_map/ppermute | solution.py:367
  80.4 12.7 %collective-permute-start.18 = (bf16[1,8,144,128]{3,2,1,0:T(8,128)(2,1)S(1)}, bf16[1,8,144,128]{3,2,1,0:T(8,128)(2,1)S(1)}, u32[]{:S(2)}, u32[]{:S(2)}) collective-permute-start(bf16[1,8,144,128]{3,2,1,0:T(8,128)(2,1)S(1)} %add_partials.20), channel_id=1, source_target_pairs={{0,2},{1,3},{2,0},{3,1},{4,6},{5,7},{6,4},{7,5},{8,10},{9,11},{10,... | collective-permute-start | bytes 884744 | tf_op jit(solution)/shard_map/ppermute | solution.py:367
  82.2 5.2 %collective-permute-start.21 = (bf16[1,4,144,128]{3,2,1,0:T(8,128)(2,1)S(1)}, bf16[1,4,144,128]{3,2,1,0:T(8,128)(2,1)S(1)}, u32[]{:S(2)}, u32[]{:S(2)}) collective-permute-start(bf16[1,4,144,128]{3,2,1,0:T(8,128)(2,1)S(1)} %get-tuple-element.141), channel_id=1, source_target_pairs={{0,16},{8,24},{16,0},{24,8},{1,17},{9,25},{17,1},{25,9},{2,18},{10... | collective-permute-start | bytes 442376 | tf_op jit(solution)/shard_map/ppermute | solution.py:367
  83.8 5.1 %collective-permute-start.22 = (bf16[1,4,144,128]{3,2,1,0:T(8,128)(2,1)S(1)}, bf16[1,4,144,128]{3,2,1,0:T(8,128)(2,1)S(1)}, u32[]{:S(2)}, u32[]{:S(2)}) collective-permute-start(bf16[1,4,144,128]{3,2,1,0:T(8,128)(2,1)S(1)} %get-tuple-element.142), channel_id=1, source_target_pairs={{0,1},{1,0},{2,3},{3,2},{4,5},{5,4},{6,7},{7,6},{8,9},{9,8},{10,11... | collective-permute-start | bytes 442376 | tf_op jit(solution)/shard_map/ppermute | solution.py:367
  (3 other events, 83.1 us)

commit v6 on v5

--- a/solution.py
+++ b/solution.py
@@ -230,30 +230,29 @@
     return total[:, :members].astype(BF16), rows.astype(BF16)
 
 
-def add_kernel(count, plan, *refs):
-    keep, got, outs = refs[:count], refs[count : 2 * count], refs[2 * count :]
-    for part, index, low, high, out, place, at in plan:
-        members = keep[part].shape[-1]
-        body, rows = added(keep[part][index, low:high], got[part][index, low:high])
-        to = slice(at, at + high - low)
-        outs[out][place, to, :members, :] = body
-        outs[out][place, to, members:, :] = rows
-
-
-def add_all(keep, got, plan, shapes):
-    count = len(keep)
-    inner = keep[0].shape[2:]
+def add_kernel(inputs, size, jobs, *refs):
+    for left, left_row, right, right_row, at, out, row, place in jobs:
+        out_ref = refs[inputs + out]
+        members = out_ref.shape[-1]
+        span, to = slice(at, at + size), slice(place, place + size)
+        body, rows = added(refs[left][left_row, span], refs[right][right_row, span])
+        out_ref[row, to, :members, :] = body
+        out_ref[row, to, members:, :] = rows
+
+
+def add_all(arrays, size, jobs, shapes):
+    inner = arrays[0].shape[2:]
     whole = pl.BlockSpec(memory_space=pltpu.VMEM)
-    size = sum(v.size for v in keep)
+    work = len(jobs) * size * inner[0] * inner[1]
     return pl.pallas_call(
-        functools.partial(add_kernel, count, plan),
+        functools.partial(add_kernel, len(arrays), size, jobs),
         out_shape=[jax.ShapeDtypeStruct((*shape, *inner), BF16) for shape in shapes],
-        in_specs=[whole] * (2 * count),
+        in_specs=[whole] * len(arrays),
         out_specs=[whole] * len(shapes),
         compiler_params=pltpu.CompilerParams(vmem_limit_bytes=8 * 2**20),
-        cost_estimate=pl.CostEstimate(flops=size * 4, bytes_accessed=size * 6, transcendentals=0),
+        cost_estimate=pl.CostEstimate(flops=work * 4, bytes_accessed=work * 6, transcendentals=0),
         name="add_partials",
-    )(*keep, *got)
+    )(*arrays)
 
 
 def product(left, right):
@@ -406,95 +405,92 @@
         rows, _ = lax.optimization_barrier((staged[-1], after))
         return partial_grams(sizes, far, core, lon_devices, requests, [*staged[:-1], rows])
 
-    def steps(far):
-        send = yield far, 1
+    along_lon = []
+    while 2 ** (len(along_lon) + 1) <= y_count:
+        along_lon.append(("lon", y_count >> len(along_lon)))
+    routes = [[("lat", 1), *along_lon], [*along_lon[:1], ("lat", 1), *along_lon[1:]]]
+
+    def leaves(target, axis, flip):
+        y, near = target
+        return near == 1 if axis == "lat" else (2 * y) & flip != 0
+
+    parts, open_chunks, on_their_way = {}, [], [[], []]
+
+    def exchange(merge):
+        nonlocal open_chunks
+        arrays, jobs, lengths, where = [], [], {}, {}
+
+        def slot(array):
+            for i, known in enumerate(arrays):
+                if known is array:
+                    return i
+            arrays.append(array)
+            return len(arrays) - 1
+
+        def take(key):
+            row = lengths.get(key, 0)
+            lengths[key] = row + 1
+            return row
+
+        for far, level, parcels in open_chunks:
+            for half, (targets, at, keep, keep_rows, got, got_rows) in enumerate(parcels):
+                for target, keep_row, got_row in zip(targets, keep_rows, got_rows):
+                    place = 0
+                    if level == len(routes[half]):
+                        key, row, place = ("total", far), 0, half * cut
+                        lengths[key] = 1
+                    elif leaves(target, *routes[half][level]):
+                        key = ("send", *routes[half][level], 0 if merge else level)
+                        row = take(key)
+                    else:
+                        key = ("keep", far, half)
+                        row = take(key)
+                    where[far, half, target] = key, row
+                    jobs.append((slot(keep), keep_row, slot(got), got_row, at, key, row, place))
+        keys = sorted(lengths, key=lambda k: (k[0], -k[-1] if k[0] == "send" else 0))
+        jobs = [(*job[:5], keys.index(job[5]), *job[6:]) for job in jobs]
+        shapes = [(lengths[k], pairs if k[0] == "total" else cut) for k in keys]
+        due = on_their_way.pop(0)
+        on_their_way.append([])
+        arrays[0], arrived = lax.optimization_barrier((arrays[0], [parts[far] for far in due]))
+        parts.update(zip(due, arrived))
+        outs = dict(zip(keys, add_all(arrays, cut, jobs, shapes)))
+        gots = {k: swap(v, k[1], k[2]) for k, v in outs.items() if k[0] == "send"}
+        still = []
+        for far, level, parcels in open_chunks:
+            if level == len(routes[0]):
+                total = outs["total", far]
+                parts[far] = swap(total, "lat", 2 * far) if far else total
+                if far:
+                    on_their_way[1].append(far)
+                continue
+            following = []
+            for half, (targets, *_) in enumerate(parcels):
+                staying = [t for t in targets if not leaves(t, *routes[half][level])]
+                leaving = [t for t in targets if leaves(t, *routes[half][level])]
+                keep_rows = [where[far, half, t][1] for t in staying]
+                got_rows = [where[far, half, t][1] for t in leaving]
+                got = gots[where[far, half, leaving[0]][0]]
+                following.append((staying, 0, outs["keep", far, half], keep_rows, got, got_rows))
+            still.append((far, level + 1, following))
+        open_chunks = still
+        return [v for k, v in outs.items() if k[0] != "keep"]
+
+    sent = []
+    for far in reversed(range(lat_devices // 2)):
+        send = grams(far, 1, sent)
         got = swap(send, "lon", 1)
-        keep = yield [got], [send]
-        left = y_count // 2
-        plan = []
-        for y in range(y_count):
-            for near in range(2):
-                plan.append((0, 2 * y + near, 0, cut, near, y, 0))
-                far_y, place = divmod(y, left)
-                plan.append((0, 2 * y + near, cut, pairs, 2 + far_y, 2 * place + near, 0))
-        keep_a, send_a, keep_b, send_b = add_all(
-            [keep[0]],
-            [keep[1]],
-            plan,
-            [(y_count, cut)] * 2 + [(2 * left, pairs - cut)] * 2,
+        keep = grams(far, 0, [send])
+        targets = [(y, near) for y in range(y_count) for near in range(2)]
+        rows = range(len(targets))
+        open_chunks.append(
+            (far, 0, [(targets, at, keep, rows, got, rows) for at in (0, cut)])
         )
-        got_a, got_b = yield [swap(send_a, "lat", 1), swap(send_b, "lon", y_count)], [send_a, send_b]
-        plan = []
-        for y in range(y_count):
-            far_y, place = divmod(y, left)
-            plan.append((0, y, 0, cut, far_y, place, 0))
-        for y in range(left):
-            for near in range(2):
-                plan.append((1, 2 * y + near, 0, pairs - cut, 2 + near, y, 0))
-        keep_a, send_a, keep_b, send_b = add_all(
-            [keep_a, keep_b],
-            [got_a, got_b],
-            plan,
-            [(left, cut)] * 2 + [(left, pairs - cut)] * 2,
-        )
-        got_a, got_b = yield [swap(send_a, "lon", y_count), swap(send_b, "lat", 1)], [send_a, send_b]
-        while left > 1:
-            left //= 2
-            plan = []
-            for part in range(2):
-                for y in range(2 * left):
-                    far_y, place = divmod(y, left)
-                    plan.append((part, y, 0, keep_a.shape[1] if part == 0 else pairs - cut, 2 * part + far_y, place, 0))
-            keep_a, send_a, keep_b, send_b = add_all(
-                [keep_a, keep_b],
-                [got_a, got_b],
-                plan,
-                [(left, cut)] * 2 + [(left, pairs - cut)] * 2,
-            )
-            got_a, got_b = yield (
-                [swap(send_a, "lon", 2 * left), swap(send_b, "lon", 2 * left)],
-                [send_a, send_b],
-            )
-        plan = [(0, 0, 0, cut, 0, 0, 0), (1, 0, 0, pairs - cut, 0, 0, cut)]
-        [total] = add_all([keep_a, keep_b], [got_a, got_b], plan, [(1, pairs)])
-        if far:
-            [total] = yield [swap(total, "lat", 2 * far)], [total]
-        parts.append(total)
-
-    parts, open_chunks, sent = [], [], []
-
-    def advance(latest):
-        nonlocal open_chunks, sent
-        flat = [w for _, waits in open_chunks for w in waits]
-        if latest is not None:
-            latest, flat = lax.optimization_barrier((latest, flat))
-        still, sent = [], []
-        for chunk, waits in open_chunks:
-            now, flat = flat[: len(waits)], flat[len(waits) :]
-            if latest is not None and chunk is newest:
-                now = [latest, *now]
-            try:
-                waits, sums = chunk.send(now)
-                still.append((chunk, waits))
-                sent += sums
-            except StopIteration:
-                pass
-        open_chunks = still
-
-    newest = None
-    for far in reversed(range(lat_devices // 2)):
-        chunk = steps(far)
-        send = grams(*next(chunk), sent)
-        waits, sums = chunk.send(send)
-        newest = chunk
-        open_chunks.append((chunk, waits))
-        keep = grams(far, 0, sums)
-        advance(keep)
-        newest = None
+        sent = exchange(far > 0)
     while open_chunks:
-        advance(None)
+        exchange(False)
     updated = analysis(
-        parts,
+        list(parts.values()),
         holders * held * block_obs,
         state_pert.reshape(patches, fields, members, columns),
         state_mean.reshape(patches, fields, columns),

time: 104 us -> 101 us (0.971)
  starting transfers between devices: 31.5 us -> 22.6 us
  waiting for transfers between devices: 21.4 us -> 27.8 us
    ppermute x23 -> x19, starting transfers between devices: 24.2 us -> 15.3 us  [swap(): return lax.ppermute(value, axis, [(i, i ^ flip) for i in range(size)])]
    ppermute x23 -> x19, waiting for transfers between devices: 14.4 us -> 20.8 us  [swap(): return lax.ppermute(value, axis, [(i, i ^ flip) for i in range(size)])]
  transfers between devices with their start and end apart: 24 -> 20, of which waited for: 8 -> 11; matrix products, arithmetic and copies ran while one was open for 0% -> 0% of each run, Pallas kernels for 25% -> 25%
where the time goes in v6:
time: 101 us
  Pallas kernels  44.9 us (44%)
  waiting for transfers between devices  27.8 us (28%)
  starting transfers between devices  22.6 us (22%)
  other arithmetic  3.23 us (3%)
  local copies, waits for them, and re-layouts  1.99 us (2%)
    pallas_call x8, Pallas kernels, partial_grams(): pl.pallas_call(functools.partial(gram_kernel, sizes, far, core), out_shap...  28.3 us
    ppermute x19, waiting for transfers between devices, swap(): return lax.ppermute(value, axis, [(i, i ^ flip) for i in range(size)])  20.8 us
    ppermute x19, starting transfers between devices, swap(): return lax.ppermute(value, axis, [(i, i ^ flip) for i in range(size)])  15.3 us
    pallas_call x1, Pallas kernels, analysis(): pl.pallas_call(functools.partial(analysis_kernel, len(parts), total_obs,...  10.4 us
    all_to_all x1, starting transfers between devices, on_device(): lax.all_to_all(table, ('lon', 'lat'), split_axis=0, concat_axis=0, tiled=...  7.3 us
    all_to_all x1, waiting for transfers between devices, on_device(): lax.all_to_all(table, ('lon', 'lat'), split_axis=0, concat_axis=0, tiled=...  7.03 us
    pallas_call x1, Pallas kernels, stage(): pl.pallas_call(functools.partial(stage_kernel, chunk), out_shape=[pltpu.V...  3.22 us
    pallas_call x6, Pallas kernels, add_all(): pl.pallas_call(functools.partial(add_kernel, len(arrays), size, jobs), ou...  2.02 us
  transfers between devices with their start and end apart: 20, of which 11 were waited for; matrix products, arithmetic and copies ran while one was open for 0% of the time, Pallas kernels for 25%

profile of v6, /device:TPU:0, one launch (start us, length us, event | category | flops | bytes accessed | tf_op | source)
XLA Modules:
  0.0 100.8 jit_solution(7360373920435650145)
XLA Ops:
  4.6 7.3 %all-to-all-start = ((s32[32,1,25]{2,1,0:T(1,128)}), s32[32,1,25]{2,1,0:T(1,128)S(1)}, u32[]{:S(2)}, u32[]{:S(2)}) async-start(s32[32,1,25]{2,1,0:T(1,128)} %bitcast.2), calls=%async_computation | async-start | bytes 32768 | tf_op jit(solution)/shard_map/all_to_all | solution.py:382
  11.9 7.0 %all-to-all-done = s32[32,1,25]{2,1,0:T(1,128)S(1)} async-done(((s32[32,1,25]{2,1,0:T(1,128)}), s32[32,1,25]{2,1,0:T(1,128)S(1)}, u32[]{:S(2)}, u32[]{:S(2)}) %all-to-all-start) | async-done | bytes 3232 | tf_op jit(solution)/shard_map/all_to_all | solution.py:382
  20.5 3.2 %stage.1 = (bf16[192,144,128]{2,1,0:T(8,128)(2,1)S(1)}, f32[192,128]{1,0:T(8,128)S(1)}, s32[192,128]{1,0:T(8,128)S(1)}, s32[192,128]{1,0:T(8,128)S(1)}, f32[8,128]{1,0:T(8,128)S(1)}) custom-call(bf16[192,128,128]{2,1,0:T(8,128)(2,1)} %anom_hbm, f32[192,128]{1,0:T(8,128)} %innov_hbm, f32[192,128]{1,0:T(8,128)} %rinv_hbm, s32[192,128]{1,0:T(8,128)} %lon_hbm, ...), custom_call_target="tpu_custom_call" | custom-call | bytes 12582912 | tf_op jit(solution)/shard_map/stage/pallas_call | solution.py:98
  23.7 3.6 %partial_grams.8 = bf16[4,8,144,128]{3,2,1,0:T(8,128)(2,1)S(1)} custom-call(s32[32,26]{1,0:T(8,128)S(4)} %hold.1.requests_ref, bf16[192,144,128]{2,1,0:T(8,128)(2,1)S(1)} %get-tuple-element.64.left_ref, f32[192,128]{1,0:T(8,128)S(1)} %get-tuple-element.65.rinv_ref, s32[192,128]{1,0:T(8,128)S(1)} %get-tuple-element.66.obs_lon_ref, ...), custom_call_target="tpu_custom_call" | custom-call | flops 20132659200 | tf_op jit(solution)/shard_map/partial_grams/pallas_call | solution.py:206
  27.4 3.5 %partial_grams.9.refs_0_ = bf16[4,8,144,128]{3,2,1,0:T(8,128)(2,1)S(1)} custom-call(s32[32,26]{1,0:T(8,128)S(4)} %hold.1.requests_ref, bf16[192,144,128]{2,1,0:T(8,128)(2,1)S(1)} %get-tuple-element.64.left_ref, f32[192,128]{1,0:T(8,128)S(1)} %get-tuple-element.65.rinv_ref, s32[192,128]{1,0:T(8,128)S(1)} %get-tuple-element.66.obs_lon_ref, ...), custom_call_target="tpu_custom_call" | custom-call | flops 20132659200 | tf_op jit(solution)/shard_map/partial_grams/pallas_call | solution.py:206
  32.5 3.5 %partial_grams.10 = bf16[4,8,144,128]{3,2,1,0:T(8,128)(2,1)S(1)} custom-call(s32[32,26]{1,0:T(8,128)S(4)} %hold.1.requests_ref, bf16[192,144,128]{2,1,0:T(8,128)(2,1)S(1)} %get-tuple-element.64.left_ref, f32[192,128]{1,0:T(8,128)S(1)} %get-tuple-element.65.rinv_ref, s32[192,128]{1,0:T(8,128)S(1)} %get-tuple-element.66.obs_lon_ref, ...), custom_call_target="tpu_custom_call" | custom-call | flops 20132659200 | tf_op jit(solution)/shard_map/partial_grams/pallas_call | solution.py:206
  36.1 3.6 %partial_grams.11.refs_4_ = bf16[4,8,144,128]{3,2,1,0:T(8,128)(2,1)S(1)} custom-call(s32[32,26]{1,0:T(8,128)S(4)} %hold.1.requests_ref, bf16[192,144,128]{2,1,0:T(8,128)(2,1)S(1)} %get-tuple-element.64.left_ref, f32[192,128]{1,0:T(8,128)S(1)} %get-tuple-element.65.rinv_ref, s32[192,128]{1,0:T(8,128)S(1)} %get-tuple-element.66.obs_lon_ref, ...), custom_call_target="tpu_custom_call" | custom-call | flops 20132659200 | tf_op jit(solution)/shard_map/partial_grams/pallas_call | solution.py:206
  42.1 1.4 %collective-permute-start.5 = (bf16[3,4,144,128]{3,2,1,0:T(8,128)(2,1)S(1)}, bf16[3,4,144,128]{3,2,1,0:T(8,128)(2,1)S(1)}, u32[]{:S(2)}, u32[]{:S(2)}) collective-permute-start(bf16[3,4,144,128]{3,2,1,0:T(8,128)(2,1)S(1)} %get-tuple-element.79), channel_id=1, source_target_pairs={{0,1},{1,0},{2,3},{3,2},{4,5},{5,4},{6,7},{7,6},{8,9},{9,8},{10,11... | collective-permute-start | bytes 1327112 | tf_op jit(solution)/shard_map/ppermute | solution.py:366
  43.6 3.5 %partial_grams.12 = bf16[4,8,144,128]{3,2,1,0:T(8,128)(2,1)S(1)} custom-call(s32[32,26]{1,0:T(8,128)S(4)} %hold.1.requests_ref, bf16[192,144,128]{2,1,0:T(8,128)(2,1)S(1)} %get-tuple-element.64.left_ref, f32[192,128]{1,0:T(8,128)S(1)} %get-tuple-element.65.rinv_ref, s32[192,128]{1,0:T(8,128)S(1)} %get-tuple-element.66.obs_lon_ref, ...), custom_call_target="tpu_custom_call" | custom-call | flops 20132659200 | tf_op jit(solution)/shard_map/partial_grams/pallas_call | solution.py:206
  47.2 3.5 %partial_grams.13.refs_6_ = bf16[4,8,144,128]{3,2,1,0:T(8,128)(2,1)S(1)} custom-call(s32[32,26]{1,0:T(8,128)S(4)} %hold.1.requests_ref, bf16[192,144,128]{2,1,0:T(8,128)(2,1)S(1)} %get-tuple-element.64.left_ref, f32[192,128]{1,0:T(8,128)S(1)} %get-tuple-element.65.rinv_ref, s32[192,128]{1,0:T(8,128)S(1)} %get-tuple-element.66.obs_lon_ref, ...), custom_call_target="tpu_custom_call" | custom-call | flops 20132659200 | tf_op jit(solution)/shard_map/partial_grams/pallas_call | solution.py:206
  50.7 2.3 %collective-permute-done.4.refs_1_ = bf16[3,4,144,128]{3,2,1,0:T(8,128)(2,1)S(1)} collective-permute-done((bf16[3,4,144,128]{3,2,1,0:T(8,128)(2,1)S(1)}, bf16[3,4,144,128]{3,2,1,0:T(8,128)(2,1)S(1)}, u32[]{:S(2)}, u32[]{:S(2)}) %collective-permute-start.4) | collective-permute-done | bytes 442400 | tf_op jit(solution)/shard_map/ppermute | solution.py:366
  55.9 1.4 %collective-permute-start.8 = (bf16[3,4,144,128]{3,2,1,0:T(8,128)(2,1)S(1)}, bf16[3,4,144,128]{3,2,1,0:T(8,128)(2,1)S(1)}, u32[]{:S(2)}, u32[]{:S(2)}) collective-permute-start(bf16[3,4,144,128]{3,2,1,0:T(8,128)(2,1)S(1)} %get-tuple-element.87), channel_id=1, source_target_pairs={{0,1},{1,0},{2,3},{3,2},{4,5},{5,4},{6,7},{7,6},{8,9},{9,8},{10,11... | collective-permute-start | bytes 1327112 | tf_op jit(solution)/shard_map/ppermute | solution.py:366
  57.3 3.5 %partial_grams.14 = bf16[4,8,144,128]{3,2,1,0:T(8,128)(2,1)S(1)} custom-call(s32[32,26]{1,0:T(8,128)S(4)} %hold.1.requests_ref, bf16[192,144,128]{2,1,0:T(8,128)(2,1)S(1)} %get-tuple-element.64.left_ref, f32[192,128]{1,0:T(8,128)S(1)} %get-tuple-element.65.rinv_ref, s32[192,128]{1,0:T(8,128)S(1)} %get-tuple-element.66.obs_lon_ref, ...), custom_call_target="tpu_custom_call" | custom-call | flops 20132659200 | tf_op jit(solution)/shard_map/partial_grams/pallas_call | solution.py:206
  60.9 3.6 %partial_grams.15.refs_6_ = bf16[4,8,144,128]{3,2,1,0:T(8,128)(2,1)S(1)} custom-call(s32[32,26]{1,0:T(8,128)S(4)} %hold.1.requests_ref, bf16[192,144,128]{2,1,0:T(8,128)(2,1)S(1)} %get-tuple-element.64.left_ref, f32[192,128]{1,0:T(8,128)S(1)} %get-tuple-element.65.rinv_ref, s32[192,128]{1,0:T(8,128)S(1)} %get-tuple-element.66.obs_lon_ref, ...), custom_call_target="tpu_custom_call" | custom-call | flops 20132659200 | tf_op jit(solution)/shard_map/partial_grams/pallas_call | solution.py:206
  64.5 1.3 %collective-permute-done.7.refs_1_ = bf16[3,4,144,128]{3,2,1,0:T(8,128)(2,1)S(1)} collective-permute-done((bf16[3,4,144,128]{3,2,1,0:T(8,128)(2,1)S(1)}, bf16[3,4,144,128]{3,2,1,0:T(8,128)(2,1)S(1)}, u32[]{:S(2)}, u32[]{:S(2)}) %collective-permute-start.7) | collective-permute-done | bytes 442400 | tf_op jit(solution)/shard_map/ppermute | solution.py:366
  66.6 1.4 %collective-permute-start.13 = (bf16[2,4,144,128]{3,2,1,0:T(8,128)(2,1)S(1)}, bf16[2,4,144,128]{3,2,1,0:T(8,128)(2,1)S(1)}, u32[]{:S(2)}, u32[]{:S(2)}) collective-permute-start(bf16[2,4,144,128]{3,2,1,0:T(8,128)(2,1)S(1)} %get-tuple-element.100), channel_id=1, source_target_pairs={{0,1},{1,0},{2,3},{3,2},{4,5},{5,4},{6,7},{7,6},{8,9},{9,8},{10,11... | collective-permute-start | bytes 884744 | tf_op jit(solution)/shard_map/ppermute | solution.py:366
  68.0 1.4 %collective-permute-start.14 = (bf16[2,4,144,128]{3,2,1,0:T(8,128)(2,1)S(1)}, bf16[2,4,144,128]{3,2,1,0:T(8,128)(2,1)S(1)}, u32[]{:S(2)}, u32[]{:S(2)}) collective-permute-start(bf16[2,4,144,128]{3,2,1,0:T(8,128)(2,1)S(1)} %get-tuple-element.102), channel_id=1, source_target_pairs={{0,16},{8,24},{16,0},{24,8},{1,17},{9,25},{17,1},{25,9},{2,18},{10... | collective-permute-start | bytes 884744 | tf_op jit(solution)/shard_map/ppermute | solution.py:366
  70.7 1.4 %collective-permute-start.15 = (bf16[1,8,144,128]{3,2,1,0:T(8,128)(2,1)S(1)}, bf16[1,8,144,128]{3,2,1,0:T(8,128)(2,1)S(1)}, u32[]{:S(2)}, u32[]{:S(2)}) collective-permute-start(bf16[1,8,144,128]{3,2,1,0:T(8,128)(2,1)S(1)} %get-tuple-element.104), channel_id=1, source_target_pairs={{0,4},{1,5},{2,6},{3,7},{4,0},{5,1},{6,2},{7,3},{8,12},{9,13},{10,... | collective-permute-start | bytes 884744 | tf_op jit(solution)/shard_map/ppermute | solution.py:366
  72.2 5.8 %collective-permute-done.11.refs_1_ = bf16[1,4,144,128]{3,2,1,0:T(8,128)(2,1)S(1)} collective-permute-done((bf16[1,4,144,128]{3,2,1,0:T(8,128)(2,1)S(1)}, bf16[1,4,144,128]{3,2,1,0:T(8,128)(2,1)S(1)}, u32[]{:S(2)}, u32[]{:S(2)}) %collective-permute-start.11) | collective-permute-done | bytes 147488 | tf_op jit(solution)/shard_map/ppermute | solution.py:366
  78.9 1.1 %collective-permute-start.17 = (bf16[1,4,144,128]{3,2,1,0:T(8,128)(2,1)S(1)}, bf16[1,4,144,128]{3,2,1,0:T(8,128)(2,1)S(1)}, u32[]{:S(2)}, u32[]{:S(2)}) collective-permute-start(bf16[1,4,144,128]{3,2,1,0:T(8,128)(2,1)S(1)} %get-tuple-element.108), channel_id=1, source_target_pairs={{0,16},{8,24},{16,0},{24,8},{1,17},{9,25},{17,1},{25,9},{2,18},{10... | collective-permute-start | bytes 442376 | tf_op jit(solution)/shard_map/ppermute | solution.py:366
  80.0 1.5 %collective-permute-start.18 = (bf16[1,4,144,128]{3,2,1,0:T(8,128)(2,1)S(1)}, bf16[1,4,144,128]{3,2,1,0:T(8,128)(2,1)S(1)}, u32[]{:S(2)}, u32[]{:S(2)}) collective-permute-start(bf16[1,4,144,128]{3,2,1,0:T(8,128)(2,1)S(1)} %get-tuple-element.110), channel_id=1, source_target_pairs={{0,1},{1,0},{2,3},{3,2},{4,5},{5,4},{6,7},{7,6},{8,9},{9,8},{10,11... | collective-permute-start | bytes 442376 | tf_op jit(solution)/shard_map/ppermute | solution.py:366
  81.6 3.1 %collective-permute-done.15.refs_1_ = bf16[1,8,144,128]{3,2,1,0:T(8,128)(2,1)S(1)} collective-permute-done((bf16[1,8,144,128]{3,2,1,0:T(8,128)(2,1)S(1)}, bf16[1,8,144,128]{3,2,1,0:T(8,128)(2,1)S(1)}, u32[]{:S(2)}, u32[]{:S(2)}) %collective-permute-start.15) | collective-permute-done | bytes 294944 | tf_op jit(solution)/shard_map/ppermute | solution.py:366
  85.3 5.1 %collective-permute-done.16.refs_2_ = bf16[1,8,144,128]{3,2,1,0:T(8,128)(2,1)S(1)} collective-permute-done((bf16[1,8,144,128]{3,2,1,0:T(8,128)(2,1)S(1)}, bf16[1,8,144,128]{3,2,1,0:T(8,128)(2,1)S(1)}, u32[]{:S(2)}, u32[]{:S(2)}) %collective-permute-start.16) | collective-permute-done | bytes 294944 | tf_op jit(solution)/shard_map/ppermute | solution.py:366
  90.4 10.4 %analysis.1 = f32[16,6,128,256]{3,2,1,0:T(8,128)} custom-call(bf16[1,8,144,128]{3,2,1,0:T(8,128)(2,1)S(1)} %collective-permute-done.10.refs_0_, bf16[1,8,144,128]{3,2,1,0:T(8,128)(2,1)S(1)} %collective-permute-done.15.refs_1_, bf16[1,8,144,128]{3,2,1,0:T(8,128)(2,1)S(1)} %collective-permute-done.16.refs_2_, ...), custom_call_target="tpu_custom_call" | custom-call | tf_op jit(solution)/shard_map/analysis/pallas_call | solution.py:344
  (59 shorter events, 16.9 us)
Async XLA Ops:
  4.6 14.3 %all-to-all-start = ((s32[32,1,25]{2,1,0:T(1,128)}), s32[32,1,25]{2,1,0:T(1,128)S(1)}, u32[]{:S(2)}, u32[]{:S(2)}) async-start(s32[32,1,25]{2,1,0:T(1,128)} %bitcast.2), calls=%async_computation | async-start | bytes 32768 | tf_op jit(solution)/shard_map/all_to_all | solution.py:382
  27.3 3.6 %collective-permute-start = (bf16[4,8,144,128]{3,2,1,0:T(8,128)(2,1)S(1)}, bf16[4,8,144,128]{3,2,1,0:T(8,128)(2,1)S(1)}, u32[]{:S(2)}, u32[]{:S(2)}) collective-permute-start(bf16[4,8,144,128]{3,2,1,0:T(8,128)(2,1)S(1)} %partial_grams.8), channel_id=1, source_target_pairs={{0,8},{8,0},{16,24},{24,16},{1,9},{9,1},{17,25},{25,17},{2,10},{10... | collective-permute-start | bytes 3538952 | tf_op jit(solution)/shard_map/ppermute | solution.py:366
  31.2 9.5 %collective-permute-start.1 = (bf16[2,4,144,128]{3,2,1,0:T(8,128)(2,1)S(1)}, bf16[2,4,144,128]{3,2,1,0:T(8,128)(2,1)S(1)}, u32[]{:S(2)}, u32[]{:S(2)}) collective-permute-start(bf16[2,4,144,128]{3,2,1,0:T(8,128)(2,1)S(1)} %get-tuple-element.71), channel_id=1, source_target_pairs={{0,1},{1,0},{2,3},{3,2},{4,5},{5,4},{6,7},{7,6},{8,9},{9,8},{10,11... | collective-permute-start | bytes 884744 | tf_op jit(solution)/shard_map/ppermute | solution.py:366
  31.9 9.1 %collective-permute-start.2 = (bf16[2,4,144,128]{3,2,1,0:T(8,128)(2,1)S(1)}, bf16[2,4,144,128]{3,2,1,0:T(8,128)(2,1)S(1)}, u32[]{:S(2)}, u32[]{:S(2)}) collective-permute-start(bf16[2,4,144,128]{3,2,1,0:T(8,128)(2,1)S(1)} %get-tuple-element.73), channel_id=1, source_target_pairs={{0,16},{8,24},{16,0},{24,8},{1,17},{9,25},{17,1},{25,9},{2,18},{10... | collective-permute-start | bytes 884744 | tf_op jit(solution)/shard_map/ppermute | solution.py:366
  36.0 5.0 %collective-permute-start.3 = (bf16[4,8,144,128]{3,2,1,0:T(8,128)(2,1)S(1)}, bf16[4,8,144,128]{3,2,1,0:T(8,128)(2,1)S(1)}, u32[]{:S(2)}, u32[]{:S(2)}) collective-permute-start(bf16[4,8,144,128]{3,2,1,0:T(8,128)(2,1)S(1)} %partial_grams.10), channel_id=1, source_target_pairs={{0,8},{8,0},{16,24},{24,16},{1,9},{9,1},{17,25},{25,17},{2,10},{10... | collective-permute-start | bytes 3538952 | tf_op jit(solution)/shard_map/ppermute | solution.py:366
  41.5 11.5 %collective-permute-start.4 = (bf16[3,4,144,128]{3,2,1,0:T(8,128)(2,1)S(1)}, bf16[3,4,144,128]{3,2,1,0:T(8,128)(2,1)S(1)}, u32[]{:S(2)}, u32[]{:S(2)}) collective-permute-start(bf16[3,4,144,128]{3,2,1,0:T(8,128)(2,1)S(1)} %get-tuple-element.77), channel_id=1, source_target_pairs={{0,16},{8,24},{16,0},{24,8},{1,17},{9,25},{17,1},{25,9},{2,18},{10... | collective-permute-start | bytes 1327112 | tf_op jit(solution)/shard_map/ppermute | solution.py:366
  42.1 11.8 %collective-permute-start.5 = (bf16[3,4,144,128]{3,2,1,0:T(8,128)(2,1)S(1)}, bf16[3,4,144,128]{3,2,1,0:T(8,128)(2,1)S(1)}, u32[]{:S(2)}, u32[]{:S(2)}) collective-permute-start(bf16[3,4,144,128]{3,2,1,0:T(8,128)(2,1)S(1)} %get-tuple-element.79), channel_id=1, source_target_pairs={{0,1},{1,0},{2,3},{3,2},{4,5},{5,4},{6,7},{7,6},{8,9},{9,8},{10,11... | collective-permute-start | bytes 1327112 | tf_op jit(solution)/shard_map/ppermute | solution.py:366
  47.1 6.8 %collective-permute-start.6 = (bf16[4,8,144,128]{3,2,1,0:T(8,128)(2,1)S(1)}, bf16[4,8,144,128]{3,2,1,0:T(8,128)(2,1)S(1)}, u32[]{:S(2)}, u32[]{:S(2)}) collective-permute-start(bf16[4,8,144,128]{3,2,1,0:T(8,128)(2,1)S(1)} %partial_grams.12), channel_id=1, source_target_pairs={{0,8},{8,0},{16,24},{24,16},{1,9},{9,1},{17,25},{25,17},{2,10},{10... | collective-permute-start | bytes 3538952 | tf_op jit(solution)/shard_map/ppermute | solution.py:366
  54.4 16.3 %collective-permute-start.10 = (bf16[1,8,144,128]{3,2,1,0:T(8,128)(2,1)S(1)}, bf16[1,8,144,128]{3,2,1,0:T(8,128)(2,1)S(1)}, u32[]{:S(2)}, u32[]{:S(2)}) collective-permute-start(bf16[1,8,144,128]{3,2,1,0:T(8,128)(2,1)S(1)} %get-tuple-element.90), channel_id=1, source_target_pairs={{0,6},{1,7},{2,4},{3,5},{4,2},{5,3},{6,0},{7,1},{8,14},{9,15},{10,... | collective-permute-start | bytes 884744 | tf_op jit(solution)/shard_map/ppermute | solution.py:366
  55.1 10.7 %collective-permute-start.7 = (bf16[3,4,144,128]{3,2,1,0:T(8,128)(2,1)S(1)}, bf16[3,4,144,128]{3,2,1,0:T(8,128)(2,1)S(1)}, u32[]{:S(2)}, u32[]{:S(2)}) collective-permute-start(bf16[3,4,144,128]{3,2,1,0:T(8,128)(2,1)S(1)} %get-tuple-element.85), channel_id=1, source_target_pairs={{0,16},{8,24},{16,0},{24,8},{1,17},{9,25},{17,1},{25,9},{2,18},{10... | collective-permute-start | bytes 1327112 | tf_op jit(solution)/shard_map/ppermute | solution.py:366
  55.9 10.2 %collective-permute-start.8 = (bf16[3,4,144,128]{3,2,1,0:T(8,128)(2,1)S(1)}, bf16[3,4,144,128]{3,2,1,0:T(8,128)(2,1)S(1)}, u32[]{:S(2)}, u32[]{:S(2)}) collective-permute-start(bf16[3,4,144,128]{3,2,1,0:T(8,128)(2,1)S(1)} %get-tuple-element.87), channel_id=1, source_target_pairs={{0,1},{1,0},{2,3},{3,2},{4,5},{5,4},{6,7},{7,6},{8,9},{9,8},{10,11... | collective-permute-start | bytes 1327112 | tf_op jit(solution)/shard_map/ppermute | solution.py:366
  57.3 33.1 %slice-start = ((s8[6291456]{0:T(1024)(128)(4,1)}), s8[4194304]{0:T(1024)(128)(4,1)S(1)}, s32[]{:S(2)}) async-start(s8[6291456]{0:T(1024)(128)(4,1)} %bitcast.8), calls=%async_computation.1 | async-start | bytes 8388608
  60.8 29.6 %slice-start.1 = ((s8[6291456]{0:T(1024)(128)(4,1)}), s8[2097152]{0:T(1024)(128)(4,1)S(1)}, s32[]{:S(2)}) async-start(s8[6291456]{0:T(1024)(128)(4,1)} %bitcast.8), calls=%async_computation.2 | async-start | bytes 4194304
  60.8 5.3 %collective-permute-start.9 = (bf16[4,8,144,128]{3,2,1,0:T(8,128)(2,1)S(1)}, bf16[4,8,144,128]{3,2,1,0:T(8,128)(2,1)S(1)}, u32[]{:S(2)}, u32[]{:S(2)}) collective-permute-start(bf16[4,8,144,128]{3,2,1,0:T(8,128)(2,1)S(1)} %partial_grams.14), channel_id=1, source_target_pairs={{0,8},{8,0},{16,24},{24,16},{1,9},{9,1},{17,25},{25,17},{2,10},{10... | collective-permute-start | bytes 3538952 | tf_op jit(solution)/shard_map/ppermute | solution.py:366
  66.1 15.5 %copy-start = (f32[8,2,6,256]{3,1,2,0:T(2,128)S(1)}, f32[8,2,6,256]{3,1,2,0:T(2,128)}, u32[]{:S(2)}) copy-start(f32[8,2,6,256]{3,1,2,0:T(2,128)} %param.10) | copy-start | bytes 294916
  66.6 11.4 %collective-permute-start.13 = (bf16[2,4,144,128]{3,2,1,0:T(8,128)(2,1)S(1)}, bf16[2,4,144,128]{3,2,1,0:T(8,128)(2,1)S(1)}, u32[]{:S(2)}, u32[]{:S(2)}) collective-permute-start(bf16[2,4,144,128]{3,2,1,0:T(8,128)(2,1)S(1)} %get-tuple-element.100), channel_id=1, source_target_pairs={{0,1},{1,0},{2,3},{3,2},{4,5},{5,4},{6,7},{7,6},{8,9},{9,8},{10,11... | collective-permute-start | bytes 884744 | tf_op jit(solution)/shard_map/ppermute | solution.py:366
  68.0 10.0 %collective-permute-start.14 = (bf16[2,4,144,128]{3,2,1,0:T(8,128)(2,1)S(1)}, bf16[2,4,144,128]{3,2,1,0:T(8,128)(2,1)S(1)}, u32[]{:S(2)}, u32[]{:S(2)}) collective-permute-start(bf16[2,4,144,128]{3,2,1,0:T(8,128)(2,1)S(1)} %get-tuple-element.102), channel_id=1, source_target_pairs={{0,16},{8,24},{16,0},{24,8},{1,17},{9,25},{17,1},{25,9},{2,18},{10... | collective-permute-start | bytes 884744 | tf_op jit(solution)/shard_map/ppermute | solution.py:366
  69.4 8.6 %collective-permute-start.11 = (bf16[1,4,144,128]{3,2,1,0:T(8,128)(2,1)S(1)}, bf16[1,4,144,128]{3,2,1,0:T(8,128)(2,1)S(1)}, u32[]{:S(2)}, u32[]{:S(2)}) collective-permute-start(bf16[1,4,144,128]{3,2,1,0:T(8,128)(2,1)S(1)} %get-tuple-element.96), channel_id=1, source_target_pairs={{0,16},{8,24},{16,0},{24,8},{1,17},{9,25},{17,1},{25,9},{2,18},{10... | collective-permute-start | bytes 442376 | tf_op jit(solution)/shard_map/ppermute | solution.py:366
  70.0 8.0 %collective-permute-start.12 = (bf16[1,4,144,128]{3,2,1,0:T(8,128)(2,1)S(1)}, bf16[1,4,144,128]{3,2,1,0:T(8,128)(2,1)S(1)}, u32[]{:S(2)}, u32[]{:S(2)}) collective-permute-start(bf16[1,4,144,128]{3,2,1,0:T(8,128)(2,1)S(1)} %get-tuple-element.98), channel_id=1, source_target_pairs={{0,1},{1,0},{2,3},{3,2},{4,5},{5,4},{6,7},{7,6},{8,9},{9,8},{10,11... | collective-permute-start | bytes 442376 | tf_op jit(solution)/shard_map/ppermute | solution.py:366
  70.7 14.0 %collective-permute-start.15 = (bf16[1,8,144,128]{3,2,1,0:T(8,128)(2,1)S(1)}, bf16[1,8,144,128]{3,2,1,0:T(8,128)(2,1)S(1)}, u32[]{:S(2)}, u32[]{:S(2)}) collective-permute-start(bf16[1,8,144,128]{3,2,1,0:T(8,128)(2,1)S(1)} %get-tuple-element.104), channel_id=1, source_target_pairs={{0,4},{1,5},{2,6},{3,7},{4,0},{5,1},{6,2},{7,3},{8,12},{9,13},{10,... | collective-permute-start | bytes 884744 | tf_op jit(solution)/shard_map/ppermute | solution.py:366
  78.2 12.1 %collective-permute-start.16 = (bf16[1,8,144,128]{3,2,1,0:T(8,128)(2,1)S(1)}, bf16[1,8,144,128]{3,2,1,0:T(8,128)(2,1)S(1)}, u32[]{:S(2)}, u32[]{:S(2)}) collective-permute-start(bf16[1,8,144,128]{3,2,1,0:T(8,128)(2,1)S(1)} %get-tuple-element.106), channel_id=1, source_target_pairs={{0,2},{1,3},{2,0},{3,1},{4,6},{5,7},{6,4},{7,5},{8,10},{9,11},{10,... | collective-permute-start | bytes 884744 | tf_op jit(solution)/shard_map/ppermute | solution.py:366
  78.9 5.8 %collective-permute-start.17 = (bf16[1,4,144,128]{3,2,1,0:T(8,128)(2,1)S(1)}, bf16[1,4,144,128]{3,2,1,0:T(8,128)(2,1)S(1)}, u32[]{:S(2)}, u32[]{:S(2)}) collective-permute-start(bf16[1,4,144,128]{3,2,1,0:T(8,128)(2,1)S(1)} %get-tuple-element.108), channel_id=1, source_target_pairs={{0,16},{8,24},{16,0},{24,8},{1,17},{9,25},{17,1},{25,9},{2,18},{10... | collective-permute-start | bytes 442376 | tf_op jit(solution)/shard_map/ppermute | solution.py:366
  80.0 5.1 %collective-permute-start.18 = (bf16[1,4,144,128]{3,2,1,0:T(8,128)(2,1)S(1)}, bf16[1,4,144,128]{3,2,1,0:T(8,128)(2,1)S(1)}, u32[]{:S(2)}, u32[]{:S(2)}) collective-permute-start(bf16[1,4,144,128]{3,2,1,0:T(8,128)(2,1)S(1)} %get-tuple-element.110), channel_id=1, source_target_pairs={{0,1},{1,0},{2,3},{3,2},{4,5},{5,4},{6,7},{7,6},{8,9},{9,8},{10,11... | collective-permute-start | bytes 442376 | tf_op jit(solution)/shard_map/ppermute | solution.py:366

commit v7 on v6

--- a/solution.py
+++ b/solution.py
@@ -22,23 +22,21 @@
 
 
 def request_table(block_list, block_count, holders, held_blocks):
-    patches, length = block_list.shape
-    slots = patches * length
+    length = block_list.shape[2]
+    slots = block_list.size
     per_owner = slots // holders
-    wanted = block_list.reshape(slots)
-    used = (lax.broadcasted_iota(jnp.int32, (patches, length), 1) < block_count[:, None]).reshape(
-        slots
-    )
-    holder = jnp.where(used, wanted // held_blocks, holders)
+    used = lax.broadcasted_iota(jnp.int32, block_list.shape, 2) < block_count[:, :, None]
+    wanted = jnp.where(used, block_list, -1).reshape(slots)
+    holder = jnp.where(wanted < 0, holders, lax.div(wanted, held_blocks))
     order = jnp.arange(slots)
     before = (holder[:, None] == holder[None, :]) & (order[None, :] < order[:, None])
     rank = jnp.sum(before.astype(jnp.int32), axis=1)
-    code = (order // length) * held_blocks + wanted % held_blocks
-    place = holder * per_owner + rank
-    hit = (place[None, :] == jnp.arange(holders * per_owner)[:, None]) & used[None, :]
-    table = jnp.sum(jnp.where(hit, code[None, :], 0), axis=1).reshape(holders, per_owner)
-    number = jnp.sum((holder[None, :] == jnp.arange(holders)[:, None]).astype(jnp.int32), axis=1)
-    return jnp.concatenate([table, number[:, None]], axis=1)
+    code = lax.div(order, length) * held_blocks + lax.rem(wanted, held_blocks)
+    place = lax.broadcasted_iota(jnp.int32, (holders, per_owner + 2, 1), 1)
+    asked = lax.broadcasted_iota(jnp.int32, (holders, per_owner + 2, 1), 0)
+    entry = jnp.where(place == per_owner, 1, jnp.where(rank == place, code, 0))
+    table = jnp.sum(jnp.where(holder == asked, entry, 0), axis=2)
+    return table + jnp.where(place == per_owner + 1, asked, 0)[:, :, 0]
 
 
 def stage_kernel(
@@ -194,6 +192,7 @@
         in_specs=[pl.BlockSpec(memory_space=pl.ANY)],
         out_specs=pl.BlockSpec(memory_space=pltpu.SMEM),
         scratch_shapes=[pltpu.SemaphoreType.DMA(())],
+        compiler_params=pltpu.CompilerParams(vmem_limit_bytes=2**20),
         name="hold",
     )(table)
 
@@ -376,13 +375,9 @@
     length = block_list.shape[2]
     held, _, block_obs = obs_anom.shape
     per_owner = patches * length // holders
-    table = request_table(
-        block_list.reshape(patches, length), block_count.reshape(patches), holders, held
-    )
+    table = request_table(block_list, block_count, holders, held)
     requests = lax.all_to_all(table, ("lon", "lat"), split_axis=0, concat_axis=0, tiled=True)
 
-    me = lax.axis_index(("lon", "lat")).astype(jnp.int32)
-    requests = jnp.concatenate([requests, jnp.full((holders, 1), me)], axis=1)
     requests, observed = lax.optimization_barrier(
         (requests, (obs_anom, innov, obs_rinv, obs_lon, obs_lat))
     )

time: 101 us -> 98.4 us (0.974)
  blocking collectives: 0 us -> 14.2 us
  starting transfers between devices: 22.6 us -> 15.3 us
  waiting for transfers between devices: 27.8 us -> 20.6 us
  other arithmetic: 3.23 us -> 1.87 us
    all_to_all x0 -> x1, blocking collectives: none -> 14.2 us  [on_device(): lax.all_to_all(table, ('lon', 'lat'), split_axis=0, concat_axis=0, tiled=...]
    all_to_all x1 -> x0, starting transfers between devices: 7.3 us -> none  [on_device(): lax.all_to_all(table, ('lon', 'lat'), split_axis=0, concat_axis=0, tiled=...]
    all_to_all x1 -> x0, waiting for transfers between devices: 7.03 us -> none  [on_device(): lax.all_to_all(table, ('lon', 'lat'), split_axis=0, concat_axis=0, tiled=...]
  transfers between devices with their start and end apart: 20 -> 19, of which waited for: 11 -> 10; matrix products, arithmetic and copies ran while one was open for 0% -> 0% of each run, Pallas kernels for 25% -> 26%
where the time goes in v7:
time: 98.4 us; the launch traced here: 98.1 us
  Pallas kernels  44.9 us (46%)
  waiting for transfers between devices  20.6 us (21%)
  starting transfers between devices  15.3 us (16%)
  blocking collectives  14.2 us (14%)
  other arithmetic  1.87 us (2%)
  local copies, waits for them, and re-layouts  1.02 us (1%)
    pallas_call x8, Pallas kernels, partial_grams(): pl.pallas_call(functools.partial(gram_kernel, sizes, far, core), out_shap...  28.4 us
    ppermute x19, waiting for transfers between devices, swap(): return lax.ppermute(value, axis, [(i, i ^ flip) for i in range(size)])  20.6 us
    ppermute x19, starting transfers between devices, swap(): return lax.ppermute(value, axis, [(i, i ^ flip) for i in range(size)])  15.3 us
    all_to_all x1, blocking collectives, on_device(): lax.all_to_all(table, ('lon', 'lat'), split_axis=0, concat_axis=0, tiled=...  14.2 us
    pallas_call x1, Pallas kernels, analysis(): pl.pallas_call(functools.partial(analysis_kernel, len(parts), total_obs,...  10.4 us
    pallas_call x1, Pallas kernels, stage(): pl.pallas_call(functools.partial(stage_kernel, chunk), out_shape=[pltpu.V...  3.22 us
    pallas_call x6, Pallas kernels, add_all(): pl.pallas_call(functools.partial(add_kernel, len(arrays), size, jobs), ou...  2.02 us
  transfers between devices with their start and end apart: 19, of which 10 were waited for; matrix products, arithmetic and copies ran while one was open for 0% of the time, Pallas kernels for 26%

profile of v7, /device:TPU:0, one launch (start us, length us, event | category | flops | bytes accessed | tf_op | source)
XLA Modules:
  0.0 98.1 jit_solution(16521292170705339514)
XLA Ops:
  2.9 14.2 %all_to_all.9 = s32[32,1,26]{2,1,0:T(1,128)S(1)} all-to-all(s32[32,1,26]{2,1,0:T(1,128)S(1)} %copy.15), channel_id=1, replica_groups=mesh['lon'=4,'lat'=8] {'lon','lat'}, dimensions={0} | all-to-all | bytes 6656 | tf_op jit(solution)/shard_map/all_to_all | solution.py:379
  17.9 3.2 %stage.1 = (bf16[192,144,128]{2,1,0:T(8,128)(2,1)S(1)}, f32[192,128]{1,0:T(8,128)S(1)}, s32[192,128]{1,0:T(8,128)S(1)}, s32[192,128]{1,0:T(8,128)S(1)}, f32[8,128]{1,0:T(8,128)S(1)}) custom-call(bf16[192,128,128]{2,1,0:T(8,128)(2,1)} %anom_hbm, f32[192,128]{1,0:T(8,128)} %innov_hbm, f32[192,128]{1,0:T(8,128)} %rinv_hbm, s32[192,128]{1,0:T(8,128)} %lon_hbm, ...), custom_call_target="tpu_custom_call" | custom-call | bytes 12582912 | tf_op jit(solution)/shard_map/stage/pallas_call | solution.py:96
  21.2 3.6 %partial_grams.8 = bf16[4,8,144,128]{3,2,1,0:T(8,128)(2,1)S(1)} custom-call(s32[32,26]{1,0:T(8,128)S(4)} %hold.1.requests_ref, bf16[192,144,128]{2,1,0:T(8,128)(2,1)S(1)} %get-tuple-element.64.left_ref, f32[192,128]{1,0:T(8,128)S(1)} %get-tuple-element.65.rinv_ref, s32[192,128]{1,0:T(8,128)S(1)} %get-tuple-element.66.obs_lon_ref, ...), custom_call_target="tpu_custom_call" | custom-call | flops 20132659200 | tf_op jit(solution)/shard_map/partial_grams/pallas_call | solution.py:205
  24.8 3.5 %partial_grams.9.refs_0_ = bf16[4,8,144,128]{3,2,1,0:T(8,128)(2,1)S(1)} custom-call(s32[32,26]{1,0:T(8,128)S(4)} %hold.1.requests_ref, bf16[192,144,128]{2,1,0:T(8,128)(2,1)S(1)} %get-tuple-element.64.left_ref, f32[192,128]{1,0:T(8,128)S(1)} %get-tuple-element.65.rinv_ref, s32[192,128]{1,0:T(8,128)S(1)} %get-tuple-element.66.obs_lon_ref, ...), custom_call_target="tpu_custom_call" | custom-call | flops 20132659200 | tf_op jit(solution)/shard_map/partial_grams/pallas_call | solution.py:205
  29.9 3.5 %partial_grams.10 = bf16[4,8,144,128]{3,2,1,0:T(8,128)(2,1)S(1)} custom-call(s32[32,26]{1,0:T(8,128)S(4)} %hold.1.requests_ref, bf16[192,144,128]{2,1,0:T(8,128)(2,1)S(1)} %get-tuple-element.64.left_ref, f32[192,128]{1,0:T(8,128)S(1)} %get-tuple-element.65.rinv_ref, s32[192,128]{1,0:T(8,128)S(1)} %get-tuple-element.66.obs_lon_ref, ...), custom_call_target="tpu_custom_call" | custom-call | flops 20132659200 | tf_op jit(solution)/shard_map/partial_grams/pallas_call | solution.py:205
  33.6 3.6 %partial_grams.11.refs_4_ = bf16[4,8,144,128]{3,2,1,0:T(8,128)(2,1)S(1)} custom-call(s32[32,26]{1,0:T(8,128)S(4)} %hold.1.requests_ref, bf16[192,144,128]{2,1,0:T(8,128)(2,1)S(1)} %get-tuple-element.64.left_ref, f32[192,128]{1,0:T(8,128)S(1)} %get-tuple-element.65.rinv_ref, s32[192,128]{1,0:T(8,128)S(1)} %get-tuple-element.66.obs_lon_ref, ...), custom_call_target="tpu_custom_call" | custom-call | flops 20132659200 | tf_op jit(solution)/shard_map/partial_grams/pallas_call | solution.py:205
  37.1 1.0 %collective-permute-done.1.refs_1_ = bf16[2,4,144,128]{3,2,1,0:T(8,128)(2,1)S(1)} collective-permute-done((bf16[2,4,144,128]{3,2,1,0:T(8,128)(2,1)S(1)}, bf16[2,4,144,128]{3,2,1,0:T(8,128)(2,1)S(1)}, u32[]{:S(2)}, u32[]{:S(2)}) %collective-permute-start.1) | collective-permute-done | bytes 294944 | tf_op jit(solution)/shard_map/ppermute | solution.py:365
  39.5 1.4 %collective-permute-start.5 = (bf16[3,4,144,128]{3,2,1,0:T(8,128)(2,1)S(1)}, bf16[3,4,144,128]{3,2,1,0:T(8,128)(2,1)S(1)}, u32[]{:S(2)}, u32[]{:S(2)}) collective-permute-start(bf16[3,4,144,128]{3,2,1,0:T(8,128)(2,1)S(1)} %get-tuple-element.79), channel_id=1, source_target_pairs={{0,1},{1,0},{2,3},{3,2},{4,5},{5,4},{6,7},{7,6},{8,9},{9,8},{10,11... | collective-permute-start | bytes 1327112 | tf_op jit(solution)/shard_map/ppermute | solution.py:365
  41.0 3.5 %partial_grams.12 = bf16[4,8,144,128]{3,2,1,0:T(8,128)(2,1)S(1)} custom-call(s32[32,26]{1,0:T(8,128)S(4)} %hold.1.requests_ref, bf16[192,144,128]{2,1,0:T(8,128)(2,1)S(1)} %get-tuple-element.64.left_ref, f32[192,128]{1,0:T(8,128)S(1)} %get-tuple-element.65.rinv_ref, s32[192,128]{1,0:T(8,128)S(1)} %get-tuple-element.66.obs_lon_ref, ...), custom_call_target="tpu_custom_call" | custom-call | flops 20132659200 | tf_op jit(solution)/shard_map/partial_grams/pallas_call | solution.py:205
  44.6 3.6 %partial_grams.13.refs_6_ = bf16[4,8,144,128]{3,2,1,0:T(8,128)(2,1)S(1)} custom-call(s32[32,26]{1,0:T(8,128)S(4)} %hold.1.requests_ref, bf16[192,144,128]{2,1,0:T(8,128)(2,1)S(1)} %get-tuple-element.64.left_ref, f32[192,128]{1,0:T(8,128)S(1)} %get-tuple-element.65.rinv_ref, s32[192,128]{1,0:T(8,128)S(1)} %get-tuple-element.66.obs_lon_ref, ...), custom_call_target="tpu_custom_call" | custom-call | flops 20132659200 | tf_op jit(solution)/shard_map/partial_grams/pallas_call | solution.py:205
  48.1 2.3 %collective-permute-done.4.refs_1_ = bf16[3,4,144,128]{3,2,1,0:T(8,128)(2,1)S(1)} collective-permute-done((bf16[3,4,144,128]{3,2,1,0:T(8,128)(2,1)S(1)}, bf16[3,4,144,128]{3,2,1,0:T(8,128)(2,1)S(1)}, u32[]{:S(2)}, u32[]{:S(2)}) %collective-permute-start.4) | collective-permute-done | bytes 442400 | tf_op jit(solution)/shard_map/ppermute | solution.py:365
  53.3 1.4 %collective-permute-start.8 = (bf16[3,4,144,128]{3,2,1,0:T(8,128)(2,1)S(1)}, bf16[3,4,144,128]{3,2,1,0:T(8,128)(2,1)S(1)}, u32[]{:S(2)}, u32[]{:S(2)}) collective-permute-start(bf16[3,4,144,128]{3,2,1,0:T(8,128)(2,1)S(1)} %get-tuple-element.87), channel_id=1, source_target_pairs={{0,1},{1,0},{2,3},{3,2},{4,5},{5,4},{6,7},{7,6},{8,9},{9,8},{10,11... | collective-permute-start | bytes 1327112 | tf_op jit(solution)/shard_map/ppermute | solution.py:365
  54.6 3.5 %partial_grams.14 = bf16[4,8,144,128]{3,2,1,0:T(8,128)(2,1)S(1)} custom-call(s32[32,26]{1,0:T(8,128)S(4)} %hold.1.requests_ref, bf16[192,144,128]{2,1,0:T(8,128)(2,1)S(1)} %get-tuple-element.64.left_ref, f32[192,128]{1,0:T(8,128)S(1)} %get-tuple-element.65.rinv_ref, s32[192,128]{1,0:T(8,128)S(1)} %get-tuple-element.66.obs_lon_ref, ...), custom_call_target="tpu_custom_call" | custom-call | flops 20132659200 | tf_op jit(solution)/shard_map/partial_grams/pallas_call | solution.py:205
  58.3 3.6 %partial_grams.15.refs_6_ = bf16[4,8,144,128]{3,2,1,0:T(8,128)(2,1)S(1)} custom-call(s32[32,26]{1,0:T(8,128)S(4)} %hold.1.requests_ref, bf16[192,144,128]{2,1,0:T(8,128)(2,1)S(1)} %get-tuple-element.64.left_ref, f32[192,128]{1,0:T(8,128)S(1)} %get-tuple-element.65.rinv_ref, s32[192,128]{1,0:T(8,128)S(1)} %get-tuple-element.66.obs_lon_ref, ...), custom_call_target="tpu_custom_call" | custom-call | flops 20132659200 | tf_op jit(solution)/shard_map/partial_grams/pallas_call | solution.py:205
  61.8 1.4 %collective-permute-done.7.refs_1_ = bf16[3,4,144,128]{3,2,1,0:T(8,128)(2,1)S(1)} collective-permute-done((bf16[3,4,144,128]{3,2,1,0:T(8,128)(2,1)S(1)}, bf16[3,4,144,128]{3,2,1,0:T(8,128)(2,1)S(1)}, u32[]{:S(2)}, u32[]{:S(2)}) %collective-permute-start.7) | collective-permute-done | bytes 442400 | tf_op jit(solution)/shard_map/ppermute | solution.py:365
  64.0 1.4 %collective-permute-start.13 = (bf16[2,4,144,128]{3,2,1,0:T(8,128)(2,1)S(1)}, bf16[2,4,144,128]{3,2,1,0:T(8,128)(2,1)S(1)}, u32[]{:S(2)}, u32[]{:S(2)}) collective-permute-start(bf16[2,4,144,128]{3,2,1,0:T(8,128)(2,1)S(1)} %get-tuple-element.100), channel_id=1, source_target_pairs={{0,1},{1,0},{2,3},{3,2},{4,5},{5,4},{6,7},{7,6},{8,9},{9,8},{10,11... | collective-permute-start | bytes 884744 | tf_op jit(solution)/shard_map/ppermute | solution.py:365
  65.4 1.4 %collective-permute-start.14 = (bf16[2,4,144,128]{3,2,1,0:T(8,128)(2,1)S(1)}, bf16[2,4,144,128]{3,2,1,0:T(8,128)(2,1)S(1)}, u32[]{:S(2)}, u32[]{:S(2)}) collective-permute-start(bf16[2,4,144,128]{3,2,1,0:T(8,128)(2,1)S(1)} %get-tuple-element.102), channel_id=1, source_target_pairs={{0,16},{8,24},{16,0},{24,8},{1,17},{9,25},{17,1},{25,9},{2,18},{10... | collective-permute-start | bytes 884744 | tf_op jit(solution)/shard_map/ppermute | solution.py:365
  68.2 1.4 %collective-permute-start.15 = (bf16[1,8,144,128]{3,2,1,0:T(8,128)(2,1)S(1)}, bf16[1,8,144,128]{3,2,1,0:T(8,128)(2,1)S(1)}, u32[]{:S(2)}, u32[]{:S(2)}) collective-permute-start(bf16[1,8,144,128]{3,2,1,0:T(8,128)(2,1)S(1)} %get-tuple-element.104), channel_id=1, source_target_pairs={{0,4},{1,5},{2,6},{3,7},{4,0},{5,1},{6,2},{7,3},{8,12},{9,13},{10,... | collective-permute-start | bytes 884744 | tf_op jit(solution)/shard_map/ppermute | solution.py:365
  69.6 5.8 %collective-permute-done.11.refs_1_ = bf16[1,4,144,128]{3,2,1,0:T(8,128)(2,1)S(1)} collective-permute-done((bf16[1,4,144,128]{3,2,1,0:T(8,128)(2,1)S(1)}, bf16[1,4,144,128]{3,2,1,0:T(8,128)(2,1)S(1)}, u32[]{:S(2)}, u32[]{:S(2)}) %collective-permute-start.11) | collective-permute-done | bytes 147488 | tf_op jit(solution)/shard_map/ppermute | solution.py:365
  76.3 1.2 %collective-permute-start.17 = (bf16[1,4,144,128]{3,2,1,0:T(8,128)(2,1)S(1)}, bf16[1,4,144,128]{3,2,1,0:T(8,128)(2,1)S(1)}, u32[]{:S(2)}, u32[]{:S(2)}) collective-permute-start(bf16[1,4,144,128]{3,2,1,0:T(8,128)(2,1)S(1)} %get-tuple-element.108), channel_id=1, source_target_pairs={{0,16},{8,24},{16,0},{24,8},{1,17},{9,25},{17,1},{25,9},{2,18},{10... | collective-permute-start | bytes 442376 | tf_op jit(solution)/shard_map/ppermute | solution.py:365
  77.5 1.5 %collective-permute-start.18 = (bf16[1,4,144,128]{3,2,1,0:T(8,128)(2,1)S(1)}, bf16[1,4,144,128]{3,2,1,0:T(8,128)(2,1)S(1)}, u32[]{:S(2)}, u32[]{:S(2)}) collective-permute-start(bf16[1,4,144,128]{3,2,1,0:T(8,128)(2,1)S(1)} %get-tuple-element.110), channel_id=1, source_target_pairs={{0,1},{1,0},{2,3},{3,2},{4,5},{5,4},{6,7},{7,6},{8,9},{9,8},{10,11... | collective-permute-start | bytes 442376 | tf_op jit(solution)/shard_map/ppermute | solution.py:365
  79.0 3.1 %collective-permute-done.15.refs_1_ = bf16[1,8,144,128]{3,2,1,0:T(8,128)(2,1)S(1)} collective-permute-done((bf16[1,8,144,128]{3,2,1,0:T(8,128)(2,1)S(1)}, bf16[1,8,144,128]{3,2,1,0:T(8,128)(2,1)S(1)}, u32[]{:S(2)}, u32[]{:S(2)}) %collective-permute-start.15) | collective-permute-done | bytes 294944 | tf_op jit(solution)/shard_map/ppermute | solution.py:365
  82.7 5.0 %collective-permute-done.16.refs_2_ = bf16[1,8,144,128]{3,2,1,0:T(8,128)(2,1)S(1)} collective-permute-done((bf16[1,8,144,128]{3,2,1,0:T(8,128)(2,1)S(1)}, bf16[1,8,144,128]{3,2,1,0:T(8,128)(2,1)S(1)}, u32[]{:S(2)}, u32[]{:S(2)}) %collective-permute-start.16) | collective-permute-done | bytes 294944 | tf_op jit(solution)/shard_map/ppermute | solution.py:365
  87.7 10.4 %analysis.1 = f32[16,6,128,256]{3,2,1,0:T(8,128)} custom-call(bf16[1,8,144,128]{3,2,1,0:T(8,128)(2,1)S(1)} %collective-permute-done.10.refs_0_, bf16[1,8,144,128]{3,2,1,0:T(8,128)(2,1)S(1)} %collective-permute-done.15.refs_1_, bf16[1,8,144,128]{3,2,1,0:T(8,128)(2,1)S(1)} %collective-permute-done.16.refs_2_, ...), custom_call_target="tpu_custom_call" | custom-call | tf_op jit(solution)/shard_map/analysis/pallas_call | solution.py:343
  (51 shorter events, 13.5 us)
Async XLA Ops:
  24.7 3.6 %collective-permute-start = (bf16[4,8,144,128]{3,2,1,0:T(8,128)(2,1)S(1)}, bf16[4,8,144,128]{3,2,1,0:T(8,128)(2,1)S(1)}, u32[]{:S(2)}, u32[]{:S(2)}) collective-permute-start(bf16[4,8,144,128]{3,2,1,0:T(8,128)(2,1)S(1)} %partial_grams.8), channel_id=1, source_target_pairs={{0,8},{8,0},{16,24},{24,16},{1,9},{9,1},{17,25},{25,17},{2,10},{10... | collective-permute-start | bytes 3538952 | tf_op jit(solution)/shard_map/ppermute | solution.py:365
  28.7 9.5 %collective-permute-start.1 = (bf16[2,4,144,128]{3,2,1,0:T(8,128)(2,1)S(1)}, bf16[2,4,144,128]{3,2,1,0:T(8,128)(2,1)S(1)}, u32[]{:S(2)}, u32[]{:S(2)}) collective-permute-start(bf16[2,4,144,128]{3,2,1,0:T(8,128)(2,1)S(1)} %get-tuple-element.71), channel_id=1, source_target_pairs={{0,1},{1,0},{2,3},{3,2},{4,5},{5,4},{6,7},{7,6},{8,9},{9,8},{10,11... | collective-permute-start | bytes 884744 | tf_op jit(solution)/shard_map/ppermute | solution.py:365
  29.3 9.1 %collective-permute-start.2 = (bf16[2,4,144,128]{3,2,1,0:T(8,128)(2,1)S(1)}, bf16[2,4,144,128]{3,2,1,0:T(8,128)(2,1)S(1)}, u32[]{:S(2)}, u32[]{:S(2)}) collective-permute-start(bf16[2,4,144,128]{3,2,1,0:T(8,128)(2,1)S(1)} %get-tuple-element.73), channel_id=1, source_target_pairs={{0,16},{8,24},{16,0},{24,8},{1,17},{9,25},{17,1},{25,9},{2,18},{10... | collective-permute-start | bytes 884744 | tf_op jit(solution)/shard_map/ppermute | solution.py:365
  33.5 5.0 %collective-permute-start.3 = (bf16[4,8,144,128]{3,2,1,0:T(8,128)(2,1)S(1)}, bf16[4,8,144,128]{3,2,1,0:T(8,128)(2,1)S(1)}, u32[]{:S(2)}, u32[]{:S(2)}) collective-permute-start(bf16[4,8,144,128]{3,2,1,0:T(8,128)(2,1)S(1)} %partial_grams.10), channel_id=1, source_target_pairs={{0,8},{8,0},{16,24},{24,16},{1,9},{9,1},{17,25},{25,17},{2,10},{10... | collective-permute-start | bytes 3538952 | tf_op jit(solution)/shard_map/ppermute | solution.py:365
  38.9 11.5 %collective-permute-start.4 = (bf16[3,4,144,128]{3,2,1,0:T(8,128)(2,1)S(1)}, bf16[3,4,144,128]{3,2,1,0:T(8,128)(2,1)S(1)}, u32[]{:S(2)}, u32[]{:S(2)}) collective-permute-start(bf16[3,4,144,128]{3,2,1,0:T(8,128)(2,1)S(1)} %get-tuple-element.77), channel_id=1, source_target_pairs={{0,16},{8,24},{16,0},{24,8},{1,17},{9,25},{17,1},{25,9},{2,18},{10... | collective-permute-start | bytes 1327112 | tf_op jit(solution)/shard_map/ppermute | solution.py:365
  39.5 11.8 %collective-permute-start.5 = (bf16[3,4,144,128]{3,2,1,0:T(8,128)(2,1)S(1)}, bf16[3,4,144,128]{3,2,1,0:T(8,128)(2,1)S(1)}, u32[]{:S(2)}, u32[]{:S(2)}) collective-permute-start(bf16[3,4,144,128]{3,2,1,0:T(8,128)(2,1)S(1)} %get-tuple-element.79), channel_id=1, source_target_pairs={{0,1},{1,0},{2,3},{3,2},{4,5},{5,4},{6,7},{7,6},{8,9},{9,8},{10,11... | collective-permute-start | bytes 1327112 | tf_op jit(solution)/shard_map/ppermute | solution.py:365
  44.5 6.8 %collective-permute-start.6 = (bf16[4,8,144,128]{3,2,1,0:T(8,128)(2,1)S(1)}, bf16[4,8,144,128]{3,2,1,0:T(8,128)(2,1)S(1)}, u32[]{:S(2)}, u32[]{:S(2)}) collective-permute-start(bf16[4,8,144,128]{3,2,1,0:T(8,128)(2,1)S(1)} %partial_grams.12), channel_id=1, source_target_pairs={{0,8},{8,0},{16,24},{24,16},{1,9},{9,1},{17,25},{25,17},{2,10},{10... | collective-permute-start | bytes 3538952 | tf_op jit(solution)/shard_map/ppermute | solution.py:365
  51.8 16.3 %collective-permute-start.10 = (bf16[1,8,144,128]{3,2,1,0:T(8,128)(2,1)S(1)}, bf16[1,8,144,128]{3,2,1,0:T(8,128)(2,1)S(1)}, u32[]{:S(2)}, u32[]{:S(2)}) collective-permute-start(bf16[1,8,144,128]{3,2,1,0:T(8,128)(2,1)S(1)} %get-tuple-element.90), channel_id=1, source_target_pairs={{0,6},{1,7},{2,4},{3,5},{4,2},{5,3},{6,0},{7,1},{8,14},{9,15},{10,... | collective-permute-start | bytes 884744 | tf_op jit(solution)/shard_map/ppermute | solution.py:365
  52.5 10.7 %collective-permute-start.7 = (bf16[3,4,144,128]{3,2,1,0:T(8,128)(2,1)S(1)}, bf16[3,4,144,128]{3,2,1,0:T(8,128)(2,1)S(1)}, u32[]{:S(2)}, u32[]{:S(2)}) collective-permute-start(bf16[3,4,144,128]{3,2,1,0:T(8,128)(2,1)S(1)} %get-tuple-element.85), channel_id=1, source_target_pairs={{0,16},{8,24},{16,0},{24,8},{1,17},{9,25},{17,1},{25,9},{2,18},{10... | collective-permute-start | bytes 1327112 | tf_op jit(solution)/shard_map/ppermute | solution.py:365
  53.3 10.3 %collective-permute-start.8 = (bf16[3,4,144,128]{3,2,1,0:T(8,128)(2,1)S(1)}, bf16[3,4,144,128]{3,2,1,0:T(8,128)(2,1)S(1)}, u32[]{:S(2)}, u32[]{:S(2)}) collective-permute-start(bf16[3,4,144,128]{3,2,1,0:T(8,128)(2,1)S(1)} %get-tuple-element.87), channel_id=1, source_target_pairs={{0,1},{1,0},{2,3},{3,2},{4,5},{5,4},{6,7},{7,6},{8,9},{9,8},{10,11... | collective-permute-start | bytes 1327112 | tf_op jit(solution)/shard_map/ppermute | solution.py:365
  54.6 33.0 %slice-start = ((s8[6291456]{0:T(1024)(128)(4,1)}), s8[4194304]{0:T(1024)(128)(4,1)S(1)}, s32[]{:S(2)}) async-start(s8[6291456]{0:T(1024)(128)(4,1)} %bitcast.6), calls=%async_computation.1 | async-start | bytes 8388608
  58.2 29.5 %slice-start.1 = ((s8[6291456]{0:T(1024)(128)(4,1)}), s8[2097152]{0:T(1024)(128)(4,1)S(1)}, s32[]{:S(2)}) async-start(s8[6291456]{0:T(1024)(128)(4,1)} %bitcast.6), calls=%async_computation.2 | async-start | bytes 4194304
  58.2 5.3 %collective-permute-start.9 = (bf16[4,8,144,128]{3,2,1,0:T(8,128)(2,1)S(1)}, bf16[4,8,144,128]{3,2,1,0:T(8,128)(2,1)S(1)}, u32[]{:S(2)}, u32[]{:S(2)}) collective-permute-start(bf16[4,8,144,128]{3,2,1,0:T(8,128)(2,1)S(1)} %partial_grams.14), channel_id=1, source_target_pairs={{0,8},{8,0},{16,24},{24,16},{1,9},{9,1},{17,25},{25,17},{2,10},{10... | collective-permute-start | bytes 3538952 | tf_op jit(solution)/shard_map/ppermute | solution.py:365
  63.5 15.5 %copy-start = (f32[8,2,6,256]{3,1,2,0:T(2,128)S(1)}, f32[8,2,6,256]{3,1,2,0:T(2,128)}, u32[]{:S(2)}) copy-start(f32[8,2,6,256]{3,1,2,0:T(2,128)} %param.10) | copy-start | bytes 294916
  64.0 11.3 %collective-permute-start.13 = (bf16[2,4,144,128]{3,2,1,0:T(8,128)(2,1)S(1)}, bf16[2,4,144,128]{3,2,1,0:T(8,128)(2,1)S(1)}, u32[]{:S(2)}, u32[]{:S(2)}) collective-permute-start(bf16[2,4,144,128]{3,2,1,0:T(8,128)(2,1)S(1)} %get-tuple-element.100), channel_id=1, source_target_pairs={{0,1},{1,0},{2,3},{3,2},{4,5},{5,4},{6,7},{7,6},{8,9},{9,8},{10,11... | collective-permute-start | bytes 884744 | tf_op jit(solution)/shard_map/ppermute | solution.py:365
  65.4 9.9 %collective-permute-start.14 = (bf16[2,4,144,128]{3,2,1,0:T(8,128)(2,1)S(1)}, bf16[2,4,144,128]{3,2,1,0:T(8,128)(2,1)S(1)}, u32[]{:S(2)}, u32[]{:S(2)}) collective-permute-start(bf16[2,4,144,128]{3,2,1,0:T(8,128)(2,1)S(1)} %get-tuple-element.102), channel_id=1, source_target_pairs={{0,16},{8,24},{16,0},{24,8},{1,17},{9,25},{17,1},{25,9},{2,18},{10... | collective-permute-start | bytes 884744 | tf_op jit(solution)/shard_map/ppermute | solution.py:365
  66.9 8.5 %collective-permute-start.11 = (bf16[1,4,144,128]{3,2,1,0:T(8,128)(2,1)S(1)}, bf16[1,4,144,128]{3,2,1,0:T(8,128)(2,1)S(1)}, u32[]{:S(2)}, u32[]{:S(2)}) collective-permute-start(bf16[1,4,144,128]{3,2,1,0:T(8,128)(2,1)S(1)} %get-tuple-element.96), channel_id=1, source_target_pairs={{0,16},{8,24},{16,0},{24,8},{1,17},{9,25},{17,1},{25,9},{2,18},{10... | collective-permute-start | bytes 442376 | tf_op jit(solution)/shard_map/ppermute | solution.py:365
  67.5 7.9 %collective-permute-start.12 = (bf16[1,4,144,128]{3,2,1,0:T(8,128)(2,1)S(1)}, bf16[1,4,144,128]{3,2,1,0:T(8,128)(2,1)S(1)}, u32[]{:S(2)}, u32[]{:S(2)}) collective-permute-start(bf16[1,4,144,128]{3,2,1,0:T(8,128)(2,1)S(1)} %get-tuple-element.98), channel_id=1, source_target_pairs={{0,1},{1,0},{2,3},{3,2},{4,5},{5,4},{6,7},{7,6},{8,9},{9,8},{10,11... | collective-permute-start | bytes 442376 | tf_op jit(solution)/shard_map/ppermute | solution.py:365
  68.2 14.0 %collective-permute-start.15 = (bf16[1,8,144,128]{3,2,1,0:T(8,128)(2,1)S(1)}, bf16[1,8,144,128]{3,2,1,0:T(8,128)(2,1)S(1)}, u32[]{:S(2)}, u32[]{:S(2)}) collective-permute-start(bf16[1,8,144,128]{3,2,1,0:T(8,128)(2,1)S(1)} %get-tuple-element.104), channel_id=1, source_target_pairs={{0,4},{1,5},{2,6},{3,7},{4,0},{5,1},{6,2},{7,3},{8,12},{9,13},{10,... | collective-permute-start | bytes 884744 | tf_op jit(solution)/shard_map/ppermute | solution.py:365
  75.6 12.1 %collective-permute-start.16 = (bf16[1,8,144,128]{3,2,1,0:T(8,128)(2,1)S(1)}, bf16[1,8,144,128]{3,2,1,0:T(8,128)(2,1)S(1)}, u32[]{:S(2)}, u32[]{:S(2)}) collective-permute-start(bf16[1,8,144,128]{3,2,1,0:T(8,128)(2,1)S(1)} %get-tuple-element.106), channel_id=1, source_target_pairs={{0,2},{1,3},{2,0},{3,1},{4,6},{5,7},{6,4},{7,5},{8,10},{9,11},{10,... | collective-permute-start | bytes 884744 | tf_op jit(solution)/shard_map/ppermute | solution.py:365
  76.3 5.8 %collective-permute-start.17 = (bf16[1,4,144,128]{3,2,1,0:T(8,128)(2,1)S(1)}, bf16[1,4,144,128]{3,2,1,0:T(8,128)(2,1)S(1)}, u32[]{:S(2)}, u32[]{:S(2)}) collective-permute-start(bf16[1,4,144,128]{3,2,1,0:T(8,128)(2,1)S(1)} %get-tuple-element.108), channel_id=1, source_target_pairs={{0,16},{8,24},{16,0},{24,8},{1,17},{9,25},{17,1},{25,9},{2,18},{10... | collective-permute-start | bytes 442376 | tf_op jit(solution)/shard_map/ppermute | solution.py:365
  77.5 5.1 %collective-permute-start.18 = (bf16[1,4,144,128]{3,2,1,0:T(8,128)(2,1)S(1)}, bf16[1,4,144,128]{3,2,1,0:T(8,128)(2,1)S(1)}, u32[]{:S(2)}, u32[]{:S(2)}) collective-permute-start(bf16[1,4,144,128]{3,2,1,0:T(8,128)(2,1)S(1)} %get-tuple-element.110), channel_id=1, source_target_pairs={{0,1},{1,0},{2,3},{3,2},{4,5},{5,4},{6,7},{7,6},{8,9},{9,8},{10,11... | collective-permute-start | bytes 442376 | tf_op jit(solution)/shard_map/ppermute | solution.py:365

commit v8 on v7

--- a/solution.py
+++ b/solution.py
@@ -411,8 +411,7 @@
 
     parts, open_chunks, on_their_way = {}, [], [[], []]
 
-    def exchange(merge):
-        nonlocal open_chunks
+    def exchange(chunks, merge):
         arrays, jobs, lengths, where = [], [], {}, {}
 
         def slot(array):
@@ -427,7 +426,7 @@
             lengths[key] = row + 1
             return row
 
-        for far, level, parcels in open_chunks:
+        for far, level, parcels in chunks:
             for half, (targets, at, keep, keep_rows, got, got_rows) in enumerate(parcels):
                 for target, keep_row, got_row in zip(targets, keep_rows, got_rows):
                     place = 0
@@ -452,11 +451,11 @@
         outs = dict(zip(keys, add_all(arrays, cut, jobs, shapes)))
         gots = {k: swap(v, k[1], k[2]) for k, v in outs.items() if k[0] == "send"}
         still = []
-        for far, level, parcels in open_chunks:
+        for far, level, parcels in chunks:
             if level == len(routes[0]):
                 total = outs["total", far]
                 parts[far] = swap(total, "lat", 2 * far) if far else total
-                if far:
+                if far and merge:
                     on_their_way[1].append(far)
                 continue
             following = []
@@ -468,8 +467,7 @@
                 got = gots[where[far, half, leaving[0]][0]]
                 following.append((staying, 0, outs["keep", far, half], keep_rows, got, got_rows))
             still.append((far, level + 1, following))
-        open_chunks = still
-        return [v for k, v in outs.items() if k[0] != "keep"]
+        return still, [v for k, v in outs.items() if k[0] != "keep"]
 
     sent = []
     for far in reversed(range(lat_devices // 2)):
@@ -481,9 +479,9 @@
         open_chunks.append(
             (far, 0, [(targets, at, keep, rows, got, rows) for at in (0, cut)])
         )
-        sent = exchange(far > 0)
+        open_chunks, sent = exchange(open_chunks, far > 0)
     while open_chunks:
-        exchange(False)
+        open_chunks = [c for chunk in open_chunks for c in exchange([chunk], False)[0]]
     updated = analysis(
         list(parts.values()),
         holders * held * block_obs,

time: 98.4 us -> 98.3 us (level)
    pallas_call x6 -> x7, Pallas kernels: 2.02 us -> 2.02 us  [add_all(): pl.pallas_call(functools.partial(add_kernel, len(arrays), size, jobs), ou...]
where the time goes in v8:
time: 98.3 us; the launch traced here: 98.1 us
  Pallas kernels  44.8 us (46%)
  waiting for transfers between devices  20.6 us (21%)
  starting transfers between devices  15.4 us (16%)
  blocking collectives  14.2 us (14%)
  other arithmetic  1.87 us (2%)
  local copies, waits for them, and re-layouts  1.02 us (1%)
    pallas_call x8, Pallas kernels, partial_grams(): pl.pallas_call(functools.partial(gram_kernel, sizes, far, core), out_shap...  28.4 us
    ppermute x19, waiting for transfers between devices, swap(): return lax.ppermute(value, axis, [(i, i ^ flip) for i in range(size)])  20.6 us
    ppermute x19, starting transfers between devices, swap(): return lax.ppermute(value, axis, [(i, i ^ flip) for i in range(size)])  15.4 us
    all_to_all x1, blocking collectives, on_device(): lax.all_to_all(table, ('lon', 'lat'), split_axis=0, concat_axis=0, tiled=...  14.2 us
    pallas_call x1, Pallas kernels, analysis(): pl.pallas_call(functools.partial(analysis_kernel, len(parts), total_obs,...  10.4 us
    pallas_call x1, Pallas kernels, stage(): pl.pallas_call(functools.partial(stage_kernel, chunk), out_shape=[pltpu.V...  3.22 us
    pallas_call x7, Pallas kernels, add_all(): pl.pallas_call(functools.partial(add_kernel, len(arrays), size, jobs), ou...  2.02 us
  transfers between devices with their start and end apart: 19, of which 10 were waited for; matrix products, arithmetic and copies ran while one was open for 0% of the time, Pallas kernels for 26%

profile of v8, /device:TPU:0, one launch (start us, length us, event | category | flops | bytes accessed | tf_op | source)
XLA Modules:
  0.0 98.1 jit_solution(15124762071333013882)
XLA Ops:
  2.9 14.2 %all_to_all.9 = s32[32,1,26]{2,1,0:T(1,128)S(1)} all-to-all(s32[32,1,26]{2,1,0:T(1,128)S(1)} %copy.15), channel_id=1, replica_groups=mesh['lon'=4,'lat'=8] {'lon','lat'}, dimensions={0} | all-to-all | bytes 6656 | tf_op jit(solution)/shard_map/all_to_all | solution.py:379
  17.9 3.2 %stage.1 = (bf16[192,144,128]{2,1,0:T(8,128)(2,1)S(1)}, f32[192,128]{1,0:T(8,128)S(1)}, s32[192,128]{1,0:T(8,128)S(1)}, s32[192,128]{1,0:T(8,128)S(1)}, f32[8,128]{1,0:T(8,128)S(1)}) custom-call(bf16[192,128,128]{2,1,0:T(8,128)(2,1)} %anom_hbm, f32[192,128]{1,0:T(8,128)} %innov_hbm, f32[192,128]{1,0:T(8,128)} %rinv_hbm, s32[192,128]{1,0:T(8,128)} %lon_hbm, ...), custom_call_target="tpu_custom_call" | custom-call | bytes 12582912 | tf_op jit(solution)/shard_map/stage/pallas_call | solution.py:96
  21.2 3.6 %partial_grams.8 = bf16[4,8,144,128]{3,2,1,0:T(8,128)(2,1)S(1)} custom-call(s32[32,26]{1,0:T(8,128)S(4)} %hold.1.requests_ref, bf16[192,144,128]{2,1,0:T(8,128)(2,1)S(1)} %get-tuple-element.61.left_ref, f32[192,128]{1,0:T(8,128)S(1)} %get-tuple-element.62.rinv_ref, s32[192,128]{1,0:T(8,128)S(1)} %get-tuple-element.63.obs_lon_ref, ...), custom_call_target="tpu_custom_call" | custom-call | flops 20132659200 | tf_op jit(solution)/shard_map/partial_grams/pallas_call | solution.py:205
  24.8 3.5 %partial_grams.9.refs_0_ = bf16[4,8,144,128]{3,2,1,0:T(8,128)(2,1)S(1)} custom-call(s32[32,26]{1,0:T(8,128)S(4)} %hold.1.requests_ref, bf16[192,144,128]{2,1,0:T(8,128)(2,1)S(1)} %get-tuple-element.61.left_ref, f32[192,128]{1,0:T(8,128)S(1)} %get-tuple-element.62.rinv_ref, s32[192,128]{1,0:T(8,128)S(1)} %get-tuple-element.63.obs_lon_ref, ...), custom_call_target="tpu_custom_call" | custom-call | flops 20132659200 | tf_op jit(solution)/shard_map/partial_grams/pallas_call | solution.py:205
  29.9 3.5 %partial_grams.10 = bf16[4,8,144,128]{3,2,1,0:T(8,128)(2,1)S(1)} custom-call(s32[32,26]{1,0:T(8,128)S(4)} %hold.1.requests_ref, bf16[192,144,128]{2,1,0:T(8,128)(2,1)S(1)} %get-tuple-element.61.left_ref, f32[192,128]{1,0:T(8,128)S(1)} %get-tuple-element.62.rinv_ref, s32[192,128]{1,0:T(8,128)S(1)} %get-tuple-element.63.obs_lon_ref, ...), custom_call_target="tpu_custom_call" | custom-call | flops 20132659200 | tf_op jit(solution)/shard_map/partial_grams/pallas_call | solution.py:205
  33.5 3.6 %partial_grams.11.refs_4_ = bf16[4,8,144,128]{3,2,1,0:T(8,128)(2,1)S(1)} custom-call(s32[32,26]{1,0:T(8,128)S(4)} %hold.1.requests_ref, bf16[192,144,128]{2,1,0:T(8,128)(2,1)S(1)} %get-tuple-element.61.left_ref, f32[192,128]{1,0:T(8,128)S(1)} %get-tuple-element.62.rinv_ref, s32[192,128]{1,0:T(8,128)S(1)} %get-tuple-element.63.obs_lon_ref, ...), custom_call_target="tpu_custom_call" | custom-call | flops 20132659200 | tf_op jit(solution)/shard_map/partial_grams/pallas_call | solution.py:205
  39.5 1.4 %collective-permute-start.5 = (bf16[3,4,144,128]{3,2,1,0:T(8,128)(2,1)S(1)}, bf16[3,4,144,128]{3,2,1,0:T(8,128)(2,1)S(1)}, u32[]{:S(2)}, u32[]{:S(2)}) collective-permute-start(bf16[3,4,144,128]{3,2,1,0:T(8,128)(2,1)S(1)} %get-tuple-element.76), channel_id=1, source_target_pairs={{0,1},{1,0},{2,3},{3,2},{4,5},{5,4},{6,7},{7,6},{8,9},{9,8},{10,11... | collective-permute-start | bytes 1327112 | tf_op jit(solution)/shard_map/ppermute | solution.py:365
  40.9 3.5 %partial_grams.12 = bf16[4,8,144,128]{3,2,1,0:T(8,128)(2,1)S(1)} custom-call(s32[32,26]{1,0:T(8,128)S(4)} %hold.1.requests_ref, bf16[192,144,128]{2,1,0:T(8,128)(2,1)S(1)} %get-tuple-element.61.left_ref, f32[192,128]{1,0:T(8,128)S(1)} %get-tuple-element.62.rinv_ref, s32[192,128]{1,0:T(8,128)S(1)} %get-tuple-element.63.obs_lon_ref, ...), custom_call_target="tpu_custom_call" | custom-call | flops 20132659200 | tf_op jit(solution)/shard_map/partial_grams/pallas_call | solution.py:205
  44.6 3.5 %partial_grams.13.refs_6_ = bf16[4,8,144,128]{3,2,1,0:T(8,128)(2,1)S(1)} custom-call(s32[32,26]{1,0:T(8,128)S(4)} %hold.1.requests_ref, bf16[192,144,128]{2,1,0:T(8,128)(2,1)S(1)} %get-tuple-element.61.left_ref, f32[192,128]{1,0:T(8,128)S(1)} %get-tuple-element.62.rinv_ref, s32[192,128]{1,0:T(8,128)S(1)} %get-tuple-element.63.obs_lon_ref, ...), custom_call_target="tpu_custom_call" | custom-call | flops 20132659200 | tf_op jit(solution)/shard_map/partial_grams/pallas_call | solution.py:205
  48.1 2.3 %collective-permute-done.4.refs_1_ = bf16[3,4,144,128]{3,2,1,0:T(8,128)(2,1)S(1)} collective-permute-done((bf16[3,4,144,128]{3,2,1,0:T(8,128)(2,1)S(1)}, bf16[3,4,144,128]{3,2,1,0:T(8,128)(2,1)S(1)}, u32[]{:S(2)}, u32[]{:S(2)}) %collective-permute-start.4) | collective-permute-done | bytes 442400 | tf_op jit(solution)/shard_map/ppermute | solution.py:365
  53.3 1.4 %collective-permute-start.8 = (bf16[3,4,144,128]{3,2,1,0:T(8,128)(2,1)S(1)}, bf16[3,4,144,128]{3,2,1,0:T(8,128)(2,1)S(1)}, u32[]{:S(2)}, u32[]{:S(2)}) collective-permute-start(bf16[3,4,144,128]{3,2,1,0:T(8,128)(2,1)S(1)} %get-tuple-element.84), channel_id=1, source_target_pairs={{0,1},{1,0},{2,3},{3,2},{4,5},{5,4},{6,7},{7,6},{8,9},{9,8},{10,11... | collective-permute-start | bytes 1327112 | tf_op jit(solution)/shard_map/ppermute | solution.py:365
  54.7 3.5 %partial_grams.14 = bf16[4,8,144,128]{3,2,1,0:T(8,128)(2,1)S(1)} custom-call(s32[32,26]{1,0:T(8,128)S(4)} %hold.1.requests_ref, bf16[192,144,128]{2,1,0:T(8,128)(2,1)S(1)} %get-tuple-element.61.left_ref, f32[192,128]{1,0:T(8,128)S(1)} %get-tuple-element.62.rinv_ref, s32[192,128]{1,0:T(8,128)S(1)} %get-tuple-element.63.obs_lon_ref, ...), custom_call_target="tpu_custom_call" | custom-call | flops 20132659200 | tf_op jit(solution)/shard_map/partial_grams/pallas_call | solution.py:205
  58.3 3.6 %partial_grams.15.refs_6_ = bf16[4,8,144,128]{3,2,1,0:T(8,128)(2,1)S(1)} custom-call(s32[32,26]{1,0:T(8,128)S(4)} %hold.1.requests_ref, bf16[192,144,128]{2,1,0:T(8,128)(2,1)S(1)} %get-tuple-element.61.left_ref, f32[192,128]{1,0:T(8,128)S(1)} %get-tuple-element.62.rinv_ref, s32[192,128]{1,0:T(8,128)S(1)} %get-tuple-element.63.obs_lon_ref, ...), custom_call_target="tpu_custom_call" | custom-call | flops 20132659200 | tf_op jit(solution)/shard_map/partial_grams/pallas_call | solution.py:205
  61.9 1.3 %collective-permute-done.7.refs_1_ = bf16[3,4,144,128]{3,2,1,0:T(8,128)(2,1)S(1)} collective-permute-done((bf16[3,4,144,128]{3,2,1,0:T(8,128)(2,1)S(1)}, bf16[3,4,144,128]{3,2,1,0:T(8,128)(2,1)S(1)}, u32[]{:S(2)}, u32[]{:S(2)}) %collective-permute-start.7) | collective-permute-done | bytes 442400 | tf_op jit(solution)/shard_map/ppermute | solution.py:365
  64.0 1.4 %collective-permute-start.15 = (bf16[2,4,144,128]{3,2,1,0:T(8,128)(2,1)S(1)}, bf16[2,4,144,128]{3,2,1,0:T(8,128)(2,1)S(1)}, u32[]{:S(2)}, u32[]{:S(2)}) collective-permute-start(bf16[2,4,144,128]{3,2,1,0:T(8,128)(2,1)S(1)} %get-tuple-element.98), channel_id=1, source_target_pairs={{0,1},{1,0},{2,3},{3,2},{4,5},{5,4},{6,7},{7,6},{8,9},{9,8},{10,11... | collective-permute-start | bytes 884744 | tf_op jit(solution)/shard_map/ppermute | solution.py:365
  65.4 1.4 %collective-permute-start.16 = (bf16[2,4,144,128]{3,2,1,0:T(8,128)(2,1)S(1)}, bf16[2,4,144,128]{3,2,1,0:T(8,128)(2,1)S(1)}, u32[]{:S(2)}, u32[]{:S(2)}) collective-permute-start(bf16[2,4,144,128]{3,2,1,0:T(8,128)(2,1)S(1)} %get-tuple-element.100), channel_id=1, source_target_pairs={{0,16},{8,24},{16,0},{24,8},{1,17},{9,25},{17,1},{25,9},{2,18},{10... | collective-permute-start | bytes 884744 | tf_op jit(solution)/shard_map/ppermute | solution.py:365
  68.1 1.5 %collective-permute-start.11 = (bf16[1,8,144,128]{3,2,1,0:T(8,128)(2,1)S(1)}, bf16[1,8,144,128]{3,2,1,0:T(8,128)(2,1)S(1)}, u32[]{:S(2)}, u32[]{:S(2)}) collective-permute-start(bf16[1,8,144,128]{3,2,1,0:T(8,128)(2,1)S(1)} %get-tuple-element.92), channel_id=1, source_target_pairs={{0,4},{1,5},{2,6},{3,7},{4,0},{5,1},{6,2},{7,3},{8,12},{9,13},{10,... | collective-permute-start | bytes 884744 | tf_op jit(solution)/shard_map/ppermute | solution.py:365
  69.6 5.8 %collective-permute-done.12.refs_1_ = bf16[1,4,144,128]{3,2,1,0:T(8,128)(2,1)S(1)} collective-permute-done((bf16[1,4,144,128]{3,2,1,0:T(8,128)(2,1)S(1)}, bf16[1,4,144,128]{3,2,1,0:T(8,128)(2,1)S(1)}, u32[]{:S(2)}, u32[]{:S(2)}) %collective-permute-start.12) | collective-permute-done | bytes 147488 | tf_op jit(solution)/shard_map/ppermute | solution.py:365
  76.3 1.2 %collective-permute-start.17 = (bf16[1,4,144,128]{3,2,1,0:T(8,128)(2,1)S(1)}, bf16[1,4,144,128]{3,2,1,0:T(8,128)(2,1)S(1)}, u32[]{:S(2)}, u32[]{:S(2)}) collective-permute-start(bf16[1,4,144,128]{3,2,1,0:T(8,128)(2,1)S(1)} %get-tuple-element.102), channel_id=1, source_target_pairs={{0,16},{8,24},{16,0},{24,8},{1,17},{9,25},{17,1},{25,9},{2,18},{10... | collective-permute-start | bytes 442376 | tf_op jit(solution)/shard_map/ppermute | solution.py:365
  77.5 1.5 %collective-permute-start.18 = (bf16[1,4,144,128]{3,2,1,0:T(8,128)(2,1)S(1)}, bf16[1,4,144,128]{3,2,1,0:T(8,128)(2,1)S(1)}, u32[]{:S(2)}, u32[]{:S(2)}) collective-permute-start(bf16[1,4,144,128]{3,2,1,0:T(8,128)(2,1)S(1)} %get-tuple-element.104), channel_id=1, source_target_pairs={{0,1},{1,0},{2,3},{3,2},{4,5},{5,4},{6,7},{7,6},{8,9},{9,8},{10,11... | collective-permute-start | bytes 442376 | tf_op jit(solution)/shard_map/ppermute | solution.py:365
  79.1 2.5 %collective-permute-done.17.refs_1_ = bf16[1,4,144,128]{3,2,1,0:T(8,128)(2,1)S(1)} collective-permute-done((bf16[1,4,144,128]{3,2,1,0:T(8,128)(2,1)S(1)}, bf16[1,4,144,128]{3,2,1,0:T(8,128)(2,1)S(1)}, u32[]{:S(2)}, u32[]{:S(2)}) %collective-permute-start.17) | collective-permute-done | bytes 147488 | tf_op jit(solution)/shard_map/ppermute | solution.py:365
  81.5 1.1 %collective-permute-done.18.refs_3_ = bf16[1,4,144,128]{3,2,1,0:T(8,128)(2,1)S(1)} collective-permute-done((bf16[1,4,144,128]{3,2,1,0:T(8,128)(2,1)S(1)}, bf16[1,4,144,128]{3,2,1,0:T(8,128)(2,1)S(1)}, u32[]{:S(2)}, u32[]{:S(2)}) %collective-permute-start.18) | collective-permute-done | bytes 147488 | tf_op jit(solution)/shard_map/ppermute | solution.py:365
  82.7 5.0 %collective-permute-done.14.refs_2_ = bf16[1,8,144,128]{3,2,1,0:T(8,128)(2,1)S(1)} collective-permute-done((bf16[1,8,144,128]{3,2,1,0:T(8,128)(2,1)S(1)}, bf16[1,8,144,128]{3,2,1,0:T(8,128)(2,1)S(1)}, u32[]{:S(2)}, u32[]{:S(2)}) %collective-permute-start.14) | collective-permute-done | bytes 294944 | tf_op jit(solution)/shard_map/ppermute | solution.py:365
  87.7 10.4 %analysis.1 = f32[16,6,128,256]{3,2,1,0:T(8,128)} custom-call(bf16[1,8,144,128]{3,2,1,0:T(8,128)(2,1)S(1)} %collective-permute-done.10.refs_0_, bf16[1,8,144,128]{3,2,1,0:T(8,128)(2,1)S(1)} %collective-permute-done.11.refs_1_, bf16[1,8,144,128]{3,2,1,0:T(8,128)(2,1)S(1)} %collective-permute-done.14.refs_2_, ...), custom_call_target="tpu_custom_call" | custom-call | tf_op jit(solution)/shard_map/analysis/pallas_call | solution.py:343
  (52 shorter events, 13.9 us)
Async XLA Ops:
  24.7 3.6 %collective-permute-start = (bf16[4,8,144,128]{3,2,1,0:T(8,128)(2,1)S(1)}, bf16[4,8,144,128]{3,2,1,0:T(8,128)(2,1)S(1)}, u32[]{:S(2)}, u32[]{:S(2)}) collective-permute-start(bf16[4,8,144,128]{3,2,1,0:T(8,128)(2,1)S(1)} %partial_grams.8), channel_id=1, source_target_pairs={{0,8},{8,0},{16,24},{24,16},{1,9},{9,1},{17,25},{25,17},{2,10},{10... | collective-permute-start | bytes 3538952 | tf_op jit(solution)/shard_map/ppermute | solution.py:365
  28.7 9.5 %collective-permute-start.1 = (bf16[2,4,144,128]{3,2,1,0:T(8,128)(2,1)S(1)}, bf16[2,4,144,128]{3,2,1,0:T(8,128)(2,1)S(1)}, u32[]{:S(2)}, u32[]{:S(2)}) collective-permute-start(bf16[2,4,144,128]{3,2,1,0:T(8,128)(2,1)S(1)} %get-tuple-element.68), channel_id=1, source_target_pairs={{0,1},{1,0},{2,3},{3,2},{4,5},{5,4},{6,7},{7,6},{8,9},{9,8},{10,11... | collective-permute-start | bytes 884744 | tf_op jit(solution)/shard_map/ppermute | solution.py:365
  29.3 9.1 %collective-permute-start.2 = (bf16[2,4,144,128]{3,2,1,0:T(8,128)(2,1)S(1)}, bf16[2,4,144,128]{3,2,1,0:T(8,128)(2,1)S(1)}, u32[]{:S(2)}, u32[]{:S(2)}) collective-permute-start(bf16[2,4,144,128]{3,2,1,0:T(8,128)(2,1)S(1)} %get-tuple-element.70), channel_id=1, source_target_pairs={{0,16},{8,24},{16,0},{24,8},{1,17},{9,25},{17,1},{25,9},{2,18},{10... | collective-permute-start | bytes 884744 | tf_op jit(solution)/shard_map/ppermute | solution.py:365
  33.5 5.0 %collective-permute-start.3 = (bf16[4,8,144,128]{3,2,1,0:T(8,128)(2,1)S(1)}, bf16[4,8,144,128]{3,2,1,0:T(8,128)(2,1)S(1)}, u32[]{:S(2)}, u32[]{:S(2)}) collective-permute-start(bf16[4,8,144,128]{3,2,1,0:T(8,128)(2,1)S(1)} %partial_grams.10), channel_id=1, source_target_pairs={{0,8},{8,0},{16,24},{24,16},{1,9},{9,1},{17,25},{25,17},{2,10},{10... | collective-permute-start | bytes 3538952 | tf_op jit(solution)/shard_map/ppermute | solution.py:365
  38.9 11.5 %collective-permute-start.4 = (bf16[3,4,144,128]{3,2,1,0:T(8,128)(2,1)S(1)}, bf16[3,4,144,128]{3,2,1,0:T(8,128)(2,1)S(1)}, u32[]{:S(2)}, u32[]{:S(2)}) collective-permute-start(bf16[3,4,144,128]{3,2,1,0:T(8,128)(2,1)S(1)} %get-tuple-element.74), channel_id=1, source_target_pairs={{0,16},{8,24},{16,0},{24,8},{1,17},{9,25},{17,1},{25,9},{2,18},{10... | collective-permute-start | bytes 1327112 | tf_op jit(solution)/shard_map/ppermute | solution.py:365
  39.5 11.8 %collective-permute-start.5 = (bf16[3,4,144,128]{3,2,1,0:T(8,128)(2,1)S(1)}, bf16[3,4,144,128]{3,2,1,0:T(8,128)(2,1)S(1)}, u32[]{:S(2)}, u32[]{:S(2)}) collective-permute-start(bf16[3,4,144,128]{3,2,1,0:T(8,128)(2,1)S(1)} %get-tuple-element.76), channel_id=1, source_target_pairs={{0,1},{1,0},{2,3},{3,2},{4,5},{5,4},{6,7},{7,6},{8,9},{9,8},{10,11... | collective-permute-start | bytes 1327112 | tf_op jit(solution)/shard_map/ppermute | solution.py:365
  44.5 6.9 %collective-permute-start.6 = (bf16[4,8,144,128]{3,2,1,0:T(8,128)(2,1)S(1)}, bf16[4,8,144,128]{3,2,1,0:T(8,128)(2,1)S(1)}, u32[]{:S(2)}, u32[]{:S(2)}) collective-permute-start(bf16[4,8,144,128]{3,2,1,0:T(8,128)(2,1)S(1)} %partial_grams.12), channel_id=1, source_target_pairs={{0,8},{8,0},{16,24},{24,16},{1,9},{9,1},{17,25},{25,17},{2,10},{10... | collective-permute-start | bytes 3538952 | tf_op jit(solution)/shard_map/ppermute | solution.py:365
  51.8 16.3 %collective-permute-start.10 = (bf16[1,8,144,128]{3,2,1,0:T(8,128)(2,1)S(1)}, bf16[1,8,144,128]{3,2,1,0:T(8,128)(2,1)S(1)}, u32[]{:S(2)}, u32[]{:S(2)}) collective-permute-start(bf16[1,8,144,128]{3,2,1,0:T(8,128)(2,1)S(1)} %get-tuple-element.87), channel_id=1, source_target_pairs={{0,6},{1,7},{2,4},{3,5},{4,2},{5,3},{6,0},{7,1},{8,14},{9,15},{10,... | collective-permute-start | bytes 884744 | tf_op jit(solution)/shard_map/ppermute | solution.py:365
  52.5 10.7 %collective-permute-start.7 = (bf16[3,4,144,128]{3,2,1,0:T(8,128)(2,1)S(1)}, bf16[3,4,144,128]{3,2,1,0:T(8,128)(2,1)S(1)}, u32[]{:S(2)}, u32[]{:S(2)}) collective-permute-start(bf16[3,4,144,128]{3,2,1,0:T(8,128)(2,1)S(1)} %get-tuple-element.82), channel_id=1, source_target_pairs={{0,16},{8,24},{16,0},{24,8},{1,17},{9,25},{17,1},{25,9},{2,18},{10... | collective-permute-start | bytes 1327112 | tf_op jit(solution)/shard_map/ppermute | solution.py:365
  53.3 10.2 %collective-permute-start.8 = (bf16[3,4,144,128]{3,2,1,0:T(8,128)(2,1)S(1)}, bf16[3,4,144,128]{3,2,1,0:T(8,128)(2,1)S(1)}, u32[]{:S(2)}, u32[]{:S(2)}) collective-permute-start(bf16[3,4,144,128]{3,2,1,0:T(8,128)(2,1)S(1)} %get-tuple-element.84), channel_id=1, source_target_pairs={{0,1},{1,0},{2,3},{3,2},{4,5},{5,4},{6,7},{7,6},{8,9},{9,8},{10,11... | collective-permute-start | bytes 1327112 | tf_op jit(solution)/shard_map/ppermute | solution.py:365
  54.7 33.0 %slice-start = ((s8[6291456]{0:T(1024)(128)(4,1)}), s8[4194304]{0:T(1024)(128)(4,1)S(1)}, s32[]{:S(2)}) async-start(s8[6291456]{0:T(1024)(128)(4,1)} %bitcast.6), calls=%async_computation.1 | async-start | bytes 8388608
  58.2 29.5 %slice-start.1 = ((s8[6291456]{0:T(1024)(128)(4,1)}), s8[2097152]{0:T(1024)(128)(4,1)S(1)}, s32[]{:S(2)}) async-start(s8[6291456]{0:T(1024)(128)(4,1)} %bitcast.6), calls=%async_computation.2 | async-start | bytes 4194304
  58.2 5.3 %collective-permute-start.9 = (bf16[4,8,144,128]{3,2,1,0:T(8,128)(2,1)S(1)}, bf16[4,8,144,128]{3,2,1,0:T(8,128)(2,1)S(1)}, u32[]{:S(2)}, u32[]{:S(2)}) collective-permute-start(bf16[4,8,144,128]{3,2,1,0:T(8,128)(2,1)S(1)} %partial_grams.14), channel_id=1, source_target_pairs={{0,8},{8,0},{16,24},{24,16},{1,9},{9,1},{17,25},{25,17},{2,10},{10... | collective-permute-start | bytes 3538952 | tf_op jit(solution)/shard_map/ppermute | solution.py:365
  63.5 15.5 %copy-start = (f32[8,2,6,256]{3,1,2,0:T(2,128)S(1)}, f32[8,2,6,256]{3,1,2,0:T(2,128)}, u32[]{:S(2)}) copy-start(f32[8,2,6,256]{3,1,2,0:T(2,128)} %param.10) | copy-start | bytes 294916
  64.0 12.2 %collective-permute-start.15 = (bf16[2,4,144,128]{3,2,1,0:T(8,128)(2,1)S(1)}, bf16[2,4,144,128]{3,2,1,0:T(8,128)(2,1)S(1)}, u32[]{:S(2)}, u32[]{:S(2)}) collective-permute-start(bf16[2,4,144,128]{3,2,1,0:T(8,128)(2,1)S(1)} %get-tuple-element.98), channel_id=1, source_target_pairs={{0,1},{1,0},{2,3},{3,2},{4,5},{5,4},{6,7},{7,6},{8,9},{9,8},{10,11... | collective-permute-start | bytes 884744 | tf_op jit(solution)/shard_map/ppermute | solution.py:365
  65.4 10.8 %collective-permute-start.16 = (bf16[2,4,144,128]{3,2,1,0:T(8,128)(2,1)S(1)}, bf16[2,4,144,128]{3,2,1,0:T(8,128)(2,1)S(1)}, u32[]{:S(2)}, u32[]{:S(2)}) collective-permute-start(bf16[2,4,144,128]{3,2,1,0:T(8,128)(2,1)S(1)} %get-tuple-element.100), channel_id=1, source_target_pairs={{0,16},{8,24},{16,0},{24,8},{1,17},{9,25},{17,1},{25,9},{2,18},{10... | collective-permute-start | bytes 884744 | tf_op jit(solution)/shard_map/ppermute | solution.py:365
  66.8 8.6 %collective-permute-start.12 = (bf16[1,4,144,128]{3,2,1,0:T(8,128)(2,1)S(1)}, bf16[1,4,144,128]{3,2,1,0:T(8,128)(2,1)S(1)}, u32[]{:S(2)}, u32[]{:S(2)}) collective-permute-start(bf16[1,4,144,128]{3,2,1,0:T(8,128)(2,1)S(1)} %get-tuple-element.94), channel_id=1, source_target_pairs={{0,16},{8,24},{16,0},{24,8},{1,17},{9,25},{17,1},{25,9},{2,18},{10... | collective-permute-start | bytes 442376 | tf_op jit(solution)/shard_map/ppermute | solution.py:365
  67.4 8.0 %collective-permute-start.13 = (bf16[1,4,144,128]{3,2,1,0:T(8,128)(2,1)S(1)}, bf16[1,4,144,128]{3,2,1,0:T(8,128)(2,1)S(1)}, u32[]{:S(2)}, u32[]{:S(2)}) collective-permute-start(bf16[1,4,144,128]{3,2,1,0:T(8,128)(2,1)S(1)} %get-tuple-element.96), channel_id=1, source_target_pairs={{0,1},{1,0},{2,3},{3,2},{4,5},{5,4},{6,7},{7,6},{8,9},{9,8},{10,11... | collective-permute-start | bytes 442376 | tf_op jit(solution)/shard_map/ppermute | solution.py:365
  68.1 14.6 %collective-permute-start.11 = (bf16[1,8,144,128]{3,2,1,0:T(8,128)(2,1)S(1)}, bf16[1,8,144,128]{3,2,1,0:T(8,128)(2,1)S(1)}, u32[]{:S(2)}, u32[]{:S(2)}) collective-permute-start(bf16[1,8,144,128]{3,2,1,0:T(8,128)(2,1)S(1)} %get-tuple-element.92), channel_id=1, source_target_pairs={{0,4},{1,5},{2,6},{3,7},{4,0},{5,1},{6,2},{7,3},{8,12},{9,13},{10,... | collective-permute-start | bytes 884744 | tf_op jit(solution)/shard_map/ppermute | solution.py:365
  75.5 12.2 %collective-permute-start.14 = (bf16[1,8,144,128]{3,2,1,0:T(8,128)(2,1)S(1)}, bf16[1,8,144,128]{3,2,1,0:T(8,128)(2,1)S(1)}, u32[]{:S(2)}, u32[]{:S(2)}) collective-permute-start(bf16[1,8,144,128]{3,2,1,0:T(8,128)(2,1)S(1)} %add_partials.11), channel_id=1, source_target_pairs={{0,2},{1,3},{2,0},{3,1},{4,6},{5,7},{6,4},{7,5},{8,10},{9,11},{10,... | collective-permute-start | bytes 884744 | tf_op jit(solution)/shard_map/ppermute | solution.py:365
  76.3 5.2 %collective-permute-start.17 = (bf16[1,4,144,128]{3,2,1,0:T(8,128)(2,1)S(1)}, bf16[1,4,144,128]{3,2,1,0:T(8,128)(2,1)S(1)}, u32[]{:S(2)}, u32[]{:S(2)}) collective-permute-start(bf16[1,4,144,128]{3,2,1,0:T(8,128)(2,1)S(1)} %get-tuple-element.102), channel_id=1, source_target_pairs={{0,16},{8,24},{16,0},{24,8},{1,17},{9,25},{17,1},{25,9},{2,18},{10... | collective-permute-start | bytes 442376 | tf_op jit(solution)/shard_map/ppermute | solution.py:365
  77.5 5.1 %collective-permute-start.18 = (bf16[1,4,144,128]{3,2,1,0:T(8,128)(2,1)S(1)}, bf16[1,4,144,128]{3,2,1,0:T(8,128)(2,1)S(1)}, u32[]{:S(2)}, u32[]{:S(2)}) collective-permute-start(bf16[1,4,144,128]{3,2,1,0:T(8,128)(2,1)S(1)} %get-tuple-element.104), channel_id=1, source_target_pairs={{0,1},{1,0},{2,3},{3,2},{4,5},{5,4},{6,7},{7,6},{8,9},{9,8},{10,11... | collective-permute-start | bytes 442376 | tf_op jit(solution)/shard_map/ppermute | solution.py:365

commit v9 on v8

--- a/solution.py
+++ b/solution.py
@@ -239,7 +239,7 @@
         out_ref[row, to, members:, :] = rows
 
 
-def add_all(arrays, size, jobs, shapes):
+def add_all(arrays, size, jobs, shapes, hides):
     inner = arrays[0].shape[2:]
     whole = pl.BlockSpec(memory_space=pltpu.VMEM)
     work = len(jobs) * size * inner[0] * inner[1]
@@ -249,7 +249,7 @@
         in_specs=[whole] * len(arrays),
         out_specs=[whole] * len(shapes),
         compiler_params=pltpu.CompilerParams(vmem_limit_bytes=8 * 2**20),
-        cost_estimate=pl.CostEstimate(flops=work * 4, bytes_accessed=work * 6, transcendentals=0),
+        cost_estimate=pl.CostEstimate(flops=work * (10000 if hides else 4), bytes_accessed=work * 6, transcendentals=0),
         name="add_partials",
     )(*arrays)
 
@@ -409,9 +409,9 @@
         y, near = target
         return near == 1 if axis == "lat" else (2 * y) & flip != 0
 
-    parts, open_chunks, on_their_way = {}, [], [[], []]
-
-    def exchange(chunks, merge):
+    parts, open_chunks, on_their_way = {}, [], [[], [], []]
+
+    def exchange(chunks, merge, behind=(), hides=False):
         arrays, jobs, lengths, where = [], [], {}, {}
 
         def slot(array):
@@ -446,9 +446,11 @@
         shapes = [(lengths[k], pairs if k[0] == "total" else cut) for k in keys]
         due = on_their_way.pop(0)
         on_their_way.append([])
-        arrays[0], arrived = lax.optimization_barrier((arrays[0], [parts[far] for far in due]))
+        arrays[0], arrived, _ = lax.optimization_barrier(
+            (arrays[0], [parts[far] for far in due], list(behind))
+        )
         parts.update(zip(due, arrived))
-        outs = dict(zip(keys, add_all(arrays, cut, jobs, shapes)))
+        outs = dict(zip(keys, add_all(arrays, cut, jobs, shapes, hides)))
         gots = {k: swap(v, k[1], k[2]) for k, v in outs.items() if k[0] == "send"}
         still = []
         for far, level, parcels in chunks:
@@ -456,7 +458,7 @@
                 total = outs["total", far]
                 parts[far] = swap(total, "lat", 2 * far) if far else total
                 if far and merge:
-                    on_their_way[1].append(far)
+                    on_their_way[2].append(far)
                 continue
             following = []
             for half, (targets, *_) in enumerate(parcels):
@@ -476,12 +478,16 @@
         keep = grams(far, 0, [send])
         targets = [(y, near) for y in range(y_count) for near in range(2)]
         rows = range(len(targets))
-        open_chunks.append(
-            (far, 0, [(targets, at, keep, rows, got, rows) for at in (0, cut)])
-        )
-        open_chunks, sent = exchange(open_chunks, far > 0)
+        if not far:
+            open_chunks, sent = exchange(open_chunks, False, behind=[keep])
+            keep, _ = lax.optimization_barrier((keep, sent))
+        newest = (far, 0, [(targets, at, keep, rows, got, rows) for at in (0, cut)])
+        if far:
+            open_chunks, sent = exchange([*open_chunks, newest], True)
+        else:
+            open_chunks += exchange([newest], False, hides=False)[0]
     while open_chunks:
-        open_chunks = [c for chunk in open_chunks for c in exchange([chunk], False)[0]]
+        open_chunks = [c for chunk in open_chunks for c in exchange([chunk], False, hides=len(open_chunks) > 1 and chunk is open_chunks[0])[0]]
     updated = analysis(
         list(parts.values()),
         holders * held * block_obs,

time: 98.3 us -> 94.1 us (0.957)
  waiting for transfers between devices: 20.6 us -> 17.5 us
  starting transfers between devices: 15.4 us -> 14.2 us
    ppermute x19, waiting for transfers between devices: 20.6 us -> 17.5 us  [swap(): return lax.ppermute(value, axis, [(i, i ^ flip) for i in range(size)])]
    ppermute x19, starting transfers between devices: 15.4 us -> 14.2 us  [swap(): return lax.ppermute(value, axis, [(i, i ^ flip) for i in range(size)])]
    pallas_call x7 -> x8, Pallas kernels: 2.02 us -> 2.04 us  [add_all(): pl.pallas_call(functools.partial(add_kernel, len(arrays), size, jobs), ou...]
  transfers between devices with their start and end apart: 19 -> 19, of which waited for: 10 -> 12; matrix products, arithmetic and copies ran while one was open for 0% -> 0% of each run, Pallas kernels for 26% -> 27%
where the time goes in v9:
time: 94.1 us; the launch traced here: 93.9 us
  Pallas kernels  44.9 us (48%)
  waiting for transfers between devices  17.5 us (19%)
  blocking collectives  14.2 us (15%)
  starting transfers between devices  14.2 us (15%)
  other arithmetic  1.87 us (2%)
  local copies, waits for them, and re-layouts  1.02 us (1%)
    pallas_call x8, Pallas kernels, partial_grams(): pl.pallas_call(functools.partial(gram_kernel, sizes, far, core), out_shap...  28.4 us
    ppermute x19, waiting for transfers between devices, swap(): return lax.ppermute(value, axis, [(i, i ^ flip) for i in range(size)])  17.5 us
    all_to_all x1, blocking collectives, on_device(): lax.all_to_all(table, ('lon', 'lat'), split_axis=0, concat_axis=0, tiled=...  14.2 us
    ppermute x19, starting transfers between devices, swap(): return lax.ppermute(value, axis, [(i, i ^ flip) for i in range(size)])  14.2 us
    pallas_call x1, Pallas kernels, analysis(): pl.pallas_call(functools.partial(analysis_kernel, len(parts), total_obs,...  10.4 us
    pallas_call x1, Pallas kernels, stage(): pl.pallas_call(functools.partial(stage_kernel, chunk), out_shape=[pltpu.V...  3.22 us
    pallas_call x8, Pallas kernels, add_all(): pl.pallas_call(functools.partial(add_kernel, len(arrays), size, jobs), ou...  2.04 us
  transfers between devices with their start and end apart: 19, of which 12 were waited for; matrix products, arithmetic and copies ran while one was open for 0% of the time, Pallas kernels for 27%

profile of v9, /device:TPU:0, one launch (start us, length us, event | category | flops | bytes accessed | tf_op | source)
XLA Modules:
  0.0 93.9 jit_solution(18251749456595329378)
XLA Ops:
  2.9 14.2 %all_to_all.9 = s32[32,1,26]{2,1,0:T(1,128)S(1)} all-to-all(s32[32,1,26]{2,1,0:T(1,128)S(1)} %copy.15), channel_id=1, replica_groups=mesh['lon'=4,'lat'=8] {'lon','lat'}, dimensions={0} | all-to-all | bytes 6656 | tf_op jit(solution)/shard_map/all_to_all | solution.py:379
  17.9 3.2 %stage.1 = (bf16[192,144,128]{2,1,0:T(8,128)(2,1)S(1)}, f32[192,128]{1,0:T(8,128)S(1)}, s32[192,128]{1,0:T(8,128)S(1)}, s32[192,128]{1,0:T(8,128)S(1)}, f32[8,128]{1,0:T(8,128)S(1)}) custom-call(bf16[192,128,128]{2,1,0:T(8,128)(2,1)} %anom_hbm, f32[192,128]{1,0:T(8,128)} %innov_hbm, f32[192,128]{1,0:T(8,128)} %rinv_hbm, s32[192,128]{1,0:T(8,128)} %lon_hbm, ...), custom_call_target="tpu_custom_call" | custom-call | bytes 12582912 | tf_op jit(solution)/shard_map/stage/pallas_call | solution.py:96
  21.2 3.5 %partial_grams.8 = bf16[4,8,144,128]{3,2,1,0:T(8,128)(2,1)S(1)} custom-call(s32[32,26]{1,0:T(8,128)S(4)} %hold.1.requests_ref, bf16[192,144,128]{2,1,0:T(8,128)(2,1)S(1)} %get-tuple-element.63.left_ref, f32[192,128]{1,0:T(8,128)S(1)} %get-tuple-element.64.rinv_ref, s32[192,128]{1,0:T(8,128)S(1)} %get-tuple-element.65.obs_lon_ref, ...), custom_call_target="tpu_custom_call" | custom-call | flops 20132659200 | tf_op jit(solution)/shard_map/partial_grams/pallas_call | solution.py:205
  24.8 3.6 %partial_grams.9.refs_0_ = bf16[4,8,144,128]{3,2,1,0:T(8,128)(2,1)S(1)} custom-call(s32[32,26]{1,0:T(8,128)S(4)} %hold.1.requests_ref, bf16[192,144,128]{2,1,0:T(8,128)(2,1)S(1)} %get-tuple-element.63.left_ref, f32[192,128]{1,0:T(8,128)S(1)} %get-tuple-element.64.rinv_ref, s32[192,128]{1,0:T(8,128)S(1)} %get-tuple-element.65.obs_lon_ref, ...), custom_call_target="tpu_custom_call" | custom-call | flops 20132659200 | tf_op jit(solution)/shard_map/partial_grams/pallas_call | solution.py:205
  29.9 3.5 %partial_grams.10 = bf16[4,8,144,128]{3,2,1,0:T(8,128)(2,1)S(1)} custom-call(s32[32,26]{1,0:T(8,128)S(4)} %hold.1.requests_ref, bf16[192,144,128]{2,1,0:T(8,128)(2,1)S(1)} %get-tuple-element.63.left_ref, f32[192,128]{1,0:T(8,128)S(1)} %get-tuple-element.64.rinv_ref, s32[192,128]{1,0:T(8,128)S(1)} %get-tuple-element.65.obs_lon_ref, ...), custom_call_target="tpu_custom_call" | custom-call | flops 20132659200 | tf_op jit(solution)/shard_map/partial_grams/pallas_call | solution.py:205
  33.5 3.6 %partial_grams.11.refs_4_ = bf16[4,8,144,128]{3,2,1,0:T(8,128)(2,1)S(1)} custom-call(s32[32,26]{1,0:T(8,128)S(4)} %hold.1.requests_ref, bf16[192,144,128]{2,1,0:T(8,128)(2,1)S(1)} %get-tuple-element.63.left_ref, f32[192,128]{1,0:T(8,128)S(1)} %get-tuple-element.64.rinv_ref, s32[192,128]{1,0:T(8,128)S(1)} %get-tuple-element.65.obs_lon_ref, ...), custom_call_target="tpu_custom_call" | custom-call | flops 20132659200 | tf_op jit(solution)/shard_map/partial_grams/pallas_call | solution.py:205
  39.5 1.4 %collective-permute-start.5 = (bf16[3,4,144,128]{3,2,1,0:T(8,128)(2,1)S(1)}, bf16[3,4,144,128]{3,2,1,0:T(8,128)(2,1)S(1)}, u32[]{:S(2)}, u32[]{:S(2)}) collective-permute-start(bf16[3,4,144,128]{3,2,1,0:T(8,128)(2,1)S(1)} %get-tuple-element.78), channel_id=1, source_target_pairs={{0,1},{1,0},{2,3},{3,2},{4,5},{5,4},{6,7},{7,6},{8,9},{9,8},{10,11... | collective-permute-start | bytes 1327112 | tf_op jit(solution)/shard_map/ppermute | solution.py:365
  40.9 3.5 %partial_grams.12 = bf16[4,8,144,128]{3,2,1,0:T(8,128)(2,1)S(1)} custom-call(s32[32,26]{1,0:T(8,128)S(4)} %hold.1.requests_ref, bf16[192,144,128]{2,1,0:T(8,128)(2,1)S(1)} %get-tuple-element.63.left_ref, f32[192,128]{1,0:T(8,128)S(1)} %get-tuple-element.64.rinv_ref, s32[192,128]{1,0:T(8,128)S(1)} %get-tuple-element.65.obs_lon_ref, ...), custom_call_target="tpu_custom_call" | custom-call | flops 20132659200 | tf_op jit(solution)/shard_map/partial_grams/pallas_call | solution.py:205
  44.6 3.6 %partial_grams.13.refs_6_ = bf16[4,8,144,128]{3,2,1,0:T(8,128)(2,1)S(1)} custom-call(s32[32,26]{1,0:T(8,128)S(4)} %hold.1.requests_ref, bf16[192,144,128]{2,1,0:T(8,128)(2,1)S(1)} %get-tuple-element.63.left_ref, f32[192,128]{1,0:T(8,128)S(1)} %get-tuple-element.64.rinv_ref, s32[192,128]{1,0:T(8,128)S(1)} %get-tuple-element.65.obs_lon_ref, ...), custom_call_target="tpu_custom_call" | custom-call | flops 20132659200 | tf_op jit(solution)/shard_map/partial_grams/pallas_call | solution.py:205
  48.1 2.3 %collective-permute-done.4.refs_1_ = bf16[3,4,144,128]{3,2,1,0:T(8,128)(2,1)S(1)} collective-permute-done((bf16[3,4,144,128]{3,2,1,0:T(8,128)(2,1)S(1)}, bf16[3,4,144,128]{3,2,1,0:T(8,128)(2,1)S(1)}, u32[]{:S(2)}, u32[]{:S(2)}) %collective-permute-start.4) | collective-permute-done | bytes 442400 | tf_op jit(solution)/shard_map/ppermute | solution.py:365
  53.3 1.4 %collective-permute-start.8 = (bf16[3,4,144,128]{3,2,1,0:T(8,128)(2,1)S(1)}, bf16[3,4,144,128]{3,2,1,0:T(8,128)(2,1)S(1)}, u32[]{:S(2)}, u32[]{:S(2)}) collective-permute-start(bf16[3,4,144,128]{3,2,1,0:T(8,128)(2,1)S(1)} %get-tuple-element.85), channel_id=1, source_target_pairs={{0,1},{1,0},{2,3},{3,2},{4,5},{5,4},{6,7},{7,6},{8,9},{9,8},{10,11... | collective-permute-start | bytes 1327112 | tf_op jit(solution)/shard_map/ppermute | solution.py:365
  54.7 3.5 %partial_grams.14 = bf16[4,8,144,128]{3,2,1,0:T(8,128)(2,1)S(1)} custom-call(s32[32,26]{1,0:T(8,128)S(4)} %hold.1.requests_ref, bf16[192,144,128]{2,1,0:T(8,128)(2,1)S(1)} %get-tuple-element.63.left_ref, f32[192,128]{1,0:T(8,128)S(1)} %get-tuple-element.64.rinv_ref, s32[192,128]{1,0:T(8,128)S(1)} %get-tuple-element.65.obs_lon_ref, ...), custom_call_target="tpu_custom_call" | custom-call | flops 20132659200 | tf_op jit(solution)/shard_map/partial_grams/pallas_call | solution.py:205
  58.3 3.6 %partial_grams.15.refs_0_ = bf16[4,8,144,128]{3,2,1,0:T(8,128)(2,1)S(1)} custom-call(s32[32,26]{1,0:T(8,128)S(4)} %hold.1.requests_ref, bf16[192,144,128]{2,1,0:T(8,128)(2,1)S(1)} %get-tuple-element.63.left_ref, f32[192,128]{1,0:T(8,128)S(1)} %get-tuple-element.64.rinv_ref, s32[192,128]{1,0:T(8,128)S(1)} %get-tuple-element.65.obs_lon_ref, ...), custom_call_target="tpu_custom_call" | custom-call | flops 20132659200 | tf_op jit(solution)/shard_map/partial_grams/pallas_call | solution.py:205
  61.9 1.3 %collective-permute-done.7.refs_1_ = bf16[3,4,144,128]{3,2,1,0:T(8,128)(2,1)S(1)} collective-permute-done((bf16[3,4,144,128]{3,2,1,0:T(8,128)(2,1)S(1)}, bf16[3,4,144,128]{3,2,1,0:T(8,128)(2,1)S(1)}, u32[]{:S(2)}, u32[]{:S(2)}) %collective-permute-start.7) | collective-permute-done | bytes 442400 | tf_op jit(solution)/shard_map/ppermute | solution.py:365
  63.8 1.5 %collective-permute-start.11 = (bf16[1,4,144,128]{3,2,1,0:T(8,128)(2,1)S(1)}, bf16[1,4,144,128]{3,2,1,0:T(8,128)(2,1)S(1)}, u32[]{:S(2)}, u32[]{:S(2)}) collective-permute-start(bf16[1,4,144,128]{3,2,1,0:T(8,128)(2,1)S(1)} %get-tuple-element.97), channel_id=1, source_target_pairs={{0,16},{8,24},{16,0},{24,8},{1,17},{9,25},{17,1},{25,9},{2,18},{10... | collective-permute-start | bytes 442376 | tf_op jit(solution)/shard_map/ppermute | solution.py:365
  65.3 1.3 %collective-permute-start.12 = (bf16[1,4,144,128]{3,2,1,0:T(8,128)(2,1)S(1)}, bf16[1,4,144,128]{3,2,1,0:T(8,128)(2,1)S(1)}, u32[]{:S(2)}, u32[]{:S(2)}) collective-permute-start(bf16[1,4,144,128]{3,2,1,0:T(8,128)(2,1)S(1)} %get-tuple-element.99), channel_id=1, source_target_pairs={{0,1},{1,0},{2,3},{3,2},{4,5},{5,4},{6,7},{7,6},{8,9},{9,8},{10,11... | collective-permute-start | bytes 442376 | tf_op jit(solution)/shard_map/ppermute | solution.py:365
  68.2 1.4 %collective-permute-start.10 = (bf16[1,8,144,128]{3,2,1,0:T(8,128)(2,1)S(1)}, bf16[1,8,144,128]{3,2,1,0:T(8,128)(2,1)S(1)}, u32[]{:S(2)}, u32[]{:S(2)}) collective-permute-start(bf16[1,8,144,128]{3,2,1,0:T(8,128)(2,1)S(1)} %get-tuple-element.95), channel_id=1, source_target_pairs={{0,4},{1,5},{2,6},{3,7},{4,0},{5,1},{6,2},{7,3},{8,12},{9,13},{10,... | collective-permute-start | bytes 884744 | tf_op jit(solution)/shard_map/ppermute | solution.py:365
  70.0 2.1 %collective-permute-done.12.refs_3_ = bf16[1,4,144,128]{3,2,1,0:T(8,128)(2,1)S(1)} collective-permute-done((bf16[1,4,144,128]{3,2,1,0:T(8,128)(2,1)S(1)}, bf16[1,4,144,128]{3,2,1,0:T(8,128)(2,1)S(1)}, u32[]{:S(2)}, u32[]{:S(2)}) %collective-permute-start.12) | collective-permute-done | bytes 147488 | tf_op jit(solution)/shard_map/ppermute | solution.py:365
  72.6 3.1 %collective-permute-done.15.refs_1_ = bf16[2,4,144,128]{3,2,1,0:T(8,128)(2,1)S(1)} collective-permute-done((bf16[2,4,144,128]{3,2,1,0:T(8,128)(2,1)S(1)}, bf16[2,4,144,128]{3,2,1,0:T(8,128)(2,1)S(1)}, u32[]{:S(2)}, u32[]{:S(2)}) %collective-permute-start.15) | collective-permute-done | bytes 294944 | tf_op jit(solution)/shard_map/ppermute | solution.py:365
  75.8 1.1 %collective-permute-start.17 = (bf16[1,4,144,128]{3,2,1,0:T(8,128)(2,1)S(1)}, bf16[1,4,144,128]{3,2,1,0:T(8,128)(2,1)S(1)}, u32[]{:S(2)}, u32[]{:S(2)}) collective-permute-start(bf16[1,4,144,128]{3,2,1,0:T(8,128)(2,1)S(1)} %get-tuple-element.106), channel_id=1, source_target_pairs={{0,16},{8,24},{16,0},{24,8},{1,17},{9,25},{17,1},{25,9},{2,18},{10... | collective-permute-start | bytes 442376 | tf_op jit(solution)/shard_map/ppermute | solution.py:365
  77.6 3.5 %collective-permute-done.17.refs_1_ = bf16[1,4,144,128]{3,2,1,0:T(8,128)(2,1)S(1)} collective-permute-done((bf16[1,4,144,128]{3,2,1,0:T(8,128)(2,1)S(1)}, bf16[1,4,144,128]{3,2,1,0:T(8,128)(2,1)S(1)}, u32[]{:S(2)}, u32[]{:S(2)}) %collective-permute-start.17) | collective-permute-done | bytes 147488 | tf_op jit(solution)/shard_map/ppermute | solution.py:365
  81.1 1.0 %collective-permute-done.18.refs_3_ = bf16[1,4,144,128]{3,2,1,0:T(8,128)(2,1)S(1)} collective-permute-done((bf16[1,4,144,128]{3,2,1,0:T(8,128)(2,1)S(1)}, bf16[1,4,144,128]{3,2,1,0:T(8,128)(2,1)S(1)}, u32[]{:S(2)}, u32[]{:S(2)}) %collective-permute-start.18) | collective-permute-done | bytes 147488 | tf_op jit(solution)/shard_map/ppermute | solution.py:365
  82.2 1.3 %collective-permute-done.13.refs_2_ = bf16[1,8,144,128]{3,2,1,0:T(8,128)(2,1)S(1)} collective-permute-done((bf16[1,8,144,128]{3,2,1,0:T(8,128)(2,1)S(1)}, bf16[1,8,144,128]{3,2,1,0:T(8,128)(2,1)S(1)}, u32[]{:S(2)}, u32[]{:S(2)}) %collective-permute-start.13) | collective-permute-done | bytes 294944 | tf_op jit(solution)/shard_map/ppermute | solution.py:365
  83.5 10.4 %analysis.1 = f32[16,6,128,256]{3,2,1,0:T(8,128)} custom-call(bf16[1,8,144,128]{3,2,1,0:T(8,128)(2,1)S(1)} %collective-permute-done.9.refs_0_, bf16[1,8,144,128]{3,2,1,0:T(8,128)(2,1)S(1)} %collective-permute-done.10.refs_1_, bf16[1,8,144,128]{3,2,1,0:T(8,128)(2,1)S(1)} %collective-permute-done.13.refs_2_, ...), custom_call_target="tpu_custom_call" | custom-call | tf_op jit(solution)/shard_map/analysis/pallas_call | solution.py:343
  (53 shorter events, 14.8 us)
Async XLA Ops:
  24.7 3.6 %collective-permute-start = (bf16[4,8,144,128]{3,2,1,0:T(8,128)(2,1)S(1)}, bf16[4,8,144,128]{3,2,1,0:T(8,128)(2,1)S(1)}, u32[]{:S(2)}, u32[]{:S(2)}) collective-permute-start(bf16[4,8,144,128]{3,2,1,0:T(8,128)(2,1)S(1)} %partial_grams.8), channel_id=1, source_target_pairs={{0,8},{8,0},{16,24},{24,16},{1,9},{9,1},{17,25},{25,17},{2,10},{10... | collective-permute-start | bytes 3538952 | tf_op jit(solution)/shard_map/ppermute | solution.py:365
  28.7 9.4 %collective-permute-start.1 = (bf16[2,4,144,128]{3,2,1,0:T(8,128)(2,1)S(1)}, bf16[2,4,144,128]{3,2,1,0:T(8,128)(2,1)S(1)}, u32[]{:S(2)}, u32[]{:S(2)}) collective-permute-start(bf16[2,4,144,128]{3,2,1,0:T(8,128)(2,1)S(1)} %get-tuple-element.70), channel_id=1, source_target_pairs={{0,1},{1,0},{2,3},{3,2},{4,5},{5,4},{6,7},{7,6},{8,9},{9,8},{10,11... | collective-permute-start | bytes 884744 | tf_op jit(solution)/shard_map/ppermute | solution.py:365
  29.3 9.1 %collective-permute-start.2 = (bf16[2,4,144,128]{3,2,1,0:T(8,128)(2,1)S(1)}, bf16[2,4,144,128]{3,2,1,0:T(8,128)(2,1)S(1)}, u32[]{:S(2)}, u32[]{:S(2)}) collective-permute-start(bf16[2,4,144,128]{3,2,1,0:T(8,128)(2,1)S(1)} %get-tuple-element.72), channel_id=1, source_target_pairs={{0,16},{8,24},{16,0},{24,8},{1,17},{9,25},{17,1},{25,9},{2,18},{10... | collective-permute-start | bytes 884744 | tf_op jit(solution)/shard_map/ppermute | solution.py:365
  33.4 5.0 %collective-permute-start.3 = (bf16[4,8,144,128]{3,2,1,0:T(8,128)(2,1)S(1)}, bf16[4,8,144,128]{3,2,1,0:T(8,128)(2,1)S(1)}, u32[]{:S(2)}, u32[]{:S(2)}) collective-permute-start(bf16[4,8,144,128]{3,2,1,0:T(8,128)(2,1)S(1)} %partial_grams.10), channel_id=1, source_target_pairs={{0,8},{8,0},{16,24},{24,16},{1,9},{9,1},{17,25},{25,17},{2,10},{10... | collective-permute-start | bytes 3538952 | tf_op jit(solution)/shard_map/ppermute | solution.py:365
  38.9 11.5 %collective-permute-start.4 = (bf16[3,4,144,128]{3,2,1,0:T(8,128)(2,1)S(1)}, bf16[3,4,144,128]{3,2,1,0:T(8,128)(2,1)S(1)}, u32[]{:S(2)}, u32[]{:S(2)}) collective-permute-start(bf16[3,4,144,128]{3,2,1,0:T(8,128)(2,1)S(1)} %get-tuple-element.76), channel_id=1, source_target_pairs={{0,16},{8,24},{16,0},{24,8},{1,17},{9,25},{17,1},{25,9},{2,18},{10... | collective-permute-start | bytes 1327112 | tf_op jit(solution)/shard_map/ppermute | solution.py:365
  39.5 11.8 %collective-permute-start.5 = (bf16[3,4,144,128]{3,2,1,0:T(8,128)(2,1)S(1)}, bf16[3,4,144,128]{3,2,1,0:T(8,128)(2,1)S(1)}, u32[]{:S(2)}, u32[]{:S(2)}) collective-permute-start(bf16[3,4,144,128]{3,2,1,0:T(8,128)(2,1)S(1)} %get-tuple-element.78), channel_id=1, source_target_pairs={{0,1},{1,0},{2,3},{3,2},{4,5},{5,4},{6,7},{7,6},{8,9},{9,8},{10,11... | collective-permute-start | bytes 1327112 | tf_op jit(solution)/shard_map/ppermute | solution.py:365
  44.5 6.8 %collective-permute-start.6 = (bf16[4,8,144,128]{3,2,1,0:T(8,128)(2,1)S(1)}, bf16[4,8,144,128]{3,2,1,0:T(8,128)(2,1)S(1)}, u32[]{:S(2)}, u32[]{:S(2)}) collective-permute-start(bf16[4,8,144,128]{3,2,1,0:T(8,128)(2,1)S(1)} %partial_grams.12), channel_id=1, source_target_pairs={{0,8},{8,0},{16,24},{24,16},{1,9},{9,1},{17,25},{25,17},{2,10},{10... | collective-permute-start | bytes 3538952 | tf_op jit(solution)/shard_map/ppermute | solution.py:365
  51.8 16.4 %collective-permute-start.9 = (bf16[1,8,144,128]{3,2,1,0:T(8,128)(2,1)S(1)}, bf16[1,8,144,128]{3,2,1,0:T(8,128)(2,1)S(1)}, u32[]{:S(2)}, u32[]{:S(2)}) collective-permute-start(bf16[1,8,144,128]{3,2,1,0:T(8,128)(2,1)S(1)} %get-tuple-element.86), channel_id=1, source_target_pairs={{0,6},{1,7},{2,4},{3,5},{4,2},{5,3},{6,0},{7,1},{8,14},{9,15},{10,... | collective-permute-start | bytes 884744 | tf_op jit(solution)/shard_map/ppermute | solution.py:365
  52.5 10.7 %collective-permute-start.7 = (bf16[3,4,144,128]{3,2,1,0:T(8,128)(2,1)S(1)}, bf16[3,4,144,128]{3,2,1,0:T(8,128)(2,1)S(1)}, u32[]{:S(2)}, u32[]{:S(2)}) collective-permute-start(bf16[3,4,144,128]{3,2,1,0:T(8,128)(2,1)S(1)} %get-tuple-element.84), channel_id=1, source_target_pairs={{0,16},{8,24},{16,0},{24,8},{1,17},{9,25},{17,1},{25,9},{2,18},{10... | collective-permute-start | bytes 1327112 | tf_op jit(solution)/shard_map/ppermute | solution.py:365
  53.3 10.3 %collective-permute-start.8 = (bf16[3,4,144,128]{3,2,1,0:T(8,128)(2,1)S(1)}, bf16[3,4,144,128]{3,2,1,0:T(8,128)(2,1)S(1)}, u32[]{:S(2)}, u32[]{:S(2)}) collective-permute-start(bf16[3,4,144,128]{3,2,1,0:T(8,128)(2,1)S(1)} %get-tuple-element.85), channel_id=1, source_target_pairs={{0,1},{1,0},{2,3},{3,2},{4,5},{5,4},{6,7},{7,6},{8,9},{9,8},{10,11... | collective-permute-start | bytes 1327112 | tf_op jit(solution)/shard_map/ppermute | solution.py:365
  58.2 8.3 %collective-permute-start.14 = (bf16[4,8,144,128]{3,2,1,0:T(8,128)(2,1)S(1)}, bf16[4,8,144,128]{3,2,1,0:T(8,128)(2,1)S(1)}, u32[]{:S(2)}, u32[]{:S(2)}) collective-permute-start(bf16[4,8,144,128]{3,2,1,0:T(8,128)(2,1)S(1)} %partial_grams.14), channel_id=1, source_target_pairs={{0,8},{8,0},{16,24},{24,16},{1,9},{9,1},{17,25},{25,17},{2,10},{10... | collective-permute-start | bytes 3538952 | tf_op jit(solution)/shard_map/ppermute | solution.py:365
  63.5 19.9 %slice-start = ((s8[6291456]{0:T(1024)(128)(4,1)}), s8[4194304]{0:T(1024)(128)(4,1)S(1)}, s32[]{:S(2)}) async-start(s8[6291456]{0:T(1024)(128)(4,1)} %bitcast.6), calls=%async_computation.1 | async-start | bytes 8388608
  63.8 6.2 %collective-permute-start.11 = (bf16[1,4,144,128]{3,2,1,0:T(8,128)(2,1)S(1)}, bf16[1,4,144,128]{3,2,1,0:T(8,128)(2,1)S(1)}, u32[]{:S(2)}, u32[]{:S(2)}) collective-permute-start(bf16[1,4,144,128]{3,2,1,0:T(8,128)(2,1)S(1)} %get-tuple-element.97), channel_id=1, source_target_pairs={{0,16},{8,24},{16,0},{24,8},{1,17},{9,25},{17,1},{25,9},{2,18},{10... | collective-permute-start | bytes 442376 | tf_op jit(solution)/shard_map/ppermute | solution.py:365
  65.3 6.8 %collective-permute-start.12 = (bf16[1,4,144,128]{3,2,1,0:T(8,128)(2,1)S(1)}, bf16[1,4,144,128]{3,2,1,0:T(8,128)(2,1)S(1)}, u32[]{:S(2)}, u32[]{:S(2)}) collective-permute-start(bf16[1,4,144,128]{3,2,1,0:T(8,128)(2,1)S(1)} %get-tuple-element.99), channel_id=1, source_target_pairs={{0,1},{1,0},{2,3},{3,2},{4,5},{5,4},{6,7},{7,6},{8,9},{9,8},{10,11... | collective-permute-start | bytes 442376 | tf_op jit(solution)/shard_map/ppermute | solution.py:365
  66.8 8.9 %collective-permute-start.15 = (bf16[2,4,144,128]{3,2,1,0:T(8,128)(2,1)S(1)}, bf16[2,4,144,128]{3,2,1,0:T(8,128)(2,1)S(1)}, u32[]{:S(2)}, u32[]{:S(2)}) collective-permute-start(bf16[2,4,144,128]{3,2,1,0:T(8,128)(2,1)S(1)} %get-tuple-element.102), channel_id=1, source_target_pairs={{0,1},{1,0},{2,3},{3,2},{4,5},{5,4},{6,7},{7,6},{8,9},{9,8},{10,11... | collective-permute-start | bytes 884744 | tf_op jit(solution)/shard_map/ppermute | solution.py:365
  67.6 8.1 %collective-permute-start.16 = (bf16[2,4,144,128]{3,2,1,0:T(8,128)(2,1)S(1)}, bf16[2,4,144,128]{3,2,1,0:T(8,128)(2,1)S(1)}, u32[]{:S(2)}, u32[]{:S(2)}) collective-permute-start(bf16[2,4,144,128]{3,2,1,0:T(8,128)(2,1)S(1)} %get-tuple-element.104), channel_id=1, source_target_pairs={{0,16},{8,24},{16,0},{24,8},{1,17},{9,25},{17,1},{25,9},{2,18},{10... | collective-permute-start | bytes 884744 | tf_op jit(solution)/shard_map/ppermute | solution.py:365
  68.2 14.0 %collective-permute-start.10 = (bf16[1,8,144,128]{3,2,1,0:T(8,128)(2,1)S(1)}, bf16[1,8,144,128]{3,2,1,0:T(8,128)(2,1)S(1)}, u32[]{:S(2)}, u32[]{:S(2)}) collective-permute-start(bf16[1,8,144,128]{3,2,1,0:T(8,128)(2,1)S(1)} %get-tuple-element.95), channel_id=1, source_target_pairs={{0,4},{1,5},{2,6},{3,7},{4,0},{5,1},{6,2},{7,3},{8,12},{9,13},{10,... | collective-permute-start | bytes 884744 | tf_op jit(solution)/shard_map/ppermute | solution.py:365
  72.0 5.5 %copy-start = (f32[8,2,6,256]{3,1,2,0:T(2,128)S(1)}, f32[8,2,6,256]{3,1,2,0:T(2,128)}, u32[]{:S(2)}) copy-start(f32[8,2,6,256]{3,1,2,0:T(2,128)} %param.10) | copy-start | bytes 294916
  72.0 11.4 %slice-start.1 = ((s8[6291456]{0:T(1024)(128)(4,1)}), s8[2097152]{0:T(1024)(128)(4,1)S(1)}, s32[]{:S(2)}) async-start(s8[6291456]{0:T(1024)(128)(4,1)} %bitcast.6), calls=%async_computation.2 | async-start | bytes 4194304
  72.1 11.3 %collective-permute-start.13 = (bf16[1,8,144,128]{3,2,1,0:T(8,128)(2,1)S(1)}, bf16[1,8,144,128]{3,2,1,0:T(8,128)(2,1)S(1)}, u32[]{:S(2)}, u32[]{:S(2)}) collective-permute-start(bf16[1,8,144,128]{3,2,1,0:T(8,128)(2,1)S(1)} %add_partials.12), channel_id=1, source_target_pairs={{0,2},{1,3},{2,0},{3,1},{4,6},{5,7},{6,4},{7,5},{8,10},{9,11},{10,... | collective-permute-start | bytes 884744 | tf_op jit(solution)/shard_map/ppermute | solution.py:365
  75.8 5.2 %collective-permute-start.17 = (bf16[1,4,144,128]{3,2,1,0:T(8,128)(2,1)S(1)}, bf16[1,4,144,128]{3,2,1,0:T(8,128)(2,1)S(1)}, u32[]{:S(2)}, u32[]{:S(2)}) collective-permute-start(bf16[1,4,144,128]{3,2,1,0:T(8,128)(2,1)S(1)} %get-tuple-element.106), channel_id=1, source_target_pairs={{0,16},{8,24},{16,0},{24,8},{1,17},{9,25},{17,1},{25,9},{2,18},{10... | collective-permute-start | bytes 442376 | tf_op jit(solution)/shard_map/ppermute | solution.py:365
  76.9 5.1 %collective-permute-start.18 = (bf16[1,4,144,128]{3,2,1,0:T(8,128)(2,1)S(1)}, bf16[1,4,144,128]{3,2,1,0:T(8,128)(2,1)S(1)}, u32[]{:S(2)}, u32[]{:S(2)}) collective-permute-start(bf16[1,4,144,128]{3,2,1,0:T(8,128)(2,1)S(1)} %get-tuple-element.108), channel_id=1, source_target_pairs={{0,1},{1,0},{2,3},{3,2},{4,5},{5,4},{6,7},{7,6},{8,9},{9,8},{10,11... | collective-permute-start | bytes 442376 | tf_op jit(solution)/shard_map/ppermute | solution.py:365

commit v10 on v9

--- a/solution.py
+++ b/solution.py
@@ -46,11 +46,13 @@
     rinv_hbm,
     lon_hbm,
     lat_hbm,
+    table_hbm,
     left_ref,
     rinv_ref,
     lon_ref,
     lat_ref,
     totals_ref,
+    table_ref,
     innov_ref,
     sems,
 ):
@@ -59,7 +61,7 @@
     for i in range(held // chunk):
         span = pl.ds(i * chunk, chunk)
         pairs.append((anom_hbm.at[span], left_ref.at[span, pl.ds(0, members), :]))
-    pairs += [(lon_hbm, lon_ref), (lat_hbm, lat_ref)]
+    pairs += [(lon_hbm, lon_ref), (lat_hbm, lat_ref), (table_hbm, table_ref)]
     copies = [pltpu.make_async_copy(a, b, sems.at[i]) for i, (a, b) in enumerate(pairs)]
     for copy in copies:
         copy.start()
@@ -67,7 +69,7 @@
     copies[1].wait()
     line = lax.broadcasted_iota(jnp.int32, (EXT, block_obs), 0)
     sums = jnp.zeros((8, block_obs), F32)
-    for i, copy in enumerate(copies[2:-2]):
+    for i, copy in enumerate(copies[2:-3]):
         copy.wait()
 
         def block(j, total, first=i * chunk):
@@ -85,11 +87,11 @@
     spread = jnp.sum(sums, axis=0, keepdims=True) / (members - 1)
     line = lax.broadcasted_iota(jnp.int32, (8, block_obs), 0)
     totals_ref[...] = jnp.where(line == 4, innovation, jnp.where(line == 5, spread, 0.0))
-    copies[-2].wait()
-    copies[-1].wait()
-
-
-def stage(anom, innov, rinv, lon, lat):
+    for copy in copies[-3:]:
+        copy.wait()
+
+
+def stage(anom, innov, rinv, lon, lat, table):
     held, members, block_obs = anom.shape
     chunk = 16 if held % 16 == 0 else held
     operands = [pltpu.with_memory_space_constraint(v, pltpu.HBM) for v in (anom, innov, rinv, lon, lat)]
@@ -101,17 +103,18 @@
             pltpu.VMEM((held, block_obs), jnp.int32),
             pltpu.VMEM((held, block_obs), jnp.int32),
             pltpu.VMEM((8, block_obs), F32),
+            pltpu.SMEM(table.shape, table.dtype),
         ],
-        in_specs=[pl.BlockSpec(memory_space=pltpu.HBM)] * 5,
-        out_specs=[pl.BlockSpec(memory_space=pltpu.VMEM)] * 5,
+        in_specs=[pl.BlockSpec(memory_space=pltpu.HBM)] * 5 + [pl.BlockSpec(memory_space=pl.ANY)],
+        out_specs=[pl.BlockSpec(memory_space=pltpu.VMEM)] * 5 + [pl.BlockSpec(memory_space=pltpu.SMEM)],
         scratch_shapes=[
             pltpu.VMEM((held, block_obs), F32),
-            pltpu.SemaphoreType.DMA((held // chunk + 4,)),
+            pltpu.SemaphoreType.DMA((held // chunk + 5,)),
         ],
         compiler_params=pltpu.CompilerParams(vmem_limit_bytes=4 * 2**20),
         cost_estimate=pl.CostEstimate(flops=0, bytes_accessed=anom.size * 4, transcendentals=0),
         name="stage",
-    )(*operands)
+    )(*operands, table)
 
 
 def gram_kernel(
@@ -177,24 +180,6 @@
             rows = jnp.where(line == place + 1, projected, rows)
         high = rows.astype(BF16).astype(F32)
         out_ref[0, pair, members:, :] = jnp.concatenate([high, rows - high], axis=0).astype(BF16)
-
-
-def hold_kernel(table_hbm, held_ref, sem):
-    copy = pltpu.make_async_copy(table_hbm, held_ref, sem)
-    copy.start()
-    copy.wait()
-
-
-def hold(table):
-    return pl.pallas_call(
-        hold_kernel,
-        out_shape=pltpu.SMEM(table.shape, table.dtype),
-        in_specs=[pl.BlockSpec(memory_space=pl.ANY)],
-        out_specs=pl.BlockSpec(memory_space=pltpu.SMEM),
-        scratch_shapes=[pltpu.SemaphoreType.DMA(())],
-        compiler_params=pltpu.CompilerParams(vmem_limit_bytes=2**20),
-        name="hold",
-    )(table)
 
 
 def partial_grams(sizes, far, core, count, requests, staged):
@@ -381,8 +366,7 @@
     requests, observed = lax.optimization_barrier(
         (requests, (obs_anom, innov, obs_rinv, obs_lon, obs_lat))
     )
-    requests = hold(requests)
-    staged = stage(*observed)
+    *staged, requests = stage(*observed, requests)
     sizes = (
         patches,
         lat_patches,

time: 94.1 us -> 93.3 us (level)
  transfers between devices with their start and end apart: 19 -> 19, of which waited for: 12 -> 13; matrix products, arithmetic and copies ran while one was open for 0% -> 0% of each run, Pallas kernels for 27% -> 28%
where the time goes in v10:
time: 93.3 us; the launch traced here: 93.1 us
  Pallas kernels  44 us (47%)
  waiting for transfers between devices  17.3 us (19%)
  starting transfers between devices  14.4 us (15%)
  blocking collectives  14.2 us (15%)
  other arithmetic  1.87 us (2%)
  local copies, waits for them, and re-layouts  1.02 us (1%)
    pallas_call x8, Pallas kernels, partial_grams(): pl.pallas_call(functools.partial(gram_kernel, sizes, far, core), out_shap...  28.3 us
    ppermute x19, waiting for transfers between devices, swap(): return lax.ppermute(value, axis, [(i, i ^ flip) for i in range(size)])  17.3 us
    ppermute x19, starting transfers between devices, swap(): return lax.ppermute(value, axis, [(i, i ^ flip) for i in range(size)])  14.4 us
    all_to_all x1, blocking collectives, on_device(): lax.all_to_all(table, ('lon', 'lat'), split_axis=0, concat_axis=0, tiled=...  14.2 us
    pallas_call x1, Pallas kernels, analysis(): pl.pallas_call(functools.partial(analysis_kernel, len(parts), total_obs,...  10.4 us
    pallas_call x1, Pallas kernels, stage(): pl.pallas_call(functools.partial(stage_kernel, chunk), out_shape=[pltpu.V...  3.23 us
    pallas_call x8, Pallas kernels, add_all(): pl.pallas_call(functools.partial(add_kernel, len(arrays), size, jobs), ou...  2.04 us
  transfers between devices with their start and end apart: 19, of which 13 were waited for; matrix products, arithmetic and copies ran while one was open for 0% of the time, Pallas kernels for 28%

profile of v10, /device:TPU:0, one launch (start us, length us, event | category | flops | bytes accessed | tf_op | source)
XLA Modules:
  0.0 93.1 jit_solution(15628983680407623855)
XLA Ops:
  2.9 14.2 %all_to_all.9 = s32[32,1,26]{2,1,0:T(1,128)S(1)} all-to-all(s32[32,1,26]{2,1,0:T(1,128)S(1)} %copy.15), channel_id=1, replica_groups=mesh['lon'=4,'lat'=8] {'lon','lat'}, dimensions={0} | all-to-all | bytes 6656 | tf_op jit(solution)/shard_map/all_to_all | solution.py:364
  17.1 3.2 %stage.1 = (bf16[192,144,128]{2,1,0:T(8,128)(2,1)S(1)}, f32[192,128]{1,0:T(8,128)S(1)}, s32[192,128]{1,0:T(8,128)S(1)}, s32[192,128]{1,0:T(8,128)S(1)}, f32[8,128]{1,0:T(8,128)S(1)}, /*index=5*/s32[32,26]{1,0:T(8,128)S(4)}) custom-call(bf16[192,128,128]{2,1,0:T(8,128)(2,1)} %anom_hbm, f32[192,128]{1,0:T(8,128)} %innov_hbm, f32[192,128]{1,0:T(8,128)} %rinv_hbm, ...), custom_call_target="tpu_custom_call" | custom-call | bytes 12582912 | tf_op jit(solution)/shard_map/stage/pallas_call | solution.py:98
  20.3 3.5 %partial_grams.8 = bf16[4,8,144,128]{3,2,1,0:T(8,128)(2,1)S(1)} custom-call(s32[32,26]{1,0:T(8,128)S(4)} %get-tuple-element.64.requests_ref, bf16[192,144,128]{2,1,0:T(8,128)(2,1)S(1)} %get-tuple-element.65.left_ref, f32[192,128]{1,0:T(8,128)S(1)} %get-tuple-element.66.rinv_ref, s32[192,128]{1,0:T(8,128)S(1)} %get-tuple-element.67.obs_lon_ref, ...), custom_call_target="tpu_custom_call" | custom-call | flops 20132659200 | tf_op jit(solution)/shard_map/partial_grams/pallas_call | solution.py:190
  24.0 3.5 %partial_grams.9.refs_0_ = bf16[4,8,144,128]{3,2,1,0:T(8,128)(2,1)S(1)} custom-call(s32[32,26]{1,0:T(8,128)S(4)} %get-tuple-element.64.requests_ref, bf16[192,144,128]{2,1,0:T(8,128)(2,1)S(1)} %get-tuple-element.65.left_ref, f32[192,128]{1,0:T(8,128)S(1)} %get-tuple-element.66.rinv_ref, s32[192,128]{1,0:T(8,128)S(1)} %get-tuple-element.67.obs_lon_ref, ...), custom_call_target="tpu_custom_call" | custom-call | flops 20132659200 | tf_op jit(solution)/shard_map/partial_grams/pallas_call | solution.py:190
  29.1 3.5 %partial_grams.10 = bf16[4,8,144,128]{3,2,1,0:T(8,128)(2,1)S(1)} custom-call(s32[32,26]{1,0:T(8,128)S(4)} %get-tuple-element.64.requests_ref, bf16[192,144,128]{2,1,0:T(8,128)(2,1)S(1)} %get-tuple-element.65.left_ref, f32[192,128]{1,0:T(8,128)S(1)} %get-tuple-element.66.rinv_ref, s32[192,128]{1,0:T(8,128)S(1)} %get-tuple-element.67.obs_lon_ref, ...), custom_call_target="tpu_custom_call" | custom-call | flops 20132659200 | tf_op jit(solution)/shard_map/partial_grams/pallas_call | solution.py:190
  32.7 3.6 %partial_grams.11.refs_4_ = bf16[4,8,144,128]{3,2,1,0:T(8,128)(2,1)S(1)} custom-call(s32[32,26]{1,0:T(8,128)S(4)} %get-tuple-element.64.requests_ref, bf16[192,144,128]{2,1,0:T(8,128)(2,1)S(1)} %get-tuple-element.65.left_ref, f32[192,128]{1,0:T(8,128)S(1)} %get-tuple-element.66.rinv_ref, s32[192,128]{1,0:T(8,128)S(1)} %get-tuple-element.67.obs_lon_ref, ...), custom_call_target="tpu_custom_call" | custom-call | flops 20132659200 | tf_op jit(solution)/shard_map/partial_grams/pallas_call | solution.py:190
  36.3 1.0 %collective-permute-done.1.refs_1_ = bf16[2,4,144,128]{3,2,1,0:T(8,128)(2,1)S(1)} collective-permute-done((bf16[2,4,144,128]{3,2,1,0:T(8,128)(2,1)S(1)}, bf16[2,4,144,128]{3,2,1,0:T(8,128)(2,1)S(1)}, u32[]{:S(2)}, u32[]{:S(2)}) %collective-permute-start.1) | collective-permute-done | bytes 294944 | tf_op jit(solution)/shard_map/ppermute | solution.py:350
  38.7 1.4 %collective-permute-start.5 = (bf16[3,4,144,128]{3,2,1,0:T(8,128)(2,1)S(1)}, bf16[3,4,144,128]{3,2,1,0:T(8,128)(2,1)S(1)}, u32[]{:S(2)}, u32[]{:S(2)}) collective-permute-start(bf16[3,4,144,128]{3,2,1,0:T(8,128)(2,1)S(1)} %get-tuple-element.80), channel_id=1, source_target_pairs={{0,1},{1,0},{2,3},{3,2},{4,5},{5,4},{6,7},{7,6},{8,9},{9,8},{10,11... | collective-permute-start | bytes 1327112 | tf_op jit(solution)/shard_map/ppermute | solution.py:350
  40.1 3.5 %partial_grams.12 = bf16[4,8,144,128]{3,2,1,0:T(8,128)(2,1)S(1)} custom-call(s32[32,26]{1,0:T(8,128)S(4)} %get-tuple-element.64.requests_ref, bf16[192,144,128]{2,1,0:T(8,128)(2,1)S(1)} %get-tuple-element.65.left_ref, f32[192,128]{1,0:T(8,128)S(1)} %get-tuple-element.66.rinv_ref, s32[192,128]{1,0:T(8,128)S(1)} %get-tuple-element.67.obs_lon_ref, ...), custom_call_target="tpu_custom_call" | custom-call | flops 20132659200 | tf_op jit(solution)/shard_map/partial_grams/pallas_call | solution.py:190
  43.8 3.5 %partial_grams.13.refs_6_ = bf16[4,8,144,128]{3,2,1,0:T(8,128)(2,1)S(1)} custom-call(s32[32,26]{1,0:T(8,128)S(4)} %get-tuple-element.64.requests_ref, bf16[192,144,128]{2,1,0:T(8,128)(2,1)S(1)} %get-tuple-element.65.left_ref, f32[192,128]{1,0:T(8,128)S(1)} %get-tuple-element.66.rinv_ref, s32[192,128]{1,0:T(8,128)S(1)} %get-tuple-element.67.obs_lon_ref, ...), custom_call_target="tpu_custom_call" | custom-call | flops 20132659200 | tf_op jit(solution)/shard_map/partial_grams/pallas_call | solution.py:190
  47.3 2.3 %collective-permute-done.4.refs_1_ = bf16[3,4,144,128]{3,2,1,0:T(8,128)(2,1)S(1)} collective-permute-done((bf16[3,4,144,128]{3,2,1,0:T(8,128)(2,1)S(1)}, bf16[3,4,144,128]{3,2,1,0:T(8,128)(2,1)S(1)}, u32[]{:S(2)}, u32[]{:S(2)}) %collective-permute-start.4) | collective-permute-done | bytes 442400 | tf_op jit(solution)/shard_map/ppermute | solution.py:350
  52.5 1.4 %collective-permute-start.8 = (bf16[3,4,144,128]{3,2,1,0:T(8,128)(2,1)S(1)}, bf16[3,4,144,128]{3,2,1,0:T(8,128)(2,1)S(1)}, u32[]{:S(2)}, u32[]{:S(2)}) collective-permute-start(bf16[3,4,144,128]{3,2,1,0:T(8,128)(2,1)S(1)} %get-tuple-element.87), channel_id=1, source_target_pairs={{0,1},{1,0},{2,3},{3,2},{4,5},{5,4},{6,7},{7,6},{8,9},{9,8},{10,11... | collective-permute-start | bytes 1327112 | tf_op jit(solution)/shard_map/ppermute | solution.py:350
  53.9 3.5 %partial_grams.14 = bf16[4,8,144,128]{3,2,1,0:T(8,128)(2,1)S(1)} custom-call(s32[32,26]{1,0:T(8,128)S(4)} %get-tuple-element.64.requests_ref, bf16[192,144,128]{2,1,0:T(8,128)(2,1)S(1)} %get-tuple-element.65.left_ref, f32[192,128]{1,0:T(8,128)S(1)} %get-tuple-element.66.rinv_ref, s32[192,128]{1,0:T(8,128)S(1)} %get-tuple-element.67.obs_lon_ref, ...), custom_call_target="tpu_custom_call" | custom-call | flops 20132659200 | tf_op jit(solution)/shard_map/partial_grams/pallas_call | solution.py:190
  57.5 3.6 %partial_grams.15.refs_0_ = bf16[4,8,144,128]{3,2,1,0:T(8,128)(2,1)S(1)} custom-call(s32[32,26]{1,0:T(8,128)S(4)} %get-tuple-element.64.requests_ref, bf16[192,144,128]{2,1,0:T(8,128)(2,1)S(1)} %get-tuple-element.65.left_ref, f32[192,128]{1,0:T(8,128)S(1)} %get-tuple-element.66.rinv_ref, s32[192,128]{1,0:T(8,128)S(1)} %get-tuple-element.67.obs_lon_ref, ...), custom_call_target="tpu_custom_call" | custom-call | flops 20132659200 | tf_op jit(solution)/shard_map/partial_grams/pallas_call | solution.py:190
  61.0 1.3 %collective-permute-done.7.refs_1_ = bf16[3,4,144,128]{3,2,1,0:T(8,128)(2,1)S(1)} collective-permute-done((bf16[3,4,144,128]{3,2,1,0:T(8,128)(2,1)S(1)}, bf16[3,4,144,128]{3,2,1,0:T(8,128)(2,1)S(1)}, u32[]{:S(2)}, u32[]{:S(2)}) %collective-permute-start.7) | collective-permute-done | bytes 442400 | tf_op jit(solution)/shard_map/ppermute | solution.py:350
  62.9 1.5 %collective-permute-start.11 = (bf16[1,4,144,128]{3,2,1,0:T(8,128)(2,1)S(1)}, bf16[1,4,144,128]{3,2,1,0:T(8,128)(2,1)S(1)}, u32[]{:S(2)}, u32[]{:S(2)}) collective-permute-start(bf16[1,4,144,128]{3,2,1,0:T(8,128)(2,1)S(1)} %get-tuple-element.99), channel_id=1, source_target_pairs={{0,16},{8,24},{16,0},{24,8},{1,17},{9,25},{17,1},{25,9},{2,18},{10... | collective-permute-start | bytes 442376 | tf_op jit(solution)/shard_map/ppermute | solution.py:350
  64.4 1.3 %collective-permute-start.12 = (bf16[1,4,144,128]{3,2,1,0:T(8,128)(2,1)S(1)}, bf16[1,4,144,128]{3,2,1,0:T(8,128)(2,1)S(1)}, u32[]{:S(2)}, u32[]{:S(2)}) collective-permute-start(bf16[1,4,144,128]{3,2,1,0:T(8,128)(2,1)S(1)} %get-tuple-element.101), channel_id=1, source_target_pairs={{0,1},{1,0},{2,3},{3,2},{4,5},{5,4},{6,7},{7,6},{8,9},{9,8},{10,11... | collective-permute-start | bytes 442376 | tf_op jit(solution)/shard_map/ppermute | solution.py:350
  67.4 1.5 %collective-permute-start.10 = (bf16[1,8,144,128]{3,2,1,0:T(8,128)(2,1)S(1)}, bf16[1,8,144,128]{3,2,1,0:T(8,128)(2,1)S(1)}, u32[]{:S(2)}, u32[]{:S(2)}) collective-permute-start(bf16[1,8,144,128]{3,2,1,0:T(8,128)(2,1)S(1)} %get-tuple-element.97), channel_id=1, source_target_pairs={{0,4},{1,5},{2,6},{3,7},{4,0},{5,1},{6,2},{7,3},{8,12},{9,13},{10,... | collective-permute-start | bytes 884744 | tf_op jit(solution)/shard_map/ppermute | solution.py:350
  69.0 2.1 %collective-permute-done.12.refs_3_ = bf16[1,4,144,128]{3,2,1,0:T(8,128)(2,1)S(1)} collective-permute-done((bf16[1,4,144,128]{3,2,1,0:T(8,128)(2,1)S(1)}, bf16[1,4,144,128]{3,2,1,0:T(8,128)(2,1)S(1)}, u32[]{:S(2)}, u32[]{:S(2)}) %collective-permute-start.12) | collective-permute-done | bytes 147488 | tf_op jit(solution)/shard_map/ppermute | solution.py:350
  71.9 3.0 %collective-permute-done.15.refs_1_ = bf16[2,4,144,128]{3,2,1,0:T(8,128)(2,1)S(1)} collective-permute-done((bf16[2,4,144,128]{3,2,1,0:T(8,128)(2,1)S(1)}, bf16[2,4,144,128]{3,2,1,0:T(8,128)(2,1)S(1)}, u32[]{:S(2)}, u32[]{:S(2)}) %collective-permute-start.15) | collective-permute-done | bytes 294944 | tf_op jit(solution)/shard_map/ppermute | solution.py:350
  75.0 1.0 %collective-permute-start.17 = (bf16[1,4,144,128]{3,2,1,0:T(8,128)(2,1)S(1)}, bf16[1,4,144,128]{3,2,1,0:T(8,128)(2,1)S(1)}, u32[]{:S(2)}, u32[]{:S(2)}) collective-permute-start(bf16[1,4,144,128]{3,2,1,0:T(8,128)(2,1)S(1)} %get-tuple-element.108), channel_id=1, source_target_pairs={{0,16},{8,24},{16,0},{24,8},{1,17},{9,25},{17,1},{25,9},{2,18},{10... | collective-permute-start | bytes 442376 | tf_op jit(solution)/shard_map/ppermute | solution.py:350
  76.8 3.4 %collective-permute-done.17.refs_1_ = bf16[1,4,144,128]{3,2,1,0:T(8,128)(2,1)S(1)} collective-permute-done((bf16[1,4,144,128]{3,2,1,0:T(8,128)(2,1)S(1)}, bf16[1,4,144,128]{3,2,1,0:T(8,128)(2,1)S(1)}, u32[]{:S(2)}, u32[]{:S(2)}) %collective-permute-start.17) | collective-permute-done | bytes 147488 | tf_op jit(solution)/shard_map/ppermute | solution.py:350
  81.4 1.3 %collective-permute-done.13.refs_2_ = bf16[1,8,144,128]{3,2,1,0:T(8,128)(2,1)S(1)} collective-permute-done((bf16[1,8,144,128]{3,2,1,0:T(8,128)(2,1)S(1)}, bf16[1,8,144,128]{3,2,1,0:T(8,128)(2,1)S(1)}, u32[]{:S(2)}, u32[]{:S(2)}) %collective-permute-start.13) | collective-permute-done | bytes 294944 | tf_op jit(solution)/shard_map/ppermute | solution.py:350
  82.6 10.4 %analysis.1 = f32[16,6,128,256]{3,2,1,0:T(8,128)} custom-call(bf16[1,8,144,128]{3,2,1,0:T(8,128)(2,1)S(1)} %collective-permute-done.9.refs_0_, bf16[1,8,144,128]{3,2,1,0:T(8,128)(2,1)S(1)} %collective-permute-done.10.refs_1_, bf16[1,8,144,128]{3,2,1,0:T(8,128)(2,1)S(1)} %collective-permute-done.13.refs_2_, ...), custom_call_target="tpu_custom_call" | custom-call | tf_op jit(solution)/shard_map/analysis/pallas_call | solution.py:328
  (52 shorter events, 14.1 us)
Async XLA Ops:
  23.9 3.6 %collective-permute-start = (bf16[4,8,144,128]{3,2,1,0:T(8,128)(2,1)S(1)}, bf16[4,8,144,128]{3,2,1,0:T(8,128)(2,1)S(1)}, u32[]{:S(2)}, u32[]{:S(2)}) collective-permute-start(bf16[4,8,144,128]{3,2,1,0:T(8,128)(2,1)S(1)} %partial_grams.8), channel_id=1, source_target_pairs={{0,8},{8,0},{16,24},{24,16},{1,9},{9,1},{17,25},{25,17},{2,10},{10... | collective-permute-start | bytes 3538952 | tf_op jit(solution)/shard_map/ppermute | solution.py:350
  27.8 9.4 %collective-permute-start.1 = (bf16[2,4,144,128]{3,2,1,0:T(8,128)(2,1)S(1)}, bf16[2,4,144,128]{3,2,1,0:T(8,128)(2,1)S(1)}, u32[]{:S(2)}, u32[]{:S(2)}) collective-permute-start(bf16[2,4,144,128]{3,2,1,0:T(8,128)(2,1)S(1)} %get-tuple-element.72), channel_id=1, source_target_pairs={{0,1},{1,0},{2,3},{3,2},{4,5},{5,4},{6,7},{7,6},{8,9},{9,8},{10,11... | collective-permute-start | bytes 884744 | tf_op jit(solution)/shard_map/ppermute | solution.py:350
  28.5 9.1 %collective-permute-start.2 = (bf16[2,4,144,128]{3,2,1,0:T(8,128)(2,1)S(1)}, bf16[2,4,144,128]{3,2,1,0:T(8,128)(2,1)S(1)}, u32[]{:S(2)}, u32[]{:S(2)}) collective-permute-start(bf16[2,4,144,128]{3,2,1,0:T(8,128)(2,1)S(1)} %get-tuple-element.74), channel_id=1, source_target_pairs={{0,16},{8,24},{16,0},{24,8},{1,17},{9,25},{17,1},{25,9},{2,18},{10... | collective-permute-start | bytes 884744 | tf_op jit(solution)/shard_map/ppermute | solution.py:350
  32.7 5.0 %collective-permute-start.3 = (bf16[4,8,144,128]{3,2,1,0:T(8,128)(2,1)S(1)}, bf16[4,8,144,128]{3,2,1,0:T(8,128)(2,1)S(1)}, u32[]{:S(2)}, u32[]{:S(2)}) collective-permute-start(bf16[4,8,144,128]{3,2,1,0:T(8,128)(2,1)S(1)} %partial_grams.10), channel_id=1, source_target_pairs={{0,8},{8,0},{16,24},{24,16},{1,9},{9,1},{17,25},{25,17},{2,10},{10... | collective-permute-start | bytes 3538952 | tf_op jit(solution)/shard_map/ppermute | solution.py:350
  38.1 11.5 %collective-permute-start.4 = (bf16[3,4,144,128]{3,2,1,0:T(8,128)(2,1)S(1)}, bf16[3,4,144,128]{3,2,1,0:T(8,128)(2,1)S(1)}, u32[]{:S(2)}, u32[]{:S(2)}) collective-permute-start(bf16[3,4,144,128]{3,2,1,0:T(8,128)(2,1)S(1)} %get-tuple-element.78), channel_id=1, source_target_pairs={{0,16},{8,24},{16,0},{24,8},{1,17},{9,25},{17,1},{25,9},{2,18},{10... | collective-permute-start | bytes 1327112 | tf_op jit(solution)/shard_map/ppermute | solution.py:350
  38.7 11.8 %collective-permute-start.5 = (bf16[3,4,144,128]{3,2,1,0:T(8,128)(2,1)S(1)}, bf16[3,4,144,128]{3,2,1,0:T(8,128)(2,1)S(1)}, u32[]{:S(2)}, u32[]{:S(2)}) collective-permute-start(bf16[3,4,144,128]{3,2,1,0:T(8,128)(2,1)S(1)} %get-tuple-element.80), channel_id=1, source_target_pairs={{0,1},{1,0},{2,3},{3,2},{4,5},{5,4},{6,7},{7,6},{8,9},{9,8},{10,11... | collective-permute-start | bytes 1327112 | tf_op jit(solution)/shard_map/ppermute | solution.py:350
  43.7 6.9 %collective-permute-start.6 = (bf16[4,8,144,128]{3,2,1,0:T(8,128)(2,1)S(1)}, bf16[4,8,144,128]{3,2,1,0:T(8,128)(2,1)S(1)}, u32[]{:S(2)}, u32[]{:S(2)}) collective-permute-start(bf16[4,8,144,128]{3,2,1,0:T(8,128)(2,1)S(1)} %partial_grams.12), channel_id=1, source_target_pairs={{0,8},{8,0},{16,24},{24,16},{1,9},{9,1},{17,25},{25,17},{2,10},{10... | collective-permute-start | bytes 3538952 | tf_op jit(solution)/shard_map/ppermute | solution.py:350
  51.0 16.4 %collective-permute-start.9 = (bf16[1,8,144,128]{3,2,1,0:T(8,128)(2,1)S(1)}, bf16[1,8,144,128]{3,2,1,0:T(8,128)(2,1)S(1)}, u32[]{:S(2)}, u32[]{:S(2)}) collective-permute-start(bf16[1,8,144,128]{3,2,1,0:T(8,128)(2,1)S(1)} %get-tuple-element.88), channel_id=1, source_target_pairs={{0,6},{1,7},{2,4},{3,5},{4,2},{5,3},{6,0},{7,1},{8,14},{9,15},{10,... | collective-permute-start | bytes 884744 | tf_op jit(solution)/shard_map/ppermute | solution.py:350
  51.7 10.7 %collective-permute-start.7 = (bf16[3,4,144,128]{3,2,1,0:T(8,128)(2,1)S(1)}, bf16[3,4,144,128]{3,2,1,0:T(8,128)(2,1)S(1)}, u32[]{:S(2)}, u32[]{:S(2)}) collective-permute-start(bf16[3,4,144,128]{3,2,1,0:T(8,128)(2,1)S(1)} %get-tuple-element.86), channel_id=1, source_target_pairs={{0,16},{8,24},{16,0},{24,8},{1,17},{9,25},{17,1},{25,9},{2,18},{10... | collective-permute-start | bytes 1327112 | tf_op jit(solution)/shard_map/ppermute | solution.py:350
  52.5 10.2 %collective-permute-start.8 = (bf16[3,4,144,128]{3,2,1,0:T(8,128)(2,1)S(1)}, bf16[3,4,144,128]{3,2,1,0:T(8,128)(2,1)S(1)}, u32[]{:S(2)}, u32[]{:S(2)}) collective-permute-start(bf16[3,4,144,128]{3,2,1,0:T(8,128)(2,1)S(1)} %get-tuple-element.87), channel_id=1, source_target_pairs={{0,1},{1,0},{2,3},{3,2},{4,5},{5,4},{6,7},{7,6},{8,9},{9,8},{10,11... | collective-permute-start | bytes 1327112 | tf_op jit(solution)/shard_map/ppermute | solution.py:350
  57.4 8.3 %collective-permute-start.14 = (bf16[4,8,144,128]{3,2,1,0:T(8,128)(2,1)S(1)}, bf16[4,8,144,128]{3,2,1,0:T(8,128)(2,1)S(1)}, u32[]{:S(2)}, u32[]{:S(2)}) collective-permute-start(bf16[4,8,144,128]{3,2,1,0:T(8,128)(2,1)S(1)} %partial_grams.14), channel_id=1, source_target_pairs={{0,8},{8,0},{16,24},{24,16},{1,9},{9,1},{17,25},{25,17},{2,10},{10... | collective-permute-start | bytes 3538952 | tf_op jit(solution)/shard_map/ppermute | solution.py:350
  62.7 20.0 %slice-start = ((s8[6291456]{0:T(1024)(128)(4,1)}), s8[4194304]{0:T(1024)(128)(4,1)S(1)}, s32[]{:S(2)}) async-start(s8[6291456]{0:T(1024)(128)(4,1)} %bitcast.6), calls=%async_computation.1 | async-start | bytes 8388608
  62.9 6.1 %collective-permute-start.11 = (bf16[1,4,144,128]{3,2,1,0:T(8,128)(2,1)S(1)}, bf16[1,4,144,128]{3,2,1,0:T(8,128)(2,1)S(1)}, u32[]{:S(2)}, u32[]{:S(2)}) collective-permute-start(bf16[1,4,144,128]{3,2,1,0:T(8,128)(2,1)S(1)} %get-tuple-element.99), channel_id=1, source_target_pairs={{0,16},{8,24},{16,0},{24,8},{1,17},{9,25},{17,1},{25,9},{2,18},{10... | collective-permute-start | bytes 442376 | tf_op jit(solution)/shard_map/ppermute | solution.py:350
  64.4 6.8 %collective-permute-start.12 = (bf16[1,4,144,128]{3,2,1,0:T(8,128)(2,1)S(1)}, bf16[1,4,144,128]{3,2,1,0:T(8,128)(2,1)S(1)}, u32[]{:S(2)}, u32[]{:S(2)}) collective-permute-start(bf16[1,4,144,128]{3,2,1,0:T(8,128)(2,1)S(1)} %get-tuple-element.101), channel_id=1, source_target_pairs={{0,1},{1,0},{2,3},{3,2},{4,5},{5,4},{6,7},{7,6},{8,9},{9,8},{10,11... | collective-permute-start | bytes 442376 | tf_op jit(solution)/shard_map/ppermute | solution.py:350
  66.0 8.9 %collective-permute-start.15 = (bf16[2,4,144,128]{3,2,1,0:T(8,128)(2,1)S(1)}, bf16[2,4,144,128]{3,2,1,0:T(8,128)(2,1)S(1)}, u32[]{:S(2)}, u32[]{:S(2)}) collective-permute-start(bf16[2,4,144,128]{3,2,1,0:T(8,128)(2,1)S(1)} %get-tuple-element.104), channel_id=1, source_target_pairs={{0,1},{1,0},{2,3},{3,2},{4,5},{5,4},{6,7},{7,6},{8,9},{9,8},{10,11... | collective-permute-start | bytes 884744 | tf_op jit(solution)/shard_map/ppermute | solution.py:350
  66.8 8.1 %collective-permute-start.16 = (bf16[2,4,144,128]{3,2,1,0:T(8,128)(2,1)S(1)}, bf16[2,4,144,128]{3,2,1,0:T(8,128)(2,1)S(1)}, u32[]{:S(2)}, u32[]{:S(2)}) collective-permute-start(bf16[2,4,144,128]{3,2,1,0:T(8,128)(2,1)S(1)} %get-tuple-element.106), channel_id=1, source_target_pairs={{0,16},{8,24},{16,0},{24,8},{1,17},{9,25},{17,1},{25,9},{2,18},{10... | collective-permute-start | bytes 884744 | tf_op jit(solution)/shard_map/ppermute | solution.py:350
  67.4 14.0 %collective-permute-start.10 = (bf16[1,8,144,128]{3,2,1,0:T(8,128)(2,1)S(1)}, bf16[1,8,144,128]{3,2,1,0:T(8,128)(2,1)S(1)}, u32[]{:S(2)}, u32[]{:S(2)}) collective-permute-start(bf16[1,8,144,128]{3,2,1,0:T(8,128)(2,1)S(1)} %get-tuple-element.97), channel_id=1, source_target_pairs={{0,4},{1,5},{2,6},{3,7},{4,0},{5,1},{6,2},{7,3},{8,12},{9,13},{10,... | collective-permute-start | bytes 884744 | tf_op jit(solution)/shard_map/ppermute | solution.py:350
  71.2 5.6 %copy-start = (f32[8,2,6,256]{3,1,2,0:T(2,128)S(1)}, f32[8,2,6,256]{3,1,2,0:T(2,128)}, u32[]{:S(2)}) copy-start(f32[8,2,6,256]{3,1,2,0:T(2,128)} %param.10) | copy-start | bytes 294916
  71.2 11.5 %slice-start.1 = ((s8[6291456]{0:T(1024)(128)(4,1)}), s8[2097152]{0:T(1024)(128)(4,1)S(1)}, s32[]{:S(2)}) async-start(s8[6291456]{0:T(1024)(128)(4,1)} %bitcast.6), calls=%async_computation.2 | async-start | bytes 4194304
  71.3 11.4 %collective-permute-start.13 = (bf16[1,8,144,128]{3,2,1,0:T(8,128)(2,1)S(1)}, bf16[1,8,144,128]{3,2,1,0:T(8,128)(2,1)S(1)}, u32[]{:S(2)}, u32[]{:S(2)}) collective-permute-start(bf16[1,8,144,128]{3,2,1,0:T(8,128)(2,1)S(1)} %add_partials.12), channel_id=1, source_target_pairs={{0,2},{1,3},{2,0},{3,1},{4,6},{5,7},{6,4},{7,5},{8,10},{9,11},{10,... | collective-permute-start | bytes 884744 | tf_op jit(solution)/shard_map/ppermute | solution.py:350
  75.0 5.2 %collective-permute-start.17 = (bf16[1,4,144,128]{3,2,1,0:T(8,128)(2,1)S(1)}, bf16[1,4,144,128]{3,2,1,0:T(8,128)(2,1)S(1)}, u32[]{:S(2)}, u32[]{:S(2)}) collective-permute-start(bf16[1,4,144,128]{3,2,1,0:T(8,128)(2,1)S(1)} %get-tuple-element.108), channel_id=1, source_target_pairs={{0,16},{8,24},{16,0},{24,8},{1,17},{9,25},{17,1},{25,9},{2,18},{10... | collective-permute-start | bytes 442376 | tf_op jit(solution)/shard_map/ppermute | solution.py:350
  76.1 5.1 %collective-permute-start.18 = (bf16[1,4,144,128]{3,2,1,0:T(8,128)(2,1)S(1)}, bf16[1,4,144,128]{3,2,1,0:T(8,128)(2,1)S(1)}, u32[]{:S(2)}, u32[]{:S(2)}) collective-permute-start(bf16[1,4,144,128]{3,2,1,0:T(8,128)(2,1)S(1)} %get-tuple-element.110), channel_id=1, source_target_pairs={{0,1},{1,0},{2,3},{3,2},{4,5},{5,4},{6,7},{7,6},{8,9},{9,8},{10,11... | collective-permute-start | bytes 442376 | tf_op jit(solution)/shard_map/ppermute | solution.py:350

commit v11 on v10

--- a/solution.py
+++ b/solution.py
@@ -165,6 +165,7 @@
     row = lax.broadcasted_iota(jnp.int32, (members, members), 0)
     column = lax.broadcasted_iota(jnp.int32, (members, members), 1)
     line = lax.broadcasted_iota(jnp.int32, (8, members), 0)
+    lane = lax.broadcasted_iota(jnp.int32, (8, members), 1)
     for pair in range(patches // 2):
         first = acc_ref[2 * pair]
         second = acc_ref[2 * pair + 1]
@@ -172,9 +173,10 @@
         out_ref[0, pair, :members, :] = packed.astype(BF16)
         rows = totals_ref[...]
         for place, values in ((0, first), (2, second)):
-            diagonal = jnp.sum(
-                jnp.where(row == column, values[:members], 0.0), axis=0, keepdims=True
-            )
+            tile = values[:8]
+            for i in range(1, members // 8):
+                tile = jnp.where(lane // 8 == i, values[8 * i : 8 * i + 8], tile)
+            diagonal = jnp.sum(jnp.where(lane % 8 == line, tile, 0.0), axis=0, keepdims=True)
             projected = values[members : members + 1] + values[members + 1 : members + 2]
             rows = jnp.where(line == place, diagonal, rows)
             rows = jnp.where(line == place + 1, projected, rows)

time: 93.3 us -> 92.7 us (level)
  Pallas kernels: 44 us -> 43 us
    pallas_call x8, Pallas kernels: 28.3 us -> 27.3 us  [partial_grams(): pl.pallas_call(functools.partial(gram_kernel, sizes, far, core), out_shap...]
  transfers between devices with their start and end apart: 19 -> 19, of which waited for: 13 -> 13; matrix products, arithmetic and copies ran while one was open for 0% -> 0% of each run, Pallas kernels for 28% -> 27%
where the time goes in v11:
time: 92.7 us; the launch traced here: 92.4 us
  Pallas kernels  43 us (46%)
  waiting for transfers between devices  17.4 us (19%)
  starting transfers between devices  14.8 us (16%)
  blocking collectives  14.2 us (15%)
  other arithmetic  1.87 us (2%)
  local copies, waits for them, and re-layouts  1.02 us (1%)
    pallas_call x8, Pallas kernels, partial_grams(): pl.pallas_call(functools.partial(gram_kernel, sizes, far, core), out_shap...  27.3 us
    ppermute x19, waiting for transfers between devices, swap(): return lax.ppermute(value, axis, [(i, i ^ flip) for i in range(size)])  17.4 us
    ppermute x19, starting transfers between devices, swap(): return lax.ppermute(value, axis, [(i, i ^ flip) for i in range(size)])  14.8 us
    all_to_all x1, blocking collectives, on_device(): lax.all_to_all(table, ('lon', 'lat'), split_axis=0, concat_axis=0, tiled=...  14.2 us
    pallas_call x1, Pallas kernels, analysis(): pl.pallas_call(functools.partial(analysis_kernel, len(parts), total_obs,...  10.4 us
    pallas_call x1, Pallas kernels, stage(): pl.pallas_call(functools.partial(stage_kernel, chunk), out_shape=[pltpu.V...  3.23 us
    pallas_call x8, Pallas kernels, add_all(): pl.pallas_call(functools.partial(add_kernel, len(arrays), size, jobs), ou...  2.04 us
  transfers between devices with their start and end apart: 19, of which 13 were waited for; matrix products, arithmetic and copies ran while one was open for 0% of the time, Pallas kernels for 27%

profile of v11, /device:TPU:0, one launch (start us, length us, event | category | flops | bytes accessed | tf_op | source)
XLA Modules:
  0.0 92.4 jit_solution(1781723608637361835)
XLA Ops:
  2.9 14.2 %all_to_all.9 = s32[32,1,26]{2,1,0:T(1,128)S(1)} all-to-all(s32[32,1,26]{2,1,0:T(1,128)S(1)} %copy.15), channel_id=1, replica_groups=mesh['lon'=4,'lat'=8] {'lon','lat'}, dimensions={0} | all-to-all | bytes 6656 | tf_op jit(solution)/shard_map/all_to_all | solution.py:366
  17.1 3.2 %stage.1 = (bf16[192,144,128]{2,1,0:T(8,128)(2,1)S(1)}, f32[192,128]{1,0:T(8,128)S(1)}, s32[192,128]{1,0:T(8,128)S(1)}, s32[192,128]{1,0:T(8,128)S(1)}, f32[8,128]{1,0:T(8,128)S(1)}, /*index=5*/s32[32,26]{1,0:T(8,128)S(4)}) custom-call(bf16[192,128,128]{2,1,0:T(8,128)(2,1)} %anom_hbm, f32[192,128]{1,0:T(8,128)} %innov_hbm, f32[192,128]{1,0:T(8,128)} %rinv_hbm, ...), custom_call_target="tpu_custom_call" | custom-call | bytes 12582912 | tf_op jit(solution)/shard_map/stage/pallas_call | solution.py:98
  20.3 3.4 %partial_grams.8 = bf16[4,8,144,128]{3,2,1,0:T(8,128)(2,1)S(1)} custom-call(s32[32,26]{1,0:T(8,128)S(4)} %get-tuple-element.64.requests_ref, bf16[192,144,128]{2,1,0:T(8,128)(2,1)S(1)} %get-tuple-element.65.left_ref, f32[192,128]{1,0:T(8,128)S(1)} %get-tuple-element.66.rinv_ref, s32[192,128]{1,0:T(8,128)S(1)} %get-tuple-element.67.obs_lon_ref, ...), custom_call_target="tpu_custom_call" | custom-call | flops 20132659200 | tf_op jit(solution)/shard_map/partial_grams/pallas_call | solution.py:192
  23.8 3.4 %partial_grams.9.refs_0_ = bf16[4,8,144,128]{3,2,1,0:T(8,128)(2,1)S(1)} custom-call(s32[32,26]{1,0:T(8,128)S(4)} %get-tuple-element.64.requests_ref, bf16[192,144,128]{2,1,0:T(8,128)(2,1)S(1)} %get-tuple-element.65.left_ref, f32[192,128]{1,0:T(8,128)S(1)} %get-tuple-element.66.rinv_ref, s32[192,128]{1,0:T(8,128)S(1)} %get-tuple-element.67.obs_lon_ref, ...), custom_call_target="tpu_custom_call" | custom-call | flops 20132659200 | tf_op jit(solution)/shard_map/partial_grams/pallas_call | solution.py:192
  28.8 3.4 %partial_grams.10 = bf16[4,8,144,128]{3,2,1,0:T(8,128)(2,1)S(1)} custom-call(s32[32,26]{1,0:T(8,128)S(4)} %get-tuple-element.64.requests_ref, bf16[192,144,128]{2,1,0:T(8,128)(2,1)S(1)} %get-tuple-element.65.left_ref, f32[192,128]{1,0:T(8,128)S(1)} %get-tuple-element.66.rinv_ref, s32[192,128]{1,0:T(8,128)S(1)} %get-tuple-element.67.obs_lon_ref, ...), custom_call_target="tpu_custom_call" | custom-call | flops 20132659200 | tf_op jit(solution)/shard_map/partial_grams/pallas_call | solution.py:192
  32.3 3.4 %partial_grams.11.refs_4_ = bf16[4,8,144,128]{3,2,1,0:T(8,128)(2,1)S(1)} custom-call(s32[32,26]{1,0:T(8,128)S(4)} %get-tuple-element.64.requests_ref, bf16[192,144,128]{2,1,0:T(8,128)(2,1)S(1)} %get-tuple-element.65.left_ref, f32[192,128]{1,0:T(8,128)S(1)} %get-tuple-element.66.rinv_ref, s32[192,128]{1,0:T(8,128)S(1)} %get-tuple-element.67.obs_lon_ref, ...), custom_call_target="tpu_custom_call" | custom-call | flops 20132659200 | tf_op jit(solution)/shard_map/partial_grams/pallas_call | solution.py:192
  35.7 1.3 %collective-permute-done.1.refs_1_ = bf16[2,4,144,128]{3,2,1,0:T(8,128)(2,1)S(1)} collective-permute-done((bf16[2,4,144,128]{3,2,1,0:T(8,128)(2,1)S(1)}, bf16[2,4,144,128]{3,2,1,0:T(8,128)(2,1)S(1)}, u32[]{:S(2)}, u32[]{:S(2)}) %collective-permute-start.1) | collective-permute-done | bytes 294944 | tf_op jit(solution)/shard_map/ppermute | solution.py:352
  38.5 1.4 %collective-permute-start.5 = (bf16[3,4,144,128]{3,2,1,0:T(8,128)(2,1)S(1)}, bf16[3,4,144,128]{3,2,1,0:T(8,128)(2,1)S(1)}, u32[]{:S(2)}, u32[]{:S(2)}) collective-permute-start(bf16[3,4,144,128]{3,2,1,0:T(8,128)(2,1)S(1)} %get-tuple-element.80), channel_id=1, source_target_pairs={{0,1},{1,0},{2,3},{3,2},{4,5},{5,4},{6,7},{7,6},{8,9},{9,8},{10,11... | collective-permute-start | bytes 1327112 | tf_op jit(solution)/shard_map/ppermute | solution.py:352
  39.9 3.4 %partial_grams.12 = bf16[4,8,144,128]{3,2,1,0:T(8,128)(2,1)S(1)} custom-call(s32[32,26]{1,0:T(8,128)S(4)} %get-tuple-element.64.requests_ref, bf16[192,144,128]{2,1,0:T(8,128)(2,1)S(1)} %get-tuple-element.65.left_ref, f32[192,128]{1,0:T(8,128)S(1)} %get-tuple-element.66.rinv_ref, s32[192,128]{1,0:T(8,128)S(1)} %get-tuple-element.67.obs_lon_ref, ...), custom_call_target="tpu_custom_call" | custom-call | flops 20132659200 | tf_op jit(solution)/shard_map/partial_grams/pallas_call | solution.py:192
  43.3 3.4 %partial_grams.13.refs_6_ = bf16[4,8,144,128]{3,2,1,0:T(8,128)(2,1)S(1)} custom-call(s32[32,26]{1,0:T(8,128)S(4)} %get-tuple-element.64.requests_ref, bf16[192,144,128]{2,1,0:T(8,128)(2,1)S(1)} %get-tuple-element.65.left_ref, f32[192,128]{1,0:T(8,128)S(1)} %get-tuple-element.66.rinv_ref, s32[192,128]{1,0:T(8,128)S(1)} %get-tuple-element.67.obs_lon_ref, ...), custom_call_target="tpu_custom_call" | custom-call | flops 20132659200 | tf_op jit(solution)/shard_map/partial_grams/pallas_call | solution.py:192
  46.8 2.6 %collective-permute-done.4.refs_1_ = bf16[3,4,144,128]{3,2,1,0:T(8,128)(2,1)S(1)} collective-permute-done((bf16[3,4,144,128]{3,2,1,0:T(8,128)(2,1)S(1)}, bf16[3,4,144,128]{3,2,1,0:T(8,128)(2,1)S(1)}, u32[]{:S(2)}, u32[]{:S(2)}) %collective-permute-start.4) | collective-permute-done | bytes 442400 | tf_op jit(solution)/shard_map/ppermute | solution.py:352
  51.1 1.1 %collective-permute-start.7 = (bf16[3,4,144,128]{3,2,1,0:T(8,128)(2,1)S(1)}, bf16[3,4,144,128]{3,2,1,0:T(8,128)(2,1)S(1)}, u32[]{:S(2)}, u32[]{:S(2)}) collective-permute-start(bf16[3,4,144,128]{3,2,1,0:T(8,128)(2,1)S(1)} %get-tuple-element.86), channel_id=1, source_target_pairs={{0,16},{8,24},{16,0},{24,8},{1,17},{9,25},{17,1},{25,9},{2,18},{10... | collective-permute-start | bytes 1327112 | tf_op jit(solution)/shard_map/ppermute | solution.py:352
  52.2 1.4 %collective-permute-start.8 = (bf16[3,4,144,128]{3,2,1,0:T(8,128)(2,1)S(1)}, bf16[3,4,144,128]{3,2,1,0:T(8,128)(2,1)S(1)}, u32[]{:S(2)}, u32[]{:S(2)}) collective-permute-start(bf16[3,4,144,128]{3,2,1,0:T(8,128)(2,1)S(1)} %get-tuple-element.87), channel_id=1, source_target_pairs={{0,1},{1,0},{2,3},{3,2},{4,5},{5,4},{6,7},{7,6},{8,9},{9,8},{10,11... | collective-permute-start | bytes 1327112 | tf_op jit(solution)/shard_map/ppermute | solution.py:352
  53.6 3.4 %partial_grams.14 = bf16[4,8,144,128]{3,2,1,0:T(8,128)(2,1)S(1)} custom-call(s32[32,26]{1,0:T(8,128)S(4)} %get-tuple-element.64.requests_ref, bf16[192,144,128]{2,1,0:T(8,128)(2,1)S(1)} %get-tuple-element.65.left_ref, f32[192,128]{1,0:T(8,128)S(1)} %get-tuple-element.66.rinv_ref, s32[192,128]{1,0:T(8,128)S(1)} %get-tuple-element.67.obs_lon_ref, ...), custom_call_target="tpu_custom_call" | custom-call | flops 20132659200 | tf_op jit(solution)/shard_map/partial_grams/pallas_call | solution.py:192
  57.1 3.4 %partial_grams.15.refs_0_ = bf16[4,8,144,128]{3,2,1,0:T(8,128)(2,1)S(1)} custom-call(s32[32,26]{1,0:T(8,128)S(4)} %get-tuple-element.64.requests_ref, bf16[192,144,128]{2,1,0:T(8,128)(2,1)S(1)} %get-tuple-element.65.left_ref, f32[192,128]{1,0:T(8,128)S(1)} %get-tuple-element.66.rinv_ref, s32[192,128]{1,0:T(8,128)S(1)} %get-tuple-element.67.obs_lon_ref, ...), custom_call_target="tpu_custom_call" | custom-call | flops 20132659200 | tf_op jit(solution)/shard_map/partial_grams/pallas_call | solution.py:192
  62.2 1.4 %collective-permute-start.11 = (bf16[1,4,144,128]{3,2,1,0:T(8,128)(2,1)S(1)}, bf16[1,4,144,128]{3,2,1,0:T(8,128)(2,1)S(1)}, u32[]{:S(2)}, u32[]{:S(2)}) collective-permute-start(bf16[1,4,144,128]{3,2,1,0:T(8,128)(2,1)S(1)} %get-tuple-element.99), channel_id=1, source_target_pairs={{0,16},{8,24},{16,0},{24,8},{1,17},{9,25},{17,1},{25,9},{2,18},{10... | collective-permute-start | bytes 442376 | tf_op jit(solution)/shard_map/ppermute | solution.py:352
  63.5 1.4 %collective-permute-start.12 = (bf16[1,4,144,128]{3,2,1,0:T(8,128)(2,1)S(1)}, bf16[1,4,144,128]{3,2,1,0:T(8,128)(2,1)S(1)}, u32[]{:S(2)}, u32[]{:S(2)}) collective-permute-start(bf16[1,4,144,128]{3,2,1,0:T(8,128)(2,1)S(1)} %get-tuple-element.101), channel_id=1, source_target_pairs={{0,1},{1,0},{2,3},{3,2},{4,5},{5,4},{6,7},{7,6},{8,9},{9,8},{10,11... | collective-permute-start | bytes 442376 | tf_op jit(solution)/shard_map/ppermute | solution.py:352
  66.6 1.4 %collective-permute-start.10 = (bf16[1,8,144,128]{3,2,1,0:T(8,128)(2,1)S(1)}, bf16[1,8,144,128]{3,2,1,0:T(8,128)(2,1)S(1)}, u32[]{:S(2)}, u32[]{:S(2)}) collective-permute-start(bf16[1,8,144,128]{3,2,1,0:T(8,128)(2,1)S(1)} %get-tuple-element.97), channel_id=1, source_target_pairs={{0,4},{1,5},{2,6},{3,7},{4,0},{5,1},{6,2},{7,3},{8,12},{9,13},{10,... | collective-permute-start | bytes 884744 | tf_op jit(solution)/shard_map/ppermute | solution.py:352
  68.4 1.9 %collective-permute-done.12.refs_3_ = bf16[1,4,144,128]{3,2,1,0:T(8,128)(2,1)S(1)} collective-permute-done((bf16[1,4,144,128]{3,2,1,0:T(8,128)(2,1)S(1)}, bf16[1,4,144,128]{3,2,1,0:T(8,128)(2,1)S(1)}, u32[]{:S(2)}, u32[]{:S(2)}) %collective-permute-start.12) | collective-permute-done | bytes 147488 | tf_op jit(solution)/shard_map/ppermute | solution.py:352
  70.9 3.2 %collective-permute-done.15.refs_1_ = bf16[2,4,144,128]{3,2,1,0:T(8,128)(2,1)S(1)} collective-permute-done((bf16[2,4,144,128]{3,2,1,0:T(8,128)(2,1)S(1)}, bf16[2,4,144,128]{3,2,1,0:T(8,128)(2,1)S(1)}, u32[]{:S(2)}, u32[]{:S(2)}) %collective-permute-start.15) | collective-permute-done | bytes 294944 | tf_op jit(solution)/shard_map/ppermute | solution.py:352
  74.2 1.1 %collective-permute-start.17 = (bf16[1,4,144,128]{3,2,1,0:T(8,128)(2,1)S(1)}, bf16[1,4,144,128]{3,2,1,0:T(8,128)(2,1)S(1)}, u32[]{:S(2)}, u32[]{:S(2)}) collective-permute-start(bf16[1,4,144,128]{3,2,1,0:T(8,128)(2,1)S(1)} %get-tuple-element.108), channel_id=1, source_target_pairs={{0,16},{8,24},{16,0},{24,8},{1,17},{9,25},{17,1},{25,9},{2,18},{10... | collective-permute-start | bytes 442376 | tf_op jit(solution)/shard_map/ppermute | solution.py:352
  76.3 3.1 %collective-permute-done.17.refs_1_ = bf16[1,4,144,128]{3,2,1,0:T(8,128)(2,1)S(1)} collective-permute-done((bf16[1,4,144,128]{3,2,1,0:T(8,128)(2,1)S(1)}, bf16[1,4,144,128]{3,2,1,0:T(8,128)(2,1)S(1)}, u32[]{:S(2)}, u32[]{:S(2)}) %collective-permute-start.17) | collective-permute-done | bytes 147488 | tf_op jit(solution)/shard_map/ppermute | solution.py:352
  80.8 1.2 %collective-permute-done.13.refs_2_ = bf16[1,8,144,128]{3,2,1,0:T(8,128)(2,1)S(1)} collective-permute-done((bf16[1,8,144,128]{3,2,1,0:T(8,128)(2,1)S(1)}, bf16[1,8,144,128]{3,2,1,0:T(8,128)(2,1)S(1)}, u32[]{:S(2)}, u32[]{:S(2)}) %collective-permute-start.13) | collective-permute-done | bytes 294944 | tf_op jit(solution)/shard_map/ppermute | solution.py:352
  82.0 10.4 %analysis.1 = f32[16,6,128,256]{3,2,1,0:T(8,128)} custom-call(bf16[1,8,144,128]{3,2,1,0:T(8,128)(2,1)S(1)} %collective-permute-done.9.refs_0_, bf16[1,8,144,128]{3,2,1,0:T(8,128)(2,1)S(1)} %collective-permute-done.10.refs_1_, bf16[1,8,144,128]{3,2,1,0:T(8,128)(2,1)S(1)} %collective-permute-done.13.refs_2_, ...), custom_call_target="tpu_custom_call" | custom-call | tf_op jit(solution)/shard_map/analysis/pallas_call | solution.py:330
  (52 shorter events, 14.8 us)
Async XLA Ops:
  23.8 3.5 %collective-permute-start = (bf16[4,8,144,128]{3,2,1,0:T(8,128)(2,1)S(1)}, bf16[4,8,144,128]{3,2,1,0:T(8,128)(2,1)S(1)}, u32[]{:S(2)}, u32[]{:S(2)}) collective-permute-start(bf16[4,8,144,128]{3,2,1,0:T(8,128)(2,1)S(1)} %partial_grams.8), channel_id=1, source_target_pairs={{0,8},{8,0},{16,24},{24,16},{1,9},{9,1},{17,25},{25,17},{2,10},{10... | collective-permute-start | bytes 3538952 | tf_op jit(solution)/shard_map/ppermute | solution.py:352
  27.6 9.5 %collective-permute-start.1 = (bf16[2,4,144,128]{3,2,1,0:T(8,128)(2,1)S(1)}, bf16[2,4,144,128]{3,2,1,0:T(8,128)(2,1)S(1)}, u32[]{:S(2)}, u32[]{:S(2)}) collective-permute-start(bf16[2,4,144,128]{3,2,1,0:T(8,128)(2,1)S(1)} %get-tuple-element.72), channel_id=1, source_target_pairs={{0,1},{1,0},{2,3},{3,2},{4,5},{5,4},{6,7},{7,6},{8,9},{9,8},{10,11... | collective-permute-start | bytes 884744 | tf_op jit(solution)/shard_map/ppermute | solution.py:352
  28.3 9.1 %collective-permute-start.2 = (bf16[2,4,144,128]{3,2,1,0:T(8,128)(2,1)S(1)}, bf16[2,4,144,128]{3,2,1,0:T(8,128)(2,1)S(1)}, u32[]{:S(2)}, u32[]{:S(2)}) collective-permute-start(bf16[2,4,144,128]{3,2,1,0:T(8,128)(2,1)S(1)} %get-tuple-element.74), channel_id=1, source_target_pairs={{0,16},{8,24},{16,0},{24,8},{1,17},{9,25},{17,1},{25,9},{2,18},{10... | collective-permute-start | bytes 884744 | tf_op jit(solution)/shard_map/ppermute | solution.py:352
  32.2 5.1 %collective-permute-start.3 = (bf16[4,8,144,128]{3,2,1,0:T(8,128)(2,1)S(1)}, bf16[4,8,144,128]{3,2,1,0:T(8,128)(2,1)S(1)}, u32[]{:S(2)}, u32[]{:S(2)}) collective-permute-start(bf16[4,8,144,128]{3,2,1,0:T(8,128)(2,1)S(1)} %partial_grams.10), channel_id=1, source_target_pairs={{0,8},{8,0},{16,24},{24,16},{1,9},{9,1},{17,25},{25,17},{2,10},{10... | collective-permute-start | bytes 3538952 | tf_op jit(solution)/shard_map/ppermute | solution.py:352
  37.8 11.5 %collective-permute-start.4 = (bf16[3,4,144,128]{3,2,1,0:T(8,128)(2,1)S(1)}, bf16[3,4,144,128]{3,2,1,0:T(8,128)(2,1)S(1)}, u32[]{:S(2)}, u32[]{:S(2)}) collective-permute-start(bf16[3,4,144,128]{3,2,1,0:T(8,128)(2,1)S(1)} %get-tuple-element.78), channel_id=1, source_target_pairs={{0,16},{8,24},{16,0},{24,8},{1,17},{9,25},{17,1},{25,9},{2,18},{10... | collective-permute-start | bytes 1327112 | tf_op jit(solution)/shard_map/ppermute | solution.py:352
  38.5 11.5 %collective-permute-start.5 = (bf16[3,4,144,128]{3,2,1,0:T(8,128)(2,1)S(1)}, bf16[3,4,144,128]{3,2,1,0:T(8,128)(2,1)S(1)}, u32[]{:S(2)}, u32[]{:S(2)}) collective-permute-start(bf16[3,4,144,128]{3,2,1,0:T(8,128)(2,1)S(1)} %get-tuple-element.80), channel_id=1, source_target_pairs={{0,1},{1,0},{2,3},{3,2},{4,5},{5,4},{6,7},{7,6},{8,9},{9,8},{10,11... | collective-permute-start | bytes 1327112 | tf_op jit(solution)/shard_map/ppermute | solution.py:352
  43.3 6.7 %collective-permute-start.6 = (bf16[4,8,144,128]{3,2,1,0:T(8,128)(2,1)S(1)}, bf16[4,8,144,128]{3,2,1,0:T(8,128)(2,1)S(1)}, u32[]{:S(2)}, u32[]{:S(2)}) collective-permute-start(bf16[4,8,144,128]{3,2,1,0:T(8,128)(2,1)S(1)} %partial_grams.12), channel_id=1, source_target_pairs={{0,8},{8,0},{16,24},{24,16},{1,9},{9,1},{17,25},{25,17},{2,10},{10... | collective-permute-start | bytes 3538952 | tf_op jit(solution)/shard_map/ppermute | solution.py:352
  50.5 16.2 %collective-permute-start.9 = (bf16[1,8,144,128]{3,2,1,0:T(8,128)(2,1)S(1)}, bf16[1,8,144,128]{3,2,1,0:T(8,128)(2,1)S(1)}, u32[]{:S(2)}, u32[]{:S(2)}) collective-permute-start(bf16[1,8,144,128]{3,2,1,0:T(8,128)(2,1)S(1)} %get-tuple-element.88), channel_id=1, source_target_pairs={{0,6},{1,7},{2,4},{3,5},{4,2},{5,3},{6,0},{7,1},{8,14},{9,15},{10,... | collective-permute-start | bytes 884744 | tf_op jit(solution)/shard_map/ppermute | solution.py:352
  51.1 10.4 %collective-permute-start.7 = (bf16[3,4,144,128]{3,2,1,0:T(8,128)(2,1)S(1)}, bf16[3,4,144,128]{3,2,1,0:T(8,128)(2,1)S(1)}, u32[]{:S(2)}, u32[]{:S(2)}) collective-permute-start(bf16[3,4,144,128]{3,2,1,0:T(8,128)(2,1)S(1)} %get-tuple-element.86), channel_id=1, source_target_pairs={{0,16},{8,24},{16,0},{24,8},{1,17},{9,25},{17,1},{25,9},{2,18},{10... | collective-permute-start | bytes 1327112 | tf_op jit(solution)/shard_map/ppermute | solution.py:352
  52.2 9.7 %collective-permute-start.8 = (bf16[3,4,144,128]{3,2,1,0:T(8,128)(2,1)S(1)}, bf16[3,4,144,128]{3,2,1,0:T(8,128)(2,1)S(1)}, u32[]{:S(2)}, u32[]{:S(2)}) collective-permute-start(bf16[3,4,144,128]{3,2,1,0:T(8,128)(2,1)S(1)} %get-tuple-element.87), channel_id=1, source_target_pairs={{0,1},{1,0},{2,3},{3,2},{4,5},{5,4},{6,7},{7,6},{8,9},{9,8},{10,11... | collective-permute-start | bytes 1327112 | tf_op jit(solution)/shard_map/ppermute | solution.py:352
  57.0 7.9 %collective-permute-start.14 = (bf16[4,8,144,128]{3,2,1,0:T(8,128)(2,1)S(1)}, bf16[4,8,144,128]{3,2,1,0:T(8,128)(2,1)S(1)}, u32[]{:S(2)}, u32[]{:S(2)}) collective-permute-start(bf16[4,8,144,128]{3,2,1,0:T(8,128)(2,1)S(1)} %partial_grams.14), channel_id=1, source_target_pairs={{0,8},{8,0},{16,24},{24,16},{1,9},{9,1},{17,25},{25,17},{2,10},{10... | collective-permute-start | bytes 3538952 | tf_op jit(solution)/shard_map/ppermute | solution.py:352
  61.9 20.1 %slice-start = ((s8[6291456]{0:T(1024)(128)(4,1)}), s8[4194304]{0:T(1024)(128)(4,1)S(1)}, s32[]{:S(2)}) async-start(s8[6291456]{0:T(1024)(128)(4,1)} %bitcast.6), calls=%async_computation.1 | async-start | bytes 8388608
  62.2 6.2 %collective-permute-start.11 = (bf16[1,4,144,128]{3,2,1,0:T(8,128)(2,1)S(1)}, bf16[1,4,144,128]{3,2,1,0:T(8,128)(2,1)S(1)}, u32[]{:S(2)}, u32[]{:S(2)}) collective-permute-start(bf16[1,4,144,128]{3,2,1,0:T(8,128)(2,1)S(1)} %get-tuple-element.99), channel_id=1, source_target_pairs={{0,16},{8,24},{16,0},{24,8},{1,17},{9,25},{17,1},{25,9},{2,18},{10... | collective-permute-start | bytes 442376 | tf_op jit(solution)/shard_map/ppermute | solution.py:352
  63.5 6.8 %collective-permute-start.12 = (bf16[1,4,144,128]{3,2,1,0:T(8,128)(2,1)S(1)}, bf16[1,4,144,128]{3,2,1,0:T(8,128)(2,1)S(1)}, u32[]{:S(2)}, u32[]{:S(2)}) collective-permute-start(bf16[1,4,144,128]{3,2,1,0:T(8,128)(2,1)S(1)} %get-tuple-element.101), channel_id=1, source_target_pairs={{0,1},{1,0},{2,3},{3,2},{4,5},{5,4},{6,7},{7,6},{8,9},{9,8},{10,11... | collective-permute-start | bytes 442376 | tf_op jit(solution)/shard_map/ppermute | solution.py:352
  65.2 8.9 %collective-permute-start.15 = (bf16[2,4,144,128]{3,2,1,0:T(8,128)(2,1)S(1)}, bf16[2,4,144,128]{3,2,1,0:T(8,128)(2,1)S(1)}, u32[]{:S(2)}, u32[]{:S(2)}) collective-permute-start(bf16[2,4,144,128]{3,2,1,0:T(8,128)(2,1)S(1)} %get-tuple-element.104), channel_id=1, source_target_pairs={{0,1},{1,0},{2,3},{3,2},{4,5},{5,4},{6,7},{7,6},{8,9},{9,8},{10,11... | collective-permute-start | bytes 884744 | tf_op jit(solution)/shard_map/ppermute | solution.py:352
  65.9 8.2 %collective-permute-start.16 = (bf16[2,4,144,128]{3,2,1,0:T(8,128)(2,1)S(1)}, bf16[2,4,144,128]{3,2,1,0:T(8,128)(2,1)S(1)}, u32[]{:S(2)}, u32[]{:S(2)}) collective-permute-start(bf16[2,4,144,128]{3,2,1,0:T(8,128)(2,1)S(1)} %get-tuple-element.106), channel_id=1, source_target_pairs={{0,16},{8,24},{16,0},{24,8},{1,17},{9,25},{17,1},{25,9},{2,18},{10... | collective-permute-start | bytes 884744 | tf_op jit(solution)/shard_map/ppermute | solution.py:352
  66.6 14.2 %collective-permute-start.10 = (bf16[1,8,144,128]{3,2,1,0:T(8,128)(2,1)S(1)}, bf16[1,8,144,128]{3,2,1,0:T(8,128)(2,1)S(1)}, u32[]{:S(2)}, u32[]{:S(2)}) collective-permute-start(bf16[1,8,144,128]{3,2,1,0:T(8,128)(2,1)S(1)} %get-tuple-element.97), channel_id=1, source_target_pairs={{0,4},{1,5},{2,6},{3,7},{4,0},{5,1},{6,2},{7,3},{8,12},{9,13},{10,... | collective-permute-start | bytes 884744 | tf_op jit(solution)/shard_map/ppermute | solution.py:352
  70.3 5.9 %copy-start = (f32[8,2,6,256]{3,1,2,0:T(2,128)S(1)}, f32[8,2,6,256]{3,1,2,0:T(2,128)}, u32[]{:S(2)}) copy-start(f32[8,2,6,256]{3,1,2,0:T(2,128)} %param.10) | copy-start | bytes 294916
  70.3 11.7 %slice-start.1 = ((s8[6291456]{0:T(1024)(128)(4,1)}), s8[2097152]{0:T(1024)(128)(4,1)S(1)}, s32[]{:S(2)}) async-start(s8[6291456]{0:T(1024)(128)(4,1)} %bitcast.6), calls=%async_computation.2 | async-start | bytes 4194304
  70.4 11.6 %collective-permute-start.13 = (bf16[1,8,144,128]{3,2,1,0:T(8,128)(2,1)S(1)}, bf16[1,8,144,128]{3,2,1,0:T(8,128)(2,1)S(1)}, u32[]{:S(2)}, u32[]{:S(2)}) collective-permute-start(bf16[1,8,144,128]{3,2,1,0:T(8,128)(2,1)S(1)} %add_partials.12), channel_id=1, source_target_pairs={{0,2},{1,3},{2,0},{3,1},{4,6},{5,7},{6,4},{7,5},{8,10},{9,11},{10,... | collective-permute-start | bytes 884744 | tf_op jit(solution)/shard_map/ppermute | solution.py:352
  74.2 5.2 %collective-permute-start.17 = (bf16[1,4,144,128]{3,2,1,0:T(8,128)(2,1)S(1)}, bf16[1,4,144,128]{3,2,1,0:T(8,128)(2,1)S(1)}, u32[]{:S(2)}, u32[]{:S(2)}) collective-permute-start(bf16[1,4,144,128]{3,2,1,0:T(8,128)(2,1)S(1)} %get-tuple-element.108), channel_id=1, source_target_pairs={{0,16},{8,24},{16,0},{24,8},{1,17},{9,25},{17,1},{25,9},{2,18},{10... | collective-permute-start | bytes 442376 | tf_op jit(solution)/shard_map/ppermute | solution.py:352
  75.3 5.1 %collective-permute-start.18 = (bf16[1,4,144,128]{3,2,1,0:T(8,128)(2,1)S(1)}, bf16[1,4,144,128]{3,2,1,0:T(8,128)(2,1)S(1)}, u32[]{:S(2)}, u32[]{:S(2)}) collective-permute-start(bf16[1,4,144,128]{3,2,1,0:T(8,128)(2,1)S(1)} %get-tuple-element.110), channel_id=1, source_target_pairs={{0,1},{1,0},{2,3},{3,2},{4,5},{5,4},{6,7},{7,6},{8,9},{9,8},{10,11... | collective-permute-start | bytes 442376 | tf_op jit(solution)/shard_map/ppermute | solution.py:352
